TPU v7x, 32 devices: a whole 2x2x4 slice. The times are simulated.
32 devices in a mesh: seq: 8 (over z, x), wt: 4 (over y, core).
Axes of the slice: x: 2, y: 2, z: 4, core: 2. Of those that a mesh axis runs over, the one named last changes fastest.
Arguments:
- tokens: bfloat16 [4096, 2560], P(('seq', 'wt'))
- norm1_gain: bfloat16 [2560], P(('seq', 'wt')), may hold values from 0.5 to 1.5
- x_weight: bfloat16 [2560, 2560], P('seq', 'wt'), may hold values from -0.125 to 0.125
- y_weight: bfloat16 [2560, 2560], P('seq', 'wt'), may hold values from -0.125 to 0.125
- conv_weight: bfloat16 [2560, 4], P(('seq', 'wt')), may hold values from -3 to 3
- conv_bias: bfloat16 [2560], P(('seq', 'wt')), may hold values from -2 to 2
- decay_gate_weight: bfloat16 [2560, 256], P(('seq', 'wt')), may hold values from -0.375 to 0.375
- decay_bias: bfloat16 [2560], P(('seq', 'wt')), may hold values from -4 to 4
- input_gate_weight: bfloat16 [2560, 256], P(('seq', 'wt')), may hold values from -0.375 to 0.375
- input_bias: bfloat16 [2560], P(('seq', 'wt')), may hold values from -4 to 4
- decay_param: float32 [2560], P(('seq', 'wt'))
- out_weight: bfloat16 [2560, 2560], P('seq', 'wt'), may hold values from -0.125 to 0.125
- norm2_gain: bfloat16 [2560], P(('seq', 'wt')), may hold values from 0.5 to 1.5
- gate_weight: bfloat16 [2560, 7680], P('seq', 'wt'), may hold values from -0.125 to 0.125
- up_weight: bfloat16 [2560, 7680], P('seq', 'wt'), may hold values from -0.125 to 0.125
- down_weight: bfloat16 [2560, 7680], P('seq', 'wt'), may hold values from -0.0625 to 0.0625
- out_grad: bfloat16 [4096, 2560], P(('seq', 'wt')), may hold values from -6 to 6
Outputs:
- block_out: bfloat16 [4096, 2560], P(('seq', 'wt'))
- tokens_grad: bfloat16 [4096, 2560], P(('seq', 'wt'))
- norm1_gain_grad: float32 [2560], P(('seq', 'wt'))
- x_weight_grad: float32 [2560, 2560], P('seq', 'wt')
- y_weight_grad: float32 [2560, 2560], P('seq', 'wt')
- conv_weight_grad: float32 [2560, 4], P(('seq', 'wt'))
- conv_bias_grad: float32 [2560], P(('seq', 'wt'))
- decay_gate_weight_grad: float32 [2560, 256], P(('seq', 'wt'))
- decay_bias_grad: float32 [2560], P(('seq', 'wt'))
- input_gate_weight_grad: float32 [2560, 256], P(('seq', 'wt'))
- input_bias_grad: float32 [2560], P(('seq', 'wt'))
- decay_param_grad: float32 [2560], P(('seq', 'wt'))
- out_weight_grad: float32 [2560, 2560], P('seq', 'wt')
- norm2_gain_grad: float32 [2560], P(('seq', 'wt'))
- gate_weight_grad: float32 [2560, 7680], P('seq', 'wt')
- up_weight_grad: float32 [2560, 7680], P('seq', 'wt')
- down_weight_grad: float32 [2560, 7680], P('seq', 'wt')
All inputs are finite; a program needn't handle non-finite values.
Results may differ from a plain program's by a relative error of at most 0.0109.
Values may be sent and summed in bfloat16 or wider, within the bound.
A program may use at most 256 MiB of HBM per device.

v0:
```python
import jax
import jax.numpy as jnp
from jax import lax
from jax.sharding import PartitionSpec as P

EPSILON = 1e-06
DECAY_SCALE = 8.0


def passed_along(x, axis, by):
    count = lax.axis_size(axis)
    pairs = [(i, i + by) for i in range(count) if 0 <= i + by < count]
    return lax.ppermute(x, axis, pairs)


def gelu_tanh(values):
    return jax.nn.gelu(values, approximate=True)


def compose(earlier, following):
    return (earlier[0] * following[0], following[0] * earlier[1] + following[1])


def token_rows(values):
    return lax.all_gather(values, "wt", axis=0, tiled=True)


def row_sums(values):
    return lax.psum_scatter(values, "wt", scatter_dimension=0, tiled=True)


def to_channels(values):
    return lax.all_to_all(values, "wt", split_axis=0, concat_axis=1, tiled=True)


def to_slices(values):
    return lax.all_to_all(values, "wt", split_axis=1, concat_axis=0, tiled=True)


def gather_weights(x_weight, y_weight, out_weight, gate_weight, up_weight, down_weight):
    return (
        lax.all_gather(x_weight, "seq", axis=0, tiled=True),
        lax.all_gather(y_weight, "seq", axis=0, tiled=True),
        lax.all_gather(out_weight, "seq", axis=0, tiled=True),
        lax.all_gather(gate_weight, "seq", axis=0, tiled=True),
        lax.all_gather(up_weight, "seq", axis=0, tiled=True),
        lax.all_gather(down_weight, "seq", axis=0, tiled=True),
    )


def contract_last(left_side, right_side):
    return lax.dot_general(
        left_side, right_side, (((1,), (1,)), ((), ())), preferred_element_type=jnp.float32
    )


def contract_rows(left_side, right_side):
    return lax.dot_general(
        left_side, right_side, (((0,), (0,)), ((), ())), preferred_element_type=jnp.float32
    )


def recurrence_terms(decay_pre, input_pre, decay_log, conv_float):
    log_decay = -DECAY_SCALE * jax.nn.softplus(-decay_log) * jax.nn.sigmoid(decay_pre)
    return (
        jnp.exp(log_decay),
        jnp.sqrt(-jnp.expm1(2.0 * log_decay)) * jax.nn.sigmoid(input_pre) * conv_float,
    )


def run_scan(retain, inflow, backward):
    lane_retain, lane_inflow = (
        lax.all_to_all(retain, ("seq", "wt"), split_axis=1, concat_axis=0, tiled=True),
        lax.all_to_all(inflow, ("seq", "wt"), split_axis=1, concat_axis=0, tiled=True),
    )
    held_state = lax.associative_scan(
        compose, (lane_retain, lane_inflow), reverse=backward, axis=0
    )[1]
    blank_row = jnp.zeros_like(held_state[:1])
    if backward:
        beside = jnp.concatenate([held_state[1:], blank_row], axis=0)
    else:
        beside = jnp.concatenate([blank_row, held_state[:-1]], axis=0)
    states, neighbor = (
        lax.all_to_all(held_state, ("seq", "wt"), split_axis=0, concat_axis=1, tiled=True),
        lax.all_to_all(beside, ("seq", "wt"), split_axis=0, concat_axis=1, tiled=True),
    )
    return (states, neighbor)


def norm_back(d_normed, normed, inverse, gain_row):
    scaled = d_normed * gain_row
    return inverse * (scaled - normed * jnp.mean(scaled * normed, axis=1, keepdims=True))


def per_device(
    tokens,
    norm1_gain,
    x_weight,
    y_weight,
    conv_weight,
    conv_bias,
    decay_gate_weight,
    decay_bias,
    input_gate_weight,
    input_bias,
    decay_param,
    out_weight,
    norm2_gain,
    gate_weight,
    up_weight,
    down_weight,
    out_grad,
):
    (
        gain_one,
        gain_two,
        taps,
        tap_bias,
        decay_rows,
        decay_shift,
        input_rows,
        input_shift,
        decay_log,
    ) = (
        lax.all_gather(norm1_gain.astype(jnp.float32), ("seq", "wt"), axis=0, tiled=True),
        lax.all_gather(norm2_gain.astype(jnp.float32), ("seq", "wt"), axis=0, tiled=True),
        lax.all_gather(conv_weight.astype(jnp.float32), ("seq", "wt"), axis=0, tiled=True),
        lax.all_gather(conv_bias.astype(jnp.float32), ("seq", "wt"), axis=0, tiled=True),
        lax.all_gather(decay_gate_weight.astype(jnp.float32), ("seq", "wt"), axis=0, tiled=True),
        lax.all_gather(decay_bias.astype(jnp.float32), ("seq", "wt"), axis=0, tiled=True),
        lax.all_gather(input_gate_weight.astype(jnp.float32), ("seq", "wt"), axis=0, tiled=True),
        lax.all_gather(input_bias.astype(jnp.float32), ("seq", "wt"), axis=0, tiled=True),
        lax.all_gather(decay_param, ("seq", "wt"), axis=0, tiled=True),
    )
    x_kernel, y_kernel, out_kernel, gate_kernel, up_kernel, down_kernel = gather_weights(
        x_weight, y_weight, out_weight, gate_weight, up_weight, down_weight
    )
    rows_dev = tokens.shape[0]
    lru_width = taps.shape[0]
    block_size = decay_rows.shape[1]
    head_count = lru_width // block_size
    reach_rows = taps.shape[1] - 1
    stream = tokens.astype(jnp.float32)
    inverse_one = lax.rsqrt(jnp.mean(stream * stream, axis=1, keepdims=True) + EPSILON)
    normed_one = stream * inverse_one
    group_one = token_rows((normed_one * gain_one).astype(jnp.bfloat16))
    x_branch = jnp.dot(group_one, x_kernel, preferred_element_type=jnp.float32).astype(jnp.bfloat16)
    y_before = jnp.dot(group_one, y_kernel, preferred_element_type=jnp.float32)
    y_gated, gelu_y_back = jax.vjp(gelu_tanh, y_before)
    x_full = to_channels(x_branch)
    rim_rows = passed_along(x_full[rows_dev - reach_rows :], ("seq", "wt"), 1)
    extended = jnp.concatenate([rim_rows, x_full], axis=0).astype(jnp.float32)
    conv_out = tap_bias + sum(
        (
            taps[:, offset] * extended[reach_rows - offset : reach_rows - offset + rows_dev]
            for offset in range(reach_rows + 1)
        )
    )
    conv_low = conv_out.astype(jnp.bfloat16)
    conv_heads = conv_low.reshape(rows_dev, head_count, block_size)
    decay_blocks = decay_rows.reshape(head_count, block_size, block_size).astype(jnp.bfloat16)
    input_blocks = input_rows.reshape(head_count, block_size, block_size).astype(jnp.bfloat16)
    decay_pre = (
        jnp.einsum(
            "thi,hij->thj", conv_heads, decay_blocks, preferred_element_type=jnp.float32
        ).reshape(rows_dev, lru_width)
        + decay_shift
    )
    input_pre = (
        jnp.einsum(
            "thi,hij->thj", conv_heads, input_blocks, preferred_element_type=jnp.float32
        ).reshape(rows_dev, lru_width)
        + input_shift
    )
    conv_float = conv_low.astype(jnp.float32)
    (retain, inflow), terms_back = jax.vjp(
        recurrence_terms, decay_pre, input_pre, decay_log, conv_float
    )
    states, before = run_scan(retain, inflow, False)
    lru_slices = to_slices(states.astype(jnp.bfloat16)).astype(jnp.float32)
    mixed_rows = (lru_slices * y_gated).astype(jnp.bfloat16)
    branch = row_sums(contract_last(mixed_rows, out_kernel))
    middle = stream + branch
    inverse_two = lax.rsqrt(jnp.mean(middle * middle, axis=1, keepdims=True) + EPSILON)
    normed_two = middle * inverse_two
    group_two = token_rows((normed_two * gain_two).astype(jnp.bfloat16))
    gate_pre = jnp.dot(group_two, gate_kernel, preferred_element_type=jnp.float32)
    up_pre = jnp.dot(group_two, up_kernel, preferred_element_type=jnp.float32)
    active, gelu_gate_back = jax.vjp(gelu_tanh, gate_pre)
    hidden = (active * up_pre).astype(jnp.bfloat16)
    feed = row_sums(contract_last(hidden, down_kernel))
    block_out = (middle + feed).astype(jnp.bfloat16)
    out_float = out_grad.astype(jnp.float32)
    grad_rows = token_rows(out_grad)
    d_hidden = jnp.dot(grad_rows, down_kernel, preferred_element_type=jnp.float32)
    d_up = (d_hidden * active).astype(jnp.bfloat16)
    d_gate = gelu_gate_back(d_hidden * up_pre)[0].astype(jnp.bfloat16)
    d_normed_two = row_sums(contract_last(d_gate, gate_kernel) + contract_last(d_up, up_kernel))
    gain_two_grad = jnp.sum(d_normed_two * normed_two, axis=0)
    d_middle = out_float + norm_back(d_normed_two, normed_two, inverse_two, gain_two)
    branch_rows = token_rows(d_middle.astype(jnp.bfloat16))
    d_mixed = jnp.dot(branch_rows, out_kernel, preferred_element_type=jnp.float32)
    d_lru = (d_mixed * y_gated).astype(jnp.bfloat16)
    d_y = gelu_y_back(d_mixed * lru_slices)[0].astype(jnp.bfloat16)
    d_states = to_channels(d_lru).astype(jnp.float32)
    after_states, next_states = run_scan(retain, retain * d_states, True)
    d_total = d_states + next_states
    d_decay_pre, d_input_pre, decay_log_grad, d_conv_direct = terms_back(
        (d_total * before, d_total)
    )
    decay_shift_grad = jnp.sum(d_decay_pre, axis=0)
    input_shift_grad = jnp.sum(d_input_pre, axis=0)
    d_decay_low = d_decay_pre.astype(jnp.bfloat16).reshape(rows_dev, head_count, block_size)
    d_input_low = d_input_pre.astype(jnp.bfloat16).reshape(rows_dev, head_count, block_size)
    d_conv = d_conv_direct + (
        jnp.einsum("thj,hij->thi", d_decay_low, decay_blocks, preferred_element_type=jnp.float32)
        + jnp.einsum("thj,hij->thi", d_input_low, input_blocks, preferred_element_type=jnp.float32)
    ).reshape(rows_dev, lru_width)
    decay_rows_grad = jnp.einsum(
        "thi,thj->hij", conv_heads, d_decay_low, preferred_element_type=jnp.float32
    ).reshape(lru_width, block_size)
    input_rows_grad = jnp.einsum(
        "thi,thj->hij", conv_heads, d_input_low, preferred_element_type=jnp.float32
    ).reshape(lru_width, block_size)
    tap_bias_grad = jnp.sum(d_conv, axis=0)
    taps_grad = jnp.stack(
        [
            jnp.sum(d_conv * extended[reach_rows - offset : reach_rows - offset + rows_dev], axis=0)
            for offset in range(reach_rows + 1)
        ],
        axis=1,
    )
    ahead = passed_along(d_conv[:reach_rows], ("seq", "wt"), -1)
    d_extended = jnp.concatenate([d_conv, ahead], axis=0)
    d_x_full = sum(
        (
            taps[:, offset] * d_extended[offset : offset + rows_dev]
            for offset in range(reach_rows + 1)
        )
    )
    d_x_branch = to_slices(d_x_full.astype(jnp.bfloat16))
    d_normed_one = row_sums(contract_last(d_x_branch, x_kernel) + contract_last(d_y, y_kernel))
    gain_one_grad = jnp.sum(d_normed_one * normed_one, axis=0)
    tokens_grad = (d_middle + norm_back(d_normed_one, normed_one, inverse_one, gain_one)).astype(
        jnp.bfloat16
    )
    weight_sums = (
        lax.psum_scatter(
            contract_rows(group_one, d_x_branch), "seq", scatter_dimension=0, tiled=True
        ),
        lax.psum_scatter(contract_rows(group_one, d_y), "seq", scatter_dimension=0, tiled=True),
        lax.psum_scatter(
            contract_rows(branch_rows, mixed_rows), "seq", scatter_dimension=0, tiled=True
        ),
        lax.psum_scatter(contract_rows(group_two, d_gate), "seq", scatter_dimension=0, tiled=True),
        lax.psum_scatter(contract_rows(group_two, d_up), "seq", scatter_dimension=0, tiled=True),
        lax.psum_scatter(contract_rows(grad_rows, hidden), "seq", scatter_dimension=0, tiled=True),
    )
    small_sums = (
        lax.psum_scatter(gain_one_grad, ("seq", "wt"), scatter_dimension=0, tiled=True),
        lax.psum_scatter(gain_two_grad, ("seq", "wt"), scatter_dimension=0, tiled=True),
        lax.psum_scatter(taps_grad, ("seq", "wt"), scatter_dimension=0, tiled=True),
        lax.psum_scatter(tap_bias_grad, ("seq", "wt"), scatter_dimension=0, tiled=True),
        lax.psum_scatter(decay_rows_grad, ("seq", "wt"), scatter_dimension=0, tiled=True),
        lax.psum_scatter(decay_shift_grad, ("seq", "wt"), scatter_dimension=0, tiled=True),
        lax.psum_scatter(input_rows_grad, ("seq", "wt"), scatter_dimension=0, tiled=True),
        lax.psum_scatter(input_shift_grad, ("seq", "wt"), scatter_dimension=0, tiled=True),
        lax.psum_scatter(decay_log_grad, ("seq", "wt"), scatter_dimension=0, tiled=True),
    )
    return (
        block_out,
        tokens_grad,
        small_sums[0],
        weight_sums[0],
        weight_sums[1],
        small_sums[2],
        small_sums[3],
        small_sums[4],
        small_sums[5],
        small_sums[6],
        small_sums[7],
        small_sums[8],
        weight_sums[2],
        small_sums[1],
        weight_sums[3],
        weight_sums[4],
        weight_sums[5],
    )


def solution(mesh):
    in_specs = (
        P(("seq", "wt"), None),
        P(("seq", "wt")),
        P("seq", "wt"),
        P("seq", "wt"),
        P(("seq", "wt"), None),
        P(("seq", "wt")),
        P(("seq", "wt"), None),
        P(("seq", "wt")),
        P(("seq", "wt"), None),
        P(("seq", "wt")),
        P(("seq", "wt")),
        P("seq", "wt"),
        P(("seq", "wt")),
        P("seq", "wt"),
        P("seq", "wt"),
        P("seq", "wt"),
        P(("seq", "wt"), None),
    )
    out_specs = (
        P(("seq", "wt"), None),
        P(("seq", "wt"), None),
        P(("seq", "wt")),
        P("seq", "wt"),
        P("seq", "wt"),
        P(("seq", "wt"), None),
        P(("seq", "wt")),
        P(("seq", "wt"), None),
        P(("seq", "wt")),
        P(("seq", "wt"), None),
        P(("seq", "wt")),
        P(("seq", "wt")),
        P("seq", "wt"),
        P(("seq", "wt")),
        P("seq", "wt"),
        P("seq", "wt"),
        P("seq", "wt"),
    )
    return jax.shard_map(
        per_device, mesh=mesh, in_specs=in_specs, out_specs=out_specs, check_vma=False
    )
```

profile of v0, /device:TPU:2, one launch (start us, length us, event | category | flops | bytes accessed | tf_op | source)
XLA Modules:
  0.0 4067.3 jit_solution(17203475673087078435)
XLA Ops:
  13.3 43.2 %all-reduce.63 = (f32[2560]{0:T(1024)S(1)}, f32[2560]{0:T(1024)S(1)}, f32[2560]{0:T(1024)S(1)}, f32[2560]{0:T(1024)S(1)}, f32[2560]{0:T(1024)S(1)}, /*index=5*/f32[2560]{0:T(1024)}) all-reduce(f32[2560]{0:T(1024)S(1)} %convert_dynamic-update-slice_fusion.3, ...), channel_id=1, replica_groups=mesh['seq'=8,'wt'=4] {'seq','wt'}, use_global_device_ids=true, to_apply=%add.52 | all-reduce | flops 15360 | bytes 122880
  82.5 63.3 %all-gather.16.cloned.1.call-done = bf16[2560,640]{1,0:T(8,128)(2,1)} async-done(((bf16[320,640]{1,0:T(8,128)(2,1)}), bf16[2560,640]{1,0:T(8,128)(2,1)}) %all-gather.16.cloned.1.call-update) | async-done | bytes 3276816 | tf_op jit(solution)/shard_map/all_gather | solution.py:42
  155.9 37.7 all-gather
  220.1 41.7 %all-gather.20.cloned.1.call-done = bf16[2560,256]{1,0:T(8,128)(2,1)} async-done(((bf16[80,256]{1,0:T(8,128)(2,1)}), bf16[2560,256]{1,0:T(8,128)(2,1)}) %all-gather.20.cloned.1.call-update) | async-done | bytes 1310736 | tf_op jit(solution)/shard_map/all_gather | solution.py:132
  283.0 23.4 slice.648
  361.5 23.8 slice.645
  617.4 23.7 slice.732
  780.1 26.7 pad.170
  806.8 26.5 pad.171
  886.4 48.8 %reduce-scatter.18.cloned.1.call-done = f32[128,2560]{1,0:T(8,128)} async-done(((f32[512,2560]{1,0:T(8,128)}), f32[128,2560]{1,0:T(8,128)}) %reduce-scatter.18.cloned.1.call-update) | async-done | bytes 1310736 | tf_op jit(solution)/shard_map/reduce_scatter | solution.py:29
  941.0 138.6 %all-gather.30.cloned.1.call-done = bf16[2560,1920]{1,0:T(8,128)(2,1)} async-done(((bf16[320,1920]{1,0:T(8,128)(2,1)}), bf16[2560,1920]{1,0:T(8,128)(2,1)}) %all-gather.30.cloned.1.call-update) | async-done | bytes 9830416 | tf_op jit(solution)/shard_map/all_gather | solution.py:46
  1079.6 26.9 all-gather.26.cloned.1.call-done
  1118.0 132.8 %all-gather.28.cloned.1.call-done = bf16[2560,1920]{1,0:T(8,128)(2,1)} async-done(((bf16[320,1920]{1,0:T(8,128)(2,1)}), bf16[2560,1920]{1,0:T(8,128)(2,1)}) %all-gather.28.cloned.1.call-update) | async-done | bytes 9830416 | tf_op jit(solution)/shard_map/all_gather | solution.py:45
  1277.1 144.2 %all-gather.32.cloned.1.call-done = bf16[2560,1920]{1,0:T(8,128)(2,1)} async-done(((bf16[320,1920]{1,0:T(8,128)(2,1)}), bf16[2560,1920]{1,0:T(8,128)(2,1)}) %all-gather.32.cloned.1.call-update) | async-done | bytes 9830416 | tf_op jit(solution)/shard_map/all_gather | solution.py:47
  1456.1 50.2 %reduce-scatter.22.cloned.1.call-done = f32[128,2560]{1,0:T(8,128)} async-done(((f32[512,2560]{1,0:T(8,128)}), f32[128,2560]{1,0:T(8,128)}) %reduce-scatter.22.cloned.1.call-update) | async-done | bytes 1310736 | tf_op jit(solution)/shard_map/reduce_scatter | solution.py:29
  1510.5 25.7 all-gather.36.cloned.1.call-done
  1629.2 23.4 slice.826
  1652.6 23.4 slice.739
  1676.0 23.4 slice.737
  2026.6 26.4 pad.250
  2053.0 26.7 pad.344
  2111.0 28.7 all-to-all-done.7
  2312.8 58.3 %reduce-scatter.24.cloned.1.call-done = f32[128,2560]{1,0:T(8,128)} async-done(((f32[512,2560]{1,0:T(8,128)}), f32[128,2560]{1,0:T(8,128)}) %reduce-scatter.24.cloned.1.call-update) | async-done | bytes 1310736 | tf_op jit(solution)/shard_map/reduce_scatter | solution.py:29
  2372.8 42.2 %all-reduce.62 = (f32[2560]{0:T(1024)S(1)}, f32[2560]{0:T(1024)S(1)}, f32[2560]{0:T(1024)S(1)}, f32[2560]{0:T(1024)S(1)}, f32[2560]{0:T(1024)S(1)}, /*index=5*/f32[2560]{0:T(1024)S(1)}) all-reduce(f32[2560]{0:T(1024)S(1)} %get-tuple-element.93, f32[2560]{0:T(1024)S(1)} %reduce_sum.142, ...), channel_id=6, replica_groups=mesh['seq'=8,'wt'=4] {'seq','wt'}, use_global_device_ids=true, to_apply=%region_9.10.clone | all-reduce | flops 15360 | bytes 122880
  2429.4 126.9 %reduce-scatter.32.cloned.1.call-done = f32[80,256]{1,0:T(8,128)} async-done(((f32[2560,256]{1,0:T(8,128)}), f32[80,256]{1,0:T(8,128)}) %reduce-scatter.32.cloned.1.call-update) | async-done | bytes 81936 | tf_op jit(solution)/shard_map/reduce_scatter | solution.py:267
  2556.4 136.7 %reduce-scatter.30.cloned.1.call-done = f32[80,256]{1,0:T(8,128)} async-done(((f32[2560,256]{1,0:T(8,128)}), f32[80,256]{1,0:T(8,128)}) %reduce-scatter.30.cloned.1.call-update) | async-done | bytes 81936 | tf_op jit(solution)/shard_map/reduce_scatter | solution.py:265
  2693.1 132.0 %reduce-scatter.34.cloned.1.call-done = f32[320,640]{1,0:T(8,128)} async-done(((f32[2560,640]{1,0:T(8,128)}), f32[320,640]{1,0:T(8,128)}) %reduce-scatter.34.cloned.1.call-update) | async-done | bytes 819216 | tf_op jit(solution)/shard_map/reduce_scatter | solution.py:253
  2825.1 125.0 %reduce-scatter.28.cloned.1.call-done = f32[320,640]{1,0:T(8,128)} async-done(((f32[2560,640]{1,0:T(8,128)}), f32[320,640]{1,0:T(8,128)}) %reduce-scatter.28.cloned.1.call-update) | async-done | bytes 819216 | tf_op jit(solution)/shard_map/reduce_scatter | solution.py:252
  2950.1 125.4 %reduce-scatter.26.cloned.1.call-done = f32[320,640]{1,0:T(8,128)} async-done(((f32[2560,640]{1,0:T(8,128)}), f32[320,640]{1,0:T(8,128)}) %reduce-scatter.26.cloned.1.call-update) | async-done | bytes 819216 | tf_op jit(solution)/shard_map/reduce_scatter | solution.py:249
  3075.5 328.3 %reduce-scatter.42.cloned.1.call-done = f32[320,1920]{1,0:T(8,128)} async-done(((f32[2560,1920]{1,0:T(8,128)}), f32[320,1920]{1,0:T(8,128)}) %reduce-scatter.42.cloned.1.call-update) | async-done | bytes 2457616
  3403.8 328.2 %reduce-scatter.38.cloned.1.call-done = f32[320,1920]{1,0:T(8,128)} async-done(((f32[2560,1920]{1,0:T(8,128)}), f32[320,1920]{1,0:T(8,128)}) %reduce-scatter.38.cloned.1.call-update) | async-done | bytes 2457616 | tf_op jit(solution)/shard_map/reduce_scatter | solution.py:257
  3732.0 328.3 %reduce-scatter.36.cloned.1.call-done = f32[320,1920]{1,0:T(8,128)} async-done(((f32[2560,1920]{1,0:T(8,128)}), f32[320,1920]{1,0:T(8,128)}) %reduce-scatter.36.cloned.1.call-update) | async-done | bytes 2457616 | tf_op jit(solution)/shard_map/reduce_scatter | solution.py:256
  (602 shorter events, 1290.9 us)
Async XLA Ops:
  7.2 75.3 %all-gather.14.cloned.1.call-start = ((), (), s32[]{:S(2)}) async-start(), calls=%async_computation.23 | async-start | bytes 3276800 | tf_op jit(solution)/shard_map/all_gather | solution.py:25
  57.6 88.2 %all-gather.16.cloned.1.call-start = ((), (), s32[]{:S(2)}) async-start(), calls=%async_computation.24 | async-start | bytes 3686400 | tf_op jit(solution)/shard_map/all_gather | solution.py:42
  58.4 150.0 %all-gather.18.cloned.1.call-start = ((), (), s32[]{:S(2)}) async-start(), calls=%async_computation.25 | async-start | bytes 1351680 | tf_op jit(solution)/shard_map/all_gather | solution.py:130
  59.1 202.7 %all-gather.20.cloned.1.call-start = ((), (), s32[]{:S(2)}) async-start(), calls=%async_computation.26 | async-start | bytes 1351680 | tf_op jit(solution)/shard_map/all_gather | solution.py:132
  151.8 42.0 %all-to-all-start = ((bf16[4,128,640]{1,2,0:T(8,128)(2,1)}), bf16[4,128,640]{1,2,0:T(8,128)(2,1)S(1)}, u32[]{:S(2)}, u32[]{:S(2)}) async-start(bf16[4,128,640]{1,2,0:T(8,128)(2,1)} %copy.123), calls=%async_computation | async-start | bytes 1310720 | tf_op jit(solution)/shard_map/all_to_all | solution.py:33
  155.3 716.9 %all-gather.22.cloned.1.call-start = ((), (), s32[]{:S(2)}) async-start(), calls=%async_computation.27 | async-start | bytes 3686400 | tf_op jit(solution)/shard_map/all_gather | solution.py:43
  217.0 58.5 %all-to-all-start.2 = ((f32[128,32,80]{0,2,1:T(8,128)}), f32[128,32,80]{0,2,1:T(8,128)}, u32[]{:S(2)}, u32[]{:S(2)}) async-start(f32[128,32,80]{0,2,1:T(8,128)} %multiply_exponential_fusion), calls=%async_computation.2 | async-start | bytes 2621440 | tf_op jit(solution)/shard_map/all_to_all | solution.py:73
  275.5 60.2 %all-to-all-start.1 = ((f32[128,32,80]{0,2,1:T(8,128)}), f32[128,32,80]{0,2,1:T(8,128)}, u32[]{:S(2)}, u32[]{:S(2)}) async-start(f32[128,32,80]{0,2,1:T(8,128)} %bitcast.250), calls=%async_computation.1 | async-start | bytes 2621440 | tf_op jit(solution)/shard_map/all_to_all | solution.py:74
  279.6 599.2 %all-gather.24.cloned.1.call-start = ((), (), s32[]{:S(2)}) async-start(), calls=%async_computation.28 | async-start | bytes 3686400 | tf_op jit(solution)/shard_map/all_gather | solution.py:44
  280.2 655.0 %reduce-scatter.18.cloned.1.call-start = ((), (), s32[]{:S(2)}) async-start(), calls=%async_computation.29 | async-start | bytes 6553600 | tf_op jit(solution)/shard_map/reduce_scatter | solution.py:29
  885.6 194.0 %all-gather.30.cloned.1.call-start = ((), (), s32[]{:S(2)}) async-start(), calls=%async_computation.32 | async-start | bytes 11059200 | tf_op jit(solution)/shard_map/all_gather | solution.py:46
  886.4 220.2 %all-gather.26.cloned.1.call-start = ((), (), s32[]{:S(2)}) async-start(), calls=%async_computation.30 | async-start | bytes 3276800 | tf_op jit(solution)/shard_map/all_gather | solution.py:25
  939.1 311.7 %all-gather.28.cloned.1.call-start = ((), (), s32[]{:S(2)}) async-start(), calls=%async_computation.31 | async-start | bytes 11059200 | tf_op jit(solution)/shard_map/all_gather | solution.py:45
  939.6 337.5 %all-gather.34.cloned.1.call-start = ((), (), s32[]{:S(2)}) async-start(), calls=%async_computation.35 | async-start | bytes 3276800 | tf_op jit(solution)/shard_map/all_gather | solution.py:25
  940.4 481.0 %all-gather.32.cloned.1.call-start = ((), (), s32[]{:S(2)}) async-start(), calls=%async_computation.33 | async-start | bytes 11059200 | tf_op jit(solution)/shard_map/all_gather | solution.py:47
  941.0 565.4 %reduce-scatter.22.cloned.1.call-start = ((), (), s32[]{:S(2)}) async-start(), calls=%async_computation.36 | async-start | bytes 6553600 | tf_op jit(solution)/shard_map/reduce_scatter | solution.py:29
  1455.7 80.5 %all-gather.36.cloned.1.call-start = ((), (), s32[]{:S(2)}) async-start(), calls=%async_computation.37 | async-start | bytes 3276800 | tf_op jit(solution)/shard_map/all_gather | solution.py:25
  1561.6 58.2 %all-to-all-start.6 = ((f32[128,32,80]{0,2,1:T(8,128)}), f32[128,32,80]{0,2,1:T(8,128)}, u32[]{:S(2)}, u32[]{:S(2)}) async-start(f32[128,32,80]{0,2,1:T(8,128)} %fusion.167), calls=%async_computation.9 | async-start | bytes 2621440 | tf_op jit(solution)/shard_map/all_to_all | solution.py:74
  1619.8 482.4 %all-to-all-start.8 = ((f32[32,128,80]{1,2,0:T(8,128)}), f32[32,128,80]{1,2,0:T(8,128)}, u32[]{:S(2)}, u32[]{:S(2)}) async-start(f32[32,128,80]{1,2,0:T(8,128)} %copy_bitcast_fusion.3), calls=%async_computation.11 | async-start | bytes 2621440 | tf_op jit(solution)/shard_map/all_to_all | solution.py:86
  2102.1 37.5 all-to-all-start.7
  2179.5 15.9 all-to-all-start.9
  2184.3 127.1 %reduce-scatter.40.cloned.1.call-start = ((), (), s32[]{:S(2)}) async-start(), calls=%async_computation.46 | async-start | bytes 1351680
  2186.0 185.1 %reduce-scatter.24.cloned.1.call-start = ((), (), s32[]{:S(2)}) async-start(), calls=%async_computation.38 | async-start | bytes 6553600 | tf_op jit(solution)/shard_map/reduce_scatter | solution.py:29
  2204.7 220.9 %reduce-scatter.20.cloned.1.call-start = ((), (), s32[]{:S(2)}) async-start(), calls=%async_computation.34 | async-start | bytes 6553600 | tf_op jit(solution)/shard_map/reduce_scatter | solution.py:29
  2216.0 340.4 %reduce-scatter.32.cloned.1.call-start = ((), (), s32[]{:S(2)}) async-start(), calls=%async_computation.42 | async-start | bytes 2703360 | tf_op jit(solution)/shard_map/reduce_scatter | solution.py:267
  2219.3 473.7 %reduce-scatter.30.cloned.1.call-start = ((), (), s32[]{:S(2)}) async-start(), calls=%async_computation.41 | async-start | bytes 2703360 | tf_op jit(solution)/shard_map/reduce_scatter | solution.py:265
  2222.4 602.7 %reduce-scatter.34.cloned.1.call-start = ((), (), s32[]{:S(2)}) async-start(), calls=%async_computation.43 | async-start | bytes 7372800 | tf_op jit(solution)/shard_map/reduce_scatter | solution.py:253
  2230.2 719.9 %reduce-scatter.28.cloned.1.call-start = ((), (), s32[]{:S(2)}) async-start(), calls=%async_computation.40 | async-start | bytes 7372800 | tf_op jit(solution)/shard_map/reduce_scatter | solution.py:252
  2236.9 838.6 %reduce-scatter.26.cloned.1.call-start = ((), (), s32[]{:S(2)}) async-start(), calls=%async_computation.39 | async-start | bytes 7372800 | tf_op jit(solution)/shard_map/reduce_scatter | solution.py:249
  2243.0 1160.8 %reduce-scatter.42.cloned.1.call-start = ((), (), s32[]{:S(2)}) async-start(), calls=%async_computation.47 | async-start | bytes 22118400
  2276.6 1455.5 %reduce-scatter.38.cloned.1.call-start = ((), (), s32[]{:S(2)}) async-start(), calls=%async_computation.45 | async-start | bytes 22118400 | tf_op jit(solution)/shard_map/reduce_scatter | solution.py:257
  2289.6 1770.8 %reduce-scatter.36.cloned.1.call-start = ((), (), s32[]{:S(2)}) async-start(), calls=%async_computation.44 | async-start | bytes 22118400 | tf_op jit(solution)/shard_map/reduce_scatter | solution.py:256
  (77 other events, 2359.7 us)
Sparse Core Ops, SparseCore 0:
  57.8 24.7 all-gather.13
  84.7 61.0 all-gather.15
  148.7 53.8 all-gather.17
  205.3 56.5 all-gather.19
  263.9 79.4 all-gather.21
  345.4 59.8 all-gather.23
  885.7 49.4 reduce-scatter.17
  937.7 141.9 all-gather.29
  1081.9 24.6 all-gather.25
  1108.8 141.9 all-gather.27
  1252.4 24.6 all-gather.33
  1279.4 141.9 all-gather.31
  1455.8 50.4 reduce-scatter.21
  1510.6 25.5 all-gather.35
  2187.1 124.2 reduce-scatter.39
  2313.9 57.1 reduce-scatter.23
  2373.5 52.0 reduce-scatter.19
  2428.4 127.9 reduce-scatter.31
  2559.3 133.7 reduce-scatter.29
  2697.6 127.4 reduce-scatter.33
  2829.3 120.7 reduce-scatter.27
  2954.7 120.7 reduce-scatter.25
  3080.0 323.7 reduce-scatter.41
  3408.1 323.8 reduce-scatter.37
  3736.5 323.7 reduce-scatter.35
where the time goes:
time: 4090 us; the launch traced here: 4070 us
  waiting for transfers between devices  2470 us (60%)
  local copies, waits for them, and re-layouts  1040 us (25%)
  blocking collectives  170 us (4%)
  matrix products  169 us (4%)
  other arithmetic  159 us (4%)
    slice x141, local copies, waits for them, and re-layouts, run_scan(): lax.associative_scan(compose, (lane_retain, lane_inflow), reverse=backwar...  690 us
    unnamed x27, waiting for transfers between devices  344 us
    reduce_scatter x1, waiting for transfers between devices, per_device(): lax.psum_scatter(contract_rows(group_two, d_gate), 'seq', scatter_dimensi...  328 us
    reduce_scatter x1, waiting for transfers between devices, per_device(): lax.psum_scatter(contract_rows(group_two, d_up), 'seq', scatter_dimension...  328 us
    pad x42, local copies, waits for them, and re-layouts, run_scan(): lax.associative_scan(compose, (lane_retain, lane_inflow), reverse=backwar...  186 us
    reduce_scatter x4, waiting for transfers between devices, row_sums(): return lax.psum_scatter(values, 'wt', scatter_dimension=0, tiled=True)  164 us
    all_gather x1, waiting for transfers between devices, gather_weights(): lax.all_gather(down_weight, 'seq', axis=0, tiled=True)  144 us
    all_gather x1, waiting for transfers between devices, gather_weights(): lax.all_gather(up_weight, 'seq', axis=0, tiled=True)  139 us
  transfers between devices with their start and end apart: 34, of which 27 were waited for; matrix products, arithmetic and copies ran while one was open for 31% of the time, Pallas kernels for 0%

commit v1 on v0

v1 whole, which is shorter than its diff:
```python
import functools

import jax
import jax.numpy as jnp
from jax import lax
from jax.experimental import pallas as pl
from jax.experimental.pallas import tpu as pltpu
from jax.sharding import PartitionSpec as P

EPSILON = 1e-06
DECAY_SCALE = 8.0
Z = 4
C = 2
LANES = 128
F32 = jnp.float32
BF16 = jnp.bfloat16


def gelu_tanh(values):
    return jax.nn.gelu(values, approximate=True)


def sizes():
    return lax.axis_size("seq") // Z, lax.axis_size("wt") // C


def places():
    inner, outer = sizes()
    s, w = lax.axis_index("seq"), lax.axis_index("wt")
    return s // inner, s % inner, w // C, w % C


def after(value, *earlier):
    return lax.optimization_barrier((value, *earlier))[0]


def z_move(value, by, senders):
    inner, _ = sizes()
    pairs = [(z * inner + x, (z + by) % Z * inner + x) for z in senders for x in range(inner)]
    return lax.ppermute(value, "seq", pairs)


def x_move(value, by):
    inner, _ = sizes()
    pairs = [(z * inner + x, z * inner + (x + by) % inner) for z in range(Z) for x in range(inner)]
    return lax.ppermute(value, "seq", pairs)


def y_move(value, by):
    _, outer = sizes()
    pairs = [(y * C + c, (y + by) % outer * C + c) for y in range(outer) for c in range(C)]
    return lax.ppermute(value, "wt", pairs)


def c_swap(value):
    _, outer = sizes()
    pairs = [(y * C + c, y * C + 1 - c) for y in range(outer) for c in range(C)]
    return lax.ppermute(value, "wt", pairs)


def line_gather(value):
    z = places()[0]
    up, down = [value], [value]
    for k in range(1, Z):
        up.append(z_move(up[-1], 1, range(k - 1, Z - 1)))
        down.append(z_move(down[-1], -1, range(1, Z - k + 1)))
    return [value] + [jnp.where(z >= k, up[k], down[Z - k]) for k in range(1, Z)]


def line_scatter(parts):
    up = down = None
    for step in range(1, Z):
        rising = parts[step] if up is None else parts[step] + up
        falling = parts[Z - step] if down is None else parts[Z - step] + down
        up = z_move(rising.astype(BF16), 1, range(0, step)).astype(F32)
        down = z_move(falling.astype(BF16), -1, range(Z - step, Z)).astype(F32)
    return parts[0] + up + down


def pick(value, index, axis):
    return lax.dynamic_index_in_dim(value, index, axis, keepdims=False)


def put(buffer, value, starts):
    return lax.dynamic_update_slice(buffer, value, starts)


def contract_last(left_side, right_side):
    return lax.dot_general(
        left_side, right_side, (((1,), (1,)), ((), ())), preferred_element_type=F32
    )


def contract_rows(left_side, right_side):
    return lax.dot_general(
        left_side, right_side, (((0,), (0,)), ((), ())), preferred_element_type=F32
    )


def multiply(left_side, right_side):
    return jnp.dot(left_side, right_side, preferred_element_type=F32)


def seq_gather(unit):
    inner, _ = sizes()
    z, x = places()[:2]
    blocks = []
    for k, block in enumerate(line_gather(unit)):
        blocks.append(((z - k) % Z, x, block))
        for j in range(1, inner):
            blocks.append(((z - k) % Z, (x - j) % inner, x_move(block, j)))
    return blocks


def assembled(blocks, rows):
    inner, _ = sizes()
    width = blocks[0][2].shape[1]
    buffer = jnp.zeros((Z, inner, rows.stop - rows.start, width), blocks[0][2].dtype)
    for z_at, x_at, block in blocks:
        buffer = put(buffer, block[rows][None, None], (z_at, x_at, 0, 0))
    return buffer


def seq_scatter(total):
    inner, _ = sizes()
    z, x = places()[:2]
    total = total.reshape(Z, inner, -1, total.shape[1])
    kept = pick(total, x, 1)
    for j in range(1, inner):
        kept = kept + x_move(pick(total, (x + j) % inner, 1).astype(BF16), j).astype(F32)
    return line_scatter([pick(kept, (z - k) % Z, 0) for k in range(Z)])


def z_exchange(weight):
    z = places()[0]
    rows, width = weight.shape
    share = -(-width // (Z * LANES)) * LANES
    padded = jnp.pad(weight, ((0, 0), (0, Z * share - width)))

    def cut(at):
        return lax.dynamic_slice(padded, (0, at * share), (rows, share))

    buffer = put(jnp.zeros((Z, rows, share), weight.dtype), cut(z)[None], (z, 0, 0))
    for k in range(1, Z):
        moved = z_move(cut((z + k) % Z), k, range(Z))
        buffer = put(buffer, moved[None], ((z - k) % Z, 0, 0))
    return buffer


def plane_gather(unit, x_first):
    inner, outer = sizes()
    x = places()[1]
    _, rows, share = unit.shape
    grid = {(0, 0): unit}
    if x_first:
        for j in range(1, inner):
            grid[j, 0] = x_move(unit, j)
        for j in range(inner):
            for i in range(1, outer):
                grid[j, i] = y_move(grid[j, 0], i)
    else:
        for i in range(1, outer):
            grid[0, i] = y_move(unit, i)
        for i in range(outer):
            for j in range(1, inner):
                grid[j, i] = x_move(grid[0, i], j)
    buffer = jnp.zeros((Z, inner, rows, outer * share), unit.dtype)
    for (j, i), block in grid.items():
        buffer = put(buffer, block[:, None], (0, (x - j) % inner, 0, i * share))
    return buffer.reshape(Z * inner * rows, outer * share)


def plane_scatter(total, width, x_first):
    inner, outer = sizes()
    z, x = places()[:2]
    share = total.shape[1] // outer
    total = total.reshape(Z, inner, -1, outer * share)
    rows = total.shape[2]

    def over_x(value):
        kept = pick(value, x, 1)
        for j in range(1, inner):
            kept = kept + x_move(pick(value, (x + j) % inner, 1).astype(BF16), j).astype(F32)
        return kept

    def over_y(value):
        kept = value[..., :share]
        for i in range(1, outer):
            sent = value[..., i * share : (i + 1) * share].astype(BF16)
            kept = kept + y_move(sent, -i).astype(F32)
        return kept

    kept = over_y(over_x(total)) if x_first else over_x(over_y(total))
    kept = kept.astype(BF16)
    buffer = put(jnp.zeros((rows, Z * share), BF16), pick(kept, z, 0), (0, z * share))
    for k in range(1, Z):
        moved = z_move(pick(kept, (z + k) % Z, 0), k, range(Z))
        buffer = put(buffer, moved, (0, (z - k) % Z * share))
    return buffer[:, :width].astype(F32)


def wt_gather(value):
    _, outer = sizes()
    _, _, y, c = places()
    rows, width = value.shape
    other = c_swap(value)
    pair = jnp.where(
        c == 0, jnp.concatenate([value, other]), jnp.concatenate([other, value])
    )
    buffer = put(jnp.zeros((outer, C * rows, width), value.dtype), pair[None], (y, 0, 0))
    for i in range(1, outer):
        buffer = put(buffer, y_move(pair, i)[None], ((y - i) % outer, 0, 0))
    return buffer.reshape(outer * C * rows, width)


def wt_scatter(product_of, *sides):
    _, outer = sizes()
    _, _, y, c = places()

    def chosen(at):
        cut = [side.reshape(outer, C, -1, side.shape[1]) for side in sides]
        return [pick(side, at, 1).reshape(-1, side.shape[3]) for side in cut]

    sent = c_swap(product_of(*chosen(1 - c)))
    kept = product_of(*chosen(c)) + sent
    kept = kept.reshape(outer, -1, kept.shape[1])
    total = pick(kept, y, 0)
    for i in range(1, outer):
        total = total + y_move(pick(kept, (y + i) % outer, 0).astype(BF16), i).astype(F32)
    return total


def group_gather(value):
    blocks = line_gather(value)
    return jnp.concatenate(blocks + [c_swap(block) for block in blocks])


def group_scatter(product_of, *sides):
    half = sides[0].shape[0] // 2
    sent = c_swap(product_of(*[side[half:] for side in sides]).astype(BF16))
    kept = product_of(*[side[:half] for side in sides]) + sent.astype(F32)
    rows = half // Z
    return line_scatter([kept[k * rows : (k + 1) * rows] for k in range(Z)])


def scan_kernel(backward, a_ref, b_ref, h_ref, p_ref):
    rows, width = a_ref.shape
    segments = 8
    length = rows // segments

    def step(i, carried):
        held, product = carried
        at = length - 1 - i if backward else i
        where = pl.ds(at, segments, stride=length)
        factor = a_ref[where, :]
        held = factor * held + b_ref[where, :]
        product = factor * product
        h_ref[where, :] = held
        p_ref[where, :] = product
        return held, product

    held, product = lax.fori_loop(
        0, length, step, (jnp.zeros((segments, width), F32), jnp.ones((segments, width), F32)),
        unroll=4,
    )
    carry = jnp.zeros((1, width), F32)
    scale = jnp.ones((1, width), F32)
    order = range(segments - 1, -1, -1) if backward else range(segments)
    for at in order:
        if at != order[0]:
            part = pl.ds(at * length, length)
            local = p_ref[part, :]
            h_ref[part, :] = h_ref[part, :] + local * carry
            p_ref[part, :] = local * scale
        carry = held[at : at + 1] + product[at : at + 1] * carry
        scale = product[at : at + 1] * scale


def local_scan(factor, inflow, backward):
    shape = jax.ShapeDtypeStruct(factor.shape, F32)
    column = pl.BlockSpec((factor.shape[0], LANES), lambda i: (0, i))
    return pl.pallas_call(
        functools.partial(scan_kernel, backward),
        out_shape=(shape, shape),
        grid=(factor.shape[1] // LANES,),
        in_specs=[column] * 2,
        out_specs=(column,) * 2,
        name="scan_back" if backward else "scan_ahead",
    )(factor, inflow)


def full_scan(factor, inflow, backward):
    count = lax.axis_size("seq")
    held, product = local_scan(factor, inflow, backward)
    end = slice(0, 1) if backward else slice(held.shape[0] - 1, None)
    ends = jnp.concatenate([product[end], held[end]])
    sign = -1 if backward else 1
    carry = jnp.zeros_like(held[:1])
    for k in range(count - 1, 0, -1):
        pairs = [(s, s + sign * k) for s in range(count) if 0 <= s + sign * k < count]
        moved = lax.ppermute(ends, "seq", pairs)
        carry = moved[:1] * carry + moved[1:]
    return held + product * carry, carry


def recurrence_terms(decay_pre, input_pre, decay_log, conv_float):
    log_decay = -DECAY_SCALE * jax.nn.softplus(-decay_log) * jax.nn.sigmoid(decay_pre)
    return (
        jnp.exp(log_decay),
        jnp.sqrt(-jnp.expm1(2.0 * log_decay)) * jax.nn.sigmoid(input_pre) * conv_float,
    )


def norm_back(d_normed, normed, inverse, gain_row):
    scaled = d_normed * gain_row
    return inverse * (scaled - normed * jnp.mean(scaled * normed, axis=1, keepdims=True))


def normed_rows(stream):
    inverse = lax.rsqrt(jnp.mean(stream * stream, axis=1, keepdims=True) + EPSILON)
    return stream * inverse, inverse


def per_device(
    tokens,
    norm1_gain,
    x_weight,
    y_weight,
    conv_weight,
    conv_bias,
    decay_gate_weight,
    decay_bias,
    input_gate_weight,
    input_bias,
    decay_param,
    out_weight,
    norm2_gain,
    gate_weight,
    up_weight,
    down_weight,
    out_grad,
):
    seq, wt = lax.axis_size("seq"), lax.axis_size("wt")
    inner, outer = sizes()
    z, x, y, c = places()
    w = lax.axis_index("wt")
    rows_dev, width = tokens.shape
    weight_rows, lru_cols = x_weight.shape
    chunk, block = decay_gate_weight.shape
    half = block // 2
    full = lru_cols - half
    taps_count = conv_weight.shape[1]
    reach = taps_count - 1
    hidden_cols = gate_weight.shape[1]

    def turned(value, axis):
        return jnp.where(c == 0, value, jnp.roll(value, -half, axis))

    def turned_back(value, axis):
        return jnp.where(c == 0, value, jnp.roll(value, half, axis))

    def in_order(own, partner, axis):
        return jnp.where(
            c == 0,
            jnp.concatenate([own, partner], axis),
            jnp.concatenate([partner, own], axis),
        )

    vectors = jnp.stack(
        [v.astype(F32) for v in (norm1_gain, norm2_gain, conv_bias, decay_bias, input_bias)]
        + [decay_param]
        + [conv_weight[:, k].astype(F32) for k in range(taps_count)]
    )
    vectors = lax.all_gather(vectors, ("seq", "wt"), axis=1, tiled=True)
    gain_one, gain_two = vectors[0], vectors[1]
    own_vectors = turned(
        lax.dynamic_slice(vectors[2:], (0, w * lru_cols), (taps_count + 4, lru_cols)), 1
    )
    tap_bias, decay_shift, input_shift, decay_log = (own_vectors[i] for i in range(4))
    taps = own_vectors[4:]

    across = [(i, i % seq * wt + i // seq) for i in range(seq * wt)]
    gates = jnp.concatenate([decay_gate_weight, input_gate_weight], axis=1)
    gates = lax.ppermute(gates, ("seq", "wt"), across)

    group_tokens = wt_gather(tokens)
    xy_unit = jnp.concatenate([turned(x_weight, 1), turned(y_weight, 1)], axis=1)
    gate_rows = chunk * 2 * block // xy_unit.shape[1]
    xy_unit = jnp.concatenate([xy_unit, gates.reshape(gate_rows, xy_unit.shape[1])])
    xy_blocks = seq_gather(xy_unit)
    xy_kernel = assembled(xy_blocks, slice(0, weight_rows)).reshape(width, 2 * lru_cols)
    gate_all = assembled(xy_blocks, slice(weight_rows, weight_rows + gate_rows))
    gate_all = turned(gate_all.reshape(lru_cols, 2 * block), 0)
    partner_rows = c_swap(gate_all[full:])
    shared_rows = in_order(gate_all[full:], partner_rows, 0)

    gate_unit = z_exchange(gate_weight)
    gate_kernel = plane_gather(gate_unit, True)
    up_unit = z_exchange(up_weight)
    up_kernel = plane_gather(up_unit, False)
    out_kernel = assembled(seq_gather(turned(out_weight, 1)), slice(0, weight_rows))
    out_kernel = out_kernel.reshape(width, lru_cols)
    down_unit = z_exchange(down_weight)
    down_kernel = plane_gather(down_unit, True)
    grad_group = group_gather(out_grad)

    stream = tokens.astype(F32)
    group_normed, _ = normed_rows(group_tokens.astype(F32))
    group_one = (group_normed * gain_one).astype(BF16)
    rows = group_one.shape[0]
    xy = multiply(group_one, xy_kernel)
    x_branch = xy[:, :lru_cols].astype(BF16)
    y_before = xy[:, lru_cols:]
    y_gated, gelu_y_back = jax.vjp(gelu_tanh, y_before)
    rim = lax.ppermute(x_branch[rows - reach :], "seq", [(i, i + 1) for i in range(seq - 1)])
    extended = jnp.concatenate([rim, x_branch], axis=0).astype(F32)
    conv_low = (
        tap_bias
        + sum(taps[k] * extended[reach - k : reach - k + rows] for k in range(taps_count))
    ).astype(BF16)
    shared_conv = in_order(conv_low[:, full:], c_swap(conv_low[:, full:]), 1)
    heads = full // block

    def of_head(value, i):
        return value[:, i * block : (i + 1) * block]

    pre_parts = [
        multiply(of_head(conv_low, i), gate_all[i * block : (i + 1) * block]) for i in range(heads)
    ]
    shared_pre = multiply(shared_conv, shared_rows).reshape(rows, 2, C, half)
    shared_pre = pick(shared_pre, c, 2)
    decay_pre = decay_shift + jnp.concatenate(
        [part[:, :block] for part in pre_parts] + [shared_pre[:, 0]], axis=1
    )
    input_pre = input_shift + jnp.concatenate(
        [part[:, block:] for part in pre_parts] + [shared_pre[:, 1]], axis=1
    )
    (retain, inflow), terms_back = jax.vjp(
        recurrence_terms, decay_pre, input_pre, decay_log, conv_low.astype(F32)
    )
    states, state_in = full_scan(retain, inflow, False)
    before = jnp.concatenate([state_in, states[:-1]])
    lru_low = states.astype(BF16).astype(F32)
    mixed_rows = (lru_low * y_gated).astype(BF16)
    branch = wt_scatter(lambda rows_: contract_last(rows_, out_kernel), mixed_rows)
    middle = stream + branch

    normed_two, inverse_two = normed_rows(middle)
    group_two = group_gather((normed_two * gain_two).astype(BF16))
    gate_pre = multiply(group_two, gate_kernel)
    up_pre = multiply(group_two, up_kernel)
    active, gelu_gate_back = jax.vjp(gelu_tanh, gate_pre)
    hidden = (active * up_pre).astype(BF16)

    d_hidden = multiply(grad_group, down_kernel)
    d_up = (d_hidden * active).astype(BF16)
    d_gate = gelu_gate_back(d_hidden * up_pre)[0].astype(BF16)
    d_normed_two = group_scatter(
        lambda g, u: contract_last(g, gate_kernel) + contract_last(u, up_kernel), d_gate, d_up
    )
    feed = group_scatter(lambda rows_: contract_last(rows_, down_kernel), hidden)
    block_out = (middle + feed).astype(BF16)
    down_grad = plane_scatter(contract_rows(grad_group, hidden), hidden_cols, True)
    gate_grad = plane_scatter(contract_rows(group_two, d_gate), hidden_cols, False)
    up_grad = plane_scatter(contract_rows(group_two, d_up), hidden_cols, True)
    gain_two_grad = jnp.sum(d_normed_two * normed_two, axis=0)
    d_middle = out_grad.astype(F32) + norm_back(d_normed_two, normed_two, inverse_two, gain_two)

    branch_rows = wt_gather(d_middle.astype(BF16))
    d_mixed = multiply(branch_rows, out_kernel)
    d_lru = (d_mixed * y_gated).astype(BF16).astype(F32)
    d_y = gelu_y_back(d_mixed * lru_low)[0].astype(BF16)
    passed, passed_in = full_scan(retain, retain * d_lru, True)
    d_total = d_lru + jnp.concatenate([passed[1:], passed_in])
    d_decay_pre, d_input_pre, decay_log_grad, d_conv_direct = terms_back(
        (d_total * before, d_total)
    )
    d_decay_low, d_input_low = d_decay_pre.astype(BF16), d_input_pre.astype(BF16)
    own_low = jnp.concatenate([d_decay_low[:, full:], d_input_low[:, full:]], axis=1)
    partner_low = c_swap(own_low)
    shared_low = jnp.concatenate(
        [
            in_order(own_low[:, :half], partner_low[:, :half], 1),
            in_order(own_low[:, half:], partner_low[:, half:], 1),
        ],
        axis=1,
    )
    lows = [
        jnp.concatenate([of_head(d_decay_low, i), of_head(d_input_low, i)], axis=1)
        for i in range(heads)
    ]
    d_conv = d_conv_direct + jnp.concatenate(
        [contract_last(lows[i], gate_all[i * block : (i + 1) * block]) for i in range(heads)]
        + [contract_last(shared_low, gate_all[full:])],
        axis=1,
    )
    gates_grad = jnp.concatenate(
        [contract_rows(of_head(conv_low, i), lows[i]) for i in range(heads)]
        + [contract_rows(conv_low[:, full:], shared_low)]
    )
    ahead = lax.ppermute(d_conv[:reach], "seq", [(i + 1, i) for i in range(seq - 1)])
    d_extended = jnp.concatenate([d_conv, ahead], axis=0)
    d_x_branch = sum(taps[k] * d_extended[k : k + rows] for k in range(taps_count)).astype(BF16)
    d_normed_one = wt_scatter(
        lambda dx, dy: contract_last(dx, xy_kernel[:, :lru_cols])
        + contract_last(dy, xy_kernel[:, lru_cols:]),
        d_x_branch,
        d_y,
    )
    normed_one, inverse_one = normed_rows(stream)
    gain_one_grad = jnp.sum(d_normed_one * normed_one, axis=0)
    tokens_grad = (d_middle + norm_back(d_normed_one, normed_one, inverse_one, gain_one)).astype(
        BF16
    )

    out_weight_grad = turned_back(seq_scatter(contract_rows(branch_rows, mixed_rows)), 1)
    y_weight_grad = turned_back(seq_scatter(contract_rows(group_one, d_y)), 1)
    x_weight_grad = turned_back(seq_scatter(contract_rows(group_one, d_x_branch)), 1)
    own_sums = jnp.stack(
        [jnp.sum(d_conv, axis=0), jnp.sum(d_decay_pre, axis=0), jnp.sum(d_input_pre, axis=0)]
        + [decay_log_grad]
        + [jnp.sum(d_conv * extended[reach - k : reach - k + rows], axis=0) for k in range(taps_count)],
        axis=1,
    )
    own_sums = jnp.concatenate([turned_back(gates_grad, 0), turned_back(own_sums, 0)], axis=1)
    own_sums = lax.psum_scatter(own_sums, "seq", scatter_dimension=0, tiled=True)
    own_sums = lax.ppermute(own_sums, ("seq", "wt"), [(to, at) for at, to in across])
    gains = lax.psum_scatter(
        jnp.stack([gain_one_grad, gain_two_grad], axis=1),
        ("seq", "wt"),
        scatter_dimension=0,
        tiled=True,
    )
    sums = own_sums[:, 2 * block :]
    return (
        block_out,
        tokens_grad,
        gains[:, 0],
        x_weight_grad,
        y_weight_grad,
        sums[:, 4:],
        sums[:, 0],
        own_sums[:, :block],
        sums[:, 1],
        own_sums[:, block : 2 * block],
        sums[:, 2],
        sums[:, 3],
        out_weight_grad,
        gains[:, 1],
        gate_grad,
        up_grad,
        down_grad,
    )


def solution(mesh):
    rows, both, lone = P(("seq", "wt"), None), P("seq", "wt"), P(("seq", "wt"))
    in_specs = (
        rows, lone, both, both, rows, lone, rows, lone, rows, lone, lone,
        both, lone, both, both, both, rows,
    )
    out_specs = (
        rows, rows, lone, both, both, rows, lone, rows, lone, rows, lone, lone,
        both, lone, both, both, both,
    )
    return jax.shard_map(
        per_device, mesh=mesh, in_specs=in_specs, out_specs=out_specs, check_vma=False
    )
```

time: 4090 us -> 1510 us (0.37)
  waiting for transfers between devices: 2470 us -> 736 us
  local copies, waits for them, and re-layouts: 1040 us -> 123 us
  starting transfers between devices: 39.1 us -> 315 us
  blocking collectives: 170 us -> 37.6 us
  other arithmetic: 159 us -> 106 us
    reduce_scatter x11 -> x1, waiting for transfers between devices: 1470 us -> 0.01 us  [per_device(): lax.psum_scatter(own_sums, 'seq', scatter_dimension=0, tiled=True)]
    slice x146 -> x53, local copies, waits for them, and re-layouts: 719 us -> 17.7 us  [the longest x16 3.61 us: turned(): return jnp.where(c == 0, value, jnp.roll(value, -half, axis))]
    ppermute x2 -> x137, waiting for transfers between devices: 6.4 us -> 619 us  [the longest x72 231 us: z_move(): return lax.ppermute(value, 'seq', pairs)]
    all_gather x12 -> x0, waiting for transfers between devices: 611 us -> none  [the longest x1 144 us: gather_weights(): lax.all_gather(down_weight, 'seq', axis=0, tiled=True)]
    ppermute x2 -> x137, starting transfers between devices: 4.68 us -> 315 us  [the longest x72 167 us: z_move(): return lax.ppermute(value, 'seq', pairs)]
    unnamed x27 -> x3, waiting for transfers between devices: 344 us -> 117 us
    pad x42 -> x0, local copies, waits for them, and re-layouts: 186 us -> none  [run_scan(): lax.associative_scan(compose, (lane_retain, lane_inflow), reverse=backwar...]
    unnamed x2 -> x0, blocking collectives: 85.4 us -> none
  transfers between devices with their start and end apart: 34 -> 139, of which waited for: 27 -> 53; matrix products, arithmetic and copies ran while one was open for 31% -> 19% of each run, Pallas kernels for 0% -> 0%
where the time goes in v1:
time: 1510 us; the launch traced here: 1490 us
  waiting for transfers between devices  736 us (49%)
  starting transfers between devices  315 us (21%)
  matrix products  135 us (9%)
  local copies, waits for them, and re-layouts  123 us (8%)
  other arithmetic  106 us (7%)
  blocking collectives  37.6 us (2%)
  between operations  19.4 us (1%)
    ppermute x72, waiting for transfers between devices, z_move(): return lax.ppermute(value, 'seq', pairs)  231 us
    ppermute x18, waiting for transfers between devices, x_move(): return lax.ppermute(value, 'seq', pairs)  182 us
    ppermute x72, starting transfers between devices, z_move(): return lax.ppermute(value, 'seq', pairs)  167 us
    ppermute x12, waiting for transfers between devices, y_move(): return lax.ppermute(value, 'wt', pairs)  143 us
    unnamed x3, waiting for transfers between devices  117 us
    ppermute x14, starting transfers between devices, full_scan(): moved = lax.ppermute(ends, 'seq', pairs)  70.2 us
    dot_general x15, matrix products, contract_last(): lax.dot_general(left_side, right_side, (((1,), (1,)), ((), ())), preferre...  57.9 us
    ppermute x1, waiting for transfers between devices, per_device(): lax.ppermute(d_conv[:reach], 'seq', [(i + 1, i) for i in range(seq - 1)])  44.6 us
  transfers between devices with their start and end apart: 139, of which 53 were waited for; matrix products, arithmetic and copies ran while one was open for 19% of the time, Pallas kernels for 0%

profile of v1, /device:TPU:2, one launch (start us, length us, event | category | flops | bytes accessed | tf_op | source)
XLA Modules:
  0.0 1485.4 jit_solution(11905653270809086164)
XLA Ops:
  32.7 37.6 %all-gather = f32[32,80,10]{1,2,0:T(8,128)S(1)} all-gather(f32[1,80,10]{1,2,0:T(8,128)S(1)} %bitcast.501), channel_id=1, replica_groups=mesh['seq'=8,'wt'=4] {'seq','wt'}, dimensions={0}, use_global_device_ids=true | all-gather | bytes 105600 | tf_op jit(solution)/shard_map/all_gather | solution.py:374
  103.0 19.0 %collective-permute-done.52 = bf16[320,512]{1,0:T(8,128)(2,1)S(1)} collective-permute-done((bf16[320,512]{1,0:T(8,128)(2,1)}, bf16[320,512]{1,0:T(8,128)(2,1)S(1)}, u32[]{:S(2)}, u32[]{:S(2)}) %collective-permute-start.52) | collective-permute-done | bytes 327712 | tf_op jit(solution)/shard_map/ppermute | solution.py:40
  137.4 12.6 collective-permute-done.59
  154.6 13.5 collective-permute-done.46
  192.4 10.4 collective-permute-done.3
  233.1 25.9 %collective-permute-done.60 = bf16[4,320,512]{2,1,0:T(8,128)(2,1)S(1)} collective-permute-done((bf16[4,320,512]{2,1,0:T(8,128)(2,1)S(1)}, bf16[4,320,512]{2,1,0:T(8,128)(2,1)S(1)}, u32[]{:S(2)}, u32[]{:S(2)}) %collective-permute-start.60) | collective-permute-done | bytes 1310752 | tf_op jit(solution)/shard_map/ppermute | solution.py:46
  265.2 29.0 %collective-permute-done.28 = bf16[320,640]{1,0:T(8,128)(2,1)S(1)} collective-permute-done((bf16[320,640]{1,0:T(8,128)(2,1)S(1)}, bf16[320,640]{1,0:T(8,128)(2,1)S(1)}, u32[]{:S(2)}, u32[]{:S(2)}) %collective-permute-start.28) | collective-permute-done | bytes 409632 | tf_op jit(solution)/shard_map/ppermute | solution.py:46
  303.8 20.4 %collective-permute-done.1 = bf16[256,2560]{1,0:T(8,128)(2,1)S(1)} collective-permute-done((bf16[256,2560]{1,0:T(8,128)(2,1)S(1)}, bf16[256,2560]{1,0:T(8,128)(2,1)S(1)}, u32[]{:S(2)}, u32[]{:S(2)}) %collective-permute-start.1) | collective-permute-done | bytes 1310752 | tf_op jit(solution)/shard_map/ppermute | solution.py:52
  335.4 13.7 collective-permute-done.7
  352.9 19.2 %collective-permute-done.8 = bf16[352,1280]{1,0:T(8,128)(2,1)S(1)} collective-permute-done((bf16[352,1280]{1,0:T(8,128)(2,1)S(1)}, bf16[352,1280]{1,0:T(8,128)(2,1)S(1)}, u32[]{:S(2)}, u32[]{:S(2)}) %collective-permute-start.8) | collective-permute-done | bytes 901152 | tf_op jit(solution)/shard_map/ppermute | solution.py:46
  374.9 16.6 %collective-permute-done.10 = bf16[352,1280]{1,0:T(8,128)(2,1)S(1)} collective-permute-done((bf16[352,1280]{1,0:T(8,128)(2,1)S(1)}, bf16[352,1280]{1,0:T(8,128)(2,1)S(1)}, u32[]{:S(2)}, u32[]{:S(2)}) %collective-permute-start.10) | collective-permute-done | bytes 901152 | tf_op jit(solution)/shard_map/ppermute | solution.py:46
  392.8 10.2 collective-permute-done.12
  519.6 59.4 %collective-permute-done.34 = bf16[128,2560]{1,0:T(8,128)(2,1)S(1)} collective-permute-done((bf16[128,2560]{1,0:T(8,128)(2,1)S(1)}, bf16[128,2560]{1,0:T(8,128)(2,1)S(1)}, u32[]{:S(2)}, u32[]{:S(2)}) %collective-permute-start.34) | collective-permute-done | bytes 655392 | tf_op jit(solution)/shard_map/ppermute | solution.py:52
  586.3 12.5 collective-permute-done.36
  621.5 12.9 collective-permute-done.38
  637.1 10.6 collective-permute-start.44
  656.7 13.3 fusion.8
  689.0 12.6 add_convert_fusion
  757.5 11.4 collective-permute-done.122
  784.6 46.3 %collective-permute-done.132 = bf16[4,320,1024]{2,1,0:T(8,128)(2,1)} collective-permute-done((bf16[4,320,1024]{2,1,0:T(8,128)(2,1)}, bf16[4,320,1024]{2,1,0:T(8,128)(2,1)}, u32[]{:S(2)}, u32[]{:S(2)}) %collective-permute-start.132) | collective-permute-done | bytes 2621472 | tf_op jit(solution)/shard_map/ppermute | solution.py:46
  843.9 10.0 collective-permute-done.82
  871.7 21.9 %collective-permute-done.133 = bf16[4,320,512]{2,1,0:T(8,128)(2,1)S(1)} collective-permute-done((bf16[4,320,512]{2,1,0:T(8,128)(2,1)S(1)}, bf16[4,320,512]{2,1,0:T(8,128)(2,1)S(1)}, u32[]{:S(2)}, u32[]{:S(2)}) %collective-permute-start.133) | collective-permute-done | bytes 1310752 | tf_op jit(solution)/shard_map/ppermute | solution.py:52
  920.2 11.0 collective-permute-done.125
  931.2 15.6 %collective-permute-start.131 = (bf16[320,512]{1,0:T(8,128)(2,1)S(1)}, bf16[320,512]{1,0:T(8,128)(2,1)S(1)}, u32[]{:S(2)}, u32[]{:S(2)}) collective-permute-start(bf16[320,512]{1,0:T(8,128)(2,1)S(1)} %get-tuple-element.186), channel_id=1, source_target_pairs={{0,24},{4,28},{8,0},{12,4},{16,8},{20,12},{24,16},{28,20},{1,25},{... | collective-permute-start | bytes 983048 | tf_op jit(solution)/shard_map/ppermute | solution.py:40
  963.4 18.9 %collective-permute-done.134 = bf16[320,512]{1,0:T(8,128)(2,1)S(1)} collective-permute-done((bf16[320,512]{1,0:T(8,128)(2,1)S(1)}, bf16[320,512]{1,0:T(8,128)(2,1)S(1)}, u32[]{:S(2)}, u32[]{:S(2)}) %collective-permute-start.134) | collective-permute-done | bytes 327712 | tf_op jit(solution)/shard_map/ppermute | solution.py:40
  983.6 10.7 collective-permute-done.135
  1020.0 25.9 %collective-permute-done.88 = bf16[256,2560]{1,0:T(8,128)(2,1)S(1)} collective-permute-done((bf16[256,2560]{1,0:T(8,128)(2,1)S(1)}, bf16[256,2560]{1,0:T(8,128)(2,1)S(1)}, u32[]{:S(2)}, u32[]{:S(2)}) %collective-permute-start.88) | collective-permute-done | bytes 1310752 | tf_op jit(solution)/shard_map/ppermute | solution.py:52
  1063.7 16.1 %collective-permute-start.91 = (f32[2,640]{1,0:T(2,128)S(1)}, f32[2,640]{1,0:T(2,128)S(1)}, u32[]{:S(2)}, u32[]{:S(2)}) collective-permute-start(f32[2,640]{1,0:T(2,128)S(1)} %pad_maximum_fusion.19), channel_id=1, source_target_pairs={{12,0},{16,4},{20,8},{24,12},{28,16},{13,1},{17,5},{21,9},{25,13},... | collective-permute-start | bytes 15368 | tf_op jit(solution)/shard_map/ppermute | solution.py:301
  1151.0 44.6 %collective-permute-done.97 = f32[3,640]{1,0:T(4,128)} collective-permute-done((f32[3,640]{1,0:T(4,128)}, f32[3,640]{1,0:T(4,128)}, u32[]{:S(2)}, u32[]{:S(2)}) %collective-permute-start.97) | collective-permute-done | bytes 7712 | tf_op jit(solution)/shard_map/ppermute | solution.py:501
  1222.4 19.6 %collective-permute-done.100 = bf16[4,320,640]{2,1,0:T(8,128)(2,1)S(1)} collective-permute-done((bf16[4,320,640]{2,1,0:T(8,128)(2,1)S(1)}, bf16[4,320,640]{2,1,0:T(8,128)(2,1)S(1)}, u32[]{:S(2)}, u32[]{:S(2)}) %collective-permute-start.100) | collective-permute-done | bytes 1638432 | tf_op jit(solution)/shard_map/ppermute | solution.py:46
  1311.9 10.2 collective-permute-done.114
  1358.9 116.8 %reduce-scatter.7.cloned.1.call-done = f32[80,2]{1,0:T(8,128)} async-done(((f32[2560,2]{1,0:T(8,128)}), f32[80,2]{1,0:T(8,128)}) %reduce-scatter.7.cloned.1.call-update) | async-done | bytes 656
  (865 shorter events, 737.9 us)
Async XLA Ops:
  8.0 1294.4 %reduce-scatter.5.cloned.1.call-start = ((), (), s32[]{:S(2)}) async-start(), calls=%async_computation.2 | async-start | bytes 1843200 | tf_op jit(solution)/shard_map/reduce_scatter | solution.py:526
  10.2 174.6 %collective-permute-start.23 = (bf16[320,640]{1,0:T(8,128)(2,1)}, bf16[320,640]{1,0:T(8,128)(2,1)}, u32[]{:S(2)}, u32[]{:S(2)}) collective-permute-start(bf16[320,640]{1,0:T(8,128)(2,1)} %get-tuple-element.151), channel_id=1, source_target_pairs={{0,4},{4,0},{8,12},{12,8},{16,20},{20,16},{24,28},{28,24},{1,5},{5... | collective-permute-start | bytes 1228808 | tf_op jit(solution)/shard_map/ppermute | solution.py:46
  10.2 194.8 %collective-permute-start.24 = (bf16[320,640]{1,0:T(8,128)(2,1)}, bf16[320,640]{1,0:T(8,128)(2,1)}, u32[]{:S(2)}, u32[]{:S(2)}) collective-permute-start(bf16[320,640]{1,0:T(8,128)(2,1)} %get-tuple-element.151), channel_id=1, source_target_pairs={{0,8},{4,12},{8,16},{12,20},{16,24},{20,28},{1,9},{5,13},{9,17},{1... | collective-permute-start | bytes 1228808 | tf_op jit(solution)/shard_map/ppermute | solution.py:40
  14.9 171.9 %collective-permute-start.25 = (bf16[320,640]{1,0:T(8,128)(2,1)}, bf16[320,640]{1,0:T(8,128)(2,1)}, u32[]{:S(2)}, u32[]{:S(2)}) collective-permute-start(bf16[320,640]{1,0:T(8,128)(2,1)} %get-tuple-element.151), channel_id=1, source_target_pairs={{8,0},{12,4},{16,8},{20,12},{24,16},{28,20},{9,1},{13,5},{17,9},{2... | collective-permute-start | bytes 1228808 | tf_op jit(solution)/shard_map/ppermute | solution.py:40
  16.9 72.2 %collective-permute-start.2 = (bf16[80,512]{1,0:T(8,128)(2,1)}, bf16[80,512]{1,0:T(8,128)(2,1)S(1)}, u32[]{:S(2)}, u32[]{:S(2)}) collective-permute-start(bf16[80,512]{1,0:T(8,128)(2,1)} %pad_maximum_fusion.15), channel_id=1, source_target_pairs={{0,0},{1,4},{2,8},{3,12},{4,16},{5,20},{6,24},{7,28},{8,1},{9,5},{... | collective-permute-start | bytes 245768 | tf_op jit(solution)/shard_map/ppermute | solution.py:384
  27.6 65.4 %collective-permute-start.51 = (bf16[320,512]{1,0:T(8,128)(2,1)}, bf16[320,512]{1,0:T(8,128)(2,1)}, u32[]{:S(2)}, u32[]{:S(2)}) collective-permute-start(bf16[320,512]{1,0:T(8,128)(2,1)} %get-tuple-element.197), channel_id=1, source_target_pairs={{0,8},{4,12},{8,16},{12,20},{16,24},{20,28},{24,0},{28,4},{1,9},{5... | collective-permute-start | bytes 983048 | tf_op jit(solution)/shard_map/ppermute | solution.py:40
  186.8 72.1 %collective-permute-start.60 = (bf16[4,320,512]{2,1,0:T(8,128)(2,1)S(1)}, bf16[4,320,512]{2,1,0:T(8,128)(2,1)S(1)}, u32[]{:S(2)}, u32[]{:S(2)}) collective-permute-start(bf16[4,320,512]{2,1,0:T(8,128)(2,1)S(1)} %bitcast_dynamic-update-slice_fusion.25), channel_id=1, source_target_pairs={{0,4},{4,0},{8,12},{12,8},{16,20},{20,16},{24,28},{28,24},{1,5},{5... | collective-permute-start | bytes 3932168 | tf_op jit(solution)/shard_map/ppermute | solution.py:46
  224.8 70.4 %collective-permute-start.61 = (bf16[4,320,512]{2,1,0:T(8,128)(2,1)S(1)}, bf16[4,320,512]{2,1,0:T(8,128)(2,1)S(1)}, u32[]{:S(2)}, u32[]{:S(2)}) collective-permute-start(bf16[4,320,512]{2,1,0:T(8,128)(2,1)S(1)} %bitcast_dynamic-update-slice_fusion.25), channel_id=1, source_target_pairs={{0,2},{1,3},{2,0},{3,1},{4,6},{5,7},{6,4},{7,5},{8,10},{9,11},{10,... | collective-permute-start | bytes 3932168 | tf_op jit(solution)/shard_map/ppermute | solution.py:52
  225.8 73.7 %collective-permute-start.48 = (bf16[4,320,512]{2,1,0:T(8,128)(2,1)}, bf16[4,320,512]{2,1,0:T(8,128)(2,1)S(1)}, u32[]{:S(2)}, u32[]{:S(2)}) collective-permute-start(bf16[4,320,512]{2,1,0:T(8,128)(2,1)} %bitcast_dynamic-update-slice_fusion.31), channel_id=1, source_target_pairs={{0,4},{4,0},{8,12},{12,8},{16,20},{20,16},{24,28},{28,24},{1,5},{5... | collective-permute-start | bytes 3932168 | tf_op jit(solution)/shard_map/ppermute | solution.py:46
  230.9 63.3 %collective-permute-start.28 = (bf16[320,640]{1,0:T(8,128)(2,1)S(1)}, bf16[320,640]{1,0:T(8,128)(2,1)S(1)}, u32[]{:S(2)}, u32[]{:S(2)}) collective-permute-start(bf16[320,640]{1,0:T(8,128)(2,1)S(1)} %get-tuple-element.149), channel_id=1, source_target_pairs={{0,4},{4,0},{8,12},{12,8},{16,20},{20,16},{24,28},{28,24},{1,5},{5... | collective-permute-start | bytes 1228808 | tf_op jit(solution)/shard_map/ppermute | solution.py:46
  329.5 124.6 %collective-permute-start.49 = (bf16[4,320,512]{2,1,0:T(8,128)(2,1)}, bf16[4,320,512]{2,1,0:T(8,128)(2,1)}, u32[]{:S(2)}, u32[]{:S(2)}) collective-permute-start(bf16[4,320,512]{2,1,0:T(8,128)(2,1)} %bitcast_dynamic-update-slice_fusion.31), channel_id=1, source_target_pairs={{0,2},{1,3},{2,0},{3,1},{4,6},{5,7},{6,4},{7,5},{8,10},{9,11},{10,... | collective-permute-start | bytes 3932168 | tf_op jit(solution)/shard_map/ppermute | solution.py:52
  329.8 131.5 %collective-permute-start.72 = (bf16[128,2560]{1,0:T(8,128)(2,1)}, bf16[128,2560]{1,0:T(8,128)(2,1)}, u32[]{:S(2)}, u32[]{:S(2)}) collective-permute-start(bf16[128,2560]{1,0:T(8,128)(2,1)} %collective-permute-done.71), channel_id=1, source_target_pairs={{8,0},{12,4},{16,8},{20,12},{9,1},{13,5},{17,9},{21,13},{10,2},{14... | collective-permute-start | bytes 1966088 | tf_op jit(solution)/shard_map/ppermute | solution.py:40
  331.1 135.5 %collective-permute-start.74 = (bf16[128,2560]{1,0:T(8,128)(2,1)}, bf16[128,2560]{1,0:T(8,128)(2,1)}, u32[]{:S(2)}, u32[]{:S(2)}) collective-permute-start(bf16[128,2560]{1,0:T(8,128)(2,1)} %collective-permute-done.70), channel_id=1, source_target_pairs={{8,16},{12,20},{16,24},{20,28},{9,17},{13,21},{17,25},{21,29},{10,... | collective-permute-start | bytes 1966088 | tf_op jit(solution)/shard_map/ppermute | solution.py:40
  484.0 134.3 %collective-permute-start.56 = (bf16[4,320,512]{2,1,0:T(8,128)(2,1)}, bf16[4,320,512]{2,1,0:T(8,128)(2,1)}, u32[]{:S(2)}, u32[]{:S(2)}) collective-permute-start(bf16[4,320,512]{2,1,0:T(8,128)(2,1)} %copy-done.75), channel_id=1, source_target_pairs={{0,4},{4,0},{8,12},{12,8},{16,20},{20,16},{24,28},{28,24},{1,5},{5... | collective-permute-start | bytes 3932168 | tf_op jit(solution)/shard_map/ppermute | solution.py:46
  500.3 80.8 %collective-permute-start.62 = (bf16[4,320,512]{2,1,0:T(8,128)(2,1)}, bf16[4,320,512]{2,1,0:T(8,128)(2,1)S(1)}, u32[]{:S(2)}, u32[]{:S(2)}) collective-permute-start(bf16[4,320,512]{2,1,0:T(8,128)(2,1)} %copy-done.76), channel_id=1, source_target_pairs={{0,2},{1,3},{2,0},{3,1},{4,6},{5,7},{6,4},{7,5},{8,10},{9,11},{10,... | collective-permute-start | bytes 3932168 | tf_op jit(solution)/shard_map/ppermute | solution.py:52
  510.5 109.4 %collective-permute-start.50 = (bf16[4,320,512]{2,1,0:T(8,128)(2,1)S(1)}, bf16[4,320,512]{2,1,0:T(8,128)(2,1)S(1)}, u32[]{:S(2)}, u32[]{:S(2)}) collective-permute-start(bf16[4,320,512]{2,1,0:T(8,128)(2,1)S(1)} %copy-done.78), channel_id=1, source_target_pairs={{0,2},{1,3},{2,0},{3,1},{4,6},{5,7},{6,4},{7,5},{8,10},{9,11},{10,... | collective-permute-start | bytes 3932168 | tf_op jit(solution)/shard_map/ppermute | solution.py:52
  517.3 61.7 %collective-permute-start.34 = (bf16[128,2560]{1,0:T(8,128)(2,1)S(1)}, bf16[128,2560]{1,0:T(8,128)(2,1)S(1)}, u32[]{:S(2)}, u32[]{:S(2)}) collective-permute-start(bf16[128,2560]{1,0:T(8,128)(2,1)S(1)} %fusion.103), channel_id=1, source_target_pairs={{0,2},{1,3},{2,0},{3,1},{4,6},{5,7},{6,4},{7,5},{8,10},{9,11},{10,... | collective-permute-start | bytes 1966088 | tf_op jit(solution)/shard_map/ppermute | solution.py:52
  519.3 60.5 %collective-permute-start.78 = (bf16[128,2560]{1,0:T(8,128)(2,1)S(1)}, bf16[128,2560]{1,0:T(8,128)(2,1)S(1)}, u32[]{:S(2)}, u32[]{:S(2)}) collective-permute-start(bf16[128,2560]{1,0:T(8,128)(2,1)S(1)} %get-tuple-element.131), channel_id=1, source_target_pairs={{0,1},{1,0},{2,3},{3,2},{4,5},{5,4},{6,7},{7,6},{8,9},{9,8},{10,11... | collective-permute-start | bytes 1966088 | tf_op jit(solution)/shard_map/ppermute | solution.py:58
  709.5 59.4 %collective-permute-start.122 = (bf16[4,2,320,512]{3,2,1,0:T(8,128)(2,1)}, bf16[4,2,320,512]{3,2,1,0:T(8,128)(2,1)}, u32[]{:S(2)}, u32[]{:S(2)}) collective-permute-start(bf16[4,2,320,512]{3,2,1,0:T(8,128)(2,1)} %slice.1037), channel_id=1, source_target_pairs={{0,2},{1,3},{2,0},{3,1},{4,6},{5,7},{6,4},{7,5},{8,10},{9,11},{10,... | collective-permute-start | bytes 7864328 | tf_op jit(solution)/shard_map/ppermute | solution.py:52
  715.5 61.8 %collective-permute-start.127 = (bf16[4,320,1024]{2,1,0:T(8,128)(2,1)}, bf16[4,320,1024]{2,1,0:T(8,128)(2,1)}, u32[]{:S(2)}, u32[]{:S(2)}) collective-permute-start(bf16[4,320,1024]{2,1,0:T(8,128)(2,1)} %fusion.16), channel_id=1, source_target_pairs={{0,4},{4,0},{8,12},{12,8},{16,20},{20,16},{24,28},{28,24},{1,5},{5... | collective-permute-start | bytes 7864328 | tf_op jit(solution)/shard_map/ppermute | solution.py:46
  730.6 100.2 %collective-permute-start.132 = (bf16[4,320,1024]{2,1,0:T(8,128)(2,1)}, bf16[4,320,1024]{2,1,0:T(8,128)(2,1)}, u32[]{:S(2)}, u32[]{:S(2)}) collective-permute-start(bf16[4,320,1024]{2,1,0:T(8,128)(2,1)} %fusion.17), channel_id=1, source_target_pairs={{0,4},{4,0},{8,12},{12,8},{16,20},{20,16},{24,28},{28,24},{1,5},{5... | collective-permute-start | bytes 7864328 | tf_op jit(solution)/shard_map/ppermute | solution.py:46
  746.7 89.1 %collective-permute-start.81 = (bf16[128,2560]{1,0:T(8,128)(2,1)}, bf16[128,2560]{1,0:T(8,128)(2,1)}, u32[]{:S(2)}, u32[]{:S(2)}) collective-permute-start(bf16[128,2560]{1,0:T(8,128)(2,1)} %get-tuple-element.161), channel_id=1, source_target_pairs={{0,8},{4,12},{1,9},{5,13},{2,10},{6,14},{3,11},{7,15}} | collective-permute-start | bytes 1966088 | tf_op jit(solution)/shard_map/ppermute | solution.py:40
  750.9 91.4 %collective-permute-start.84 = (bf16[128,2560]{1,0:T(8,128)(2,1)}, bf16[128,2560]{1,0:T(8,128)(2,1)S(1)}, u32[]{:S(2)}, u32[]{:S(2)}) collective-permute-start(bf16[128,2560]{1,0:T(8,128)(2,1)} %get-tuple-element.162), channel_id=1, source_target_pairs={{24,16},{28,20},{25,17},{29,21},{26,18},{30,22},{27,19},{31,23}} | collective-permute-start | bytes 1966088 | tf_op jit(solution)/shard_map/ppermute | solution.py:40
  768.9 68.5 %collective-permute-start.64 = (bf16[128,2560]{1,0:T(8,128)(2,1)}, bf16[128,2560]{1,0:T(8,128)(2,1)}, u32[]{:S(2)}, u32[]{:S(2)}) collective-permute-start(bf16[128,2560]{1,0:T(8,128)(2,1)} %get-tuple-element.165), channel_id=1, source_target_pairs={{0,8},{4,12},{1,9},{5,13},{2,10},{6,14},{3,11},{7,15}} | collective-permute-start | bytes 1966088 | tf_op jit(solution)/shard_map/ppermute | solution.py:40
  777.3 118.4 %collective-permute-start.67 = (bf16[128,2560]{1,0:T(8,128)(2,1)}, bf16[128,2560]{1,0:T(8,128)(2,1)}, u32[]{:S(2)}, u32[]{:S(2)}) collective-permute-start(bf16[128,2560]{1,0:T(8,128)(2,1)} %get-tuple-element.166), channel_id=1, source_target_pairs={{24,16},{28,20},{25,17},{29,21},{26,18},{30,22},{27,19},{31,23}} | collective-permute-start | bytes 1966088 | tf_op jit(solution)/shard_map/ppermute | solution.py:40
  861.1 98.7 %collective-permute-start.85 = (bf16[128,2560]{1,0:T(8,128)(2,1)S(1)}, bf16[128,2560]{1,0:T(8,128)(2,1)S(1)}, u32[]{:S(2)}, u32[]{:S(2)}) collective-permute-start(bf16[128,2560]{1,0:T(8,128)(2,1)S(1)} %get-tuple-element.160), channel_id=1, source_target_pairs={{16,8},{20,12},{24,16},{28,20},{17,9},{21,13},{25,17},{29,21},{18,... | collective-permute-start | bytes 1966088 | tf_op jit(solution)/shard_map/ppermute | solution.py:40
  867.6 127.4 %collective-permute-start.83 = (bf16[128,2560]{1,0:T(8,128)(2,1)S(1)}, bf16[128,2560]{1,0:T(8,128)(2,1)S(1)}, u32[]{:S(2)}, u32[]{:S(2)}) collective-permute-start(bf16[128,2560]{1,0:T(8,128)(2,1)S(1)} %get-tuple-element.159), channel_id=1, source_target_pairs={{0,8},{4,12},{8,16},{12,20},{16,24},{20,28},{1,9},{5,13},{9,17},{1... | collective-permute-start | bytes 1966088 | tf_op jit(solution)/shard_map/ppermute | solution.py:40
  1114.8 99.7 %collective-permute-start.107 = (bf16[4,320,640]{2,1,0:T(8,128)(2,1)}, bf16[4,320,640]{2,1,0:T(8,128)(2,1)}, u32[]{:S(2)}, u32[]{:S(2)}) collective-permute-start(bf16[4,320,640]{2,1,0:T(8,128)(2,1)} %fusion.25), channel_id=1, source_target_pairs={{0,4},{4,0},{8,12},{12,8},{16,20},{20,16},{24,28},{28,24},{1,5},{5... | collective-permute-start | bytes 4915208 | tf_op jit(solution)/shard_map/ppermute | solution.py:46
  1115.6 103.6 %collective-permute-start.115 = (bf16[4,320,640]{2,1,0:T(8,128)(2,1)}, bf16[4,320,640]{2,1,0:T(8,128)(2,1)}, u32[]{:S(2)}, u32[]{:S(2)}) collective-permute-start(bf16[4,320,640]{2,1,0:T(8,128)(2,1)} %fusion.26), channel_id=1, source_target_pairs={{0,4},{4,0},{8,12},{12,8},{16,20},{20,16},{24,28},{28,24},{1,5},{5... | collective-permute-start | bytes 4915208 | tf_op jit(solution)/shard_map/ppermute | solution.py:46
  1150.8 324.9 %reduce-scatter.7.cloned.1.call-start = ((), (), s32[]{:S(2)}) async-start(), calls=%async_computation.3 | async-start | bytes 1351680
  1211.1 86.6 %collective-permute-start.98 = (f32[256,2560]{1,0:T(8,128)S(1)}, f32[256,2560]{1,0:T(8,128)S(1)}, u32[]{:S(2)}, u32[]{:S(2)}) collective-permute-start(f32[256,2560]{1,0:T(8,128)S(1)} %convolution_add_fusion), channel_id=1, source_target_pairs={{0,1},{1,0},{2,3},{3,2},{4,5},{5,4},{6,7},{7,6},{8,9},{9,8},{10,11... | collective-permute-start | bytes 7864328 | tf_op jit(solution)/shard_map/ppermute | solution.py:58
  1293.6 63.0 %collective-permute-start.103 = (bf16[320,640]{1,0:T(8,128)(2,1)}, bf16[320,640]{1,0:T(8,128)(2,1)}, u32[]{:S(2)}, u32[]{:S(2)}) collective-permute-start(bf16[320,640]{1,0:T(8,128)(2,1)} %get-tuple-element.176), channel_id=1, source_target_pairs={{0,8},{4,12},{8,16},{12,20},{16,24},{20,28},{1,9},{5,13},{9,17},{1... | collective-permute-start | bytes 1228808 | tf_op jit(solution)/shard_map/ppermute | solution.py:40
  (263 other events, 6784.4 us)
Sparse Core Ops, SparseCore 0:
  1150.9 68.7 reduce-scatter.4
Sparse Core Ops, SparseCore 1:
  1353.2 122.4 reduce-scatter.6

commit v2 on v1

--- a/solution.py
+++ b/solution.py
@@ -14,6 +14,7 @@
 LANES = 128
 F32 = jnp.float32
 BF16 = jnp.bfloat16
+MESH = pl.DeviceIdType.MESH
 
 
 def gelu_tanh(values):
@@ -38,6 +39,10 @@
     inner, _ = sizes()
     pairs = [(z * inner + x, (z + by) % Z * inner + x) for z in senders for x in range(inner)]
     return lax.ppermute(value, "seq", pairs)
+
+
+def z_turn(value, by):
+    return z_move(value, by, range(Z))
 
 
 def x_move(value, by):
@@ -101,26 +106,6 @@
     return jnp.dot(left_side, right_side, preferred_element_type=F32)
 
 
-def seq_gather(unit):
-    inner, _ = sizes()
-    z, x = places()[:2]
-    blocks = []
-    for k, block in enumerate(line_gather(unit)):
-        blocks.append(((z - k) % Z, x, block))
-        for j in range(1, inner):
-            blocks.append(((z - k) % Z, (x - j) % inner, x_move(block, j)))
-    return blocks
-
-
-def assembled(blocks, rows):
-    inner, _ = sizes()
-    width = blocks[0][2].shape[1]
-    buffer = jnp.zeros((Z, inner, rows.stop - rows.start, width), blocks[0][2].dtype)
-    for z_at, x_at, block in blocks:
-        buffer = put(buffer, block[rows][None, None], (z_at, x_at, 0, 0))
-    return buffer
-
-
 def seq_scatter(total):
     inner, _ = sizes()
     z, x = places()[:2]
@@ -131,45 +116,6 @@
     return line_scatter([pick(kept, (z - k) % Z, 0) for k in range(Z)])
 
 
-def z_exchange(weight):
-    z = places()[0]
-    rows, width = weight.shape
-    share = -(-width // (Z * LANES)) * LANES
-    padded = jnp.pad(weight, ((0, 0), (0, Z * share - width)))
-
-    def cut(at):
-        return lax.dynamic_slice(padded, (0, at * share), (rows, share))
-
-    buffer = put(jnp.zeros((Z, rows, share), weight.dtype), cut(z)[None], (z, 0, 0))
-    for k in range(1, Z):
-        moved = z_move(cut((z + k) % Z), k, range(Z))
-        buffer = put(buffer, moved[None], ((z - k) % Z, 0, 0))
-    return buffer
-
-
-def plane_gather(unit, x_first):
-    inner, outer = sizes()
-    x = places()[1]
-    _, rows, share = unit.shape
-    grid = {(0, 0): unit}
-    if x_first:
-        for j in range(1, inner):
-            grid[j, 0] = x_move(unit, j)
-        for j in range(inner):
-            for i in range(1, outer):
-                grid[j, i] = y_move(grid[j, 0], i)
-    else:
-        for i in range(1, outer):
-            grid[0, i] = y_move(unit, i)
-        for i in range(outer):
-            for j in range(1, inner):
-                grid[j, i] = x_move(grid[0, i], j)
-    buffer = jnp.zeros((Z, inner, rows, outer * share), unit.dtype)
-    for (j, i), block in grid.items():
-        buffer = put(buffer, block[:, None], (0, (x - j) % inner, 0, i * share))
-    return buffer.reshape(Z * inner * rows, outer * share)
-
-
 def plane_scatter(total, width, x_first):
     inner, outer = sizes()
     z, x = places()[:2]
@@ -241,6 +187,360 @@
     kept = product_of(*[side[:half] for side in sides]) + sent.astype(F32)
     rows = half // Z
     return line_scatter([kept[k * rows : (k + 1) * rows] for k in range(Z)])
+
+
+class Sends:
+    def __init__(self, sems):
+        self.sems, self.started = sems, []
+
+    def start(self, when, source, target, arrival, device):
+        copy = pltpu.make_async_remote_copy(
+            src_ref=source,
+            dst_ref=target,
+            send_sem=self.sems.at[len(self.started)],
+            recv_sem=arrival,
+            device_id=device,
+            device_id_type=MESH,
+        )
+        if when is True:
+            copy.start()
+        else:
+            pl.when(when)(copy.start)
+        self.started.append((when, copy))
+
+    def finish(self):
+        for when, copy in self.started:
+            if when is True:
+                copy.wait_send()
+            else:
+                pl.when(when)(copy.wait_send)
+
+
+def arrived(target, arrival, device):
+    pltpu.make_async_remote_copy(
+        src_ref=target, dst_ref=target, send_sem=arrival, recv_sem=arrival,
+        device_id=device, device_id_type=MESH,
+    ).wait_recv()
+
+
+def gather_kernel(shape, *refs):
+    inner, outer = shape
+    (tokens, grads, vectors, gates, xy, out, gate, up, down) = refs[:9]
+    (tokens_to, grads_to, vectors_to, gates_to, xy_to, out_to, gate_to, up_to, down_to) = refs[9:18]
+    send_sems, local_sems, line_sems, plane_sems, rows_sems, grads_sems, vector_sems = refs[18:]
+    seq, wt = Z * inner, outer * C
+    s, w = lax.axis_index("seq"), lax.axis_index("wt")
+    z, x, y, c = s // inner, s % inner, w // C, w % C
+    sends = Sends(send_sems)
+    here = []
+
+    def at_z(to):
+        return {"seq": to * inner + x, "wt": w}
+
+    def at_x(by):
+        return {"seq": z * inner + (x + by) % inner, "wt": w}
+
+    def at_y(by):
+        return {"seq": s, "wt": (y + by) % outer * C + c}
+
+    at_c = {"seq": s, "wt": y * C + 1 - c}
+
+    def keep(source, target, waited=False):
+        copy = pltpu.make_async_copy(source, target, local_sems.at[len(here)])
+        copy.start()
+        here.append((waited, copy))
+        return copy
+
+    barrier = pltpu.get_barrier_semaphore()
+
+    def greet(i, carried):
+        @pl.when(i != s * wt + w)
+        def _():
+            pl.semaphore_signal(
+                barrier, inc=1, device_id={"seq": i // wt, "wt": i % wt}, device_id_type=MESH
+            )
+
+        return carried
+
+    lax.fori_loop(0, seq * wt, greet, 0)
+    pl.semaphore_wait(barrier, seq * wt - 1)
+
+    class Line:
+        def __init__(self, index, source, target):
+            self.source, self.target = source, target
+            self.sems = line_sems.at[index]
+
+        def forward(self, block, at, up_when, down_when):
+            place = self.target.at[at, x]
+            arrival = self.sems.at[at, x]
+            sends.start(up_when, block, place, arrival, at_z(jnp.minimum(z + 1, Z - 1)))
+            sends.start(down_when, block, place, arrival, at_z(jnp.maximum(z - 1, 0)))
+            return place, arrival
+
+        def across(self, when, block, at):
+            for j in range(1, inner):
+                sends.start(when, block, self.target.at[at, x], self.sems.at[at, x], at_x(j))
+
+        def begin(self):
+            keep(self.source, self.target.at[z, x])
+            self.forward(self.source, z, z < Z - 1, z > 0)
+            self.across(True, self.source, z)
+
+        def step(self, k):
+            for at, there, up_when, down_when in (
+                (jnp.maximum(z - k, 0), z - k >= 0, (z - k >= 0) & (z < Z - 1), None),
+                (jnp.minimum(z + k, Z - 1), z + k < Z, None, (z + k < Z) & (z > 0)),
+            ):
+                place, arrival = self.target.at[at, x], self.sems.at[at, x]
+
+                @pl.when(there)
+                def _(place=place, arrival=arrival):
+                    arrived(place, arrival, at_c)
+
+                if up_when is not None:
+                    sends.start(up_when, place, place, arrival, at_z(jnp.minimum(z + 1, Z - 1)))
+                else:
+                    sends.start(down_when, place, place, arrival, at_z(jnp.maximum(z - 1, 0)))
+                self.across(there, place, at)
+
+        def finish(self):
+            for at in range(Z):
+                for j in range(1, inner):
+                    from_x = (x + inner - j) % inner
+                    arrived(self.target.at[at, from_x], self.sems.at[at, from_x], at_c)
+
+    class Plane:
+        def __init__(self, index, source, target, x_first):
+            self.source, self.target, self.x_first = source, target, x_first
+            self.share = source.shape[1] // Z
+            self.sems = plane_sems.at[index]
+
+        def cut(self, at):
+            return self.source.at[:, pl.ds(pl.multiple_of(at * self.share, LANES), self.share)]
+
+        def place(self, at, x_at, i):
+            return self.target.at[at, x_at, :, i * self.share : (i + 1) * self.share]
+
+        def begin(self):
+            self.own = keep(self.cut(z), self.place(z, x, 0), True)
+            for k in range(1, Z):
+                to = (z + k) % Z
+                sends.start(True, self.cut(to), self.place(z, x, 0), self.sems.at[z, 0, 0], at_z(to))
+
+        def over_x(self, at, i):
+            place = self.place(at, x, i)
+            for j in range(1, inner):
+                sends.start(True, place, place, self.sems.at[at, j, i], at_x(j))
+
+        def over_y(self, at, j):
+            x_at = (x + inner - j) % inner
+            for i in range(1, outer):
+                sends.start(
+                    True, self.place(at, x_at, 0), self.place(at, x_at, i),
+                    self.sems.at[at, j, i], at_y(i),
+                )
+
+        def got(self, at, j, i):
+            arrived(self.place(at, (x + inner - j) % inner, i), self.sems.at[at, j, i], at_c)
+
+        def first(self, k):
+            at = (z + Z - k) % Z
+            if k == 0:
+                self.own.wait()
+            else:
+                self.got(at, 0, 0)
+            if self.x_first[k]:
+                self.over_x(at, 0)
+                self.over_y(at, 0)
+            else:
+                self.over_y(at, 0)
+                self.over_x(at, 0)
+
+        def second(self, k):
+            at = (z + Z - k) % Z
+            if self.x_first[k]:
+                for j in range(1, inner):
+                    self.got(at, j, 0)
+                    self.over_y(at, j)
+            else:
+                for i in range(1, outer):
+                    self.got(at, 0, i)
+                    self.over_x(at, i)
+
+        def finish(self, k):
+            at = (z + Z - k) % Z
+            for j in range(inner):
+                for i in range(outer):
+                    done = i == 0 if self.x_first[k] else j == 0
+                    if not done:
+                        self.got(at, j, i)
+
+    lines = [Line(0, xy, xy_to), Line(1, gates, gates_to), Line(2, out, out_to)]
+    order_xy, order_yx = [True] * Z, [False] * Z
+    planes = [
+        Plane(0, gate, gate_to, order_xy),
+        Plane(1, up, up_to, order_yx),
+        Plane(2, down, down_to, [k % 2 == 0 for k in range(Z)]),
+    ]
+
+    me = s * wt + w
+    keep(vectors, vectors_to.at[me])
+
+    def vector_copy(i):
+        return pltpu.make_async_remote_copy(
+            src_ref=vectors, dst_ref=vectors_to.at[me],
+            send_sem=vector_sems.at[0, i], recv_sem=vector_sems.at[1, me],
+            device_id={"seq": i // wt, "wt": i % wt}, device_id_type=MESH,
+        )
+
+    def vector_send(i, carried):
+        pl.when(i != me)(lambda: vector_copy(i).start())
+        return carried
+
+    def tokens_begin():
+        keep(tokens, tokens_to.at[w])
+        sends.start(True, tokens, tokens_to.at[w], rows_sems.at[w], at_c)
+        for i in range(1, outer):
+            sends.start(True, tokens, tokens_to.at[w], rows_sems.at[w], at_y(i))
+
+    def tokens_step():
+        for i in range(1, outer):
+            at = (y + outer - i) % outer * C + c
+            arrived(tokens_to.at[at], rows_sems.at[at], at_c)
+            sends.start(True, tokens_to.at[at], tokens_to.at[at], rows_sems.at[at], at_c)
+
+    def tokens_finish():
+        for i in range(outer):
+            at = (y + outer - i) % outer * C + 1 - c
+            arrived(tokens_to.at[at], rows_sems.at[at], at_c)
+
+    def grads_place(own, at, z_to):
+        return grads_to.at[own, (z_to - at + Z) % Z]
+
+    def grads_forward(at, source, there, way):
+        z_to = jnp.minimum(z + 1, Z - 1) if way > 0 else jnp.maximum(z - 1, 0)
+        room = z < Z - 1 if way > 0 else z > 0
+        when = room if there is None else there & room
+        sends.start(when, source, grads_place(0, at, z_to), grads_sems.at[0, at], at_z(z_to))
+
+    def grads_begin():
+        keep(grads, grads_place(0, z, z))
+        grads_forward(z, grads, None, 1)
+        grads_forward(z, grads, None, -1)
+        sends.start(True, grads, grads_place(1, z, z), grads_sems.at[1, z], at_c)
+
+    def grads_step(k):
+        for at, there, way in (
+            (jnp.maximum(z - k, 0), z - k >= 0, 1),
+            (jnp.minimum(z + k, Z - 1), z + k < Z, -1),
+        ):
+            place = grads_place(0, at, z)
+
+            @pl.when(there)
+            def _(place=place, at=at):
+                arrived(place, grads_sems.at[0, at], at_c)
+
+            grads_forward(at, place, there, way)
+            sends.start(there, place, grads_place(1, at, z), grads_sems.at[1, at], at_c)
+
+    def grads_finish():
+        for at in range(Z):
+            arrived(grads_place(1, at, z), grads_sems.at[1, at], at_c)
+
+    lines[0].begin()
+    tokens_begin()
+    lines[1].begin()
+    lax.fori_loop(0, seq * wt, vector_send, 0)
+    for k in range(1, Z):
+        lines[1].step(k)
+        lines[0].step(k)
+        if k == 1:
+            tokens_step()
+    planes[0].begin()
+    lines[2].begin()
+    planes[0].first(0)
+    for k in range(1, Z):
+        lines[2].step(k)
+        planes[0].first(k)
+    planes[1].begin()
+    for k in range(Z):
+        planes[1].first(k)
+        planes[0].second(k)
+    planes[2].begin()
+    for k in range(Z):
+        planes[2].first(k)
+        planes[1].second(k)
+    grads_begin()
+    for k in range(Z):
+        planes[2].second(k)
+    for k in range(1, Z):
+        grads_step(k)
+
+    for line in lines:
+        line.finish()
+    tokens_finish()
+    grads_finish()
+    for plane in planes:
+        for k in range(Z):
+            plane.finish(k)
+
+    def vector_wait(i, carried):
+        @pl.when(i != me)
+        def _():
+            vector_copy(i).wait_send()
+            arrived(vectors_to.at[i], vector_sems.at[1, i], at_c)
+
+        return carried
+
+    lax.fori_loop(0, seq * wt, vector_wait, 0)
+    sends.finish()
+    for waited, copy in here:
+        if not waited:
+            copy.wait()
+
+
+def gather_all(tokens, grads, vectors, gates, xy, out, gate, up, down):
+    inner, outer = sizes()
+    seq, wt = Z * inner, outer * C
+
+    def buffer(*shape, like):
+        return jax.ShapeDtypeStruct(shape, like.dtype)
+
+    def plane(weight):
+        rows, columns = weight.shape
+        return buffer(Z, inner, rows, outer * columns // Z, like=weight)
+
+    shapes = (
+        buffer(wt, *tokens.shape, like=tokens),
+        buffer(C, Z, *grads.shape, like=grads),
+        buffer(seq * wt, *vectors.shape, like=vectors),
+        buffer(Z, inner, *gates.shape, like=gates),
+        buffer(Z, inner, *xy.shape, like=xy),
+        buffer(Z, inner, *out.shape, like=out),
+        plane(gate),
+        plane(up),
+        plane(down),
+    )
+    copies = 3 * (2 + inner + (Z - 1) * 2 * inner) + 3 * (Z - 1 + Z * (inner + 2 * outer + inner * outer))
+    copies += 2 * outer + 3 + 4 * Z
+    dma = pltpu.SemaphoreType.DMA
+    return pl.pallas_call(
+        functools.partial(gather_kernel, (inner, outer)),
+        out_shape=shapes,
+        in_specs=[pl.BlockSpec(memory_space=pl.ANY)] * 9,
+        out_specs=[pl.BlockSpec(memory_space=pl.ANY)] * 9,
+        scratch_shapes=[
+            dma((copies,)),
+            dma((16,)),
+            dma((3, Z, inner)),
+            dma((3, Z, inner, outer)),
+            dma((wt,)),
+            dma((C, Z)),
+            dma((2, seq * wt)),
+        ],
+        compiler_params=pltpu.CompilerParams(collective_id=0, has_side_effects=True),
+        name="gather_all",
+    )(tokens, grads, vectors, gates, xy, out, gate, up, down)
 
 
 def scan_kernel(backward, a_ref, b_ref, h_ref, p_ref):
@@ -371,38 +671,41 @@
         + [decay_param]
         + [conv_weight[:, k].astype(F32) for k in range(taps_count)]
     )
-    vectors = lax.all_gather(vectors, ("seq", "wt"), axis=1, tiled=True)
+    vectors = jnp.pad(vectors, ((0, -vectors.shape[0] % 8), (0, -chunk % LANES)))
+
+    across = [(i, i % seq * wt + i // seq) for i in range(seq * wt)]
+    gates = jnp.concatenate([decay_gate_weight, input_gate_weight], axis=1)
+    gates = lax.ppermute(gates, ("seq", "wt"), across)
+
+    def padded(weight):
+        share = -(-hidden_cols // (Z * LANES)) * LANES
+        return jnp.pad(weight, ((0, 0), (0, Z * share - hidden_cols)))
+
+    xy_unit = jnp.concatenate([turned(x_weight, 1), turned(y_weight, 1)], axis=1)
+    (
+        group_tokens, grad_group, vectors, gate_all, xy_kernel, out_kernel,
+        gate_kernel, up_kernel, down_kernel,
+    ) = gather_all(
+        tokens, out_grad, vectors, gates, xy_unit, turned(out_weight, 1),
+        padded(gate_weight), padded(up_weight), padded(down_weight),
+    )
+    group_tokens = group_tokens.reshape(-1, width)
+    grad_group = grad_group.reshape(-1, width)
+    vectors = jnp.moveaxis(vectors[:, : 6 + taps_count, :chunk], 0, 1).reshape(6 + taps_count, -1)
     gain_one, gain_two = vectors[0], vectors[1]
     own_vectors = turned(
         lax.dynamic_slice(vectors[2:], (0, w * lru_cols), (taps_count + 4, lru_cols)), 1
     )
     tap_bias, decay_shift, input_shift, decay_log = (own_vectors[i] for i in range(4))
     taps = own_vectors[4:]
-
-    across = [(i, i % seq * wt + i // seq) for i in range(seq * wt)]
-    gates = jnp.concatenate([decay_gate_weight, input_gate_weight], axis=1)
-    gates = lax.ppermute(gates, ("seq", "wt"), across)
-
-    group_tokens = wt_gather(tokens)
-    xy_unit = jnp.concatenate([turned(x_weight, 1), turned(y_weight, 1)], axis=1)
-    gate_rows = chunk * 2 * block // xy_unit.shape[1]
-    xy_unit = jnp.concatenate([xy_unit, gates.reshape(gate_rows, xy_unit.shape[1])])
-    xy_blocks = seq_gather(xy_unit)
-    xy_kernel = assembled(xy_blocks, slice(0, weight_rows)).reshape(width, 2 * lru_cols)
-    gate_all = assembled(xy_blocks, slice(weight_rows, weight_rows + gate_rows))
+    xy_kernel = xy_kernel.reshape(width, -1)
+    out_kernel = out_kernel.reshape(width, -1)
+    gate_kernel = gate_kernel.reshape(width, -1)
+    up_kernel = up_kernel.reshape(width, -1)
+    down_kernel = down_kernel.reshape(width, -1)
     gate_all = turned(gate_all.reshape(lru_cols, 2 * block), 0)
     partner_rows = c_swap(gate_all[full:])
     shared_rows = in_order(gate_all[full:], partner_rows, 0)
-
-    gate_unit = z_exchange(gate_weight)
-    gate_kernel = plane_gather(gate_unit, True)
-    up_unit = z_exchange(up_weight)
-    up_kernel = plane_gather(up_unit, False)
-    out_kernel = assembled(seq_gather(turned(out_weight, 1)), slice(0, weight_rows))
-    out_kernel = out_kernel.reshape(width, lru_cols)
-    down_unit = z_exchange(down_weight)
-    down_kernel = plane_gather(down_unit, True)
-    grad_group = group_gather(out_grad)
 
     stream = tokens.astype(F32)
     group_normed, _ = normed_rows(group_tokens.astype(F32))
@@ -525,17 +828,18 @@
     own_sums = jnp.concatenate([turned_back(gates_grad, 0), turned_back(own_sums, 0)], axis=1)
     own_sums = lax.psum_scatter(own_sums, "seq", scatter_dimension=0, tiled=True)
     own_sums = lax.ppermute(own_sums, ("seq", "wt"), [(to, at) for at, to in across])
-    gains = lax.psum_scatter(
-        jnp.stack([gain_one_grad, gain_two_grad], axis=1),
-        ("seq", "wt"),
-        scatter_dimension=0,
-        tiled=True,
-    )
+    gains = jnp.stack([gain_one_grad, gain_two_grad])
+    for move, count in ((c_swap, None), (y_move, outer), (x_move, inner), (z_turn, Z)):
+        if count is None:
+            gains = gains + move(gains)
+        else:
+            gains = gains + sum(move(gains, j) for j in range(1, count))
+    gains = lax.dynamic_slice(gains, (0, (lax.axis_index("seq") * wt + w) * chunk), (2, chunk))
     sums = own_sums[:, 2 * block :]
     return (
         block_out,
         tokens_grad,
-        gains[:, 0],
+        gains[0],
         x_weight_grad,
         y_weight_grad,
         sums[:, 4:],
@@ -546,7 +850,7 @@
         sums[:, 2],
         sums[:, 3],
         out_weight_grad,
-        gains[:, 1],
+        gains[1],
         gate_grad,
         up_grad,
         down_grad,

time: 1510 us -> 1210 us (0.80)
  waiting for transfers between devices: 736 us -> 323 us
  Pallas kernels: 13.4 us -> 280 us
  starting transfers between devices: 315 us -> 256 us
  local copies, waits for them, and re-layouts: 123 us -> 85 us
  blocking collectives: 37.6 us -> 0 us
    pallas_call x0 -> x1, Pallas kernels: none -> 267 us  [gather_all(): pl.pallas_call(functools.partial(gather_kernel, (inner, outer)), out_shap...]
    ppermute x72 -> x48, waiting for transfers between devices: 231 us -> 101 us  [z_move(): return lax.ppermute(value, 'seq', pairs)]
    unnamed x3 -> x1, waiting for transfers between devices: 117 us -> 0.02 us
    ppermute x18 -> x7, waiting for transfers between devices: 182 us -> 85 us  [x_move(): return lax.ppermute(value, 'seq', pairs)]
    ppermute x12 -> x7, waiting for transfers between devices: 143 us -> 84.2 us  [y_move(): return lax.ppermute(value, 'wt', pairs)]
    ppermute x14, starting transfers between devices: 70.2 us -> 25.8 us  [full_scan(): moved = lax.ppermute(ends, 'seq', pairs)]
    all_gather x1 -> x0, blocking collectives: 37.6 us -> none  [per_device(): vectors = lax.all_gather(vectors, ('seq', 'wt'), axis=1, tiled=True)]
    dynamic_update_slice x57 -> x13, local copies, waits for them, and re-layouts: 29.5 us -> 0.54 us  [put(): return lax.dynamic_update_slice(buffer, value, starts)]
  transfers between devices with their start and end apart: 139 -> 94, of which waited for: 53 -> 35; matrix products, arithmetic and copies ran while one was open for 19% -> 17% of each run, Pallas kernels for 0% -> 0%
where the time goes in v2:
time: 1210 us; the launch traced here: 1200 us
  waiting for transfers between devices  323 us (27%)
  Pallas kernels  280 us (23%)
  starting transfers between devices  256 us (21%)
  matrix products  141 us (12%)
  other arithmetic  93.2 us (8%)
  local copies, waits for them, and re-layouts  85 us (7%)
  between operations  17.5 us (1%)
    pallas_call x1, Pallas kernels, gather_all(): pl.pallas_call(functools.partial(gather_kernel, (inner, outer)), out_shap...  267 us
    ppermute x48, starting transfers between devices, z_move(): return lax.ppermute(value, 'seq', pairs)  169 us
    ppermute x48, waiting for transfers between devices, z_move(): return lax.ppermute(value, 'seq', pairs)  101 us
    ppermute x7, waiting for transfers between devices, x_move(): return lax.ppermute(value, 'seq', pairs)  85 us
    ppermute x7, waiting for transfers between devices, y_move(): return lax.ppermute(value, 'wt', pairs)  84.2 us
    dot_general x15, matrix products, contract_last(): lax.dot_general(left_side, right_side, (((1,), (1,)), ((), ())), preferre...  60 us
    dot_general x8, matrix products, multiply(): return jnp.dot(left_side, right_side, preferred_element_type=F32)  44.9 us
    dot_general x9, matrix products, contract_rows(): lax.dot_general(left_side, right_side, (((0,), (0,)), ((), ())), preferre...  36.3 us
  transfers between devices with their start and end apart: 94, of which 35 were waited for; matrix products, arithmetic and copies ran while one was open for 17% of the time, Pallas kernels for 0%

profile of v2, /device:TPU:2, one launch (start us, length us, event | category | flops | bytes accessed | tf_op | source)
XLA Modules:
  0.0 1196.2 jit_solution(7881749265941709671)
XLA Ops:
  8.3 7.3 collective-permute-start
  23.8 266.6 %gather_all.1 = (bf16[4,128,2560]{2,1,0:T(8,128)(2,1)}, bf16[2,4,128,2560]{3,2,1,0:T(8,128)(2,1)}, f32[32,16,128]{2,1,0:T(8,128)}, bf16[4,2,80,512]{3,2,1,0:T(8,...) custom-call(bf16[128,2560]{1,0:T(8,128)(2,1)} %refs_0_.1, ...), custom_call_target="tpu_custom_call" | custom-call | tf_op jit(solution)/shard_map/gather_all/pallas_call | solution.py:527
  300.1 7.9 fusion.187
  366.7 16.1 %collective-permute-done.12 = bf16[128,2560]{1,0:T(8,128)(2,1)S(1)} collective-permute-done((bf16[128,2560]{1,0:T(8,128)(2,1)S(1)}, bf16[128,2560]{1,0:T(8,128)(2,1)S(1)}, u32[]{:S(2)}, u32[]{:S(2)}) %collective-permute-start.12) | collective-permute-done | bytes 655392 | tf_op jit(solution)/shard_map/ppermute | solution.py:57
  392.7 10.9 collective-permute-done.14
  404.9 10.5 fusion.190
  428.6 7.9 copy.115
  448.9 11.4 collective-permute-start.22
  464.0 9.2 fusion.189
  473.3 11.7 fusion.8
  491.1 7.4 fusion.192
  504.4 12.8 %add_convert_fusion = bf16[512,2560]{1,0:T(8,128)(2,1)} fusion(f32[512,2560]{1,0:T(8,128)} %fusion.72, bf16[2560,1024]{1,0:T(8,128)(2,1)} %bitcast.352, bf16[1024,1024]{1,0:T(8,128)(2,1)} %get-tuple-element.160), kind=kOutput, calls=%fused_computation.12 | convolution fusion | flops 2686976000 | bytes 14155776 | tf_op jit(solution)/shard_map/dot_general | solution.py:94
  517.4 7.3 convolution_convert_fusion
  530.9 8.2 fusion.21
  568.8 17.3 %collective-permute-done.78 = bf16[4,2,320,512]{3,2,1,0:T(8,128)(2,1)} collective-permute-done((bf16[4,2,320,512]{3,2,1,0:T(8,128)(2,1)}, bf16[4,2,320,512]{3,2,1,0:T(8,128)(2,1)}, u32[]{:S(2)}, u32[]{:S(2)}) %collective-permute-start.78) | collective-permute-done | bytes 2621472 | tf_op jit(solution)/shard_map/ppermute | solution.py:57
  602.0 43.5 %collective-permute-done.88 = bf16[4,320,1024]{2,1,0:T(8,128)(2,1)} collective-permute-done((bf16[4,320,1024]{2,1,0:T(8,128)(2,1)}, bf16[4,320,1024]{2,1,0:T(8,128)(2,1)}, u32[]{:S(2)}, u32[]{:S(2)}) %collective-permute-start.88) | collective-permute-done | bytes 2621472 | tf_op jit(solution)/shard_map/ppermute | solution.py:51
  659.3 16.1 %collective-permute-done.79 = bf16[4,320,512]{2,1,0:T(8,128)(2,1)} collective-permute-done((bf16[4,320,512]{2,1,0:T(8,128)(2,1)}, bf16[4,320,512]{2,1,0:T(8,128)(2,1)}, u32[]{:S(2)}, u32[]{:S(2)}) %collective-permute-start.79) | collective-permute-done | bytes 1310752 | tf_op jit(solution)/shard_map/ppermute | solution.py:51
  686.4 21.6 %collective-permute-done.89 = bf16[4,320,512]{2,1,0:T(8,128)(2,1)S(1)} collective-permute-done((bf16[4,320,512]{2,1,0:T(8,128)(2,1)S(1)}, bf16[4,320,512]{2,1,0:T(8,128)(2,1)S(1)}, u32[]{:S(2)}, u32[]{:S(2)}) %collective-permute-start.89) | collective-permute-done | bytes 1310752 | tf_op jit(solution)/shard_map/ppermute | solution.py:57
  724.7 16.8 %collective-permute-done.85 = bf16[320,512]{1,0:T(8,128)(2,1)S(1)} collective-permute-done((bf16[320,512]{1,0:T(8,128)(2,1)S(1)}, bf16[320,512]{1,0:T(8,128)(2,1)S(1)}, u32[]{:S(2)}, u32[]{:S(2)}) %collective-permute-start.85) | collective-permute-done | bytes 327712 | tf_op jit(solution)/shard_map/ppermute | solution.py:41
  741.5 16.0 %collective-permute-start.87 = (bf16[320,512]{1,0:T(8,128)(2,1)S(1)}, bf16[320,512]{1,0:T(8,128)(2,1)S(1)}, u32[]{:S(2)}, u32[]{:S(2)}) collective-permute-start(bf16[320,512]{1,0:T(8,128)(2,1)S(1)} %get-tuple-element.190), channel_id=1, source_target_pairs={{0,24},{4,28},{8,0},{12,4},{16,8},{20,12},{24,16},{28,20},{1,25},{... | collective-permute-start | bytes 983048 | tf_op jit(solution)/shard_map/ppermute | solution.py:41
  767.8 30.5 %collective-permute-start.26 = (bf16[128,2560]{1,0:T(8,128)(2,1)S(1)}, bf16[128,2560]{1,0:T(8,128)(2,1)S(1)}, u32[]{:S(2)}, u32[]{:S(2)}) collective-permute-start(bf16[128,2560]{1,0:T(8,128)(2,1)S(1)} %get-tuple-element.167), channel_id=1, source_target_pairs={{0,8},{4,12},{8,16},{12,20},{16,24},{20,28},{1,9},{5,13},{9,17},{1... | collective-permute-start | bytes 1966088 | tf_op jit(solution)/shard_map/ppermute | solution.py:41
  801.5 21.7 %collective-permute-start.92 = (bf16[320,512]{1,0:T(8,128)(2,1)S(1)}, bf16[320,512]{1,0:T(8,128)(2,1)S(1)}, u32[]{:S(2)}, u32[]{:S(2)}) collective-permute-start(bf16[320,512]{1,0:T(8,128)(2,1)S(1)} %get-tuple-element.187), channel_id=1, source_target_pairs={{0,24},{4,28},{8,0},{12,4},{16,8},{20,12},{24,16},{28,20},{1,25},{... | collective-permute-start | bytes 983048 | tf_op jit(solution)/shard_map/ppermute | solution.py:41
  823.3 10.1 collective-permute-done.36
  834.0 13.5 %collective-permute-done.29 = bf16[128,2560]{1,0:T(8,128)(2,1)S(1)} collective-permute-done((bf16[128,2560]{1,0:T(8,128)(2,1)S(1)}, bf16[128,2560]{1,0:T(8,128)(2,1)S(1)}, u32[]{:S(2)}, u32[]{:S(2)}) %collective-permute-start.29) | collective-permute-done | bytes 655392 | tf_op jit(solution)/shard_map/ppermute | solution.py:41
  860.6 25.5 %collective-permute-done.38 = bf16[256,2560]{1,0:T(8,128)(2,1)S(1)} collective-permute-done((bf16[256,2560]{1,0:T(8,128)(2,1)S(1)}, bf16[256,2560]{1,0:T(8,128)(2,1)S(1)}, u32[]{:S(2)}, u32[]{:S(2)}) %collective-permute-start.38) | collective-permute-done | bytes 1310752 | tf_op jit(solution)/shard_map/ppermute | solution.py:57
  940.3 9.3 collective-permute-start.71
  977.9 31.8 %collective-permute-done.47 = f32[3,640]{1,0:T(4,128)} collective-permute-done((f32[3,640]{1,0:T(4,128)}, f32[3,640]{1,0:T(4,128)}, u32[]{:S(2)}, u32[]{:S(2)}) %collective-permute-start.47) | collective-permute-done | bytes 7712 | tf_op jit(solution)/shard_map/ppermute | solution.py:804
  1035.7 22.9 %collective-permute-done.56 = bf16[4,320,640]{2,1,0:T(8,128)(2,1)} collective-permute-done((bf16[4,320,640]{2,1,0:T(8,128)(2,1)}, bf16[4,320,640]{2,1,0:T(8,128)(2,1)}, u32[]{:S(2)}, u32[]{:S(2)}) %collective-permute-start.56) | collective-permute-done | bytes 1638432 | tf_op jit(solution)/shard_map/ppermute | solution.py:51
  1091.5 7.3 collective-permute-done.73
  1124.5 7.2 collective-permute-start.70
  1133.9 10.2 collective-permute-done.70
  1150.0 8.6 collective-permute-done.69
  (656 shorter events, 453.5 us)
Async XLA Ops:
  7.3 1117.2 %reduce-scatter.2.cloned.1.call-start = ((), (), s32[]{:S(2)}) async-start(), calls=%async_computation.1 | async-start | bytes 1843200 | tf_op jit(solution)/shard_map/reduce_scatter | solution.py:829
  526.9 59.2 %collective-permute-start.78 = (bf16[4,2,320,512]{3,2,1,0:T(8,128)(2,1)}, bf16[4,2,320,512]{3,2,1,0:T(8,128)(2,1)}, u32[]{:S(2)}, u32[]{:S(2)}) collective-permute-start(bf16[4,2,320,512]{3,2,1,0:T(8,128)(2,1)} %slice.936), channel_id=1, source_target_pairs={{0,2},{1,3},{2,0},{3,1},{4,6},{5,7},{6,4},{7,5},{8,10},{9,11},{10,... | collective-permute-start | bytes 7864328 | tf_op jit(solution)/shard_map/ppermute | solution.py:57
  530.3 64.3 %collective-permute-start.83 = (bf16[4,320,1024]{2,1,0:T(8,128)(2,1)}, bf16[4,320,1024]{2,1,0:T(8,128)(2,1)}, u32[]{:S(2)}, u32[]{:S(2)}) collective-permute-start(bf16[4,320,1024]{2,1,0:T(8,128)(2,1)} %fusion.16), channel_id=1, source_target_pairs={{0,4},{4,0},{8,12},{12,8},{16,20},{20,16},{24,28},{28,24},{1,5},{5... | collective-permute-start | bytes 7864328 | tf_op jit(solution)/shard_map/ppermute | solution.py:51
  544.8 100.6 %collective-permute-start.88 = (bf16[4,320,1024]{2,1,0:T(8,128)(2,1)}, bf16[4,320,1024]{2,1,0:T(8,128)(2,1)}, u32[]{:S(2)}, u32[]{:S(2)}) collective-permute-start(bf16[4,320,1024]{2,1,0:T(8,128)(2,1)} %fusion.17), channel_id=1, source_target_pairs={{0,4},{4,0},{8,12},{12,8},{16,20},{20,16},{24,28},{28,24},{1,5},{5... | collective-permute-start | bytes 7864328 | tf_op jit(solution)/shard_map/ppermute | solution.py:51
  556.5 93.9 %collective-permute-start.31 = (bf16[128,2560]{1,0:T(8,128)(2,1)}, bf16[128,2560]{1,0:T(8,128)(2,1)}, u32[]{:S(2)}, u32[]{:S(2)}) collective-permute-start(bf16[128,2560]{1,0:T(8,128)(2,1)} %get-tuple-element.165), channel_id=1, source_target_pairs={{0,8},{4,12},{1,9},{5,13},{2,10},{6,14},{3,11},{7,15}} | collective-permute-start | bytes 1966088 | tf_op jit(solution)/shard_map/ppermute | solution.py:41
  560.7 149.7 %collective-permute-start.34 = (bf16[128,2560]{1,0:T(8,128)(2,1)}, bf16[128,2560]{1,0:T(8,128)(2,1)S(1)}, u32[]{:S(2)}, u32[]{:S(2)}) collective-permute-start(bf16[128,2560]{1,0:T(8,128)(2,1)} %get-tuple-element.166), channel_id=1, source_target_pairs={{24,16},{28,20},{25,17},{29,21},{26,18},{30,22},{27,19},{31,23}} | collective-permute-start | bytes 1966088 | tf_op jit(solution)/shard_map/ppermute | solution.py:41
  586.1 65.9 %collective-permute-start.24 = (bf16[128,2560]{1,0:T(8,128)(2,1)}, bf16[128,2560]{1,0:T(8,128)(2,1)}, u32[]{:S(2)}, u32[]{:S(2)}) collective-permute-start(bf16[128,2560]{1,0:T(8,128)(2,1)} %get-tuple-element.169), channel_id=1, source_target_pairs={{0,8},{4,12},{1,9},{5,13},{2,10},{6,14},{3,11},{7,15}} | collective-permute-start | bytes 1966088 | tf_op jit(solution)/shard_map/ppermute | solution.py:41
  594.6 120.0 %collective-permute-start.27 = (bf16[128,2560]{1,0:T(8,128)(2,1)}, bf16[128,2560]{1,0:T(8,128)(2,1)}, u32[]{:S(2)}, u32[]{:S(2)}) collective-permute-start(bf16[128,2560]{1,0:T(8,128)(2,1)} %get-tuple-element.170), channel_id=1, source_target_pairs={{24,16},{28,20},{25,17},{29,21},{26,18},{30,22},{27,19},{31,23}} | collective-permute-start | bytes 1966088 | tf_op jit(solution)/shard_map/ppermute | solution.py:41
  652.0 55.9 %collective-permute-start.89 = (bf16[4,320,512]{2,1,0:T(8,128)(2,1)S(1)}, bf16[4,320,512]{2,1,0:T(8,128)(2,1)S(1)}, u32[]{:S(2)}, u32[]{:S(2)}) collective-permute-start(bf16[4,320,512]{2,1,0:T(8,128)(2,1)S(1)} %slice.937), channel_id=1, source_target_pairs={{0,2},{1,3},{2,0},{3,1},{4,6},{5,7},{6,4},{7,5},{8,10},{9,11},{10,... | collective-permute-start | bytes 3932168 | tf_op jit(solution)/shard_map/ppermute | solution.py:57
  675.4 37.4 %collective-permute-start.32 = (bf16[128,2560]{1,0:T(8,128)(2,1)S(1)}, bf16[128,2560]{1,0:T(8,128)(2,1)S(1)}, u32[]{:S(2)}, u32[]{:S(2)}) collective-permute-start(bf16[128,2560]{1,0:T(8,128)(2,1)S(1)} %add_convert_fusion.4), channel_id=1, source_target_pairs={{0,8},{4,12},{8,16},{12,20},{1,9},{5,13},{9,17},{13,21},{2,10},{6,... | collective-permute-start | bytes 1966088 | tf_op jit(solution)/shard_map/ppermute | solution.py:41
  710.3 47.3 %collective-permute-start.81 = (bf16[320,512]{1,0:T(8,128)(2,1)S(1)}, bf16[320,512]{1,0:T(8,128)(2,1)S(1)}, u32[]{:S(2)}, u32[]{:S(2)}) collective-permute-start(bf16[320,512]{1,0:T(8,128)(2,1)S(1)} %get-tuple-element.194), channel_id=1, source_target_pairs={{0,16},{4,20},{8,24},{12,28},{16,0},{20,4},{24,8},{28,12},{1,17},{... | collective-permute-start | bytes 983048 | tf_op jit(solution)/shard_map/ppermute | solution.py:41
  712.8 48.9 %collective-permute-start.82 = (bf16[320,512]{1,0:T(8,128)(2,1)S(1)}, bf16[320,512]{1,0:T(8,128)(2,1)S(1)}, u32[]{:S(2)}, u32[]{:S(2)}) collective-permute-start(bf16[320,512]{1,0:T(8,128)(2,1)S(1)} %get-tuple-element.193), channel_id=1, source_target_pairs={{0,24},{4,28},{8,0},{12,4},{16,8},{20,12},{24,16},{28,20},{1,25},{... | collective-permute-start | bytes 983048 | tf_op jit(solution)/shard_map/ppermute | solution.py:41
  716.8 42.6 %collective-permute-start.86 = (bf16[320,512]{1,0:T(8,128)(2,1)S(1)}, bf16[320,512]{1,0:T(8,128)(2,1)S(1)}, u32[]{:S(2)}, u32[]{:S(2)}) collective-permute-start(bf16[320,512]{1,0:T(8,128)(2,1)S(1)} %get-tuple-element.191), channel_id=1, source_target_pairs={{0,16},{4,20},{8,24},{12,28},{16,0},{20,4},{24,8},{28,12},{1,17},{... | collective-permute-start | bytes 983048 | tf_op jit(solution)/shard_map/ppermute | solution.py:41
  724.0 43.8 %collective-permute-start.35 = (bf16[128,2560]{1,0:T(8,128)(2,1)S(1)}, bf16[128,2560]{1,0:T(8,128)(2,1)S(1)}, u32[]{:S(2)}, u32[]{:S(2)}) collective-permute-start(bf16[128,2560]{1,0:T(8,128)(2,1)S(1)} %get-tuple-element.164), channel_id=1, source_target_pairs={{16,8},{20,12},{24,16},{28,20},{17,9},{21,13},{25,17},{29,21},{18,... | collective-permute-start | bytes 1966088 | tf_op jit(solution)/shard_map/ppermute | solution.py:41
  757.6 42.3 %collective-permute-start.90 = (bf16[320,512]{1,0:T(8,128)(2,1)S(1)}, bf16[320,512]{1,0:T(8,128)(2,1)S(1)}, u32[]{:S(2)}, u32[]{:S(2)}) collective-permute-start(bf16[320,512]{1,0:T(8,128)(2,1)S(1)} %get-tuple-element.189), channel_id=1, source_target_pairs={{0,8},{4,12},{8,16},{12,20},{16,24},{20,28},{24,0},{28,4},{1,9},{5... | collective-permute-start | bytes 983048 | tf_op jit(solution)/shard_map/ppermute | solution.py:41
  759.4 42.1 %collective-permute-start.91 = (bf16[320,512]{1,0:T(8,128)(2,1)S(1)}, bf16[320,512]{1,0:T(8,128)(2,1)S(1)}, u32[]{:S(2)}, u32[]{:S(2)}) collective-permute-start(bf16[320,512]{1,0:T(8,128)(2,1)S(1)} %get-tuple-element.188), channel_id=1, source_target_pairs={{0,16},{4,20},{8,24},{12,28},{16,0},{20,4},{24,8},{28,12},{1,17},{... | collective-permute-start | bytes 983048 | tf_op jit(solution)/shard_map/ppermute | solution.py:41
  761.7 61.6 %collective-permute-start.33 = (bf16[128,2560]{1,0:T(8,128)(2,1)S(1)}, bf16[128,2560]{1,0:T(8,128)(2,1)S(1)}, u32[]{:S(2)}, u32[]{:S(2)}) collective-permute-start(bf16[128,2560]{1,0:T(8,128)(2,1)S(1)} %get-tuple-element.163), channel_id=1, source_target_pairs={{0,8},{4,12},{8,16},{12,20},{16,24},{20,28},{1,9},{5,13},{9,17},{1... | collective-permute-start | bytes 1966088 | tf_op jit(solution)/shard_map/ppermute | solution.py:41
  767.8 66.2 %collective-permute-start.26 = (bf16[128,2560]{1,0:T(8,128)(2,1)S(1)}, bf16[128,2560]{1,0:T(8,128)(2,1)S(1)}, u32[]{:S(2)}, u32[]{:S(2)}) collective-permute-start(bf16[128,2560]{1,0:T(8,128)(2,1)S(1)} %get-tuple-element.167), channel_id=1, source_target_pairs={{0,8},{4,12},{8,16},{12,20},{16,24},{20,28},{1,9},{5,13},{9,17},{1... | collective-permute-start | bytes 1966088 | tf_op jit(solution)/shard_map/ppermute | solution.py:41
  799.9 47.6 %collective-permute-start.29 = (bf16[128,2560]{1,0:T(8,128)(2,1)S(1)}, bf16[128,2560]{1,0:T(8,128)(2,1)S(1)}, u32[]{:S(2)}, u32[]{:S(2)}) collective-permute-start(bf16[128,2560]{1,0:T(8,128)(2,1)S(1)} %add_convert_fusion.5), channel_id=1, source_target_pairs={{8,0},{12,4},{16,8},{20,12},{24,16},{28,20},{9,1},{13,5},{17,9},{2... | collective-permute-start | bytes 1966088 | tf_op jit(solution)/shard_map/ppermute | solution.py:41
  801.5 52.4 %collective-permute-start.92 = (bf16[320,512]{1,0:T(8,128)(2,1)S(1)}, bf16[320,512]{1,0:T(8,128)(2,1)S(1)}, u32[]{:S(2)}, u32[]{:S(2)}) collective-permute-start(bf16[320,512]{1,0:T(8,128)(2,1)S(1)} %get-tuple-element.187), channel_id=1, source_target_pairs={{0,24},{4,28},{8,0},{12,4},{16,8},{20,12},{24,16},{28,20},{1,25},{... | collective-permute-start | bytes 983048 | tf_op jit(solution)/shard_map/ppermute | solution.py:41
  899.2 37.6 %collective-permute-start.39 = (f32[2,640]{1,0:T(2,128)S(1)}, f32[2,640]{1,0:T(2,128)S(1)}, u32[]{:S(2)}, u32[]{:S(2)}) collective-permute-start(f32[2,640]{1,0:T(2,128)S(1)} %pad_maximum_fusion.19), channel_id=1, source_target_pairs={{4,0},{8,4},{12,8},{16,12},{20,16},{24,20},{28,24},{5,1},{9,5},{13... | collective-permute-start | bytes 15368 | tf_op jit(solution)/shard_map/ppermute | solution.py:601
  903.8 36.4 %collective-permute-start.41 = (f32[2,640]{1,0:T(2,128)S(1)}, f32[2,640]{1,0:T(2,128)S(1)}, u32[]{:S(2)}, u32[]{:S(2)}) collective-permute-start(f32[2,640]{1,0:T(2,128)S(1)} %pad_maximum_fusion.19), channel_id=1, source_target_pairs={{12,0},{16,4},{20,8},{24,12},{28,16},{13,1},{17,5},{21,9},{25,13},... | collective-permute-start | bytes 15368 | tf_op jit(solution)/shard_map/ppermute | solution.py:601
  906.4 43.2 %collective-permute-start.43 = (f32[2,640]{1,0:T(2,128)S(1)}, f32[2,640]{1,0:T(2,128)S(1)}, u32[]{:S(2)}, u32[]{:S(2)}) collective-permute-start(f32[2,640]{1,0:T(2,128)S(1)} %pad_maximum_fusion.19), channel_id=1, source_target_pairs={{20,0},{24,4},{28,8},{21,1},{25,5},{29,9},{22,2},{26,6},{30,10},{2... | collective-permute-start | bytes 15368 | tf_op jit(solution)/shard_map/ppermute | solution.py:601
  940.3 85.4 %collective-permute-start.63 = (bf16[4,320,640]{2,1,0:T(8,128)(2,1)}, bf16[4,320,640]{2,1,0:T(8,128)(2,1)}, u32[]{:S(2)}, u32[]{:S(2)}) collective-permute-start(bf16[4,320,640]{2,1,0:T(8,128)(2,1)} %fusion.27), channel_id=1, source_target_pairs={{0,4},{4,0},{8,12},{12,8},{16,20},{20,16},{24,28},{28,24},{1,5},{5... | collective-permute-start | bytes 4915208 | tf_op jit(solution)/shard_map/ppermute | solution.py:51
  940.3 92.3 %collective-permute-start.71 = (bf16[4,320,640]{2,1,0:T(8,128)(2,1)}, bf16[4,320,640]{2,1,0:T(8,128)(2,1)}, u32[]{:S(2)}, u32[]{:S(2)}) collective-permute-start(bf16[4,320,640]{2,1,0:T(8,128)(2,1)} %fusion.28), channel_id=1, source_target_pairs={{0,4},{4,0},{8,12},{12,8},{16,20},{20,16},{24,28},{28,24},{1,5},{5... | collective-permute-start | bytes 4915208 | tf_op jit(solution)/shard_map/ppermute | solution.py:51
  971.5 38.2 %collective-permute-start.47 = (f32[3,640]{1,0:T(4,128)}, f32[3,640]{1,0:T(4,128)}, u32[]{:S(2)}, u32[]{:S(2)}) collective-permute-start(f32[3,640]{1,0:T(4,128)} %slice.672), channel_id=1, source_target_pairs={{4,0},{8,4},{12,8},{16,12},{20,16},{24,20},{28,24},{5,1},{9,5},{13... | collective-permute-start | bytes 23048 | tf_op jit(solution)/shard_map/ppermute | solution.py:804
  1017.5 41.2 %collective-permute-start.56 = (bf16[4,320,640]{2,1,0:T(8,128)(2,1)}, bf16[4,320,640]{2,1,0:T(8,128)(2,1)}, u32[]{:S(2)}, u32[]{:S(2)}) collective-permute-start(bf16[4,320,640]{2,1,0:T(8,128)(2,1)} %fusion.26), channel_id=1, source_target_pairs={{0,4},{4,0},{8,12},{12,8},{16,20},{20,16},{24,28},{28,24},{1,5},{5... | collective-permute-start | bytes 4915208 | tf_op jit(solution)/shard_map/ppermute | solution.py:51
  1025.6 96.1 %collective-permute-start.48 = (f32[256,2560]{1,0:T(8,128)S(1)}, f32[256,2560]{1,0:T(8,128)S(1)}, u32[]{:S(2)}, u32[]{:S(2)}) collective-permute-start(f32[256,2560]{1,0:T(8,128)S(1)} %convolution_add_fusion), channel_id=1, source_target_pairs={{0,1},{1,0},{2,3},{3,2},{4,5},{5,4},{6,7},{7,6},{8,9},{9,8},{10,11... | collective-permute-start | bytes 7864328 | tf_op jit(solution)/shard_map/ppermute | solution.py:63
  1031.5 47.4 %collective-permute-start.67 = (bf16[320,640]{1,0:T(8,128)(2,1)S(1)}, bf16[320,640]{1,0:T(8,128)(2,1)S(1)}, u32[]{:S(2)}, u32[]{:S(2)}) collective-permute-start(bf16[320,640]{1,0:T(8,128)(2,1)S(1)} %get-tuple-element.179), channel_id=1, source_target_pairs={{24,16},{28,20},{25,17},{29,21},{26,18},{30,22},{27,19},{31,23}} | collective-permute-start | bytes 1228808 | tf_op jit(solution)/shard_map/ppermute | solution.py:41
  1098.8 51.1 %collective-permute-start.66 = (bf16[320,640]{1,0:T(8,128)(2,1)}, bf16[320,640]{1,0:T(8,128)(2,1)}, u32[]{:S(2)}, u32[]{:S(2)}) collective-permute-start(bf16[320,640]{1,0:T(8,128)(2,1)} %get-tuple-element.176), channel_id=1, source_target_pairs={{0,8},{4,12},{8,16},{12,20},{16,24},{20,28},{1,9},{5,13},{9,17},{1... | collective-permute-start | bytes 1228808 | tf_op jit(solution)/shard_map/ppermute | solution.py:41
  1107.6 53.8 %collective-permute-start.74 = (bf16[320,640]{1,0:T(8,128)(2,1)}, bf16[320,640]{1,0:T(8,128)(2,1)}, u32[]{:S(2)}, u32[]{:S(2)}) collective-permute-start(bf16[320,640]{1,0:T(8,128)(2,1)} %get-tuple-element.172), channel_id=1, source_target_pairs={{0,8},{4,12},{8,16},{12,20},{16,24},{20,28},{1,9},{5,13},{9,17},{1... | collective-permute-start | bytes 1228808 | tf_op jit(solution)/shard_map/ppermute | solution.py:41
  1117.5 61.1 %collective-permute-start.59 = (bf16[320,640]{1,0:T(8,128)(2,1)}, bf16[320,640]{1,0:T(8,128)(2,1)}, u32[]{:S(2)}, u32[]{:S(2)}) collective-permute-start(bf16[320,640]{1,0:T(8,128)(2,1)} %get-tuple-element.180), channel_id=1, source_target_pairs={{0,8},{4,12},{8,16},{12,20},{16,24},{20,28},{1,9},{5,13},{9,17},{1... | collective-permute-start | bytes 1228808 | tf_op jit(solution)/shard_map/ppermute | solution.py:41
  (192 other events, 2640.9 us)
Sparse Core Ops, SparseCore 0:
  1021.5 74.8 reduce-scatter.1

commit v3 on v2

--- a/solution.py
+++ b/solution.py
@@ -116,47 +116,35 @@
     return line_scatter([pick(kept, (z - k) % Z, 0) for k in range(Z)])
 
 
-def plane_scatter(total, width, x_first):
+def plane_scatter(left_side, right_side, width, x_first, gate):
     inner, outer = sizes()
     z, x = places()[:2]
-    share = total.shape[1] // outer
-    total = total.reshape(Z, inner, -1, outer * share)
-    rows = total.shape[2]
+    share = right_side.shape[1] // outer
 
     def over_x(value):
-        kept = pick(value, x, 1)
+        total = pick(value, x, 1).astype(F32)
         for j in range(1, inner):
-            kept = kept + x_move(pick(value, (x + j) % inner, 1).astype(BF16), j).astype(F32)
-        return kept
-
-    def over_y(value):
-        kept = value[..., :share]
+            total = total + x_move(pick(value, (x + j) % inner, 1), j).astype(F32)
+        return total.astype(BF16)
+
+    def over_y(parts):
+        total = parts[0].astype(F32)
         for i in range(1, outer):
-            sent = value[..., i * share : (i + 1) * share].astype(BF16)
-            kept = kept + y_move(sent, -i).astype(F32)
-        return kept
-
-    kept = over_y(over_x(total)) if x_first else over_x(over_y(total))
-    kept = kept.astype(BF16)
+            total = total + y_move(parts[i], -i).astype(F32)
+        return total.astype(BF16)
+
+    parts = []
+    for i in range(outer):
+        part = contract_rows(left_side, right_side[:, i * share : (i + 1) * share]).astype(BF16)
+        parts.append(part.reshape(Z, inner, -1, share))
+    rows = parts[0].shape[2]
+    kept = over_y([over_x(part) for part in parts]) if x_first else over_x(over_y(parts))
+    kept = after(kept, gate)
     buffer = put(jnp.zeros((rows, Z * share), BF16), pick(kept, z, 0), (0, z * share))
     for k in range(1, Z):
         moved = z_move(pick(kept, (z + k) % Z, 0), k, range(Z))
         buffer = put(buffer, moved, (0, (z - k) % Z * share))
     return buffer[:, :width].astype(F32)
-
-
-def wt_gather(value):
-    _, outer = sizes()
-    _, _, y, c = places()
-    rows, width = value.shape
-    other = c_swap(value)
-    pair = jnp.where(
-        c == 0, jnp.concatenate([value, other]), jnp.concatenate([other, value])
-    )
-    buffer = put(jnp.zeros((outer, C * rows, width), value.dtype), pair[None], (y, 0, 0))
-    for i in range(1, outer):
-        buffer = put(buffer, y_move(pair, i)[None], ((y - i) % outer, 0, 0))
-    return buffer.reshape(outer * C * rows, width)
 
 
 def wt_scatter(product_of, *sides):
@@ -174,11 +162,6 @@
     for i in range(1, outer):
         total = total + y_move(pick(kept, (y + i) % outer, 0).astype(BF16), i).astype(F32)
     return total
-
-
-def group_gather(value):
-    blocks = line_gather(value)
-    return jnp.concatenate(blocks + [c_swap(block) for block in blocks])
 
 
 def group_scatter(product_of, *sides):
@@ -543,64 +526,737 @@
     )(tokens, grads, vectors, gates, xy, out, gate, up, down)
 
 
-def scan_kernel(backward, a_ref, b_ref, h_ref, p_ref):
-    rows, width = a_ref.shape
-    segments = 8
-    length = rows // segments
+class Place:
+    def __init__(self, shape):
+        self.inner, self.outer = shape
+        self.s, self.w = lax.axis_index("seq"), lax.axis_index("wt")
+        self.z, self.x = self.s // self.inner, self.s % self.inner
+        self.y, self.c = self.w // C, self.w % C
+        self.at_c = {"seq": self.s, "wt": self.y * C + 1 - self.c}
+        self.z_up, self.z_down = jnp.minimum(self.z + 1, Z - 1), jnp.maximum(self.z - 1, 0)
+
+    def at_z(self, to):
+        return {"seq": to * self.inner + self.x, "wt": self.w}
+
+    def at_x(self, by):
+        return {"seq": self.z * self.inner + (self.x + by) % self.inner, "wt": self.w}
+
+    def at_y(self, by):
+        return {"seq": self.s, "wt": (self.y + self.outer + by) % self.outer * C + self.c}
+
+    def greet(self):
+        barrier = pltpu.get_barrier_semaphore()
+        devices = [self.at_c]
+        devices += [self.at_z((self.z + k) % Z) for k in range(1, Z)]
+        devices += [self.at_x(j) for j in range(1, self.inner)]
+        devices += [self.at_y(i) for i in range(1, self.outer)]
+        for device in devices:
+            pl.semaphore_signal(barrier, inc=1, device_id=device, device_id_type=MESH)
+        pl.semaphore_wait(barrier, len(devices))
+
+
+def each_rows(count, step, body):
+    def run(i, carried):
+        body(pl.ds(pl.multiple_of(i * step, step), step))
+        return carried
+
+    lax.fori_loop(0, count // step, run, 0)
+
+
+class WtRows:
+    def __init__(self, me, sends, source, target, sems):
+        self.me, self.sends, self.source, self.target, self.sems = me, sends, source, target, sems
+
+    def begin(self):
+        me = self.me
+        for device in [me.at_y(i) for i in range(1, me.outer)] + [me.at_c]:
+            self.sends.start(True, self.source, self.target.at[me.w], self.sems.at[me.w], device)
+
+    def step(self):
+        me = self.me
+        for i in range(1, me.outer):
+            at = (me.y + me.outer - i) % me.outer * C + me.c
+            arrived(self.target.at[at], self.sems.at[at], me.at_c)
+            self.sends.start(True, self.target.at[at], self.target.at[at], self.sems.at[at], me.at_c)
+
+    def finish(self):
+        me = self.me
+        for i in range(me.outer):
+            at = (me.y + me.outer - i) % me.outer * C + 1 - me.c
+            arrived(self.target.at[at], self.sems.at[at], me.at_c)
+
+
+class GroupRows:
+    def __init__(self, me, sends, source, target, sems):
+        self.me, self.sends, self.source, self.target, self.sems = me, sends, source, target, sems
+
+    def place(self, own, at, z_to):
+        return self.target.at[own, (z_to - at + Z) % Z]
+
+    def forward(self, at, source, there, way):
+        me = self.me
+        z_to = me.z_up if way > 0 else me.z_down
+        room = me.z < Z - 1 if way > 0 else me.z > 0
+        when = room if there is None else there & room
+        self.sends.start(
+            when, source, self.place(0, at, z_to), self.sems.at[0, at], me.at_z(z_to)
+        )
+
+    def begin(self):
+        me = self.me
+        self.forward(me.z, self.source, None, 1)
+        self.forward(me.z, self.source, None, -1)
+        self.sends.start(
+            True, self.source, self.place(1, me.z, me.z), self.sems.at[1, me.z], me.at_c
+        )
+
+    def step(self, k):
+        me = self.me
+        for at, there, way in (
+            (jnp.maximum(me.z - k, 0), me.z - k >= 0, 1),
+            (jnp.minimum(me.z + k, Z - 1), me.z + k < Z, -1),
+        ):
+            place = self.place(0, at, me.z)
+
+            @pl.when(there)
+            def _(place=place, at=at):
+                arrived(place, self.sems.at[0, at], me.at_c)
+
+            self.forward(at, place, there, way)
+            self.sends.start(there, place, self.place(1, at, me.z), self.sems.at[1, at], me.at_c)
+
+    def finish(self):
+        me = self.me
+        for at in range(Z):
+            arrived(self.place(1, at, me.z), self.sems.at[1, at], me.at_c)
+
+
+def branch_kernel(
+    shape, sent, own, tokens, gain, group_to, middle, own_v, c_in, y_out, y_in, low,
+    send_sems, local_sems, c_sems, y_sems, group_sems,
+):
+    me = Place(shape)
+    outer = me.outer
+    rows = tokens.shape[0]
+    sends = Sends(send_sems)
+    load = pltpu.make_async_copy(own, own_v, local_sems.at[0])
+    load.start()
+    me.greet()
+    order = [(me.y + i) % outer for i in list(range(1, outer)) + [0]]
+    for at in order:
+        sends.start(True, sent.at[at], c_in.at[at], c_sems.at[at], me.at_c)
+    load.wait()
+    for i, at in enumerate(order):
+        arrived(c_in.at[at], c_sems.at[at], me.at_c)
+        if i < outer - 1:
+            each_rows(rows, 16, lambda r, i=i, at=at: y_out.__setitem__(
+                (i, r), (own_v[at, r] + c_in[at, r]).astype(BF16)))
+            sends.start(True, y_out.at[i], y_in.at[i], y_sems.at[i], me.at_y(i + 1))
+    for i in range(outer - 1):
+        arrived(y_in.at[i], y_sems.at[i], me.at_c)
+
+    def work(r):
+        total = tokens[r].astype(F32) + own_v[me.y, r] + c_in[me.y, r]
+        for i in range(outer - 1):
+            total = total + y_in[i, r].astype(F32)
+        inverse = lax.rsqrt(jnp.mean(total * total, axis=1, keepdims=True) + EPSILON)
+        middle[r] = total
+        low[r] = (total * inverse * gain[...]).astype(BF16)
+
+    each_rows(rows, 16, work)
+    keep = pltpu.make_async_copy(low, group_to.at[0, 0], local_sems.at[1])
+    keep.start()
+    group = GroupRows(me, sends, low, group_to, group_sems)
+    group.begin()
+    for k in range(1, Z):
+        group.step(k)
+    group.finish()
+    sends.finish()
+    keep.wait()
+
+
+def branch_and_group(sent, own, tokens, gain):
+    inner, outer = sizes()
+    rows, width = tokens.shape
+    dma = pltpu.SemaphoreType.DMA
+    vmem, anywhere = pl.BlockSpec(memory_space=pltpu.VMEM), pl.BlockSpec(memory_space=pl.ANY)
+    return pl.pallas_call(
+        functools.partial(branch_kernel, (inner, outer)),
+        out_shape=(
+            jax.ShapeDtypeStruct((C, Z, rows, width), BF16),
+            jax.ShapeDtypeStruct((rows, width), F32),
+        ),
+        in_specs=[anywhere, anywhere, vmem, vmem],
+        out_specs=(anywhere, vmem),
+        scratch_shapes=[
+            pltpu.VMEM((outer, rows, width), F32),
+            pltpu.VMEM((outer, rows, width), F32),
+            pltpu.VMEM((outer - 1, rows, width), BF16),
+            pltpu.VMEM((outer - 1, rows, width), BF16),
+            pltpu.VMEM((rows, width), BF16),
+            dma((2 * outer + 3 + 4 * (Z - 1),)),
+            dma((2,)),
+            dma((outer,)),
+            dma((outer - 1,)),
+            dma((C, Z)),
+        ],
+        compiler_params=pltpu.CompilerParams(
+            collective_id=1, has_side_effects=True, vmem_limit_bytes=40 * 1024 * 1024
+        ),
+        name="branch_and_group",
+    )(sent, own, tokens, gain)
+
+
+def line_order():
+    order = []
+    for k in [n for t in range(1, Z) for n in (t, Z - t)] + [0]:
+        if k not in order:
+            order.append(k)
+    return order
+
+
+def line_sum(me, sends, rows, term, ready, store, held, up, down, between=None):
+    z = me.z
+    waited = set()
+
+    def wait_for(k):
+        if k not in waited:
+            ready(k)
+            waited.add(k)
+
+    def add(when, target, slot, k, received=None):
+        def body(r):
+            value = term(k, r)
+            if received is not None:
+                value = value + received[slot - 1, r].astype(F32)
+            target[slot, r] = value.astype(BF16)
+
+        pl.when(when)(lambda: each_rows(rows, 16, body))
+
+    for t in range(1, Z):
+        slot = t - 1
+        for k, (out, into, sems), has, when, to in (
+            (t, up, z > 0, (z <= t - 1) & (z < Z - 1), me.z_up),
+            (Z - t, down, z < Z - 1, (z >= Z - t) & (z > 0), me.z_down),
+        ):
+            wait_for(k)
+            if t == 1:
+                add(when, out, slot, k)
+            else:
+                pl.when(when & has)(
+                    lambda into=into, sems=sems, slot=slot: arrived(
+                        into.at[slot - 1], sems.at[slot - 1], me.at_c
+                    )
+                )
+                add(when & has, out, slot, k, into)
+                add(when & jnp.logical_not(has), out, slot, k)
+            sends.start(when, out.at[slot], into.at[slot], sems.at[slot], me.at_z(to))
+        if between is not None:
+            between(t)
+    wait_for(0)
+    each_rows(rows, 16, lambda r: store(r, term(0, r)))
+    for (_, into, sems), has in ((up, z > 0), (down, z < Z - 1)):
+
+        @pl.when(has)
+        def _(into=into, sems=sems):
+            arrived(into.at[Z - 2], sems.at[Z - 2], me.at_c)
+            each_rows(rows, 16, lambda r: store(r, held(r) + into[Z - 2, r].astype(F32)))
+
+
+class PlaneTerms:
+    def __init__(self, me, sends, parts, target, sems, over_x, blocks):
+        self.me, self.sends, self.parts, self.target, self.sems = me, sends, parts, target, sems
+        self.over_x, self.blocks = over_x, blocks
+
+    def begin(self):
+        me = self.me
+        if self.over_x:
+            for j in range(1, me.inner):
+                for i, part in enumerate(self.parts):
+                    self.sends.start(
+                        True, part.at[self.blocks, (me.x + j) % me.inner],
+                        self.target.at[j - 1, i], self.sems.at[j - 1, i], me.at_x(j),
+                    )
+        else:
+            for i in range(1, me.outer):
+                self.sends.start(
+                    True, self.parts[i].at[self.blocks], self.target.at[i - 1],
+                    self.sems.at[0, i - 1], me.at_y(-i),
+                )
+
+    def finish(self):
+        me = self.me
+        if self.over_x:
+            for j in range(1, me.inner):
+                for i in range(me.outer):
+                    arrived(self.target.at[j - 1, i], self.sems.at[j - 1, i], me.at_c)
+        else:
+            for i in range(1, me.outer):
+                arrived(self.target.at[i - 1], self.sems.at[0, i - 1], me.at_c)
+
+
+def middle_kernel(shape, *refs):
+    outer = shape[1]
+    sent, own, middle, grads, gain = refs[:5]
+    parts = refs[5 : 5 + 3 * outer]
+    rows_to, d_middle, gain_grad = refs[5 + 3 * outer : 8 + 3 * outer]
+    targets = refs[8 + 3 * outer : 12 + 3 * outer]
+    middle_body(
+        shape, sent, own, middle, grads, gain, parts, targets, rows_to, d_middle, gain_grad,
+        *refs[12 + 3 * outer :],
+    )
+
+
+def plane_units(me, sends, parts, targets, sems):
+    outer = me.outer
+    gate, up, down = (parts[n * outer : (n + 1) * outer] for n in range(3))
+    every, low, high = slice(0, Z), slice(0, Z // 2), slice(Z // 2, Z)
+    return [
+        PlaneTerms(me, sends, down, targets[0], sems.at[0], True, every),
+        PlaneTerms(me, sends, gate, targets[1], sems.at[1], False, every),
+        PlaneTerms(me, sends, up, targets[2], sems.at[2], True, low),
+        PlaneTerms(me, sends, up, targets[3], sems.at[3], False, high),
+    ]
+
+
+def middle_body(
+    shape, sent, own, middle, grads, gain, parts, targets, rows_to, d_middle, gain_grad,
+    own_v, c_in, up_out, up_in, down_out, down_in, low,
+    send_sems, local_sems, c_sems, up_sems, down_sems, rows_sems, unit_sems,
+):
+    me = Place(shape)
+    rows = middle.shape[0]
+    sends = Sends(send_sems)
+    load = pltpu.make_async_copy(own, own_v, local_sems.at[0])
+    load.start()
+    me.greet()
+    for k in line_order():
+        sends.start(True, sent.at[k], c_in.at[k], c_sems.at[k], me.at_c)
+    units = plane_units(me, sends, parts, targets, unit_sems)
+    for unit in units:
+        unit.begin()
+    load.wait()
+
+    def ready(k):
+        arrived(c_in.at[k], c_sems.at[k], me.at_c)
+
+    def term(k, r):
+        return own_v[k, r] + c_in[k, r].astype(F32)
+
+    def store(r, value):
+        own_v[0, r] = value
+
+    line_sum(
+        me, sends, rows, term, ready, store, lambda r: own_v[0, r],
+        (up_out, up_in, up_sems), (down_out, down_in, down_sems),
+    )
+    gain_grad[...] = jnp.zeros_like(gain_grad)
+
+    def work(r):
+        values = middle[r]
+        inverse = lax.rsqrt(jnp.mean(values * values, axis=1, keepdims=True) + EPSILON)
+        normed = values * inverse
+        d_normed = own_v[0, r]
+        gain_grad[...] += d_normed * normed
+        scaled = d_normed * gain[...]
+        passed = inverse * (scaled - normed * jnp.mean(scaled * normed, axis=1, keepdims=True))
+        total = grads[r].astype(F32) + passed
+        d_middle[r] = total
+        low[r] = total.astype(BF16)
+
+    each_rows(rows, 16, work)
+    keep = pltpu.make_async_copy(low, rows_to.at[me.w], local_sems.at[1])
+    keep.start()
+    gather = WtRows(me, sends, low, rows_to, rows_sems)
+    gather.begin()
+    gather.step()
+    gather.finish()
+    for unit in units:
+        unit.finish()
+    sends.finish()
+    keep.wait()
+
+
+def middle_and_rows(sent, own, middle, grads, gain, parts):
+    inner, outer = sizes()
+    rows, width = middle.shape
+    unit_rows, share = parts[0].shape[2:]
+    over_x, over_y = (inner - 1, outer), (outer - 1,)
+    targets = [
+        jax.ShapeDtypeStruct(shape, BF16)
+        for shape in (
+            (*over_x, Z, unit_rows, share),
+            (*over_y, Z, inner, unit_rows, share),
+            (*over_x, Z // 2, unit_rows, share),
+            (*over_y, Z // 2, inner, unit_rows, share),
+        )
+    ]
+    unit_copies = 2 * (inner - 1) * outer + 2 * (outer - 1)
+    dma = pltpu.SemaphoreType.DMA
+    vmem, anywhere = pl.BlockSpec(memory_space=pltpu.VMEM), pl.BlockSpec(memory_space=pl.ANY)
+    return pl.pallas_call(
+        functools.partial(middle_kernel, (inner, outer)),
+        out_shape=(
+            jax.ShapeDtypeStruct((outer * C, rows, width), BF16),
+            jax.ShapeDtypeStruct((rows, width), F32),
+            jax.ShapeDtypeStruct((16, width), F32),
+            *targets,
+        ),
+        in_specs=[anywhere, anywhere, vmem, vmem, vmem] + [anywhere] * (3 * outer),
+        out_specs=(anywhere, vmem, vmem) + (anywhere,) * 4,
+        scratch_shapes=[
+            pltpu.VMEM((Z, rows, width), F32),
+            pltpu.VMEM((Z, rows, width), BF16),
+        ]
+        + [pltpu.VMEM((Z - 1, rows, width), BF16)] * 4
+        + [
+            pltpu.VMEM((rows, width), BF16),
+            dma((Z + 2 * (Z - 1) + 2 * outer + unit_copies,)),
+            dma((2,)),
+            dma((Z,)),
+            dma((Z - 1,)),
+            dma((Z - 1,)),
+            dma((outer * C,)),
+            dma((4, max(inner - 1, 1), outer)),
+        ],
+        compiler_params=pltpu.CompilerParams(
+            collective_id=2, has_side_effects=True, vmem_limit_bytes=48 * 1024 * 1024
+        ),
+        name="middle_and_rows",
+    )(sent, own, middle, grads, gain, *parts)
+
+
+class RowsSum:
+    def __init__(self, me, sends, terms, total, scratch, sems):
+        self.me, self.sends, self.terms, self.total = me, sends, terms, total
+        self.own, self.x_in, *ways = scratch
+        self.own_sems, self.x_sems, up_sems, down_sems = sems
+        self.up, self.down = (*ways[:2], up_sems), (*ways[2:], down_sems)
+
+    def begin(self):
+        me = self.me
+        self.loads = {}
+        for k in line_order():
+            at = (me.z + Z - k) % Z
+            for j in range(1, me.inner):
+                self.sends.start(
+                    True, self.terms.at[at, (me.x + j) % me.inner], self.x_in.at[j - 1, k],
+                    self.x_sems.at[j - 1, k], me.at_x(j),
+                )
+            self.loads[k] = pltpu.make_async_copy(
+                self.terms.at[at, me.x], self.own.at[k], self.own_sems.at[k]
+            )
+            self.loads[k].start()
+
+    def run(self, between=None):
+        me = self.me
+
+        def ready(k):
+            self.loads[k].wait()
+            for j in range(1, me.inner):
+                arrived(self.x_in.at[j - 1, k], self.x_sems.at[j - 1, k], me.at_c)
+
+        def term(k, r):
+            value = self.own[k, r].astype(F32)
+            for j in range(1, me.inner):
+                value = value + self.x_in[j - 1, k, r].astype(F32)
+            return value
+
+        def store(r, value):
+            self.total[r] = value
+
+        line_sum(
+            me, self.sends, self.total.shape[0], term, ready, store, lambda r: self.total[r],
+            self.up, self.down, between,
+        )
+
+
+def sums_kernel(shape, *refs):
+    inner, outer = shape
+    (units, wide, narrow, sent, own, tokens, gain, d_middle, gain_two_grad, vectors) = refs[:10]
+    (units_to, wide_to, narrow_to, tokens_grad, gains, vectors_to) = refs[10:16]
+    wide_scratch, narrow_scratch = refs[16:22], refs[22:28]
+    (own_v, c_in, y_out, y_in, all_in, vec_in) = refs[28:34]
+    (send_sems, local_sems, unit_sems, c_sems, y_sems, all_sems, vec_sems) = refs[34:41]
+    wide_sems, narrow_sems = refs[41:45], refs[45:49]
+    me = Place(shape)
+    rows = tokens.shape[0]
+    share = units.shape[3]
+    count = units.shape[0]
+    sends = Sends(send_sems)
+    loads = [pltpu.make_async_copy(own, own_v, local_sems.at[0])]
+    loads[0].start()
+    me.greet()
+
+    order = [(me.y + i) % outer for i in list(range(1, outer)) + [0]]
+    for at in order:
+        sends.start(True, sent.at[at], c_in.at[at], c_sems.at[at], me.at_c)
+    narrow_sum = RowsSum(me, sends, narrow, narrow_to, narrow_scratch, narrow_sems)
+    wide_sum = RowsSum(me, sends, wide, wide_to, wide_scratch, wide_sems)
+    narrow_sum.begin()
+    wide_sum.begin()
+
+    def columns(n, at):
+        return units_to.at[n, :, pl.ds(pl.multiple_of(at * share, LANES), share)]
+
+    def units_begin():
+        for n in range(count):
+            copy = pltpu.make_async_copy(units.at[n, me.z], columns(n, me.z), local_sems.at[1 + n])
+            copy.start()
+            loads.append(copy)
+            for k in range(1, Z):
+                to = (me.z + k) % Z
+                sends.start(
+                    True, units.at[n, to], columns(n, me.z), unit_sems.at[n, me.z], me.at_z(to)
+                )
+
+    def units_finish():
+        for n in range(count):
+            for k in range(1, Z):
+                at = (me.z + Z - k) % Z
+                arrived(columns(n, at), unit_sems.at[n, at], me.at_c)
+
+    units_begin()
+
+    def exchange(held, into, sems, first, devices):
+        for n, device in enumerate(devices):
+            sends.start(True, held, into.at[first + n], sems.at[first + n], device)
+
+    def gathered(held, into, sems, first, devices):
+        for n, _ in enumerate(devices):
+            arrived(into.at[first + n], sems.at[first + n], me.at_c)
+        total = into[first]
+        for n in range(1, len(devices)):
+            total = total + into[first + n]
+        return held[...] + total
+
+    stages = [
+        [me.at_c],
+        [me.at_y(i) for i in range(1, outer)],
+        [me.at_x(j) for j in range(1, inner)],
+        [me.at_z((me.z + k) % Z) for k in range(1, Z)],
+    ]
+    at_stage = [0]
+    for stage in stages:
+        at_stage.append(at_stage[-1] + len(stage))
+
+    loads[0].wait()
+    for i, at in enumerate(order):
+        arrived(c_in.at[at], c_sems.at[at], me.at_c)
+        if i < outer - 1:
+            each_rows(rows, 16, lambda r, i=i, at=at: y_out.__setitem__(
+                (i, r), (own_v[at, r] + c_in[at, r]).astype(BF16)))
+            sends.start(True, y_out.at[i], y_in.at[i], y_sems.at[i], me.at_y(i + 1))
+    x_stage, z_stage = stages[2], stages[3]
+    exchange(vectors, vec_in, vec_sems, 0, x_stage)
+    narrow_sum.run()
+    vectors_to[0] = gathered(vectors, vec_in, vec_sems, 0, x_stage)
+    exchange(vectors_to.at[0], vec_in, vec_sems, len(x_stage), z_stage)
+    for i in range(outer - 1):
+        arrived(y_in.at[i], y_sems.at[i], me.at_c)
+    gains[0] = jnp.zeros_like(gains[0])
+
+    def work(r):
+        d_normed = own_v[me.y, r] + c_in[me.y, r]
+        for i in range(outer - 1):
+            d_normed = d_normed + y_in[i, r].astype(F32)
+        stream = tokens[r].astype(F32)
+        inverse = lax.rsqrt(jnp.mean(stream * stream, axis=1, keepdims=True) + EPSILON)
+        normed = stream * inverse
+        part = d_normed * normed
+        gains[0, 0:8] += part[0:8] + part[8:16]
+        scaled = d_normed * gain[...]
+        passed = inverse * (scaled - normed * jnp.mean(scaled * normed, axis=1, keepdims=True))
+        tokens_grad[r] = (d_middle[r] + passed).astype(BF16)
+
+    each_rows(rows, 16, work)
+    gains[0, 8:16] = gain_two_grad[0:8] + gain_two_grad[8:16]
+    exchange(gains.at[0], all_in, all_sems, 0, stages[0])
+
+    def between(t):
+        if t <= 3:
+            held, into = gains.at[t - 1], gains.at[t]
+            into[...] = gathered(held, all_in, all_sems, at_stage[t - 1], stages[t - 1])
+            exchange(into, all_in, all_sems, at_stage[t], stages[t])
+
+    wide_sum.run(between)
+    gains[4] = gathered(gains.at[3], all_in, all_sems, at_stage[3], stages[3])
+    vectors_to[1] = gathered(vectors_to.at[0], vec_in, vec_sems, len(x_stage), z_stage)
+    units_finish()
+    sends.finish()
+    for copy in loads[1:]:
+        copy.wait()
+
+
+def last_sums(units, wide, narrow, sent, own, tokens, gain, d_middle, gain_two_grad, vectors):
+    inner, outer = sizes()
+    rows, width = tokens.shape
+    dma = pltpu.SemaphoreType.DMA
+    vmem, anywhere = pl.BlockSpec(memory_space=pltpu.VMEM), pl.BlockSpec(memory_space=pl.ANY)
+
+    def scratch(terms):
+        one = terms.shape[2:]
+        return [pltpu.VMEM((Z, *one), BF16), pltpu.VMEM((inner - 1, Z, *one), BF16)] + [
+            pltpu.VMEM((Z - 1, *one), BF16)
+        ] * 4
+
+    peers = 1 + (outer - 1) + (inner - 1) + (Z - 1)
+    count, _, unit_rows, share = units.shape
+    copies = 2 * outer - 1 + 2 * (Z * (inner - 1) + 2 * (Z - 1)) + count * (Z - 1)
+    copies += peers + (inner - 1) + (Z - 1)
+    line_sems = [dma((Z,)), dma((inner - 1, Z)), dma((Z - 1,)), dma((Z - 1,))]
+    return pl.pallas_call(
+        functools.partial(sums_kernel, (inner, outer)),
+        out_shape=(
+            jax.ShapeDtypeStruct((count, unit_rows, Z * share), BF16),
+            jax.ShapeDtypeStruct(wide.shape[2:], F32),
+            jax.ShapeDtypeStruct(narrow.shape[2:], F32),
+            jax.ShapeDtypeStruct((rows, width), BF16),
+            jax.ShapeDtypeStruct((5, 16, width), F32),
+            jax.ShapeDtypeStruct((2, *vectors.shape), F32),
+        ),
+        in_specs=[anywhere] * 5 + [vmem] * 5,
+        out_specs=(anywhere,) + (vmem,) * 5,
+        scratch_shapes=scratch(wide)
+        + scratch(narrow)
+        + [
+            pltpu.VMEM((outer, rows, width), F32),
+            pltpu.VMEM((outer, rows, width), F32),
+            pltpu.VMEM((outer - 1, rows, width), BF16),
+            pltpu.VMEM((outer - 1, rows, width), BF16),
+            pltpu.VMEM((peers, 16, width), F32),
+            pltpu.VMEM((inner - 1 + Z - 1, *vectors.shape), F32),
+            dma((copies,)),
+            dma((1 + count,)),
+            dma((count, Z)),
+            dma((outer,)),
+            dma((outer - 1,)),
+            dma((peers,)),
+            dma((inner - 1 + Z - 1,)),
+        ]
+        + line_sems * 2,
+        compiler_params=pltpu.CompilerParams(
+            collective_id=5, has_side_effects=True, vmem_limit_bytes=58 * 1024 * 1024
+        ),
+        name="last_sums",
+    )(units, wide, narrow, sent, own, tokens, gain, d_middle, gain_two_grad, vectors)
+
+
+def scan_kernel(backward, factors, inflows, states, entered, products, ends, ends_in, carry, send_sems, arrivals):
+    seq = ends_in.shape[0]
+    s = lax.axis_index("seq")
+    rows, width = factors.shape
+    barrier = pltpu.get_barrier_semaphore()
+
+    def device(at):
+        return {"seq": at, "wt": lax.axis_index("wt")}
+
+    def greet(i, carried):
+        @pl.when(i != s)
+        def _():
+            pl.semaphore_signal(barrier, inc=1, device_id=device(i), device_id_type=MESH)
+
+        return carried
+
+    lax.fori_loop(0, seq, greet, 0)
+    group = 8
+    at_row = lax.broadcasted_iota(jnp.int32, (group, width), 0)
 
     def step(i, carried):
         held, product = carried
-        at = length - 1 - i if backward else i
-        where = pl.ds(at, segments, stride=length)
-        factor = a_ref[where, :]
-        held = factor * held + b_ref[where, :]
-        product = factor * product
-        h_ref[where, :] = held
-        p_ref[where, :] = product
-        return held, product
+        i = rows // group - 1 - i if backward else i
+        where = pl.ds(pl.multiple_of(i * group, group), group)
+        factor, inflow = factors[where, :], inflows[where, :]
+        for by in (1, 2, 4):
+            inside = at_row < group - by if backward else at_row >= by
+            turn = group - by if backward else by
+            inflow = factor * jnp.where(inside, pltpu.roll(inflow, turn, 0), 0.0) + inflow
+            factor = factor * jnp.where(inside, pltpu.roll(factor, turn, 0), 1.0)
+        inflow = inflow + factor * held
+        factor = factor * product
+        states[where, :] = inflow
+        products[where, :] = factor
+        last = slice(0, 1) if backward else slice(group - 1, group)
+        return inflow[last], factor[last]
 
     held, product = lax.fori_loop(
-        0, length, step, (jnp.zeros((segments, width), F32), jnp.ones((segments, width), F32)),
-        unroll=4,
-    )
-    carry = jnp.zeros((1, width), F32)
-    scale = jnp.ones((1, width), F32)
-    order = range(segments - 1, -1, -1) if backward else range(segments)
-    for at in order:
-        if at != order[0]:
-            part = pl.ds(at * length, length)
-            local = p_ref[part, :]
-            h_ref[part, :] = h_ref[part, :] + local * carry
-            p_ref[part, :] = local * scale
-        carry = held[at : at + 1] + product[at : at + 1] * carry
-        scale = product[at : at + 1] * scale
-
-
-def local_scan(factor, inflow, backward):
-    shape = jax.ShapeDtypeStruct(factor.shape, F32)
-    column = pl.BlockSpec((factor.shape[0], LANES), lambda i: (0, i))
+        0, rows // group, step, (jnp.zeros((1, width), F32), jnp.ones((1, width), F32))
+    )
+    ends[0:1] = product
+    ends[1:2] = held
+    pl.semaphore_wait(barrier, seq - 1)
+
+    def copy_to(i):
+        return pltpu.make_async_remote_copy(
+            src_ref=ends, dst_ref=ends_in.at[s], send_sem=send_sems.at[i], recv_sem=arrivals.at[s],
+            device_id=device(i), device_id_type=MESH,
+        )
+
+    def later(i):
+        return i < s if backward else i > s
+
+    def send(i, carried):
+        pl.when(later(i))(lambda: copy_to(i).start())
+        return carried
+
+    lax.fori_loop(0, seq, send, 0)
+    carry[...] = jnp.zeros_like(carry)
+
+    def receive(n, carried):
+        i = seq - 1 - n if backward else n
+
+        @pl.when(jnp.logical_not(later(i)) & (i != s))
+        def _():
+            arrived(ends_in.at[i], arrivals.at[i], device((s + 1) % seq))
+            carry[0:1] = ends_in[i, 0:1] * carry[0:1] + ends_in[i, 1:2]
+
+        return carried
+
+    lax.fori_loop(0, seq, receive, 0)
+    entering = carry[0:1]
+    entered[...] = entering
+
+    def spread(i, carried):
+        where = pl.ds(pl.multiple_of(i * group, group), group)
+        states[where, :] += products[where, :] * entering
+        return carried
+
+    lax.fori_loop(0, rows // group, spread, 0)
+
+    def sent(i, carried):
+        pl.when(later(i))(lambda: copy_to(i).wait_send())
+        return carried
+
+    lax.fori_loop(0, seq, sent, 0)
+
+
+def full_scan(factor, inflow, backward):
+    seq = lax.axis_size("seq")
+    rows, width = factor.shape
+    vmem = pl.BlockSpec(memory_space=pltpu.VMEM)
     return pl.pallas_call(
         functools.partial(scan_kernel, backward),
-        out_shape=(shape, shape),
-        grid=(factor.shape[1] // LANES,),
-        in_specs=[column] * 2,
-        out_specs=(column,) * 2,
+        out_shape=(
+            jax.ShapeDtypeStruct((rows, width), F32),
+            jax.ShapeDtypeStruct((1, width), F32),
+        ),
+        in_specs=[vmem, vmem],
+        out_specs=(vmem, vmem),
+        scratch_shapes=[
+            pltpu.VMEM((rows, width), F32),
+            pltpu.VMEM((8, width), F32),
+            pltpu.VMEM((seq, 8, width), F32),
+            pltpu.VMEM((8, width), F32),
+            pltpu.SemaphoreType.DMA((seq,)),
+            pltpu.SemaphoreType.DMA((seq,)),
+        ],
+        compiler_params=pltpu.CompilerParams(
+            collective_id=4 if backward else 3,
+            has_side_effects=True,
+            vmem_limit_bytes=32 * 1024 * 1024,
+        ),
         name="scan_back" if backward else "scan_ahead",
     )(factor, inflow)
-
-
-def full_scan(factor, inflow, backward):
-    count = lax.axis_size("seq")
-    held, product = local_scan(factor, inflow, backward)
-    end = slice(0, 1) if backward else slice(held.shape[0] - 1, None)
-    ends = jnp.concatenate([product[end], held[end]])
-    sign = -1 if backward else 1
-    carry = jnp.zeros_like(held[:1])
-    for k in range(count - 1, 0, -1):
-        pairs = [(s, s + sign * k) for s in range(count) if 0 <= s + sign * k < count]
-        moved = lax.ppermute(ends, "seq", pairs)
-        carry = moved[:1] * carry + moved[1:]
-    return held + product * carry, carry
 
 
 def recurrence_terms(decay_pre, input_pre, decay_log, conv_float):
@@ -745,11 +1401,17 @@
     before = jnp.concatenate([state_in, states[:-1]])
     lru_low = states.astype(BF16).astype(F32)
     mixed_rows = (lru_low * y_gated).astype(BF16)
-    branch = wt_scatter(lambda rows_: contract_last(rows_, out_kernel), mixed_rows)
-    middle = stream + branch
-
-    normed_two, inverse_two = normed_rows(middle)
-    group_two = group_gather((normed_two * gain_two).astype(BF16))
+    mixed_parts = mixed_rows.reshape(outer, C, rows_dev, lru_cols)
+
+    def branch_of(at):
+        part = pick(mixed_parts, at, 1).reshape(outer * rows_dev, lru_cols)
+        return contract_last(part, out_kernel).reshape(outer, rows_dev, width)
+
+    group_two, middle = branch_and_group(
+        branch_of(1 - c), branch_of(c), tokens, gain_two[None]
+    )
+    group_two = group_two.reshape(C * Z * rows_dev, width)
+
     gate_pre = multiply(group_two, gate_kernel)
     up_pre = multiply(group_two, up_kernel)
     active, gelu_gate_back = jax.vjp(gelu_tanh, gate_pre)
@@ -758,18 +1420,66 @@
     d_hidden = multiply(grad_group, down_kernel)
     d_up = (d_hidden * active).astype(BF16)
     d_gate = gelu_gate_back(d_hidden * up_pre)[0].astype(BF16)
-    d_normed_two = group_scatter(
-        lambda g, u: contract_last(g, gate_kernel) + contract_last(u, up_kernel), d_gate, d_up
-    )
-    feed = group_scatter(lambda rows_: contract_last(rows_, down_kernel), hidden)
+    half_rows = Z * rows_dev
+
+    def d_normed_of(part):
+        total = contract_last(d_gate[part], gate_kernel) + contract_last(d_up[part], up_kernel)
+        return total.reshape(Z, rows_dev, width)
+
+    def terms_of(left_side, right_side):
+        share = right_side.shape[1] // outer
+        return [
+            contract_rows(left_side, right_side[:, i * share : (i + 1) * share])
+            .astype(BF16)
+            .reshape(Z, inner, weight_rows, share)
+            for i in range(outer)
+        ]
+
+    gate_terms = terms_of(group_two, d_gate)
+    up_terms = terms_of(group_two, d_up)
+    down_terms = terms_of(grad_group, hidden)
+    branch_rows, d_middle, gain_two_grad, *came = middle_and_rows(
+        d_normed_of(slice(half_rows, None)).astype(BF16),
+        d_normed_of(slice(0, half_rows)),
+        middle,
+        out_grad,
+        gain_two[None],
+        gate_terms + up_terms + down_terms,
+    )
+    branch_rows = branch_rows.reshape(-1, width)
+
+    def added_over_x(terms, moved):
+        return [
+            sum((moved[j - 1, i].astype(F32) for j in range(1, inner)), pick(term, x, 1).astype(F32))
+            for i, term in enumerate(terms)
+        ]
+
+    def added_over_y(term, moved):
+        return sum((moved[i - 1].astype(F32) for i in range(1, outer)), term.astype(F32))
+
+    half_z = Z // 2
+    down_x = added_over_x(down_terms, came[0])
+    gate_y = added_over_y(gate_terms[0], came[1])
+    up_x = added_over_x([term[:half_z] for term in up_terms], came[2])
+    up_y = added_over_y(up_terms[0][half_z:], came[3])
+    by_y = [jnp.concatenate([down_x[i], up_x[i]]).astype(BF16) for i in range(outer)]
+    by_y = sum(
+        (y_move(by_y[i], -i).astype(F32) for i in range(1, outer)),
+        jnp.concatenate([down_x[0], up_x[0]]),
+    )
+    by_x_all = jnp.concatenate([gate_y, up_y])
+    by_x = sum(
+        (
+            x_move(pick(by_x_all, (x + j) % inner, 1).astype(BF16), j).astype(F32)
+            for j in range(1, inner)
+        ),
+        pick(by_x_all, x, 1),
+    )
+    units = jnp.stack([by_x[:Z], jnp.concatenate([by_y[Z:], by_x[Z:]]), by_y[:Z]]).astype(BF16)
+
+    feed = group_scatter(lambda rows_: contract_last(rows_, down_kernel), after(hidden, d_middle))
     block_out = (middle + feed).astype(BF16)
-    down_grad = plane_scatter(contract_rows(grad_group, hidden), hidden_cols, True)
-    gate_grad = plane_scatter(contract_rows(group_two, d_gate), hidden_cols, False)
-    up_grad = plane_scatter(contract_rows(group_two, d_up), hidden_cols, True)
-    gain_two_grad = jnp.sum(d_normed_two * normed_two, axis=0)
-    d_middle = out_grad.astype(F32) + norm_back(d_normed_two, normed_two, inverse_two, gain_two)
-
-    branch_rows = wt_gather(d_middle.astype(BF16))
+
     d_mixed = multiply(branch_rows, out_kernel)
     d_lru = (d_mixed * y_gated).astype(BF16).astype(F32)
     d_y = gelu_y_back(d_mixed * lru_low)[0].astype(BF16)
@@ -804,44 +1514,55 @@
     ahead = lax.ppermute(d_conv[:reach], "seq", [(i + 1, i) for i in range(seq - 1)])
     d_extended = jnp.concatenate([d_conv, ahead], axis=0)
     d_x_branch = sum(taps[k] * d_extended[k : k + rows] for k in range(taps_count)).astype(BF16)
-    d_normed_one = wt_scatter(
-        lambda dx, dy: contract_last(dx, xy_kernel[:, :lru_cols])
-        + contract_last(dy, xy_kernel[:, lru_cols:]),
-        d_x_branch,
-        d_y,
-    )
-    normed_one, inverse_one = normed_rows(stream)
-    gain_one_grad = jnp.sum(d_normed_one * normed_one, axis=0)
-    tokens_grad = (d_middle + norm_back(d_normed_one, normed_one, inverse_one, gain_one)).astype(
-        BF16
-    )
-
-    out_weight_grad = turned_back(seq_scatter(contract_rows(branch_rows, mixed_rows)), 1)
-    y_weight_grad = turned_back(seq_scatter(contract_rows(group_one, d_y)), 1)
-    x_weight_grad = turned_back(seq_scatter(contract_rows(group_one, d_x_branch)), 1)
+    dx_parts = d_x_branch.reshape(outer, C, rows_dev, lru_cols)
+    dy_parts = d_y.reshape(outer, C, rows_dev, lru_cols)
+
+    def d_normed_one_of(at):
+        dx, dy = (
+            pick(parts, at, 1).reshape(outer * rows_dev, lru_cols) for parts in (dx_parts, dy_parts)
+        )
+        total = contract_last(dx, xy_kernel[:, :lru_cols]) + contract_last(
+            dy, xy_kernel[:, lru_cols:]
+        )
+        return total.reshape(outer, rows_dev, width)
+
+    wide = jnp.concatenate(
+        [
+            contract_rows(group_one, d_x_branch),
+            contract_rows(group_one, d_y),
+            contract_rows(branch_rows, mixed_rows),
+        ],
+        axis=1,
+    )
+    wide = wide.astype(BF16).reshape(Z, inner, weight_rows, 3 * lru_cols)
+    narrow = turned_back(gates_grad, 0).astype(BF16).reshape(Z, inner, chunk, 2 * block)
+    narrow = jnp.pad(narrow, ((0, 0), (0, 0), (0, -chunk % 16), (0, 0)))
     own_sums = jnp.stack(
         [jnp.sum(d_conv, axis=0), jnp.sum(d_decay_pre, axis=0), jnp.sum(d_input_pre, axis=0)]
         + [decay_log_grad]
         + [jnp.sum(d_conv * extended[reach - k : reach - k + rows], axis=0) for k in range(taps_count)],
-        axis=1,
-    )
-    own_sums = jnp.concatenate([turned_back(gates_grad, 0), turned_back(own_sums, 0)], axis=1)
-    own_sums = lax.psum_scatter(own_sums, "seq", scatter_dimension=0, tiled=True)
+    )
+    own_sums = turned_back(own_sums, 1)
+    units, wide, narrow, tokens_grad, gains, own_sums = last_sums(
+        units, wide, narrow, d_normed_one_of(1 - c), d_normed_one_of(c), tokens, gain_one[None],
+        d_middle, gain_two_grad, own_sums,
+    )
+    weight_grads = [
+        turned_back(wide[:, n * lru_cols : (n + 1) * lru_cols], 1) for n in range(3)
+    ]
+    gate_grad, up_grad, down_grad = (units[n, :, :hidden_cols].astype(F32) for n in range(3))
+    gains = gains[4].reshape(2, 8, width).sum(axis=1)
+    gains = lax.dynamic_slice(gains, (0, (lax.axis_index("seq") * wt + w) * chunk), (2, chunk))
+    sums = lax.dynamic_slice(own_sums[1], (0, lax.axis_index("seq") * chunk), (taps_count + 4, chunk))
+    own_sums = jnp.concatenate([narrow[:chunk], sums.T], axis=1)
     own_sums = lax.ppermute(own_sums, ("seq", "wt"), [(to, at) for at, to in across])
-    gains = jnp.stack([gain_one_grad, gain_two_grad])
-    for move, count in ((c_swap, None), (y_move, outer), (x_move, inner), (z_turn, Z)):
-        if count is None:
-            gains = gains + move(gains)
-        else:
-            gains = gains + sum(move(gains, j) for j in range(1, count))
-    gains = lax.dynamic_slice(gains, (0, (lax.axis_index("seq") * wt + w) * chunk), (2, chunk))
     sums = own_sums[:, 2 * block :]
     return (
         block_out,
         tokens_grad,
         gains[0],
-        x_weight_grad,
-        y_weight_grad,
+        weight_grads[0],
+        weight_grads[1],
         sums[:, 4:],
         sums[:, 0],
         own_sums[:, :block],
@@ -849,7 +1570,7 @@
         own_sums[:, block : 2 * block],
         sums[:, 2],
         sums[:, 3],
-        out_weight_grad,
+        weight_grads[2],
         gains[1],
         gate_grad,
         up_grad,

time: 1210 us -> 1000 us (0.83)
  Pallas kernels: 280 us -> 674 us
  waiting for transfers between devices: 323 us -> 29.5 us
  starting transfers between devices: 256 us -> 28.9 us
  other arithmetic: 93.2 us -> 58.1 us
  local copies, waits for them, and re-layouts: 85 us -> 51.6 us
  between operations: 17.5 us -> 2.61 us
    pallas_call x2 -> x5, Pallas kernels: 13.3 us -> 412 us  [the longest x1 218 us: last_sums(): pl.pallas_call(functools.partial(sums_kernel, (inner, outer)), out_shape=...]
    ppermute x48 -> x6, starting transfers between devices: 169 us -> 14.9 us  [z_move(): return lax.ppermute(value, 'seq', pairs)]
    ppermute x7 -> x1, waiting for transfers between devices: 85 us -> 0.01 us  [x_move(): return lax.ppermute(value, 'seq', pairs)]
    ppermute x7 -> x1, waiting for transfers between devices: 84.2 us -> 0.01 us  [y_move(): return lax.ppermute(value, 'wt', pairs)]
    ppermute x48 -> x6, waiting for transfers between devices: 101 us -> 21.4 us  [z_move(): return lax.ppermute(value, 'seq', pairs)]
    ppermute x14 -> x0, starting transfers between devices: 25.8 us -> none  [full_scan(): moved = lax.ppermute(ends, 'seq', pairs)]
    add x17 -> x2, other arithmetic: 26 us -> 1.16 us  [added_over_y(): sum((moved[i - 1].astype(F32) for i in range(1, outer)), term.astype(F32))]
    ppermute x1, waiting for transfers between devices: 31.8 us -> 7.84 us  [per_device(): lax.ppermute(d_conv[:reach], 'seq', [(i + 1, i) for i in range(seq - 1)])]
  transfers between devices with their start and end apart: 94 -> 16, of which waited for: 35 -> 5; matrix products, arithmetic and copies ran while one was open for 17% -> 10% of each run, Pallas kernels for 0% -> 22%
where the time goes in v3:
time: 1000 us; the launch traced here: 985 us
  Pallas kernels  674 us (67%)
  matrix products  140 us (14%)
  other arithmetic  58.1 us (6%)
  local copies, waits for them, and re-layouts  51.6 us (5%)
  waiting for transfers between devices  29.5 us (3%)
  starting transfers between devices  28.9 us (3%)
    pallas_call x1, Pallas kernels, gather_all(): pl.pallas_call(functools.partial(gather_kernel, (inner, outer)), out_shap...  262 us
    pallas_call x1, Pallas kernels, last_sums(): pl.pallas_call(functools.partial(sums_kernel, (inner, outer)), out_shape=...  218 us
    pallas_call x1, Pallas kernels, middle_and_rows(): pl.pallas_call(functools.partial(middle_kernel, (inner, outer)), out_shap...  106 us
    pallas_call x1, Pallas kernels, branch_and_group(): pl.pallas_call(functools.partial(branch_kernel, (inner, outer)), out_shap...  73.5 us
    dot_general x15, matrix products, contract_last(): lax.dot_general(left_side, right_side, (((1,), (1,)), ((), ())), preferre...  54.7 us
    dot_general x8, matrix products, multiply(): return jnp.dot(left_side, right_side, preferred_element_type=F32)  45.9 us
    dot_general x12, matrix products, contract_rows(): lax.dot_general(left_side, right_side, (((0,), (0,)), ((), ())), preferre...  39.4 us
    ppermute x6, waiting for transfers between devices, z_move(): return lax.ppermute(value, 'seq', pairs)  21.4 us
  transfers between devices with their start and end apart: 16, of which 5 were waited for; matrix products, arithmetic and copies ran while one was open for 10% of the time, Pallas kernels for 22%

profile of v3, /device:TPU:2, one launch (start us, length us, event | category | flops | bytes accessed | tf_op | source)
XLA Modules:
  0.0 984.6 jit_solution(2868935779332107865)
XLA Ops:
  1.7 4.5 collective-permute-start
  14.8 261.7 %gather_all.1 = (bf16[4,128,2560]{2,1,0:T(8,128)(2,1)}, bf16[2,4,128,2560]{3,2,1,0:T(8,128)(2,1)}, f32[32,16,128]{2,1,0:T(8,128)}, bf16[4,2,80,512]{3,2,1,0:T(8,...) custom-call(bf16[128,2560]{1,0:T(8,128)(2,1)} %refs_5_.1, ...), custom_call_target="tpu_custom_call" | custom-call | tf_op jit(solution)/shard_map/gather_all/pallas_call | solution.py:510
  287.1 8.7 fusion.142
  300.9 7.1 fusion.144
  322.9 6.3 scan_ahead.1
  333.9 73.5 %branch_and_group.1 = (bf16[2,4,128,2560]{3,2,1,0:T(8,128)(2,1)S(1)}, f32[128,2560]{1,0:T(8,128)S(1)}) custom-call(f32[2,128,2560]{2,1,0:T(8,128)S(1)} %fusion.86.sent, f32[2,128,2560]{2,1,0:T(8,128)S(1)} %fusion.84.own, bf16[128,2560]{1,0:T(8,128)(2,1)S(1)} %copy-done, f32[1,2560]{1,0:T(1,128)S(1)} %slice.457.gain.refs_4_), custom_call_target="tpu_custom_call" | custom-call | tf_op jit(solution)/shard_map/branch_and_group/pallas_call | solution.py:683
  407.4 9.0 fusion.143
  416.3 12.4 %fusion.8 = (bf16[1024,1024]{1,0:T(8,128)(2,1)S(1)}, bf16[1024,1024]{1,0:T(8,128)(2,1)S(1)}, bf16[1024,1024]{1,0:T(8,128)(2,1)}) fusion(f32[1024,1024]{1,0:T(8,128)} %fusion.144, f32[1024,1024]{1,0:T(8,128)} %fusion.143, bf16[1024,2560]{1,0:T(8,128)(2,1)S(1)} %bitcast.210, bf16[2560,1024]{1,0:T(8,128)(2,1)S(1)} %bitcast.281), kind=kOutput, calls=%fused_computation.29 | convolution fusion | flops 5395972096 | bytes 25165824 | tf_op jit(solution)/shard_map/dot_general | solution.py:106
  428.8 7.8 fusion.68
  436.6 7.1 fusion.65
  443.7 4.2 convolution_convert_fusion.6
  447.9 4.2 convolution_convert_fusion.5
  458.6 4.3 convolution_convert_fusion.2
  462.9 4.4 convolution_convert_fusion.1
  467.3 6.0 add_convert_fusion
  473.3 6.4 convolution_add_fusion
  482.6 105.8 %middle_and_rows.1 = (bf16[4,128,2560]{2,1,0:T(8,128)(2,1)}, f32[128,2560]{1,0:T(8,128)S(1)}, f32[16,2560]{1,0:T(8,128)S(1)}, bf16[1,2,4,320,512]{4,3,2,1,0:T(8,...) custom-call(bf16[4,128,2560]{2,1,0:T(8,128)(2,1)} %bitcast.250, ...), custom_call_target="tpu_custom_call" | custom-call | tf_op jit(solution)/shard_map/middle_and_rows/pallas_call | solution.py:897
  588.4 6.8 convert_multiply_fusion
  595.2 8.6 scan_back.1
  619.1 4.3 convolution_convert_fusion
  635.2 4.8 copy.69
  640.1 5.9 convolution_convert_fusion.7
  646.6 3.9 convolution_convert_fusion.8
  670.8 7.8 collective-permute-done.14
  679.3 4.9 convolution_add_fusion.2
  689.5 4.8 pad_maximum_fusion.refs_1_
  702.7 4.7 convert_add_fusion.1
  713.1 217.9 %last_sums.1 = (bf16[3,320,2048]{2,1,0:T(8,128)(2,1)}, f32[320,1920]{1,0:T(8,128)}, f32[80,512]{1,0:T(8,128)}, bf16[128,2560]{1,0:T(8,128)(2,1)}, f32[5,16,2560]{2,1,0:T(8,128)}, /*index=5*/f32[2,8,640]{2,1,0:T(8,128)}) custom-call(bf16[3,4,320,512]{3,2,1,0:T(8,128)(2,1)} %pad_maximum_fusion.1.refs_0_, bf16[4,2,320,1920]{3,2,1,0:T(8,128)(2,1)} %pad_maximum_fusion.refs_1_, ...), custom_call_target="tpu_custom_call" | custom-call | tf_op jit(solution)/shard_map/last_sums/pallas_call | solution.py:1108
  936.5 4.3 collective-permute-start.6
  944.9 8.2 collective-permute-done.6
  958.5 4.4 collective-permute-start.7
  970.9 10.1 %collective-permute-done.10 = bf16[128,2560]{1,0:T(8,128)(2,1)S(1)} collective-permute-done((bf16[128,2560]{1,0:T(8,128)(2,1)}, bf16[128,2560]{1,0:T(8,128)(2,1)S(1)}, u32[]{:S(2)}, u32[]{:S(2)}) %collective-permute-start.10) | collective-permute-done | bytes 655392 | tf_op jit(solution)/shard_map/ppermute | solution.py:41
  (395 shorter events, 147.1 us)
Async XLA Ops:
  1.7 12.5 %collective-permute-start = (bf16[80,512]{1,0:T(8,128)(2,1)S(1)}, bf16[80,512]{1,0:T(8,128)(2,1)S(1)}, u32[]{:S(2)}, u32[]{:S(2)}) collective-permute-start(bf16[80,512]{1,0:T(8,128)(2,1)S(1)} %pad_maximum_fusion.18), channel_id=1, source_target_pairs={{0,0},{1,4},{2,8},{3,12},{4,16},{5,20},{6,24},{7,28},{8,1},{9,5},{... | collective-permute-start | bytes 245768 | tf_op jit(solution)/shard_map/ppermute | solution.py:1334
  285.5 15.3 %slice-start.14 = ((s8[5242880]{0:T(1024)(128)(4,1)}), s8[4194304]{0:T(1024)(128)(4,1)S(1)}, s32[]{:S(2)}) async-start(s8[5242880]{0:T(1024)(128)(4,1)} %bitcast.270), calls=%async_computation.14 | async-start | bytes 8388608
  285.5 15.3 %slice-start.24 = ((s8[5242880]{0:T(1024)(128)(4,1)}), s8[4194304]{0:T(1024)(128)(4,1)S(1)}, s32[]{:S(2)}) async-start(s8[5242880]{0:T(1024)(128)(4,1)} %bitcast.286), calls=%async_computation.24 | async-start | bytes 8388608
  287.0 13.8 %slice-start.15 = ((s8[5242880]{0:T(1024)(128)(4,1)}), s8[1048576]{0:T(1024)(128)(4,1)S(1)}, s32[]{:S(2)}) async-start(s8[5242880]{0:T(1024)(128)(4,1)} %bitcast.270), calls=%async_computation.15 | async-start | bytes 2097152
  287.0 13.8 %slice-start.25 = ((s8[5242880]{0:T(1024)(128)(4,1)}), s8[1048576]{0:T(1024)(128)(4,1)S(1)}, s32[]{:S(2)}) async-start(s8[5242880]{0:T(1024)(128)(4,1)} %bitcast.286), calls=%async_computation.25 | async-start | bytes 2097152
  296.3 15.9 %collective-permute-start.1 = (bf16[3,640]{1,0:T(4,128)(2,1)}, bf16[3,640]{1,0:T(4,128)(2,1)S(1)}, u32[]{:S(2)}, u32[]{:S(2)}) collective-permute-start(bf16[3,640]{1,0:T(4,128)(2,1)} %slice.535), channel_id=1, source_target_pairs={{0,4},{4,8},{8,12},{12,16},{16,20},{20,24},{24,28},{1,5},{5,9},{9,... | collective-permute-start | bytes 11528 | tf_op jit(solution)/shard_map/ppermute | solution.py:1374
  308.2 7.0 collective-permute-start.3
  314.0 1.4 collective-permute-start.2
  333.9 82.5 %slice-start.20 = ((s8[5242880]{0:T(1024)(128)(4,1)}), s8[1048576]{0:T(1024)(128)(4,1)S(1)}, s32[]{:S(2)}) async-start(s8[5242880]{0:T(1024)(128)(4,1)} %bitcast.279), calls=%async_computation.20 | async-start | bytes 2097152
  455.3 25.6 %copy-start.22 = (bf16[2560,512]{1,0:T(8,128)(2,1)}, bf16[2560,512]{1,0:T(8,128)(2,1)S(1)}, u32[]{:S(2)}) copy-start(bf16[2560,512]{1,0:T(8,128)(2,1)S(1)} %convolution_convert_fusion.4) | copy-start | bytes 7864324
  458.6 21.2 %copy-start.33 = (bf16[2560,512]{1,0:T(8,128)(2,1)}, bf16[2560,512]{1,0:T(8,128)(2,1)S(1)}, u32[]{:S(2)}) copy-start(bf16[2560,512]{1,0:T(8,128)(2,1)S(1)} %convolution_convert_fusion.3) | copy-start | bytes 7864324
  482.6 105.9 %copy-start.12 = (f32[512,256]{1,0:T(8,128)S(1)}, f32[512,256]{1,0:T(8,128)}, u32[]{:S(2)}) copy-start(f32[512,256]{1,0:T(8,128)} %copy-done.11) | copy-start | bytes 1572868
  595.2 13.9 %copy-start.34 = (bf16[512,640]{1,0:T(8,128)(2,1)}, bf16[512,640]{1,0:T(8,128)(2,1)S(1)}, u32[]{:S(2)}) copy-start(bf16[512,640]{1,0:T(8,128)(2,1)S(1)} %get-tuple-element.134) | copy-start | bytes 1966084
  605.6 13.4 %slice-start.16 = ((s8[5242880]{0:T(1024)(128)(4,1)}), s8[4194304]{0:T(1024)(128)(4,1)S(1)}, s32[]{:S(2)}) async-start(s8[5242880]{0:T(1024)(128)(4,1)} %bitcast.273), calls=%async_computation.16 | async-start | bytes 8388608
  623.4 77.7 %collective-permute-start.4 = (bf16[512,2560]{1,0:T(8,128)(2,1)}, bf16[512,2560]{1,0:T(8,128)(2,1)}, u32[]{:S(2)}, u32[]{:S(2)}) collective-permute-start(bf16[512,2560]{1,0:T(8,128)(2,1)} %convolution_convert_fusion), channel_id=1, source_target_pairs={{0,1},{1,0},{2,3},{3,2},{4,5},{5,4},{6,7},{7,6},{8,9},{9,8},{10,11... | collective-permute-start | bytes 7864328 | tf_op jit(solution)/shard_map/ppermute | solution.py:63
  628.7 68.3 %collective-permute-start.12 = (bf16[6,320,512]{2,1,0:T(8,128)(2,1)}, bf16[6,320,512]{2,1,0:T(8,128)(2,1)}, u32[]{:S(2)}, u32[]{:S(2)}) collective-permute-start(bf16[6,320,512]{2,1,0:T(8,128)(2,1)} %pad_maximum_fusion.2), channel_id=1, source_target_pairs={{0,2},{1,3},{2,0},{3,1},{4,6},{5,7},{6,4},{7,5},{8,10},{9,11},{10,... | collective-permute-start | bytes 5898248 | tf_op jit(solution)/shard_map/ppermute | solution.py:57
  635.2 59.1 %collective-permute-start.11 = (bf16[6,320,512]{2,1,0:T(8,128)(2,1)}, bf16[6,320,512]{2,1,0:T(8,128)(2,1)}, u32[]{:S(2)}, u32[]{:S(2)}) collective-permute-start(bf16[6,320,512]{2,1,0:T(8,128)(2,1)} %fusion.23), channel_id=1, source_target_pairs={{0,4},{4,0},{8,12},{12,8},{16,20},{20,16},{24,28},{28,24},{1,5},{5... | collective-permute-start | bytes 5898248 | tf_op jit(solution)/shard_map/ppermute | solution.py:51
  640.1 10.5 %slice-start.2 = ((s8[6553600]{0:T(1024)(128)(4,1)}), s8[4194304]{0:T(1024)(128)(4,1)S(1)}, s32[]{:S(2)}) async-start(s8[6553600]{0:T(1024)(128)(4,1)} %bitcast.219), calls=%async_computation.2 | async-start | bytes 8388608
  646.0 11.5 %collective-permute-start.13 = (bf16[512,256]{1,0:T(8,128)(2,1)S(1)}, bf16[512,256]{1,0:T(8,128)(2,1)S(1)}, u32[]{:S(2)}, u32[]{:S(2)}) collective-permute-start(bf16[512,256]{1,0:T(8,128)(2,1)S(1)} %pad_maximum_fusion.15), channel_id=1, source_target_pairs={{0,1},{1,0},{2,3},{3,2},{4,5},{5,4},{6,7},{7,6},{8,9},{9,8},{10,11... | collective-permute-start | bytes 786440 | tf_op jit(solution)/shard_map/ppermute | solution.py:63
  663.1 15.5 %copy-start.36 = (f32[512,640]{1,0:T(8,128)S(1)}, f32[512,640]{1,0:T(8,128)}, u32[]{:S(2)}) copy-start(f32[512,640]{1,0:T(8,128)} %get-tuple-element.132) | copy-start | bytes 3932164
  664.0 14.6 %collective-permute-start.14 = (f32[3,640]{1,0:T(4,128)S(1)}, f32[3,640]{1,0:T(4,128)S(1)}, u32[]{:S(2)}, u32[]{:S(2)}) collective-permute-start(f32[3,640]{1,0:T(4,128)S(1)} %slice.590), channel_id=1, source_target_pairs={{4,0},{8,4},{12,8},{16,12},{20,16},{24,20},{28,24},{5,1},{9,5},{13... | collective-permute-start | bytes 23048 | tf_op jit(solution)/shard_map/ppermute | solution.py:1514
  707.5 227.5 %collective-permute-start.5 = (bf16[128,2560]{1,0:T(8,128)(2,1)S(1)}, bf16[128,2560]{1,0:T(8,128)(2,1)S(1)}, u32[]{:S(2)}, u32[]{:S(2)}) collective-permute-start(bf16[128,2560]{1,0:T(8,128)(2,1)S(1)} %get-tuple-element.142), channel_id=1, source_target_pairs={{0,8},{4,12},{1,9},{5,13},{2,10},{6,14},{3,11},{7,15}} | collective-permute-start | bytes 1966088 | tf_op jit(solution)/shard_map/ppermute | solution.py:41
  932.9 10.2 %copy-start.27 = (f32[320,1920]{1,0:T(8,128)S(1)}, f32[320,1920]{1,0:T(8,128)}, u32[]{:S(2)}) copy-start(f32[320,1920]{1,0:T(8,128)} %get-tuple-element.71) | copy-start | bytes 7372804
  932.9 20.2 %slice-start.6 = ((s8[5242880]{0:T(1024)(128)(4,1)}), s8[4194304]{0:T(1024)(128)(4,1)S(1)}, s32[]{:S(2)}) async-start(s8[5242880]{0:T(1024)(128)(4,1)} %bitcast.229), calls=%async_computation.6 | async-start | bytes 8388608
  934.2 10.7 %collective-permute-start.8 = (bf16[128,2560]{1,0:T(8,128)(2,1)S(1)}, bf16[128,2560]{1,0:T(8,128)(2,1)S(1)}, u32[]{:S(2)}, u32[]{:S(2)}) collective-permute-start(bf16[128,2560]{1,0:T(8,128)(2,1)S(1)} %get-tuple-element.143), channel_id=1, source_target_pairs={{24,16},{28,20},{25,17},{29,21},{26,18},{30,22},{27,19},{31,23}} | collective-permute-start | bytes 1966088 | tf_op jit(solution)/shard_map/ppermute | solution.py:41
  936.5 16.6 %collective-permute-start.6 = (bf16[128,2560]{1,0:T(8,128)(2,1)S(1)}, bf16[128,2560]{1,0:T(8,128)(2,1)S(1)}, u32[]{:S(2)}, u32[]{:S(2)}) collective-permute-start(bf16[128,2560]{1,0:T(8,128)(2,1)S(1)} %add_convert_fusion.4), channel_id=1, source_target_pairs={{0,8},{4,12},{8,16},{12,20},{1,9},{5,13},{9,17},{13,21},{2,10},{6,... | collective-permute-start | bytes 1966088 | tf_op jit(solution)/shard_map/ppermute | solution.py:41
  940.8 12.3 %slice-start.7 = ((s8[5242880]{0:T(1024)(128)(4,1)}), s8[1048576]{0:T(1024)(128)(4,1)S(1)}, s32[]{:S(2)}) async-start(s8[5242880]{0:T(1024)(128)(4,1)} %bitcast.229), calls=%async_computation.7 | async-start | bytes 2097152
  940.8 24.9 %collective-permute-start.15 = (f32[80,520]{1,0:T(8,128)S(1)}, f32[80,520]{1,0:T(8,128)S(1)}, u32[]{:S(2)}, u32[]{:S(2)}) collective-permute-start(f32[80,520]{1,0:T(8,128)S(1)} %pad_maximum_fusion.17), channel_id=1, source_target_pairs={{0,0},{4,1},{8,2},{12,3},{16,4},{20,5},{24,6},{28,7},{1,8},{5,9},{... | collective-permute-start | bytes 499208 | tf_op jit(solution)/shard_map/ppermute | solution.py:1558
  953.5 9.4 collective-permute-start.9
  958.5 12.5 %collective-permute-start.7 = (bf16[128,2560]{1,0:T(8,128)(2,1)S(1)}, bf16[128,2560]{1,0:T(8,128)(2,1)S(1)}, u32[]{:S(2)}, u32[]{:S(2)}) collective-permute-start(bf16[128,2560]{1,0:T(8,128)(2,1)S(1)} %get-tuple-element.140), channel_id=1, source_target_pairs={{0,8},{4,12},{8,16},{12,20},{16,24},{20,28},{1,9},{5,13},{9,17},{1... | collective-permute-start | bytes 1966088 | tf_op jit(solution)/shard_map/ppermute | solution.py:41
  963.9 17.2 %collective-permute-start.10 = (bf16[128,2560]{1,0:T(8,128)(2,1)}, bf16[128,2560]{1,0:T(8,128)(2,1)S(1)}, u32[]{:S(2)}, u32[]{:S(2)}) collective-permute-start(bf16[128,2560]{1,0:T(8,128)(2,1)} %add_convert_fusion.1), channel_id=1, source_target_pairs={{8,0},{12,4},{16,8},{20,12},{24,16},{28,20},{9,1},{13,5},{17,9},{2... | collective-permute-start | bytes 1966088 | tf_op jit(solution)/shard_map/ppermute | solution.py:41
  967.9 15.6 %copy-start.65 = (bf16[128,2560]{1,0:T(8,128)(2,1)S(1)}, bf16[128,2560]{1,0:T(8,128)(2,1)}, u32[]{:S(2)}) copy-start(bf16[128,2560]{1,0:T(8,128)(2,1)} %get-tuple-element.224) | copy-start | bytes 1966084
  (98 other events, 376.6 us)

commit v4 on v3

--- a/solution.py
+++ b/solution.py
@@ -162,6 +162,11 @@
     for i in range(1, outer):
         total = total + y_move(pick(kept, (y + i) % outer, 0).astype(BF16), i).astype(F32)
     return total
+
+
+def group_gather(value):
+    blocks = line_gather(value)
+    return jnp.concatenate(blocks + [c_swap(block) for block in blocks])
 
 
 def group_scatter(product_of, *sides):
@@ -208,9 +213,9 @@
 
 def gather_kernel(shape, *refs):
     inner, outer = shape
-    (tokens, grads, vectors, gates, xy, out, gate, up, down) = refs[:9]
-    (tokens_to, grads_to, vectors_to, gates_to, xy_to, out_to, gate_to, up_to, down_to) = refs[9:18]
-    send_sems, local_sems, line_sems, plane_sems, rows_sems, grads_sems, vector_sems = refs[18:]
+    (tokens, vectors, gates, xy, out, gate, up, down) = refs[:8]
+    (tokens_to, vectors_to, gates_to, xy_to, out_to, gate_to, up_to, down_to) = refs[8:16]
+    (gates_own, send_sems, local_sems, line_sems, plane_sems, rows_sems, vector_sems, turn_sems) = refs[16:]
     seq, wt = Z * inner, outer * C
     s, w = lax.axis_index("seq"), lax.axis_index("wt")
     z, x, y, c = s // inner, s % inner, w // C, w % C
@@ -293,8 +298,8 @@
                     arrived(self.target.at[at, from_x], self.sems.at[at, from_x], at_c)
 
     class Plane:
-        def __init__(self, index, source, target, x_first):
-            self.source, self.target, self.x_first = source, target, x_first
+        def __init__(self, index, source, target, x_first, whole):
+            self.source, self.target, self.x_first, self.whole = source, target, x_first, whole
             self.share = source.shape[1] // Z
             self.sems = plane_sems.at[index]
 
@@ -332,38 +337,34 @@
                 self.own.wait()
             else:
                 self.got(at, 0, 0)
-            if self.x_first[k]:
+            if self.x_first or self.whole:
                 self.over_x(at, 0)
+            if self.whole or not self.x_first:
                 self.over_y(at, 0)
-            else:
-                self.over_y(at, 0)
-                self.over_x(at, 0)
 
         def second(self, k):
             at = (z + Z - k) % Z
-            if self.x_first[k]:
+            if self.x_first:
                 for j in range(1, inner):
                     self.got(at, j, 0)
-                    self.over_y(at, j)
+                    if self.whole:
+                        self.over_y(at, j)
             else:
                 for i in range(1, outer):
                     self.got(at, 0, i)
-                    self.over_x(at, i)
 
         def finish(self, k):
-            at = (z + Z - k) % Z
-            for j in range(inner):
-                for i in range(outer):
-                    done = i == 0 if self.x_first[k] else j == 0
-                    if not done:
+            if self.whole:
+                at = (z + Z - k) % Z
+                for j in range(inner):
+                    for i in range(1, outer):
                         self.got(at, j, i)
 
-    lines = [Line(0, xy, xy_to), Line(1, gates, gates_to), Line(2, out, out_to)]
-    order_xy, order_yx = [True] * Z, [False] * Z
+    lines = [Line(0, xy, xy_to), Line(1, gates_own, gates_to), Line(2, out, out_to)]
     planes = [
-        Plane(0, gate, gate_to, order_xy),
-        Plane(1, up, up_to, order_yx),
-        Plane(2, down, down_to, [k % 2 == 0 for k in range(Z)]),
+        Plane(0, gate, gate_to, True, True),
+        Plane(1, up, up_to, False, False),
+        Plane(2, down, down_to, True, False),
     ]
 
     me = s * wt + w
@@ -397,41 +398,25 @@
             at = (y + outer - i) % outer * C + 1 - c
             arrived(tokens_to.at[at], rows_sems.at[at], at_c)
 
-    def grads_place(own, at, z_to):
-        return grads_to.at[own, (z_to - at + Z) % Z]
-
-    def grads_forward(at, source, there, way):
-        z_to = jnp.minimum(z + 1, Z - 1) if way > 0 else jnp.maximum(z - 1, 0)
-        room = z < Z - 1 if way > 0 else z > 0
-        when = room if there is None else there & room
-        sends.start(when, source, grads_place(0, at, z_to), grads_sems.at[0, at], at_z(z_to))
-
-    def grads_begin():
-        keep(grads, grads_place(0, z, z))
-        grads_forward(z, grads, None, 1)
-        grads_forward(z, grads, None, -1)
-        sends.start(True, grads, grads_place(1, z, z), grads_sems.at[1, z], at_c)
-
-    def grads_step(k):
-        for at, there, way in (
-            (jnp.maximum(z - k, 0), z - k >= 0, 1),
-            (jnp.minimum(z + k, Z - 1), z + k < Z, -1),
-        ):
-            place = grads_place(0, at, z)
-
-            @pl.when(there)
-            def _(place=place, at=at):
-                arrived(place, grads_sems.at[0, at], at_c)
-
-            grads_forward(at, place, there, way)
-            sends.start(there, place, grads_place(1, at, z), grads_sems.at[1, at], at_c)
-
-    def grads_finish():
-        for at in range(Z):
-            arrived(grads_place(1, at, z), grads_sems.at[1, at], at_c)
-
+    to_seq, to_wt = me % seq, me // seq
+    from_me = w * seq + s
+    turn = pltpu.make_async_remote_copy(
+        src_ref=gates, dst_ref=gates_own, send_sem=turn_sems.at[0], recv_sem=turn_sems.at[1],
+        device_id={"seq": to_seq, "wt": to_wt}, device_id_type=MESH,
+    )
+    stay = pltpu.make_async_copy(gates, gates_own, turn_sems.at[2])
+    here_too = from_me == me
+
+    pl.when(jnp.logical_not(here_too))(turn.start)
+    pl.when(here_too)(stay.start)
     lines[0].begin()
     tokens_begin()
+
+    @pl.when(jnp.logical_not(here_too))
+    def _():
+        arrived(gates_own, turn_sems.at[1], at_c)
+
+    pl.when(here_too)(stay.wait)
     lines[1].begin()
     lax.fori_loop(0, seq * wt, vector_send, 0)
     for k in range(1, Z):
@@ -439,33 +424,27 @@
         lines[0].step(k)
         if k == 1:
             tokens_step()
+            planes[1].begin()
+    for k in range(Z):
+        planes[1].first(k)
     planes[0].begin()
     lines[2].begin()
     planes[0].first(0)
     for k in range(1, Z):
         lines[2].step(k)
         planes[0].first(k)
-    planes[1].begin()
-    for k in range(Z):
-        planes[1].first(k)
-        planes[0].second(k)
     planes[2].begin()
     for k in range(Z):
         planes[2].first(k)
-        planes[1].second(k)
-    grads_begin()
-    for k in range(Z):
-        planes[2].second(k)
-    for k in range(1, Z):
-        grads_step(k)
+        planes[0].second(k)
 
     for line in lines:
         line.finish()
     tokens_finish()
-    grads_finish()
-    for plane in planes:
-        for k in range(Z):
-            plane.finish(k)
+    for k in range(Z):
+        planes[1].second(k)
+        planes[2].second(k)
+        planes[0].finish(k)
 
     def vector_wait(i, carried):
         @pl.when(i != me)
@@ -475,6 +454,7 @@
 
         return carried
 
+    pl.when(jnp.logical_not(here_too))(turn.wait_send)
     lax.fori_loop(0, seq * wt, vector_wait, 0)
     sends.finish()
     for waited, copy in here:
@@ -482,7 +462,7 @@
             copy.wait()
 
 
-def gather_all(tokens, grads, vectors, gates, xy, out, gate, up, down):
+def gather_all(tokens, vectors, gates, xy, out, gate, up, down):
     inner, outer = sizes()
     seq, wt = Z * inner, outer * C
 
@@ -495,7 +475,6 @@
 
     shapes = (
         buffer(wt, *tokens.shape, like=tokens),
-        buffer(C, Z, *grads.shape, like=grads),
         buffer(seq * wt, *vectors.shape, like=vectors),
         buffer(Z, inner, *gates.shape, like=gates),
         buffer(Z, inner, *xy.shape, like=xy),
@@ -510,20 +489,21 @@
     return pl.pallas_call(
         functools.partial(gather_kernel, (inner, outer)),
         out_shape=shapes,
-        in_specs=[pl.BlockSpec(memory_space=pl.ANY)] * 9,
-        out_specs=[pl.BlockSpec(memory_space=pl.ANY)] * 9,
+        in_specs=[pl.BlockSpec(memory_space=pl.ANY)] * 8,
+        out_specs=[pl.BlockSpec(memory_space=pl.ANY)] * 8,
         scratch_shapes=[
+            pltpu.VMEM(gates.shape, gates.dtype),
             dma((copies,)),
             dma((16,)),
             dma((3, Z, inner)),
             dma((3, Z, inner, outer)),
             dma((wt,)),
-            dma((C, Z)),
             dma((2, seq * wt)),
+            dma((3,)),
         ],
         compiler_params=pltpu.CompilerParams(collective_id=0, has_side_effects=True),
         name="gather_all",
-    )(tokens, grads, vectors, gates, xy, out, gate, up, down)
+    )(tokens, vectors, gates, xy, out, gate, up, down)
 
 
 class Place:
@@ -632,11 +612,14 @@
 
 
 def branch_kernel(
-    shape, sent, own, tokens, gain, group_to, middle, own_v, c_in, y_out, y_in, low,
-    send_sems, local_sems, c_sems, y_sems, group_sems,
+    shape, sent, own, tokens, gain, up_held, down_held, group_to, middle, up_to, down_to,
+    own_v, c_in, y_out, y_in, low,
+    send_sems, local_sems, c_sems, y_sems, group_sems, up_sems, down_sems,
 ):
+    del up_held, down_held
     me = Place(shape)
-    outer = me.outer
+    inner, outer = shape
+    share = up_to.shape[3] // outer
     rows = tokens.shape[0]
     sends = Sends(send_sems)
     load = pltpu.make_async_copy(own, own_v, local_sems.at[0])
@@ -645,6 +628,14 @@
     order = [(me.y + i) % outer for i in list(range(1, outer)) + [0]]
     for at in order:
         sends.start(True, sent.at[at], c_in.at[at], c_sems.at[at], me.at_c)
+
+    def columns(held, x_at, i):
+        return held.at[:, x_at, :, i * share : (i + 1) * share]
+
+    for j in range(1, inner):
+        for i in range(outer):
+            place = columns(up_to, me.x, i)
+            sends.start(True, place, place, up_sems.at[j - 1, i], me.at_x(j))
     load.wait()
     for i, at in enumerate(order):
         arrived(c_in.at[at], c_sems.at[at], me.at_c)
@@ -654,6 +645,13 @@
             sends.start(True, y_out.at[i], y_in.at[i], y_sems.at[i], me.at_y(i + 1))
     for i in range(outer - 1):
         arrived(y_in.at[i], y_sems.at[i], me.at_c)
+    for i in range(1, outer):
+        for j in range(inner):
+            x_at = (me.x + inner - j) % inner
+            sends.start(
+                True, columns(down_to, x_at, 0), columns(down_to, x_at, i),
+                down_sems.at[i - 1, j], me.at_y(i),
+            )
 
     def work(r):
         total = tokens[r].astype(F32) + own_v[me.y, r] + c_in[me.y, r]
@@ -671,11 +669,19 @@
     for k in range(1, Z):
         group.step(k)
     group.finish()
+    for j in range(1, inner):
+        for i in range(outer):
+            x_at = (me.x + inner - j) % inner
+            arrived(columns(up_to, x_at, i), up_sems.at[j - 1, i], me.at_c)
+    for i in range(1, outer):
+        for j in range(inner):
+            x_at = (me.x + inner - j) % inner
+            arrived(columns(down_to, x_at, i), down_sems.at[i - 1, j], me.at_c)
     sends.finish()
     keep.wait()
 
 
-def branch_and_group(sent, own, tokens, gain):
+def branch_and_group(sent, own, tokens, gain, up, down):
     inner, outer = sizes()
     rows, width = tokens.shape
     dma = pltpu.SemaphoreType.DMA
@@ -685,26 +691,31 @@
         out_shape=(
             jax.ShapeDtypeStruct((C, Z, rows, width), BF16),
             jax.ShapeDtypeStruct((rows, width), F32),
+            jax.ShapeDtypeStruct(up.shape, up.dtype),
+            jax.ShapeDtypeStruct(down.shape, down.dtype),
         ),
-        in_specs=[anywhere, anywhere, vmem, vmem],
-        out_specs=(anywhere, vmem),
+        in_specs=[anywhere, anywhere, vmem, vmem, anywhere, anywhere],
+        out_specs=(anywhere, vmem, anywhere, anywhere),
+        input_output_aliases={4: 2, 5: 3},
         scratch_shapes=[
             pltpu.VMEM((outer, rows, width), F32),
             pltpu.VMEM((outer, rows, width), F32),
             pltpu.VMEM((outer - 1, rows, width), BF16),
             pltpu.VMEM((outer - 1, rows, width), BF16),
             pltpu.VMEM((rows, width), BF16),
-            dma((2 * outer + 3 + 4 * (Z - 1),)),
+            dma((2 * outer + 3 + 4 * (Z - 1) + (inner - 1) * outer + inner * (outer - 1),)),
             dma((2,)),
             dma((outer,)),
             dma((outer - 1,)),
             dma((C, Z)),
+            dma((inner - 1, outer)),
+            dma((outer - 1, inner)),
         ],
         compiler_params=pltpu.CompilerParams(
             collective_id=1, has_side_effects=True, vmem_limit_bytes=40 * 1024 * 1024
         ),
         name="branch_and_group",
-    )(sent, own, tokens, gain)
+    )(sent, own, tokens, gain, up, down)
 
 
 def line_order():
@@ -717,12 +728,6 @@
 
 def line_sum(me, sends, rows, term, ready, store, held, up, down, between=None):
     z = me.z
-    waited = set()
-
-    def wait_for(k):
-        if k not in waited:
-            ready(k)
-            waited.add(k)
 
     def add(when, target, slot, k, received=None):
         def body(r):
@@ -739,7 +744,7 @@
             (t, up, z > 0, (z <= t - 1) & (z < Z - 1), me.z_up),
             (Z - t, down, z < Z - 1, (z >= Z - t) & (z > 0), me.z_down),
         ):
-            wait_for(k)
+            pl.when(when)(lambda k=k: ready(k))
             if t == 1:
                 add(when, out, slot, k)
             else:
@@ -753,7 +758,7 @@
             sends.start(when, out.at[slot], into.at[slot], sems.at[slot], me.at_z(to))
         if between is not None:
             between(t)
-    wait_for(0)
+    ready(0)
     each_rows(rows, 16, lambda r: store(r, term(0, r)))
     for (_, into, sems), has in ((up, z > 0), (down, z < Z - 1)):
 
@@ -764,9 +769,9 @@
 
 
 class PlaneTerms:
-    def __init__(self, me, sends, parts, target, sems, over_x, blocks):
+    def __init__(self, me, sends, parts, target, sems, over_x):
         self.me, self.sends, self.parts, self.target, self.sems = me, sends, parts, target, sems
-        self.over_x, self.blocks = over_x, blocks
+        self.over_x = over_x
 
     def begin(self):
         me = self.me
@@ -774,13 +779,13 @@
             for j in range(1, me.inner):
                 for i, part in enumerate(self.parts):
                     self.sends.start(
-                        True, part.at[self.blocks, (me.x + j) % me.inner],
+                        True, part.at[:, (me.x + j) % me.inner],
                         self.target.at[j - 1, i], self.sems.at[j - 1, i], me.at_x(j),
                     )
         else:
             for i in range(1, me.outer):
                 self.sends.start(
-                    True, self.parts[i].at[self.blocks], self.target.at[i - 1],
+                    True, self.parts[i], self.target.at[i - 1],
                     self.sems.at[0, i - 1], me.at_y(-i),
                 )
 
@@ -797,59 +802,78 @@
 
 def middle_kernel(shape, *refs):
     outer = shape[1]
-    sent, own, middle, grads, gain = refs[:5]
-    parts = refs[5 : 5 + 3 * outer]
-    rows_to, d_middle, gain_grad = refs[5 + 3 * outer : 8 + 3 * outer]
-    targets = refs[8 + 3 * outer : 12 + 3 * outer]
+    sent, own, middle, grads, gain, feed_sent, feed_own = refs[:7]
+    parts = refs[7 : 7 + 3 * outer]
+    rows_to, d_middle, gain_grad, block_out = refs[7 + 3 * outer : 11 + 3 * outer]
+    targets = refs[11 + 3 * outer : 14 + 3 * outer]
+    scratch = refs[14 + 3 * outer :]
     middle_body(
-        shape, sent, own, middle, grads, gain, parts, targets, rows_to, d_middle, gain_grad,
-        *refs[12 + 3 * outer :],
-    )
+        shape, sent, own, middle, grads, gain, feed_sent, feed_own, parts, targets,
+        rows_to, d_middle, gain_grad, block_out, scratch[:9], scratch[9:18], *scratch[18:],
+    )
+
+
+class PairSum:
+    def __init__(self, me, sends, sent, own, scratch):
+        self.me, self.sends, self.sent = me, sends, sent
+        (
+            self.held, self.c_in, up_out, up_in, down_out, down_in,
+            self.c_sems, up_sems, down_sems,
+        ) = scratch
+        self.up, self.down = (up_out, up_in, up_sems), (down_out, down_in, down_sems)
+
+    def begin(self):
+        for k in line_order():
+            self.sends.start(
+                True, self.sent.at[k], self.c_in.at[k], self.c_sems.at[k], self.me.at_c
+            )
+
+    def run(self):
+        def ready(k):
+            arrived(self.c_in.at[k], self.c_sems.at[k], self.me.at_c)
+
+        def term(k, r):
+            return self.held[k, r] + self.c_in[k, r].astype(F32)
+
+        def store(r, value):
+            self.held[0, r] = value
+
+        line_sum(
+            self.me, self.sends, self.held.shape[1], term, ready, store,
+            lambda r: self.held[0, r], self.up, self.down,
+        )
 
 
 def plane_units(me, sends, parts, targets, sems):
     outer = me.outer
-    gate, up, down = (parts[n * outer : (n + 1) * outer] for n in range(3))
-    every, low, high = slice(0, Z), slice(0, Z // 2), slice(Z // 2, Z)
     return [
-        PlaneTerms(me, sends, down, targets[0], sems.at[0], True, every),
-        PlaneTerms(me, sends, gate, targets[1], sems.at[1], False, every),
-        PlaneTerms(me, sends, up, targets[2], sems.at[2], True, low),
-        PlaneTerms(me, sends, up, targets[3], sems.at[3], False, high),
+        PlaneTerms(me, sends, parts[n * outer : (n + 1) * outer], targets[n], sems.at[n], n != 1)
+        for n in (1, 2, 0)
     ]
 
 
 def middle_body(
-    shape, sent, own, middle, grads, gain, parts, targets, rows_to, d_middle, gain_grad,
-    own_v, c_in, up_out, up_in, down_out, down_in, low,
-    send_sems, local_sems, c_sems, up_sems, down_sems, rows_sems, unit_sems,
+    shape, sent, own, middle, grads, gain, feed_sent, feed_own, parts, targets,
+    rows_to, d_middle, gain_grad, block_out, sum_scratch, feed_scratch, low,
+    send_sems, local_sems, rows_sems, unit_sems,
 ):
     me = Place(shape)
     rows = middle.shape[0]
     sends = Sends(send_sems)
-    load = pltpu.make_async_copy(own, own_v, local_sems.at[0])
+    total = PairSum(me, sends, sent, own, sum_scratch)
+    feed = PairSum(me, sends, feed_sent, feed_own, feed_scratch)
+    load = pltpu.make_async_copy(own, total.held, local_sems.at[0])
+    feed_load = pltpu.make_async_copy(feed_own, feed.held, local_sems.at[2])
     load.start()
     me.greet()
-    for k in line_order():
-        sends.start(True, sent.at[k], c_in.at[k], c_sems.at[k], me.at_c)
+    total.begin()
     units = plane_units(me, sends, parts, targets, unit_sems)
     for unit in units:
         unit.begin()
+    feed_load.start()
     load.wait()
-
-    def ready(k):
-        arrived(c_in.at[k], c_sems.at[k], me.at_c)
-
-    def term(k, r):
-        return own_v[k, r] + c_in[k, r].astype(F32)
-
-    def store(r, value):
-        own_v[0, r] = value
-
-    line_sum(
-        me, sends, rows, term, ready, store, lambda r: own_v[0, r],
-        (up_out, up_in, up_sems), (down_out, down_in, down_sems),
-    )
+    total.run()
+    own_v = total.held
     gain_grad[...] = jnp.zeros_like(gain_grad)
 
     def work(r):
@@ -869,6 +893,11 @@
     keep.start()
     gather = WtRows(me, sends, low, rows_to, rows_sems)
     gather.begin()
+    feed.begin()
+    feed_load.wait()
+    feed.run()
+    each_rows(rows, 16, lambda r: block_out.__setitem__(
+        r, (middle[r] + feed.held[0, r]).astype(BF16)))
     gather.step()
     gather.finish()
     for unit in units:
@@ -877,7 +906,7 @@
     keep.wait()
 
 
-def middle_and_rows(sent, own, middle, grads, gain, parts):
+def middle_and_rows(sent, own, middle, grads, gain, feed_sent, feed_own, parts):
     inner, outer = sizes()
     rows, width = middle.shape
     unit_rows, share = parts[0].shape[2:]
@@ -887,12 +916,14 @@
         for shape in (
             (*over_x, Z, unit_rows, share),
             (*over_y, Z, inner, unit_rows, share),
-            (*over_x, Z // 2, unit_rows, share),
-            (*over_y, Z // 2, inner, unit_rows, share),
+            (*over_x, Z, unit_rows, share),
         )
     ]
-    unit_copies = 2 * (inner - 1) * outer + 2 * (outer - 1)
+    unit_copies = 2 * (inner - 1) * outer + (outer - 1)
+    pair_scratch = [pltpu.VMEM((Z, rows, width), F32), pltpu.VMEM((Z, rows, width), BF16)]
+    pair_scratch += [pltpu.VMEM((Z - 1, rows, width), BF16)] * 4
     dma = pltpu.SemaphoreType.DMA
+    pair_scratch += [dma((Z,)), dma((Z - 1,)), dma((Z - 1,))]
     vmem, anywhere = pl.BlockSpec(memory_space=pltpu.VMEM), pl.BlockSpec(memory_space=pl.ANY)
     return pl.pallas_call(
         functools.partial(middle_kernel, (inner, outer)),
@@ -900,30 +931,24 @@
             jax.ShapeDtypeStruct((outer * C, rows, width), BF16),
             jax.ShapeDtypeStruct((rows, width), F32),
             jax.ShapeDtypeStruct((16, width), F32),
+            jax.ShapeDtypeStruct((rows, width), BF16),
             *targets,
         ),
-        in_specs=[anywhere, anywhere, vmem, vmem, vmem] + [anywhere] * (3 * outer),
-        out_specs=(anywhere, vmem, vmem) + (anywhere,) * 4,
-        scratch_shapes=[
-            pltpu.VMEM((Z, rows, width), F32),
-            pltpu.VMEM((Z, rows, width), BF16),
-        ]
-        + [pltpu.VMEM((Z - 1, rows, width), BF16)] * 4
+        in_specs=[anywhere, anywhere, vmem, vmem, vmem] + [anywhere] * (2 + 3 * outer),
+        out_specs=(anywhere, vmem, vmem, vmem) + (anywhere,) * 3,
+        scratch_shapes=pair_scratch * 2
         + [
             pltpu.VMEM((rows, width), BF16),
-            dma((Z + 2 * (Z - 1) + 2 * outer + unit_copies,)),
-            dma((2,)),
-            dma((Z,)),
-            dma((Z - 1,)),
-            dma((Z - 1,)),
+            dma((2 * (Z + 2 * (Z - 1)) + 2 * outer + unit_copies,)),
+            dma((3,)),
             dma((outer * C,)),
-            dma((4, max(inner - 1, 1), outer)),
+            dma((3, inner - 1, outer)),
         ],
         compiler_params=pltpu.CompilerParams(
-            collective_id=2, has_side_effects=True, vmem_limit_bytes=48 * 1024 * 1024
+            collective_id=2, has_side_effects=True, vmem_limit_bytes=56 * 1024 * 1024
         ),
         name="middle_and_rows",
-    )(sent, own, middle, grads, gain, *parts)
+    )(sent, own, middle, grads, gain, feed_sent, feed_own, *parts)
 
 
 class RowsSum:
@@ -933,20 +958,31 @@
         self.own_sems, self.x_sems, up_sems, down_sems = sems
         self.up, self.down = (*ways[:2], up_sems), (*ways[2:], down_sems)
 
-    def begin(self):
+    def load(self):
         me = self.me
-        self.loads = {}
-        for k in line_order():
+        self.loads = []
+        for k in range(Z):
+            self.loads.append(
+                pltpu.make_async_copy(
+                    self.terms.at[(me.z + Z - k) % Z, me.x], self.own.at[k], self.own_sems.at[k]
+                )
+            )
+            self.loads[k].start()
+
+    def begin(self, turns):
+        me = self.me
+        for turn in turns:
+            if turn == Z - 1:
+                k = 0
+            else:
+                k = (jnp.minimum(me.z, Z - 1 - me.z) + turn) % (Z - 1) + 1
+                k = jnp.where(me.z < Z // 2, k, Z - k)
             at = (me.z + Z - k) % Z
             for j in range(1, me.inner):
                 self.sends.start(
                     True, self.terms.at[at, (me.x + j) % me.inner], self.x_in.at[j - 1, k],
                     self.x_sems.at[j - 1, k], me.at_x(j),
                 )
-            self.loads[k] = pltpu.make_async_copy(
-                self.terms.at[at, me.x], self.own.at[k], self.own_sems.at[k]
-            )
-            self.loads[k].start()
 
     def run(self, between=None):
         me = self.me
@@ -973,19 +1009,24 @@
 
 def sums_kernel(shape, *refs):
     inner, outer = shape
-    (units, wide, narrow, sent, own, tokens, gain, d_middle, gain_two_grad, vectors) = refs[:10]
-    (units_to, wide_to, narrow_to, tokens_grad, gains, vectors_to) = refs[10:16]
-    wide_scratch, narrow_scratch = refs[16:22], refs[22:28]
-    (own_v, c_in, y_out, y_in, all_in, vec_in) = refs[28:34]
-    (send_sems, local_sems, unit_sems, c_sems, y_sems, all_sems, vec_sems) = refs[34:41]
-    wide_sems, narrow_sems = refs[41:45], refs[45:49]
+    units, units_y, units_x = refs[:3]
+    refs = refs[3:]
+    (wide, narrow, sent, own, tokens, gain, d_middle, gain_two_grad, vectors, units_to) = refs[:10]
+    refs = refs[1:]
+    (wide_to, narrow_to, tokens_grad, gains, vectors_to) = refs[9:14]
+    wide_scratch, narrow_scratch = refs[14:20], refs[20:26]
+    (own_v, c_in, y_out, y_in, all_in, vec_in) = refs[26:32]
+    (send_sems, local_sems, c_sems, y_sems, all_sems, vec_sems) = refs[32:38]
+    wide_sems, narrow_sems = refs[38:42], refs[42:46]
+    units_v, units_y_in, units_x_in, unit_sems, units_y_sems, units_x_sems = refs[46:]
+    share = units.shape[3]
     me = Place(shape)
     rows = tokens.shape[0]
-    share = units.shape[3]
-    count = units.shape[0]
     sends = Sends(send_sems)
-    loads = [pltpu.make_async_copy(own, own_v, local_sems.at[0])]
-    loads[0].start()
+    load = pltpu.make_async_copy(own, own_v, local_sems.at[0])
+    load.start()
+    units_load = pltpu.make_async_copy(units, units_v, local_sems.at[1])
+    units_load.start()
     me.greet()
 
     order = [(me.y + i) % outer for i in list(range(1, outer)) + [0]]
@@ -993,30 +1034,64 @@
         sends.start(True, sent.at[at], c_in.at[at], c_sems.at[at], me.at_c)
     narrow_sum = RowsSum(me, sends, narrow, narrow_to, narrow_scratch, narrow_sems)
     wide_sum = RowsSum(me, sends, wide, wide_to, wide_scratch, wide_sems)
-    narrow_sum.begin()
-    wide_sum.begin()
+    narrow_sum.load()
+    wide_sum.load()
+    narrow_sum.begin(range(Z))
 
     def columns(n, at):
         return units_to.at[n, :, pl.ds(pl.multiple_of(at * share, LANES), share)]
 
-    def units_begin():
-        for n in range(count):
-            copy = pltpu.make_async_copy(units.at[n, me.z], columns(n, me.z), local_sems.at[1 + n])
-            copy.start()
-            loads.append(copy)
-            for k in range(1, Z):
-                to = (me.z + k) % Z
+    def units_begin_y():
+        for n in range(2):
+            for i in range(1, outer):
                 sends.start(
-                    True, units.at[n, to], columns(n, me.z), unit_sems.at[n, me.z], me.at_z(to)
+                    True, units_y.at[i - 1, n], units_y_in.at[i - 1, n],
+                    units_y_sems.at[i - 1, n], me.at_y(-i),
                 )
 
+    def units_begin_x():
+        for j in range(1, inner):
+            sends.start(
+                True, units_x.at[j - 1], units_x_in.at[j - 1], units_x_sems.at[j - 1], me.at_x(j)
+            )
+
+    kept = []
+
+    def unit_pass_on(n, came):
+        def body(r):
+            for at in range(Z):
+                total = units_v[n, at, r].astype(F32)
+                for part in came:
+                    total = total + part[at, r].astype(F32)
+                units_v[n, at, r] = total.astype(BF16)
+
+        each_rows(units_v.shape[2], 16, body)
+        copy = pltpu.make_async_copy(units_v.at[n, me.z], columns(n, me.z), local_sems.at[2 + n])
+        copy.start()
+        kept.append(copy)
+        for k in range(1, Z):
+            to = (me.z + k) % Z
+            sends.start(
+                True, units_v.at[n, to], columns(n, me.z), unit_sems.at[n, me.z], me.at_z(to)
+            )
+
+    def unit_over_y(n):
+        for i in range(1, outer):
+            arrived(units_y_in.at[i - 1, n], units_y_sems.at[i - 1, n], me.at_c)
+        unit_pass_on(2 * n, [units_y_in.at[i - 1, n] for i in range(1, outer)])
+
+    def unit_over_x():
+        for j in range(1, inner):
+            arrived(units_x_in.at[j - 1], units_x_sems.at[j - 1], me.at_c)
+        unit_pass_on(1, [units_x_in.at[j - 1] for j in range(1, inner)])
+
     def units_finish():
-        for n in range(count):
+        for n in range(3):
             for k in range(1, Z):
                 at = (me.z + Z - k) % Z
                 arrived(columns(n, at), unit_sems.at[n, at], me.at_c)
-
-    units_begin()
+        for copy in kept:
+            copy.wait()
 
     def exchange(held, into, sems, first, devices):
         for n, device in enumerate(devices):
@@ -1033,25 +1108,30 @@
     stages = [
         [me.at_c],
         [me.at_y(i) for i in range(1, outer)],
+        [me.at_z((me.z + k) % Z) for k in range(1, Z)],
         [me.at_x(j) for j in range(1, inner)],
-        [me.at_z((me.z + k) % Z) for k in range(1, Z)],
     ]
     at_stage = [0]
     for stage in stages:
         at_stage.append(at_stage[-1] + len(stage))
 
-    loads[0].wait()
+    z_stage, x_stage = stages[2], stages[3]
+    exchange(vectors, vec_in, vec_sems, 0, x_stage)
+    wide_sum.begin(range(2))
+    units_begin_x()
+    wide_sum.begin(range(2, Z))
+
+    load.wait()
     for i, at in enumerate(order):
         arrived(c_in.at[at], c_sems.at[at], me.at_c)
         if i < outer - 1:
             each_rows(rows, 16, lambda r, i=i, at=at: y_out.__setitem__(
                 (i, r), (own_v[at, r] + c_in[at, r]).astype(BF16)))
             sends.start(True, y_out.at[i], y_in.at[i], y_sems.at[i], me.at_y(i + 1))
-    x_stage, z_stage = stages[2], stages[3]
-    exchange(vectors, vec_in, vec_sems, 0, x_stage)
-    narrow_sum.run()
+    units_begin_y()
     vectors_to[0] = gathered(vectors, vec_in, vec_sems, 0, x_stage)
     exchange(vectors_to.at[0], vec_in, vec_sems, len(x_stage), z_stage)
+    narrow_sum.run()
     for i in range(outer - 1):
         arrived(y_in.at[i], y_sems.at[i], me.at_c)
     gains[0] = jnp.zeros_like(gains[0])
@@ -1073,7 +1153,14 @@
     gains[0, 8:16] = gain_two_grad[0:8] + gain_two_grad[8:16]
     exchange(gains.at[0], all_in, all_sems, 0, stages[0])
 
+    units_load.wait()
+
     def between(t):
+        if t == 1:
+            unit_over_y(0)
+        if t == 2:
+            unit_over_y(1)
+            unit_over_x()
         if t <= 3:
             held, into = gains.at[t - 1], gains.at[t]
             into[...] = gathered(held, all_in, all_sems, at_stage[t - 1], stages[t - 1])
@@ -1084,11 +1171,9 @@
     vectors_to[1] = gathered(vectors_to.at[0], vec_in, vec_sems, len(x_stage), z_stage)
     units_finish()
     sends.finish()
-    for copy in loads[1:]:
-        copy.wait()
-
-
-def last_sums(units, wide, narrow, sent, own, tokens, gain, d_middle, gain_two_grad, vectors):
+
+
+def last_sums(units, units_y, units_x, wide, narrow, sent, own, tokens, gain, d_middle, gain_two_grad, vectors):
     inner, outer = sizes()
     rows, width = tokens.shape
     dma = pltpu.SemaphoreType.DMA
@@ -1101,21 +1186,21 @@
         ] * 4
 
     peers = 1 + (outer - 1) + (inner - 1) + (Z - 1)
-    count, _, unit_rows, share = units.shape
-    copies = 2 * outer - 1 + 2 * (Z * (inner - 1) + 2 * (Z - 1)) + count * (Z - 1)
-    copies += peers + (inner - 1) + (Z - 1)
+    copies = 2 * outer - 1 + 2 * (Z * (inner - 1) + 2 * (Z - 1))
+    copies += peers + (inner - 1) + (Z - 1) + 2 * (outer - 1) + (inner - 1) + 3 * (Z - 1)
+    _, _, unit_rows, share = units.shape
     line_sems = [dma((Z,)), dma((inner - 1, Z)), dma((Z - 1,)), dma((Z - 1,))]
     return pl.pallas_call(
         functools.partial(sums_kernel, (inner, outer)),
         out_shape=(
-            jax.ShapeDtypeStruct((count, unit_rows, Z * share), BF16),
+            jax.ShapeDtypeStruct((3, unit_rows, Z * share), BF16),
             jax.ShapeDtypeStruct(wide.shape[2:], F32),
             jax.ShapeDtypeStruct(narrow.shape[2:], F32),
             jax.ShapeDtypeStruct((rows, width), BF16),
             jax.ShapeDtypeStruct((5, 16, width), F32),
             jax.ShapeDtypeStruct((2, *vectors.shape), F32),
         ),
-        in_specs=[anywhere] * 5 + [vmem] * 5,
+        in_specs=[anywhere] * 7 + [vmem] * 5,
         out_specs=(anywhere,) + (vmem,) * 5,
         scratch_shapes=scratch(wide)
         + scratch(narrow)
@@ -1127,19 +1212,26 @@
             pltpu.VMEM((peers, 16, width), F32),
             pltpu.VMEM((inner - 1 + Z - 1, *vectors.shape), F32),
             dma((copies,)),
-            dma((1 + count,)),
-            dma((count, Z)),
+            dma((5,)),
             dma((outer,)),
             dma((outer - 1,)),
             dma((peers,)),
             dma((inner - 1 + Z - 1,)),
         ]
-        + line_sems * 2,
+        + line_sems * 2
+        + [
+            pltpu.VMEM(units.shape, BF16),
+            pltpu.VMEM(units_y.shape, BF16),
+            pltpu.VMEM(units_x.shape, BF16),
+            dma((3, Z)),
+            dma((outer - 1, 2)),
+            dma((inner - 1,)),
+        ],
         compiler_params=pltpu.CompilerParams(
             collective_id=5, has_side_effects=True, vmem_limit_bytes=58 * 1024 * 1024
         ),
         name="last_sums",
-    )(units, wide, narrow, sent, own, tokens, gain, d_middle, gain_two_grad, vectors)
+    )(units, units_y, units_x, wide, narrow, sent, own, tokens, gain, d_middle, gain_two_grad, vectors)
 
 
 def scan_kernel(backward, factors, inflows, states, entered, products, ends, ends_in, carry, send_sems, arrivals):
@@ -1331,7 +1423,6 @@
 
     across = [(i, i % seq * wt + i // seq) for i in range(seq * wt)]
     gates = jnp.concatenate([decay_gate_weight, input_gate_weight], axis=1)
-    gates = lax.ppermute(gates, ("seq", "wt"), across)
 
     def padded(weight):
         share = -(-hidden_cols // (Z * LANES)) * LANES
@@ -1339,14 +1430,13 @@
 
     xy_unit = jnp.concatenate([turned(x_weight, 1), turned(y_weight, 1)], axis=1)
     (
-        group_tokens, grad_group, vectors, gate_all, xy_kernel, out_kernel,
-        gate_kernel, up_kernel, down_kernel,
+        group_tokens, vectors, gate_all, xy_kernel, out_kernel, gate_kernel, up_kernel, down_kernel,
     ) = gather_all(
-        tokens, out_grad, vectors, gates, xy_unit, turned(out_weight, 1),
+        tokens, vectors, gates, xy_unit, turned(out_weight, 1),
         padded(gate_weight), padded(up_weight), padded(down_weight),
     )
     group_tokens = group_tokens.reshape(-1, width)
-    grad_group = grad_group.reshape(-1, width)
+    grad_group = group_gather(after(out_grad, group_tokens))
     vectors = jnp.moveaxis(vectors[:, : 6 + taps_count, :chunk], 0, 1).reshape(6 + taps_count, -1)
     gain_one, gain_two = vectors[0], vectors[1]
     own_vectors = turned(
@@ -1357,8 +1447,6 @@
     xy_kernel = xy_kernel.reshape(width, -1)
     out_kernel = out_kernel.reshape(width, -1)
     gate_kernel = gate_kernel.reshape(width, -1)
-    up_kernel = up_kernel.reshape(width, -1)
-    down_kernel = down_kernel.reshape(width, -1)
     gate_all = turned(gate_all.reshape(lru_cols, 2 * block), 0)
     partner_rows = c_swap(gate_all[full:])
     shared_rows = in_order(gate_all[full:], partner_rows, 0)
@@ -1407,9 +1495,11 @@
         part = pick(mixed_parts, at, 1).reshape(outer * rows_dev, lru_cols)
         return contract_last(part, out_kernel).reshape(outer, rows_dev, width)
 
-    group_two, middle = branch_and_group(
-        branch_of(1 - c), branch_of(c), tokens, gain_two[None]
-    )
+    group_two, middle, up_kernel, down_kernel = branch_and_group(
+        branch_of(1 - c), branch_of(c), tokens, gain_two[None], up_kernel, down_kernel
+    )
+    up_kernel = up_kernel.reshape(width, -1)
+    down_kernel = down_kernel.reshape(width, -1)
     group_two = group_two.reshape(C * Z * rows_dev, width)
 
     gate_pre = multiply(group_two, gate_kernel)
@@ -1438,12 +1528,17 @@
     gate_terms = terms_of(group_two, d_gate)
     up_terms = terms_of(group_two, d_up)
     down_terms = terms_of(grad_group, hidden)
-    branch_rows, d_middle, gain_two_grad, *came = middle_and_rows(
+    def feed_of(part):
+        return contract_last(hidden[part], down_kernel).reshape(Z, rows_dev, width)
+
+    branch_rows, d_middle, gain_two_grad, block_out, *came = middle_and_rows(
         d_normed_of(slice(half_rows, None)).astype(BF16),
         d_normed_of(slice(0, half_rows)),
         middle,
         out_grad,
         gain_two[None],
+        feed_of(slice(half_rows, None)).astype(BF16),
+        feed_of(slice(0, half_rows)),
         gate_terms + up_terms + down_terms,
     )
     branch_rows = branch_rows.reshape(-1, width)
@@ -1457,28 +1552,12 @@
     def added_over_y(term, moved):
         return sum((moved[i - 1].astype(F32) for i in range(1, outer)), term.astype(F32))
 
-    half_z = Z // 2
-    down_x = added_over_x(down_terms, came[0])
-    gate_y = added_over_y(gate_terms[0], came[1])
-    up_x = added_over_x([term[:half_z] for term in up_terms], came[2])
-    up_y = added_over_y(up_terms[0][half_z:], came[3])
-    by_y = [jnp.concatenate([down_x[i], up_x[i]]).astype(BF16) for i in range(outer)]
-    by_y = sum(
-        (y_move(by_y[i], -i).astype(F32) for i in range(1, outer)),
-        jnp.concatenate([down_x[0], up_x[0]]),
-    )
-    by_x_all = jnp.concatenate([gate_y, up_y])
-    by_x = sum(
-        (
-            x_move(pick(by_x_all, (x + j) % inner, 1).astype(BF16), j).astype(F32)
-            for j in range(1, inner)
-        ),
-        pick(by_x_all, x, 1),
-    )
-    units = jnp.stack([by_x[:Z], jnp.concatenate([by_y[Z:], by_x[Z:]]), by_y[:Z]]).astype(BF16)
-
-    feed = group_scatter(lambda rows_: contract_last(rows_, down_kernel), after(hidden, d_middle))
-    block_out = (middle + feed).astype(BF16)
+    gate_x = added_over_x(gate_terms, came[0])
+    up_y = added_over_y(up_terms[0], came[1])
+    down_x = added_over_x(down_terms, came[2])
+    units = jnp.stack([gate_x[0], pick(up_y, x, 1), down_x[0]]).astype(BF16)
+    units_y = jnp.stack([jnp.stack([gate_x[i], down_x[i]]) for i in range(1, outer)]).astype(BF16)
+    units_x = jnp.stack([pick(up_y, (x + j) % inner, 1) for j in range(1, inner)]).astype(BF16)
 
     d_mixed = multiply(branch_rows, out_kernel)
     d_lru = (d_mixed * y_gated).astype(BF16).astype(F32)
@@ -1543,14 +1622,14 @@
         + [jnp.sum(d_conv * extended[reach - k : reach - k + rows], axis=0) for k in range(taps_count)],
     )
     own_sums = turned_back(own_sums, 1)
-    units, wide, narrow, tokens_grad, gains, own_sums = last_sums(
-        units, wide, narrow, d_normed_one_of(1 - c), d_normed_one_of(c), tokens, gain_one[None],
+    placed, wide, narrow, tokens_grad, gains, own_sums = last_sums(
+        units, units_y, units_x, wide, narrow, d_normed_one_of(1 - c), d_normed_one_of(c), tokens, gain_one[None],
         d_middle, gain_two_grad, own_sums,
     )
     weight_grads = [
         turned_back(wide[:, n * lru_cols : (n + 1) * lru_cols], 1) for n in range(3)
     ]
-    gate_grad, up_grad, down_grad = (units[n, :, :hidden_cols].astype(F32) for n in range(3))
+    gate_grad, up_grad, down_grad = (placed[n, :, :hidden_cols].astype(F32) for n in range(3))
     gains = gains[4].reshape(2, 8, width).sum(axis=1)
     gains = lax.dynamic_slice(gains, (0, (lax.axis_index("seq") * wt + w) * chunk), (2, chunk))
     sums = lax.dynamic_slice(own_sums[1], (0, lax.axis_index("seq") * chunk), (taps_count + 4, chunk))

time: 1000 us -> 952 us (0.952)
  Pallas kernels: 674 us -> 642 us
  starting transfers between devices: 28.9 us -> 18.1 us
    pallas_call x1, Pallas kernels: 262 us -> 222 us  [gather_all(): pl.pallas_call(functools.partial(gather_kernel, (inner, outer)), out_shap...]
    pallas_call x1, Pallas kernels: 218 us -> 195 us  [last_sums(): pl.pallas_call(functools.partial(sums_kernel, (inner, outer)), out_shape=...]
    pallas_call x1, Pallas kernels: 106 us -> 127 us  [middle_and_rows(): pl.pallas_call(functools.partial(middle_kernel, (inner, outer)), out_shap...]
    ppermute x1, waiting for transfers between devices: 0.01 us -> 14.8 us  [per_device(): lax.ppermute(own_sums, ('seq', 'wt'), [(to, at) for at, to in across])]
  transfers between devices with their start and end apart: 16 -> 16, of which waited for: 5 -> 6; matrix products, arithmetic and copies ran while one was open for 10% -> 9% of each run, Pallas kernels for 22% -> 33%
where the time goes in v4:
time: 952 us; the launch traced here: 946 us
  Pallas kernels  642 us (67%)
  matrix products  140 us (15%)
  other arithmetic  63.1 us (7%)
  local copies, waits for them, and re-layouts  49.3 us (5%)
  waiting for transfers between devices  30.6 us (3%)
  starting transfers between devices  18.1 us (2%)
    pallas_call x1, Pallas kernels, gather_all(): pl.pallas_call(functools.partial(gather_kernel, (inner, outer)), out_shap...  222 us
    pallas_call x1, Pallas kernels, last_sums(): pl.pallas_call(functools.partial(sums_kernel, (inner, outer)), out_shape=...  195 us
    pallas_call x1, Pallas kernels, middle_and_rows(): pl.pallas_call(functools.partial(middle_kernel, (inner, outer)), out_shap...  127 us
    pallas_call x1, Pallas kernels, branch_and_group(): pl.pallas_call(functools.partial(branch_kernel, (inner, outer)), out_shap...  83.1 us
    dot_general x15, matrix products, contract_last(): lax.dot_general(left_side, right_side, (((1,), (1,)), ((), ())), preferre...  51 us
    dot_general x8, matrix products, multiply(): return jnp.dot(left_side, right_side, preferred_element_type=F32)  45.2 us
    dot_general x12, matrix products, contract_rows(): lax.dot_general(left_side, right_side, (((0,), (0,)), ((), ())), preferre...  43.5 us
  transfers between devices with their start and end apart: 16, of which 6 were waited for; matrix products, arithmetic and copies ran while one was open for 9% of the time, Pallas kernels for 33%

profile of v4, /device:TPU:2, one launch (start us, length us, event | category | flops | bytes accessed | tf_op | source)
XLA Modules:
  0.0 945.6 jit_solution(10171514631436875517)
XLA Ops:
  0.7 4.5 collective-permute-start
  15.1 221.6 %gather_all.1 = (bf16[4,128,2560]{2,1,0:T(8,128)(2,1)}, f32[32,16,128]{2,1,0:T(8,128)}, bf16[4,2,80,512]{3,2,1,0:T(8,128)(2,1)}, bf16[4,2,320,1280]{3,2,1,0:T(8,...) custom-call(bf16[128,2560]{1,0:T(8,128)(2,1)} %refs_7_.1, ...), custom_call_target="tpu_custom_call" | custom-call | tf_op jit(solution)/shard_map/gather_all/pallas_call | solution.py:489
  244.1 5.0 fusion.134
  258.3 4.4 copy.66
  274.6 6.9 scan_ahead.1
  286.1 83.1 %branch_and_group.1 = (bf16[2,4,128,2560]{3,2,1,0:T(8,128)(2,1)S(1)}, f32[128,2560]{1,0:T(8,128)S(1)}, bf16[4,2,320,1024]{3,2,1,0:T(8,128)(2,1)}, bf16[4,2,320,1024]{3,2,1,0:T(8,128)(2,1)}) custom-call(f32[2,128,2560]{2,1,0:T(8,128)S(1)} %fusion.79.sent, f32[2,128,2560]{2,1,0:T(8,128)S(1)} %fusion.77.own, ...), custom_call_target="tpu_custom_call", output_to_operand_aliasing={{2}: (4, {}), {3}: (5, {})} | custom-call | tf_op jit(solution)/shard_map/branch_and_group/pallas_call | solution.py:689
  370.5 9.0 fusion.135
  380.2 7.8 collective-permute-done.2
  389.4 9.0 fusion.136
  399.1 6.8 collective-permute-done.3
  412.9 14.0 %multiply_convert_fusion.1 = (bf16[1024,1024]{1,0:T(8,128)(2,1)S(1)}, bf16[1024,1024]{1,0:T(8,128)(2,1)}, bf16[1024,1024]{1,0:T(8,128)(2,1)S(1)}) fusion(f32[1024,1024]{1,0:T(8,128)} %fusion.135, f32[1024,1024]{1,0:T(8,128)} %fusion.136, bf16[1024,2560]{1,0:T(8,128)(2,1)} %copy-done.68, bf16[2560,1024]{1,0:T(8,128)(2,1)S(1)} %bitcast.224), kind=kOutput, calls=%fused_computation.26 | convolution fusion | flops 5395972096 | bytes 25165824 | tf_op jit(solution)/shard_map/dot_general | solution.py:106
  426.9 6.8 fusion.64
  433.7 4.7 fusion.61
  438.4 4.2 convolution_convert_fusion.5
  442.7 4.2 convolution_convert_fusion.4
  446.9 4.2 convolution_convert_fusion.3
  451.1 4.2 convolution_convert_fusion.2
  455.6 4.3 convolution_convert_fusion.1
  459.9 4.4 convolution_convert_fusion
  464.3 6.0 add_convert_fusion
  470.3 6.4 convolution_add_fusion
  476.7 4.3 convolution_convert_fusion.6.refs_5_
  481.0 4.8 fusion.137.refs_6_
  485.8 126.8 %middle_and_rows.1 = (bf16[4,128,2560]{2,1,0:T(8,128)(2,1)}, f32[128,2560]{1,0:T(8,128)}, f32[16,2560]{1,0:T(8,128)}, bf16[128,2560]{1,0:T(8,128)(2,1)}, bf16[1,...) custom-call(bf16[4,128,2560]{2,1,0:T(8,128)(2,1)} %bitcast.228, ...), custom_call_target="tpu_custom_call" | custom-call | tf_op jit(solution)/shard_map/middle_and_rows/pallas_call | solution.py:928
  624.6 6.2 convert_multiply_fusion.2
  630.8 8.4 scan_back.1
  655.0 4.6 copy.70
  659.6 6.0 convolution_convert_fusion.7
  711.0 4.6 pad_maximum_fusion.refs_3_
  715.6 195.4 %last_sums.1 = (bf16[3,320,2048]{2,1,0:T(8,128)(2,1)}, f32[320,1920]{1,0:T(8,128)}, f32[80,512]{1,0:T(8,128)}, bf16[128,2560]{1,0:T(8,128)(2,1)}, f32[5,16,2560]{2,1,0:T(8,128)}, /*index=5*/f32[2,8,640]{2,1,0:T(8,128)}) custom-call(bf16[3,4,320,512]{3,2,1,0:T(8,128)(2,1)} %pad_maximum_fusion.1.refs_0_, ...), custom_call_target="tpu_custom_call" | custom-call | tf_op jit(solution)/shard_map/last_sums/pallas_call | solution.py:1193
  917.8 5.4 bitcast_convert_fusion
  925.4 14.8 %collective-permute-done.15 = f32[80,520]{1,0:T(8,128)S(1)} collective-permute-done((f32[80,520]{1,0:T(8,128)S(1)}, f32[80,520]{1,0:T(8,128)S(1)}, u32[]{:S(2)}, u32[]{:S(2)}) %collective-permute-start.15) | collective-permute-done | bytes 166432 | tf_op jit(solution)/shard_map/ppermute | solution.py:1637
  (361 shorter events, 140.1 us)
Async XLA Ops:
  0.7 378.9 %collective-permute-start = (bf16[128,2560]{1,0:T(8,128)(2,1)}, bf16[128,2560]{1,0:T(8,128)(2,1)}, u32[]{:S(2)}, u32[]{:S(2)}) collective-permute-start(bf16[128,2560]{1,0:T(8,128)(2,1)} %refs_3_.1), channel_id=1, source_target_pairs={{0,8},{4,12},{8,16},{12,20},{16,24},{20,28},{1,9},{5,13},{9,17},{1... | collective-permute-start | bytes 1966088 | tf_op jit(solution)/shard_map/ppermute | solution.py:41
  5.2 364.1 %collective-permute-start.1 = (bf16[128,2560]{1,0:T(8,128)(2,1)}, bf16[128,2560]{1,0:T(8,128)(2,1)}, u32[]{:S(2)}, u32[]{:S(2)}) collective-permute-start(bf16[128,2560]{1,0:T(8,128)(2,1)} %refs_3_.1), channel_id=1, source_target_pairs={{8,0},{12,4},{16,8},{20,12},{24,16},{28,20},{9,1},{13,5},{17,9},{2... | collective-permute-start | bytes 1966088 | tf_op jit(solution)/shard_map/ppermute | solution.py:41
  6.4 402.0 %collective-permute-start.6 = (bf16[128,2560]{1,0:T(8,128)(2,1)}, bf16[128,2560]{1,0:T(8,128)(2,1)}, u32[]{:S(2)}, u32[]{:S(2)}) collective-permute-start(bf16[128,2560]{1,0:T(8,128)(2,1)} %refs_3_.1), channel_id=1, source_target_pairs={{0,1},{1,0},{2,3},{3,2},{4,5},{5,4},{6,7},{7,6},{8,9},{9,8},{10,11... | collective-permute-start | bytes 1966088 | tf_op jit(solution)/shard_map/ppermute | solution.py:63
  244.1 7.8 copy-start.38
  249.7 13.7 %collective-permute-start.10 = (bf16[3,640]{1,0:T(4,128)(2,1)}, bf16[3,640]{1,0:T(4,128)(2,1)}, u32[]{:S(2)}, u32[]{:S(2)}) collective-permute-start(bf16[3,640]{1,0:T(4,128)(2,1)} %slice.478), channel_id=1, source_target_pairs={{0,4},{4,8},{8,12},{12,16},{16,20},{20,24},{24,28},{1,5},{5,9},{9,... | collective-permute-start | bytes 11528 | tf_op jit(solution)/shard_map/ppermute | solution.py:1462
  252.2 13.0 %copy-start.39 = (bf16[640,512]{1,0:T(8,128)(2,1)}, bf16[640,512]{1,0:T(8,128)(2,1)S(1)}, u32[]{:S(2)}) copy-start(bf16[640,512]{1,0:T(8,128)(2,1)S(1)} %maximum_select_fusion.4) | copy-start | bytes 1966084
  252.8 13.9 %collective-permute-start.12 = (bf16[128,512]{1,0:T(8,128)(2,1)}, bf16[128,512]{1,0:T(8,128)(2,1)}, u32[]{:S(2)}, u32[]{:S(2)}) collective-permute-start(bf16[128,512]{1,0:T(8,128)(2,1)} %slice.496), channel_id=1, source_target_pairs={{0,1},{1,0},{2,3},{3,2},{4,5},{5,4},{6,7},{7,6},{8,9},{9,8},{10,11... | collective-permute-start | bytes 393224 | tf_op jit(solution)/shard_map/ppermute | solution.py:63
  258.2 27.9 %copy-start.2 = (f32[1,2560]{1,0:T(1,128)}, f32[1,2560]{1,0:T(1,128)S(1)}, u32[]{:S(2)}) copy-start(f32[1,2560]{1,0:T(1,128)S(1)} %slice.413.gain.refs_4_) | copy-start | bytes 30724
  265.7 1.3 collective-permute-start.11
  265.8 358.8 %copy-start.7 = (f32[512,256]{1,0:T(8,128)}, f32[512,256]{1,0:T(8,128)S(1)}, u32[]{:S(2)}) copy-start(f32[512,256]{1,0:T(8,128)S(1)} %get-tuple-element.171) | copy-start | bytes 1572868
  369.2 10.3 %copy-start.1 = (f32[128,2560]{1,0:T(8,128)}, f32[128,2560]{1,0:T(8,128)S(1)}, u32[]{:S(2)}) copy-start(f32[128,2560]{1,0:T(8,128)S(1)} %get-tuple-element.60.refs_2_) | copy-start | bytes 3932164
  369.2 18.9 %collective-permute-start.2 = (bf16[128,2560]{1,0:T(8,128)(2,1)}, bf16[128,2560]{1,0:T(8,128)(2,1)S(1)}, u32[]{:S(2)}, u32[]{:S(2)}) collective-permute-start(bf16[128,2560]{1,0:T(8,128)(2,1)} %collective-permute-done.1), channel_id=1, source_target_pairs={{8,0},{12,4},{16,8},{20,12},{9,1},{13,5},{17,9},{21,13},{10,2},{14... | collective-permute-start | bytes 1966088 | tf_op jit(solution)/shard_map/ppermute | solution.py:41
  370.5 35.4 %slice-start.12 = ((s8[5242880]{0:T(1024)(128)(4,1)}), s8[4194304]{0:T(1024)(128)(4,1)S(1)}, s32[]{:S(2)}) async-start(s8[5242880]{0:T(1024)(128)(4,1)} %bitcast.251), calls=%async_computation.12 | async-start | bytes 8388608
  379.5 18.8 %collective-permute-start.4 = (bf16[128,2560]{1,0:T(8,128)(2,1)}, bf16[128,2560]{1,0:T(8,128)(2,1)S(1)}, u32[]{:S(2)}, u32[]{:S(2)}) collective-permute-start(bf16[128,2560]{1,0:T(8,128)(2,1)} %collective-permute-done), channel_id=1, source_target_pairs={{8,16},{12,20},{16,24},{20,28},{9,17},{13,21},{17,25},{21,29},{10,... | collective-permute-start | bytes 1966088 | tf_op jit(solution)/shard_map/ppermute | solution.py:41
  388.1 17.8 %collective-permute-start.3 = (bf16[128,2560]{1,0:T(8,128)(2,1)S(1)}, bf16[128,2560]{1,0:T(8,128)(2,1)S(1)}, u32[]{:S(2)}, u32[]{:S(2)}) collective-permute-start(bf16[128,2560]{1,0:T(8,128)(2,1)S(1)} %collective-permute-done.2), channel_id=1, source_target_pairs={{8,0},{12,4},{9,1},{13,5},{10,2},{14,6},{11,3},{15,7}} | collective-permute-start | bytes 1966088 | tf_op jit(solution)/shard_map/ppermute | solution.py:41
  389.4 16.5 %slice-start.13 = ((s8[5242880]{0:T(1024)(128)(4,1)}), s8[1048576]{0:T(1024)(128)(4,1)S(1)}, s32[]{:S(2)}) async-start(s8[5242880]{0:T(1024)(128)(4,1)} %bitcast.251), calls=%async_computation.13 | async-start | bytes 2097152
  398.4 8.5 collective-permute-start.5
  406.1 3.6 collective-permute-start.7
  406.3 3.4 collective-permute-start.8
  408.4 2.2 collective-permute-start.9
  409.7 17.2 %slice-start.16 = ((s8[5242880]{0:T(1024)(128)(4,1)}), s8[1048576]{0:T(1024)(128)(4,1)S(1)}, s32[]{:S(2)}) async-start(s8[5242880]{0:T(1024)(128)(4,1)} %bitcast.258), calls=%async_computation.16 | async-start | bytes 2097152
  412.9 14.0 %slice-start.17 = ((s8[5242880]{0:T(1024)(128)(4,1)}), s8[4194304]{0:T(1024)(128)(4,1)S(1)}, s32[]{:S(2)}) async-start(s8[5242880]{0:T(1024)(128)(4,1)} %bitcast.258), calls=%async_computation.17 | async-start | bytes 8388608
  426.9 24.2 %copy-start.80 = (bf16[1024,1024]{1,0:T(8,128)(2,1)}, bf16[1024,1024]{1,0:T(8,128)(2,1)S(1)}, u32[]{:S(2)}) copy-start(bf16[1024,1024]{1,0:T(8,128)(2,1)S(1)} %get-tuple-element.147) | copy-start | bytes 6291460
  446.9 8.6 slice-start.14
  455.6 8.7 slice-start.2
  615.8 8.8 copy-start.20
  630.8 13.1 %copy-start.25 = (bf16[512,640]{1,0:T(8,128)(2,1)}, bf16[512,640]{1,0:T(8,128)(2,1)S(1)}, u32[]{:S(2)}) copy-start(bf16[512,640]{1,0:T(8,128)(2,1)S(1)} %get-tuple-element.136) | copy-start | bytes 1966084
  665.7 13.0 %collective-permute-start.13 = (bf16[512,256]{1,0:T(8,128)(2,1)S(1)}, bf16[512,256]{1,0:T(8,128)(2,1)S(1)}, u32[]{:S(2)}, u32[]{:S(2)}) collective-permute-start(bf16[512,256]{1,0:T(8,128)(2,1)S(1)} %pad_maximum_fusion.15), channel_id=1, source_target_pairs={{0,1},{1,0},{2,3},{3,2},{4,5},{5,4},{6,7},{7,6},{8,9},{9,8},{10,11... | collective-permute-start | bytes 786440 | tf_op jit(solution)/shard_map/ppermute | solution.py:63
  686.6 6.5 collective-permute-start.14
  693.6 10.7 %slice-start = ((s8[6553600]{0:T(1024)(128)(4,1)}), s8[4194304]{0:T(1024)(128)(4,1)S(1)}, s32[]{:S(2)}) async-start(s8[6553600]{0:T(1024)(128)(4,1)} %bitcast.197), calls=%async_computation | async-start | bytes 8388608
  915.9 24.3 %collective-permute-start.15 = (f32[80,520]{1,0:T(8,128)S(1)}, f32[80,520]{1,0:T(8,128)S(1)}, u32[]{:S(2)}, u32[]{:S(2)}) collective-permute-start(f32[80,520]{1,0:T(8,128)S(1)} %pad_maximum_fusion.17), channel_id=1, source_target_pairs={{0,0},{4,1},{8,2},{12,3},{16,4},{20,5},{24,6},{28,7},{1,8},{5,9},{... | collective-permute-start | bytes 499208 | tf_op jit(solution)/shard_map/ppermute | solution.py:1637
  924.9 19.4 %copy-start.58 = (bf16[128,2560]{1,0:T(8,128)(2,1)S(1)}, bf16[128,2560]{1,0:T(8,128)(2,1)}, u32[]{:S(2)}) copy-start(bf16[128,2560]{1,0:T(8,128)(2,1)} %get-tuple-element.226) | copy-start | bytes 1966084
  (85 other events, 279.6 us)

commit v5 on v4

--- a/solution.py
+++ b/solution.py
@@ -31,45 +31,16 @@
     return s // inner, s % inner, w // C, w % C
 
 
-def after(value, *earlier):
-    return lax.optimization_barrier((value, *earlier))[0]
-
-
 def z_move(value, by, senders):
     inner, _ = sizes()
     pairs = [(z * inner + x, (z + by) % Z * inner + x) for z in senders for x in range(inner)]
     return lax.ppermute(value, "seq", pairs)
 
 
-def z_turn(value, by):
-    return z_move(value, by, range(Z))
-
-
-def x_move(value, by):
-    inner, _ = sizes()
-    pairs = [(z * inner + x, z * inner + (x + by) % inner) for z in range(Z) for x in range(inner)]
-    return lax.ppermute(value, "seq", pairs)
-
-
-def y_move(value, by):
-    _, outer = sizes()
-    pairs = [(y * C + c, (y + by) % outer * C + c) for y in range(outer) for c in range(C)]
-    return lax.ppermute(value, "wt", pairs)
-
-
 def c_swap(value):
     _, outer = sizes()
     pairs = [(y * C + c, y * C + 1 - c) for y in range(outer) for c in range(C)]
     return lax.ppermute(value, "wt", pairs)
-
-
-def line_gather(value):
-    z = places()[0]
-    up, down = [value], [value]
-    for k in range(1, Z):
-        up.append(z_move(up[-1], 1, range(k - 1, Z - 1)))
-        down.append(z_move(down[-1], -1, range(1, Z - k + 1)))
-    return [value] + [jnp.where(z >= k, up[k], down[Z - k]) for k in range(1, Z)]
 
 
 def line_scatter(parts):
@@ -86,10 +57,6 @@
     return lax.dynamic_index_in_dim(value, index, axis, keepdims=False)
 
 
-def put(buffer, value, starts):
-    return lax.dynamic_update_slice(buffer, value, starts)
-
-
 def contract_last(left_side, right_side):
     return lax.dot_general(
         left_side, right_side, (((1,), (1,)), ((), ())), preferred_element_type=F32
@@ -104,77 +71,6 @@
 
 def multiply(left_side, right_side):
     return jnp.dot(left_side, right_side, preferred_element_type=F32)
-
-
-def seq_scatter(total):
-    inner, _ = sizes()
-    z, x = places()[:2]
-    total = total.reshape(Z, inner, -1, total.shape[1])
-    kept = pick(total, x, 1)
-    for j in range(1, inner):
-        kept = kept + x_move(pick(total, (x + j) % inner, 1).astype(BF16), j).astype(F32)
-    return line_scatter([pick(kept, (z - k) % Z, 0) for k in range(Z)])
-
-
-def plane_scatter(left_side, right_side, width, x_first, gate):
-    inner, outer = sizes()
-    z, x = places()[:2]
-    share = right_side.shape[1] // outer
-
-    def over_x(value):
-        total = pick(value, x, 1).astype(F32)
-        for j in range(1, inner):
-            total = total + x_move(pick(value, (x + j) % inner, 1), j).astype(F32)
-        return total.astype(BF16)
-
-    def over_y(parts):
-        total = parts[0].astype(F32)
-        for i in range(1, outer):
-            total = total + y_move(parts[i], -i).astype(F32)
-        return total.astype(BF16)
-
-    parts = []
-    for i in range(outer):
-        part = contract_rows(left_side, right_side[:, i * share : (i + 1) * share]).astype(BF16)
-        parts.append(part.reshape(Z, inner, -1, share))
-    rows = parts[0].shape[2]
-    kept = over_y([over_x(part) for part in parts]) if x_first else over_x(over_y(parts))
-    kept = after(kept, gate)
-    buffer = put(jnp.zeros((rows, Z * share), BF16), pick(kept, z, 0), (0, z * share))
-    for k in range(1, Z):
-        moved = z_move(pick(kept, (z + k) % Z, 0), k, range(Z))
-        buffer = put(buffer, moved, (0, (z - k) % Z * share))
-    return buffer[:, :width].astype(F32)
-
-
-def wt_scatter(product_of, *sides):
-    _, outer = sizes()
-    _, _, y, c = places()
-
-    def chosen(at):
-        cut = [side.reshape(outer, C, -1, side.shape[1]) for side in sides]
-        return [pick(side, at, 1).reshape(-1, side.shape[3]) for side in cut]
-
-    sent = c_swap(product_of(*chosen(1 - c)))
-    kept = product_of(*chosen(c)) + sent
-    kept = kept.reshape(outer, -1, kept.shape[1])
-    total = pick(kept, y, 0)
-    for i in range(1, outer):
-        total = total + y_move(pick(kept, (y + i) % outer, 0).astype(BF16), i).astype(F32)
-    return total
-
-
-def group_gather(value):
-    blocks = line_gather(value)
-    return jnp.concatenate(blocks + [c_swap(block) for block in blocks])
-
-
-def group_scatter(product_of, *sides):
-    half = sides[0].shape[0] // 2
-    sent = c_swap(product_of(*[side[half:] for side in sides]).astype(BF16))
-    kept = product_of(*[side[:half] for side in sides]) + sent.astype(F32)
-    rows = half // Z
-    return line_scatter([kept[k * rows : (k + 1) * rows] for k in range(Z)])
 
 
 class Sends:
@@ -213,13 +109,15 @@
 
 def gather_kernel(shape, *refs):
     inner, outer = shape
-    (tokens, vectors, gates, xy, out, gate, up, down) = refs[:8]
-    (tokens_to, vectors_to, gates_to, xy_to, out_to, gate_to, up_to, down_to) = refs[8:16]
-    (gates_own, send_sems, local_sems, line_sems, plane_sems, rows_sems, vector_sems, turn_sems) = refs[16:]
+    (tokens, grads, vectors, gates, xy, out, gate, up, down) = refs[:9]
+    (tokens_to, grads_to, vectors_to, gates_to, xy_to, out_to, gate_to, up_to, down_to) = refs[9:18]
+    gates_own, send_sems, local_sems, line_sems, plane_sems, rows_sems = refs[18:24]
+    vector_sems, turn_sems, group_sems = refs[24:]
     seq, wt = Z * inner, outer * C
     s, w = lax.axis_index("seq"), lax.axis_index("wt")
     z, x, y, c = s // inner, s % inner, w // C, w % C
     sends = Sends(send_sems)
+    group = GroupRows(Place(shape), sends, grads, grads_to, group_sems)
     here = []
 
     def at_z(to):
@@ -269,10 +167,16 @@
             for j in range(1, inner):
                 sends.start(when, block, self.target.at[at, x], self.sems.at[at, x], at_x(j))
 
-        def begin(self):
+        def begin_z(self):
             keep(self.source, self.target.at[z, x])
             self.forward(self.source, z, z < Z - 1, z > 0)
+
+        def begin_x(self):
             self.across(True, self.source, z)
+
+        def begin(self):
+            self.begin_z()
+            self.begin_x()
 
         def step(self, k):
             for at, there, up_when, down_when in (
@@ -418,25 +322,32 @@
 
     pl.when(here_too)(stay.wait)
     lines[1].begin()
+    lines[2].begin_z()
     lax.fori_loop(0, seq * wt, vector_send, 0)
     for k in range(1, Z):
         lines[1].step(k)
         lines[0].step(k)
         if k == 1:
             tokens_step()
+    lines[2].begin_x()
+    for k in range(1, Z):
+        lines[2].step(k)
+        if k == Z - 2:
+            planes[0].begin()
+            planes[2].begin()
             planes[1].begin()
     for k in range(Z):
-        planes[1].first(k)
-    planes[0].begin()
-    lines[2].begin()
-    planes[0].first(0)
-    for k in range(1, Z):
-        lines[2].step(k)
         planes[0].first(k)
-    planes[2].begin()
     for k in range(Z):
         planes[2].first(k)
+    keep(grads, group.place(0, z, z))
+    group.begin()
+    for k in range(Z):
+        planes[1].first(k)
         planes[0].second(k)
+    for k in range(1, Z):
+        group.step(k)
+    group.finish()
 
     for line in lines:
         line.finish()
@@ -462,7 +373,7 @@
             copy.wait()
 
 
-def gather_all(tokens, vectors, gates, xy, out, gate, up, down):
+def gather_all(tokens, grads, vectors, gates, xy, out, gate, up, down):
     inner, outer = sizes()
     seq, wt = Z * inner, outer * C
 
@@ -475,6 +386,7 @@
 
     shapes = (
         buffer(wt, *tokens.shape, like=tokens),
+        buffer(C, Z, *grads.shape, like=grads),
         buffer(seq * wt, *vectors.shape, like=vectors),
         buffer(Z, inner, *gates.shape, like=gates),
         buffer(Z, inner, *xy.shape, like=xy),
@@ -489,8 +401,8 @@
     return pl.pallas_call(
         functools.partial(gather_kernel, (inner, outer)),
         out_shape=shapes,
-        in_specs=[pl.BlockSpec(memory_space=pl.ANY)] * 8,
-        out_specs=[pl.BlockSpec(memory_space=pl.ANY)] * 8,
+        in_specs=[pl.BlockSpec(memory_space=pl.ANY)] * 9,
+        out_specs=[pl.BlockSpec(memory_space=pl.ANY)] * 9,
         scratch_shapes=[
             pltpu.VMEM(gates.shape, gates.dtype),
             dma((copies,)),
@@ -500,10 +412,11 @@
             dma((wt,)),
             dma((2, seq * wt)),
             dma((3,)),
+            dma((C, Z)),
         ],
         compiler_params=pltpu.CompilerParams(collective_id=0, has_side_effects=True),
         name="gather_all",
-    )(tokens, vectors, gates, xy, out, gate, up, down)
+    )(tokens, grads, vectors, gates, xy, out, gate, up, down)
 
 
 class Place:
@@ -769,9 +682,9 @@
 
 
 class PlaneTerms:
-    def __init__(self, me, sends, parts, target, sems, over_x):
+    def __init__(self, me, sends, parts, target, sems, over_x, blocks):
         self.me, self.sends, self.parts, self.target, self.sems = me, sends, parts, target, sems
-        self.over_x = over_x
+        self.over_x, self.blocks = over_x, blocks
 
     def begin(self):
         me = self.me
@@ -779,13 +692,13 @@
             for j in range(1, me.inner):
                 for i, part in enumerate(self.parts):
                     self.sends.start(
-                        True, part.at[:, (me.x + j) % me.inner],
+                        True, part.at[self.blocks, (me.x + j) % me.inner],
                         self.target.at[j - 1, i], self.sems.at[j - 1, i], me.at_x(j),
                     )
         else:
             for i in range(1, me.outer):
                 self.sends.start(
-                    True, self.parts[i], self.target.at[i - 1],
+                    True, self.parts[i].at[self.blocks], self.target.at[i - 1],
                     self.sems.at[0, i - 1], me.at_y(-i),
                 )
 
@@ -805,8 +718,8 @@
     sent, own, middle, grads, gain, feed_sent, feed_own = refs[:7]
     parts = refs[7 : 7 + 3 * outer]
     rows_to, d_middle, gain_grad, block_out = refs[7 + 3 * outer : 11 + 3 * outer]
-    targets = refs[11 + 3 * outer : 14 + 3 * outer]
-    scratch = refs[14 + 3 * outer :]
+    targets = refs[11 + 3 * outer : 15 + 3 * outer]
+    scratch = refs[15 + 3 * outer :]
     middle_body(
         shape, sent, own, middle, grads, gain, feed_sent, feed_own, parts, targets,
         rows_to, d_middle, gain_grad, block_out, scratch[:9], scratch[9:18], *scratch[18:],
@@ -846,9 +759,13 @@
 
 def plane_units(me, sends, parts, targets, sems):
     outer = me.outer
+    gate, up, down = (parts[n * outer : (n + 1) * outer] for n in range(3))
+    every, low, high = slice(0, Z), slice(0, Z // 2), slice(Z // 2, Z)
     return [
-        PlaneTerms(me, sends, parts[n * outer : (n + 1) * outer], targets[n], sems.at[n], n != 1)
-        for n in (1, 2, 0)
+        PlaneTerms(me, sends, gate, targets[0], sems.at[0], True, every),
+        PlaneTerms(me, sends, up, targets[1], sems.at[1], False, every),
+        PlaneTerms(me, sends, down, targets[2], sems.at[2], True, low),
+        PlaneTerms(me, sends, down, targets[3], sems.at[3], False, high),
     ]
 
 
@@ -916,10 +833,11 @@
         for shape in (
             (*over_x, Z, unit_rows, share),
             (*over_y, Z, inner, unit_rows, share),
-            (*over_x, Z, unit_rows, share),
+            (*over_x, Z // 2, unit_rows, share),
+            (*over_y, Z // 2, inner, unit_rows, share),
         )
     ]
-    unit_copies = 2 * (inner - 1) * outer + (outer - 1)
+    unit_copies = 2 * (inner - 1) * outer + 2 * (outer - 1)
     pair_scratch = [pltpu.VMEM((Z, rows, width), F32), pltpu.VMEM((Z, rows, width), BF16)]
     pair_scratch += [pltpu.VMEM((Z - 1, rows, width), BF16)] * 4
     dma = pltpu.SemaphoreType.DMA
@@ -935,14 +853,14 @@
             *targets,
         ),
         in_specs=[anywhere, anywhere, vmem, vmem, vmem] + [anywhere] * (2 + 3 * outer),
-        out_specs=(anywhere, vmem, vmem, vmem) + (anywhere,) * 3,
+        out_specs=(anywhere, vmem, vmem, vmem) + (anywhere,) * 4,
         scratch_shapes=pair_scratch * 2
         + [
             pltpu.VMEM((rows, width), BF16),
             dma((2 * (Z + 2 * (Z - 1)) + 2 * outer + unit_copies,)),
             dma((3,)),
             dma((outer * C,)),
-            dma((3, inner - 1, outer)),
+            dma((4, inner - 1, outer)),
         ],
         compiler_params=pltpu.CompilerParams(
             collective_id=2, has_side_effects=True, vmem_limit_bytes=56 * 1024 * 1024
@@ -1041,31 +959,41 @@
     def columns(n, at):
         return units_to.at[n, :, pl.ds(pl.multiple_of(at * share, LANES), share)]
 
+    low, high, extra = slice(0, Z // 2), slice(Z // 2, Z), slice(Z, Z + Z // 2)
+    every = slice(0, Z)
+
     def units_begin_y():
-        for n in range(2):
+        for n, blocks in enumerate((every, extra)):
             for i in range(1, outer):
                 sends.start(
-                    True, units_y.at[i - 1, n], units_y_in.at[i - 1, n],
+                    True, units_y.at[i - 1, blocks], units_y_in.at[i - 1, blocks],
                     units_y_sems.at[i - 1, n], me.at_y(-i),
                 )
 
     def units_begin_x():
-        for j in range(1, inner):
-            sends.start(
-                True, units_x.at[j - 1], units_x_in.at[j - 1], units_x_sems.at[j - 1], me.at_x(j)
-            )
+        for n, blocks in enumerate((every, extra)):
+            for j in range(1, inner):
+                sends.start(
+                    True, units_x.at[j - 1, blocks], units_x_in.at[j - 1, blocks],
+                    units_x_sems.at[j - 1, n], me.at_x(j),
+                )
 
     kept = []
 
-    def unit_pass_on(n, came):
+    def unit_add(n, blocks, came, came_blocks, sems, count):
+        for i in range(count):
+            arrived(came.at[i, came_blocks], sems.at[i], me.at_c)
+
         def body(r):
-            for at in range(Z):
-                total = units_v[n, at, r].astype(F32)
-                for part in came:
-                    total = total + part[at, r].astype(F32)
-                units_v[n, at, r] = total.astype(BF16)
+            for at in range(blocks.stop - blocks.start):
+                total = units_v[n, blocks.start + at, r].astype(F32)
+                for i in range(count):
+                    total = total + came[i, came_blocks.start + at, r].astype(F32)
+                units_v[n, blocks.start + at, r] = total.astype(BF16)
 
         each_rows(units_v.shape[2], 16, body)
+
+    def unit_pass_on(n):
         copy = pltpu.make_async_copy(units_v.at[n, me.z], columns(n, me.z), local_sems.at[2 + n])
         copy.start()
         kept.append(copy)
@@ -1075,15 +1003,18 @@
                 True, units_v.at[n, to], columns(n, me.z), unit_sems.at[n, me.z], me.at_z(to)
             )
 
-    def unit_over_y(n):
-        for i in range(1, outer):
-            arrived(units_y_in.at[i - 1, n], units_y_sems.at[i - 1, n], me.at_c)
-        unit_pass_on(2 * n, [units_y_in.at[i - 1, n] for i in range(1, outer)])
-
-    def unit_over_x():
-        for j in range(1, inner):
-            arrived(units_x_in.at[j - 1], units_x_sems.at[j - 1], me.at_c)
-        unit_pass_on(1, [units_x_in.at[j - 1] for j in range(1, inner)])
+    def unit_gate():
+        unit_add(0, every, units_y_in, every, units_y_sems.at[:, 0], outer - 1)
+        unit_pass_on(0)
+
+    def unit_down():
+        unit_add(2, low, units_y_in, extra, units_y_sems.at[:, 1], outer - 1)
+        unit_add(2, high, units_x_in, extra, units_x_sems.at[:, 1], inner - 1)
+        unit_pass_on(2)
+
+    def unit_up():
+        unit_add(1, every, units_x_in, every, units_x_sems.at[:, 0], inner - 1)
+        unit_pass_on(1)
 
     def units_finish():
         for n in range(3):
@@ -1117,9 +1048,10 @@
 
     z_stage, x_stage = stages[2], stages[3]
     exchange(vectors, vec_in, vec_sems, 0, x_stage)
-    wide_sum.begin(range(2))
     units_begin_x()
-    wide_sum.begin(range(2, Z))
+    wide_sum.begin(range(Z))
+
+    units_begin_y()
 
     load.wait()
     for i, at in enumerate(order):
@@ -1128,13 +1060,14 @@
             each_rows(rows, 16, lambda r, i=i, at=at: y_out.__setitem__(
                 (i, r), (own_v[at, r] + c_in[at, r]).astype(BF16)))
             sends.start(True, y_out.at[i], y_in.at[i], y_sems.at[i], me.at_y(i + 1))
-    units_begin_y()
     vectors_to[0] = gathered(vectors, vec_in, vec_sems, 0, x_stage)
     exchange(vectors_to.at[0], vec_in, vec_sems, len(x_stage), z_stage)
     narrow_sum.run()
-    for i in range(outer - 1):
-        arrived(y_in.at[i], y_sems.at[i], me.at_c)
-    gains[0] = jnp.zeros_like(gains[0])
+    vectors_to[1] = gathered(vectors_to.at[0], vec_in, vec_sems, len(x_stage), z_stage)
+    units_load.wait()
+    unit_gate()
+    unit_up()
+    unit_down()
 
     def work(r):
         d_normed = own_v[me.y, r] + c_in[me.y, r]
@@ -1149,26 +1082,26 @@
         passed = inverse * (scaled - normed * jnp.mean(scaled * normed, axis=1, keepdims=True))
         tokens_grad[r] = (d_middle[r] + passed).astype(BF16)
 
-    each_rows(rows, 16, work)
-    gains[0, 8:16] = gain_two_grad[0:8] + gain_two_grad[8:16]
-    exchange(gains.at[0], all_in, all_sems, 0, stages[0])
-
-    units_load.wait()
+    def gains_step(n):
+        if n > 0:
+            gains[n] = gathered(
+                gains.at[n - 1], all_in, all_sems, at_stage[n - 1], stages[n - 1]
+            )
+        if n < len(stages):
+            exchange(gains.at[n], all_in, all_sems, at_stage[n], stages[n])
 
     def between(t):
         if t == 1:
-            unit_over_y(0)
-        if t == 2:
-            unit_over_y(1)
-            unit_over_x()
-        if t <= 3:
-            held, into = gains.at[t - 1], gains.at[t]
-            into[...] = gathered(held, all_in, all_sems, at_stage[t - 1], stages[t - 1])
-            exchange(into, all_in, all_sems, at_stage[t], stages[t])
+            for i in range(outer - 1):
+                arrived(y_in.at[i], y_sems.at[i], me.at_c)
+            gains[0] = jnp.zeros_like(gains[0])
+            each_rows(rows, 16, work)
+            gains[0, 8:16] = gain_two_grad[0:8] + gain_two_grad[8:16]
+        gains_step(t - 1)
 
     wide_sum.run(between)
-    gains[4] = gathered(gains.at[3], all_in, all_sems, at_stage[3], stages[3])
-    vectors_to[1] = gathered(vectors_to.at[0], vec_in, vec_sems, len(x_stage), z_stage)
+    for n in range(Z - 1, len(stages) + 1):
+        gains_step(n)
     units_finish()
     sends.finish()
 
@@ -1187,7 +1120,7 @@
 
     peers = 1 + (outer - 1) + (inner - 1) + (Z - 1)
     copies = 2 * outer - 1 + 2 * (Z * (inner - 1) + 2 * (Z - 1))
-    copies += peers + (inner - 1) + (Z - 1) + 2 * (outer - 1) + (inner - 1) + 3 * (Z - 1)
+    copies += peers + (inner - 1) + (Z - 1) + 2 * (outer - 1) + 2 * (inner - 1) + 3 * (Z - 1)
     _, _, unit_rows, share = units.shape
     line_sems = [dma((Z,)), dma((inner - 1, Z)), dma((Z - 1,)), dma((Z - 1,))]
     return pl.pallas_call(
@@ -1225,7 +1158,7 @@
             pltpu.VMEM(units_x.shape, BF16),
             dma((3, Z)),
             dma((outer - 1, 2)),
-            dma((inner - 1,)),
+            dma((inner - 1, 2)),
         ],
         compiler_params=pltpu.CompilerParams(
             collective_id=5, has_side_effects=True, vmem_limit_bytes=58 * 1024 * 1024
@@ -1357,11 +1290,6 @@
         jnp.exp(log_decay),
         jnp.sqrt(-jnp.expm1(2.0 * log_decay)) * jax.nn.sigmoid(input_pre) * conv_float,
     )
-
-
-def norm_back(d_normed, normed, inverse, gain_row):
-    scaled = d_normed * gain_row
-    return inverse * (scaled - normed * jnp.mean(scaled * normed, axis=1, keepdims=True))
 
 
 def normed_rows(stream):
@@ -1430,13 +1358,14 @@
 
     xy_unit = jnp.concatenate([turned(x_weight, 1), turned(y_weight, 1)], axis=1)
     (
-        group_tokens, vectors, gate_all, xy_kernel, out_kernel, gate_kernel, up_kernel, down_kernel,
+        group_tokens, grad_group, vectors, gate_all, xy_kernel, out_kernel,
+        gate_kernel, up_kernel, down_kernel,
     ) = gather_all(
-        tokens, vectors, gates, xy_unit, turned(out_weight, 1),
+        tokens, out_grad, vectors, gates, xy_unit, turned(out_weight, 1),
         padded(gate_weight), padded(up_weight), padded(down_weight),
     )
     group_tokens = group_tokens.reshape(-1, width)
-    grad_group = group_gather(after(out_grad, group_tokens))
+    grad_group = grad_group.reshape(-1, width)
     vectors = jnp.moveaxis(vectors[:, : 6 + taps_count, :chunk], 0, 1).reshape(6 + taps_count, -1)
     gain_one, gain_two = vectors[0], vectors[1]
     own_vectors = turned(
@@ -1552,12 +1481,21 @@
     def added_over_y(term, moved):
         return sum((moved[i - 1].astype(F32) for i in range(1, outer)), term.astype(F32))
 
+    half_z = Z // 2
     gate_x = added_over_x(gate_terms, came[0])
     up_y = added_over_y(up_terms[0], came[1])
-    down_x = added_over_x(down_terms, came[2])
-    units = jnp.stack([gate_x[0], pick(up_y, x, 1), down_x[0]]).astype(BF16)
-    units_y = jnp.stack([jnp.stack([gate_x[i], down_x[i]]) for i in range(1, outer)]).astype(BF16)
-    units_x = jnp.stack([pick(up_y, (x + j) % inner, 1) for j in range(1, inner)]).astype(BF16)
+    down_x = added_over_x([term[:half_z] for term in down_terms], came[2])
+    down_y = added_over_y(down_terms[0][half_z:], came[3])
+    all_y = jnp.concatenate([up_y, down_y])
+    kept_x = pick(all_y, x, 1)
+    units = jnp.concatenate([gate_x[0], kept_x[:Z], down_x[0], kept_x[Z:]]).astype(BF16)
+    units = units.reshape(3, Z, weight_rows, -1)
+    units_y = jnp.stack(
+        [jnp.concatenate([gate_x[i], down_x[i]]).astype(BF16) for i in range(1, outer)]
+    )
+    units_x = jnp.stack(
+        [pick(all_y, (x + j) % inner, 1).astype(BF16) for j in range(1, inner)]
+    )
 
     d_mixed = multiply(branch_rows, out_kernel)
     d_lru = (d_mixed * y_gated).astype(BF16).astype(F32)

time: 952 us -> 905 us (0.951)
  waiting for transfers between devices: 30.6 us -> 7.06 us
  Pallas kernels: 642 us -> 621 us
    another operation x6 -> x0, other arithmetic: 16 us -> none
    pallas_call x1, Pallas kernels: 127 us -> 112 us  [middle_and_rows(): pl.pallas_call(functools.partial(middle_kernel, (inner, outer)), out_shap...]
    ppermute x6 -> x0, waiting for transfers between devices: 14.7 us -> none  [z_move(): return lax.ppermute(value, 'seq', pairs)]
    ppermute x1, starting transfers between devices: 2.12 us -> 15 us  [per_device(): lax.ppermute(x_branch[rows - reach:], 'seq', [(i, i + 1) for i in range(s...]
    ppermute x6 -> x0, starting transfers between devices: 9.71 us -> none  [z_move(): return lax.ppermute(value, 'seq', pairs)]
  transfers between devices with their start and end apart: 16 -> 6, of which waited for: 6 -> 3; matrix products, arithmetic and copies ran while one was open for 9% -> 4% of each run, Pallas kernels for 33% -> 0%
where the time goes in v5:
time: 905 us; the launch traced here: 899 us
  Pallas kernels  621 us (69%)
  matrix products  139 us (15%)
  other arithmetic  54.6 us (6%)
  local copies, waits for them, and re-layouts  54.4 us (6%)
  starting transfers between devices  20 us (2%)
    pallas_call x1, Pallas kernels, gather_all(): pl.pallas_call(functools.partial(gather_kernel, (inner, outer)), out_shap...  214 us
    pallas_call x1, Pallas kernels, last_sums(): pl.pallas_call(functools.partial(sums_kernel, (inner, outer)), out_shape=...  198 us
    pallas_call x1, Pallas kernels, middle_and_rows(): pl.pallas_call(functools.partial(middle_kernel, (inner, outer)), out_shap...  112 us
    pallas_call x1, Pallas kernels, branch_and_group(): pl.pallas_call(functools.partial(branch_kernel, (inner, outer)), out_shap...  79.3 us
    dot_general x15, matrix products, contract_last(): lax.dot_general(left_side, right_side, (((1,), (1,)), ((), ())), preferre...  56 us
    dot_general x8, matrix products, multiply(): return jnp.dot(left_side, right_side, preferred_element_type=F32)  41.6 us
    dot_general x12, matrix products, contract_rows(): lax.dot_general(left_side, right_side, (((0,), (0,)), ((), ())), preferre...  41.4 us
    pallas_call x2, Pallas kernels, full_scan(): pl.pallas_call(functools.partial(scan_kernel, backward), out_shape=(jax.S...  18.3 us
  transfers between devices with their start and end apart: 6, of which 3 were waited for; matrix products, arithmetic and copies ran while one was open for 4% of the time, Pallas kernels for 0%

profile of v5, /device:TPU:2, one launch (start us, length us, event | category | flops | bytes accessed | tf_op | source)
XLA Modules:
  0.0 898.5 jit_solution(9316260679589542904)
XLA Ops:
  10.2 213.6 %gather_all.1 = (bf16[4,128,2560]{2,1,0:T(8,128)(2,1)}, bf16[2,4,128,2560]{3,2,1,0:T(8,128)(2,1)}, f32[32,16,128]{2,1,0:T(8,128)}, bf16[4,2,80,512]{3,2,1,0:T(8,...) custom-call(bf16[128,2560]{1,0:T(8,128)(2,1)} %refs_7_.1, ...), custom_call_target="tpu_custom_call" | custom-call | tf_op jit(solution)/shard_map/gather_all/pallas_call | solution.py:401
  231.2 5.0 fusion.138
  236.8 15.0 %collective-permute-start = (bf16[3,640]{1,0:T(4,128)(2,1)}, bf16[3,640]{1,0:T(4,128)(2,1)}, u32[]{:S(2)}, u32[]{:S(2)}) collective-permute-start(bf16[3,640]{1,0:T(4,128)(2,1)} %slice.517), channel_id=1, source_target_pairs={{0,4},{4,8},{8,12},{12,16},{16,20},{20,24},{24,28},{1,5},{5,9},{9,... | collective-permute-start | bytes 11528 | tf_op jit(solution)/shard_map/ppermute | solution.py:1391
  257.8 4.4 copy.67
  274.2 8.8 scan_ahead.1
  287.7 79.3 %branch_and_group.1 = (bf16[2,4,128,2560]{3,2,1,0:T(8,128)(2,1)S(1)}, f32[128,2560]{1,0:T(8,128)S(1)}, bf16[4,2,320,1024]{3,2,1,0:T(8,128)(2,1)}, bf16[4,2,320,1024]{3,2,1,0:T(8,128)(2,1)}) custom-call(f32[2,128,2560]{2,1,0:T(8,128)S(1)} %fusion.82.sent, f32[2,128,2560]{2,1,0:T(8,128)S(1)} %fusion.80.own, ...), custom_call_target="tpu_custom_call", output_to_operand_aliasing={{2}: (4, {}), {3}: (5, {})} | custom-call | tf_op jit(solution)/shard_map/branch_and_group/pallas_call | solution.py:602
  367.1 9.3 %fusion.140 = f32[1024,1024]{1,0:T(8,128)} fusion(bf16[1024,2560]{1,0:T(8,128)(2,1)S(1)} %bitcast.212, bf16[2560,1024]{1,0:T(8,128)(2,1)} %bitcast.283), kind=kOutput, calls=%fused_computation.273 | convolution fusion | flops 5368709120 | bytes 14680064 | tf_op jit(solution)/shard_map/dot_general | solution.py:73
  376.4 8.9 fusion.139
  385.3 12.3 %multiply_convert_fusion.1 = (bf16[1024,1024]{1,0:T(8,128)(2,1)S(1)}, bf16[1024,1024]{1,0:T(8,128)(2,1)}, bf16[1024,1024]{1,0:T(8,128)(2,1)S(1)}) fusion(f32[1024,1024]{1,0:T(8,128)} %fusion.140, f32[1024,1024]{1,0:T(8,128)} %fusion.139, bf16[1024,2560]{1,0:T(8,128)(2,1)S(1)} %bitcast.213, bf16[2560,1024]{1,0:T(8,128)(2,1)S(1)} %bitcast.243), kind=kOutput, calls=%fused_computation.29 | convolution fusion | flops 5395972096 | bytes 25165824 | tf_op jit(solution)/shard_map/dot_general | solution.py:73
  397.6 8.8 fusion.66
  406.4 7.1 fusion.63
  413.5 4.2 convolution_convert_fusion.5
  417.7 4.3 convolution_convert_fusion.4
  422.1 4.2 convolution_convert_fusion.3
  426.3 4.3 convolution_convert_fusion.2
  438.2 7.2 add_convert_fusion
  445.5 6.8 convolution_add_fusion
  452.3 4.2 convolution_convert_fusion.6.refs_5_
  456.5 4.7 fusion.141.refs_6_
  463.6 111.6 %middle_and_rows.1 = (bf16[4,128,2560]{2,1,0:T(8,128)(2,1)}, f32[128,2560]{1,0:T(8,128)}, f32[16,2560]{1,0:T(8,128)}, bf16[128,2560]{1,0:T(8,128)(2,1)}, bf16[1,...) custom-call(bf16[4,128,2560]{2,1,0:T(8,128)(2,1)} %bitcast.253, ...), custom_call_target="tpu_custom_call" | custom-call | tf_op jit(solution)/shard_map/middle_and_rows/pallas_call | solution.py:846
  575.2 3.5 convert_add_fusion
  584.2 4.1 convert_multiply_fusion
  588.3 9.5 %scan_back.1 = (f32[512,640]{1,0:T(8,128)S(1)}, f32[1,640]{1,0:T(1,128)S(1)}) custom-call(f32[512,640]{1,0:T(8,128)S(1)} %get-tuple-element.167.factors, f32[512,640]{1,0:T(8,128)S(1)} %get-tuple-element.137.inflows), custom_call_target="tpu_custom_call" | custom-call | tf_op jit(solution)/shard_map/scan_back/pallas_call | solution.py:1262
  599.0 3.5 multiply_reduce_fusion.5
  614.7 4.6 copy.71
  619.4 5.9 convolution_convert_fusion.7
  629.4 4.0 convolution_convert_fusion.8
  652.4 4.1 convolution_convert_fusion.9
  669.7 4.7 pad_maximum_fusion.refs_3_
  674.3 198.5 %last_sums.1 = (bf16[3,320,2048]{2,1,0:T(8,128)(2,1)}, f32[320,1920]{1,0:T(8,128)}, f32[80,512]{1,0:T(8,128)}, bf16[128,2560]{1,0:T(8,128)(2,1)}, f32[5,16,2560]{2,1,0:T(8,128)}, /*index=5*/f32[2,8,640]{2,1,0:T(8,128)}) custom-call(bf16[3,4,320,512]{3,2,1,0:T(8,128)(2,1)} %bitcast.225, bf16[1,6,320,512]{3,2,1,0:T(8,128)(2,1)} %pad_maximum_fusion.2.refs_1_, ...), custom_call_target="tpu_custom_call" | custom-call | tf_op jit(solution)/shard_map/last_sums/pallas_call | solution.py:1126
  879.6 5.4 bitcast_convert_fusion
  887.2 6.2 collective-permute-done.5
  (331 shorter events, 118.3 us)
Async XLA Ops:
  231.2 20.7 %copy-start.41 = (bf16[4,2,80,512]{3,2,1,0:T(8,128)(2,1)S(1)}, bf16[4,2,80,512]{3,2,1,0:T(8,128)(2,1)}, u32[]{:S(2)}) copy-start(bf16[4,2,80,512]{3,2,1,0:T(8,128)(2,1)} %get-tuple-element.52) | copy-start | bytes 1966084
  236.2 16.0 %copy-start.69 = (bf16[512,1280]{1,0:T(8,128)(2,1)}, bf16[512,1280]{1,0:T(8,128)(2,1)S(1)}, u32[]{:S(2)}) copy-start(bf16[512,1280]{1,0:T(8,128)(2,1)S(1)} %get-tuple-element.199) | copy-start | bytes 3932164
  236.8 26.1 %collective-permute-start = (bf16[3,640]{1,0:T(4,128)(2,1)}, bf16[3,640]{1,0:T(4,128)(2,1)}, u32[]{:S(2)}, u32[]{:S(2)}) collective-permute-start(bf16[3,640]{1,0:T(4,128)(2,1)} %slice.517), channel_id=1, source_target_pairs={{0,4},{4,8},{8,12},{12,16},{16,20},{20,24},{24,28},{1,5},{5,9},{9,... | collective-permute-start | bytes 11528 | tf_op jit(solution)/shard_map/ppermute | solution.py:1391
  252.2 12.5 %copy-start.42 = (bf16[640,512]{1,0:T(8,128)(2,1)}, bf16[640,512]{1,0:T(8,128)(2,1)S(1)}, u32[]{:S(2)}) copy-start(bf16[640,512]{1,0:T(8,128)(2,1)S(1)} %maximum_select_fusion.4) | copy-start | bytes 1966084
  252.9 13.5 %collective-permute-start.2 = (bf16[128,512]{1,0:T(8,128)(2,1)}, bf16[128,512]{1,0:T(8,128)(2,1)}, u32[]{:S(2)}, u32[]{:S(2)}) collective-permute-start(bf16[128,512]{1,0:T(8,128)(2,1)} %slice.535), channel_id=1, source_target_pairs={{0,1},{1,0},{2,3},{3,2},{4,5},{5,4},{6,7},{7,6},{8,9},{9,8},{10,11... | collective-permute-start | bytes 393224 | tf_op jit(solution)/shard_map/ppermute | solution.py:43
  257.8 29.9 %copy-start.2 = (f32[1,2560]{1,0:T(1,128)}, f32[1,2560]{1,0:T(1,128)S(1)}, u32[]{:S(2)}) copy-start(f32[1,2560]{1,0:T(1,128)S(1)} %slice.443.gain.refs_4_) | copy-start | bytes 30724
  265.3 1.3 collective-permute-start.1
  265.4 317.4 %copy-start.7 = (f32[512,256]{1,0:T(8,128)}, f32[512,256]{1,0:T(8,128)S(1)}, u32[]{:S(2)}) copy-start(f32[512,256]{1,0:T(8,128)S(1)} %get-tuple-element.173) | copy-start | bytes 1572868
  274.2 8.9 copy-start.62
  367.0 9.4 %copy-start.1 = (f32[128,2560]{1,0:T(8,128)}, f32[128,2560]{1,0:T(8,128)S(1)}, u32[]{:S(2)}) copy-start(f32[128,2560]{1,0:T(8,128)S(1)} %get-tuple-element.61.refs_2_) | copy-start | bytes 3932164
  367.1 9.4 %copy-start.27 = (bf16[4,2,320,1024]{3,2,1,0:T(8,128)(2,1)S(1)}, bf16[4,2,320,1024]{3,2,1,0:T(8,128)(2,1)}, u32[]{:S(2)}) copy-start(bf16[4,2,320,1024]{3,2,1,0:T(8,128)(2,1)} %get-tuple-element.57) | copy-start | bytes 15728644
  367.1 18.3 %slice-start.2 = ((s8[5242880]{0:T(1024)(128)(4,1)}), s8[4194304]{0:T(1024)(128)(4,1)S(1)}, s32[]{:S(2)}) async-start(s8[5242880]{0:T(1024)(128)(4,1)} %bitcast.241), calls=%async_computation.2 | async-start | bytes 8388608
  376.4 8.9 slice-start.3
  397.6 28.7 %copy-start.86 = (bf16[1024,1024]{1,0:T(8,128)(2,1)}, bf16[1024,1024]{1,0:T(8,128)(2,1)S(1)}, u32[]{:S(2)}) copy-start(bf16[1024,1024]{1,0:T(8,128)(2,1)S(1)} %get-tuple-element.143) | copy-start | bytes 6291460
  397.6 8.8 copy-start.87
  422.1 9.6 %slice-start.10 = ((s8[5242880]{0:T(1024)(128)(4,1)}), s8[4194304]{0:T(1024)(128)(4,1)S(1)}, s32[]{:S(2)}) async-start(s8[5242880]{0:T(1024)(128)(4,1)} %bitcast.279), calls=%async_computation.10 | async-start | bytes 8388608
  435.0 26.2 %copy-start.16 = (bf16[2560,512]{1,0:T(8,128)(2,1)}, bf16[2560,512]{1,0:T(8,128)(2,1)S(1)}, u32[]{:S(2)}) copy-start(bf16[2560,512]{1,0:T(8,128)(2,1)S(1)} %convolution_convert_fusion.1) | copy-start | bytes 7864324
  438.2 24.2 %copy-start.21 = (bf16[2560,512]{1,0:T(8,128)(2,1)}, bf16[2560,512]{1,0:T(8,128)(2,1)S(1)}, u32[]{:S(2)}) copy-start(bf16[2560,512]{1,0:T(8,128)(2,1)S(1)} %convolution_convert_fusion) | copy-start | bytes 7864324
  445.5 6.8 copy-start.59
  588.3 14.1 %copy-start.24 = (bf16[512,640]{1,0:T(8,128)(2,1)}, bf16[512,640]{1,0:T(8,128)(2,1)S(1)}, u32[]{:S(2)}) copy-start(bf16[512,640]{1,0:T(8,128)(2,1)S(1)} %get-tuple-element.138) | copy-start | bytes 1966084
  602.4 9.9 %copy-start.23 = (bf16[2560,512]{1,0:T(8,128)(2,1)S(1)}, bf16[2560,512]{1,0:T(8,128)(2,1)}, u32[]{:S(2)}) copy-start(bf16[2560,512]{1,0:T(8,128)(2,1)} %convolution_convert_fusion.4) | copy-start | bytes 7864324
  606.0 6.4 copy-start.38
  619.3 6.1 copy-start.33
  619.4 6.1 copy-start.34
  619.4 6.1 copy-start.52
  625.3 13.7 %collective-permute-start.3 = (bf16[512,256]{1,0:T(8,128)(2,1)S(1)}, bf16[512,256]{1,0:T(8,128)(2,1)S(1)}, u32[]{:S(2)}, u32[]{:S(2)}) collective-permute-start(bf16[512,256]{1,0:T(8,128)(2,1)S(1)} %pad_maximum_fusion.15), channel_id=1, source_target_pairs={{0,1},{1,0},{2,3},{3,2},{4,5},{5,4},{6,7},{7,6},{8,9},{9,8},{10,11... | collective-permute-start | bytes 786440 | tf_op jit(solution)/shard_map/ppermute | solution.py:43
  644.4 7.4 copy-start.26
  645.3 6.5 collective-permute-start.4
  652.4 10.7 %slice-start = ((s8[6553600]{0:T(1024)(128)(4,1)}), s8[4194304]{0:T(1024)(128)(4,1)S(1)}, s32[]{:S(2)}) async-start(s8[6553600]{0:T(1024)(128)(4,1)} %bitcast.221), calls=%async_computation | async-start | bytes 8388608
  656.5 6.5 slice-start.1
  877.7 15.7 %collective-permute-start.5 = (f32[80,520]{1,0:T(8,128)S(1)}, f32[80,520]{1,0:T(8,128)S(1)}, u32[]{:S(2)}, u32[]{:S(2)}) collective-permute-start(f32[80,520]{1,0:T(8,128)S(1)} %pad_maximum_fusion.17), channel_id=1, source_target_pairs={{0,0},{4,1},{8,2},{12,3},{16,4},{20,5},{24,6},{28,7},{1,8},{5,9},{... | collective-permute-start | bytes 499208 | tf_op jit(solution)/shard_map/ppermute | solution.py:1575
  886.7 10.9 %copy-start.64 = (bf16[128,2560]{1,0:T(8,128)(2,1)S(1)}, bf16[128,2560]{1,0:T(8,128)(2,1)}, u32[]{:S(2)}) copy-start(bf16[128,2560]{1,0:T(8,128)(2,1)} %get-tuple-element.228) | copy-start | bytes 1966084
  (74 other events, 201.1 us)

commit v6 on v5

--- a/solution.py
+++ b/solution.py
@@ -642,33 +642,33 @@
 def line_sum(me, sends, rows, term, ready, store, held, up, down, between=None):
     z = me.z
 
-    def add(when, target, slot, k, received=None):
+    def add(when, target, slot, k, received=None, came=0):
         def body(r):
             value = term(k, r)
             if received is not None:
-                value = value + received[slot - 1, r].astype(F32)
+                value = value + received[came, r].astype(F32)
             target[slot, r] = value.astype(BF16)
 
         pl.when(when)(lambda: each_rows(rows, 16, body))
 
     for t in range(1, Z):
         slot = t - 1
-        for k, (out, into, sems), has, when, to in (
-            (t, up, z > 0, (z <= t - 1) & (z < Z - 1), me.z_up),
-            (Z - t, down, z < Z - 1, (z >= Z - t) & (z > 0), me.z_down),
+        for k, (out, into, sems), out_slot, has, when, to in (
+            (t, up, slot, z > 0, (z <= t - 1) & (z < Z - 1), me.z_up),
+            (Z - t, down, Z - 1 - t, z < Z - 1, (z >= Z - t) & (z > 0), me.z_down),
         ):
             pl.when(when)(lambda k=k: ready(k))
             if t == 1:
-                add(when, out, slot, k)
+                add(when, out, out_slot, k)
             else:
                 pl.when(when & has)(
                     lambda into=into, sems=sems, slot=slot: arrived(
                         into.at[slot - 1], sems.at[slot - 1], me.at_c
                     )
                 )
-                add(when & has, out, slot, k, into)
-                add(when & jnp.logical_not(has), out, slot, k)
-            sends.start(when, out.at[slot], into.at[slot], sems.at[slot], me.at_z(to))
+                add(when & has, out, out_slot, k, into, slot - 1)
+                add(when & jnp.logical_not(has), out, out_slot, k)
+            sends.start(when, out.at[out_slot], into.at[slot], sems.at[slot], me.at_z(to))
         if between is not None:
             between(t)
     ready(0)
@@ -925,18 +925,89 @@
         )
 
 
+class ProductsSum(RowsSum):
+    def __init__(self, me, sends, factors, total, scratch, sems):
+        self.me, self.sends, self.total = me, sends, total
+        self.factors = factors
+        self.held, self.x_in, out, up_in, down_in, *self.lefts = scratch
+        self.own_sems, self.x_sems, up_sems, down_sems = sems
+        self.up, self.down = (out, up_in, up_sems), (out, down_in, down_sems)
+
+    def load(self):
+        self.loads = []
+        for n, (left, _) in enumerate(self.factors):
+            copy = pltpu.make_async_copy(left, self.lefts[n], self.own_sems.at[n])
+            copy.start()
+            self.loads.append(copy)
+
+    def begin(self, turns):
+        me = self.me
+        while self.loads:
+            self.loads.pop().wait()
+        rows, span = self.total.shape[0], self.held.shape[1]
+        for turn in turns:
+            if turn == Z - 1:
+                k = 0
+            else:
+                k = (jnp.minimum(me.z, Z - 1 - me.z) + turn) % (Z - 1) + 1
+                k = jnp.where(me.z < Z // 2, k, Z - k)
+            at = (me.z + Z - k) % Z
+
+            def tile(i, carried, k=k, at=at):
+                first = 0
+                down = pl.ds(pl.multiple_of(i * LANES, LANES), LANES)
+                across = pl.ds(pl.multiple_of(at * span + i * LANES, LANES), LANES)
+                for n, (_, rights) in enumerate(self.factors):
+                    left = self.lefts[n][:, across]
+                    for right in rights:
+                        columns = slice(first, first + right.shape[1])
+                        self.held[k, down, columns] = contract_rows(left, right[...]).astype(BF16)
+                        first += right.shape[1]
+                return carried
+
+            lax.fori_loop(0, span // LANES, tile, 0)
+            for j in range(1, me.inner):
+                part = pl.ds(pl.multiple_of((me.x + j) % me.inner * rows, 16), rows)
+                self.sends.start(
+                    True, self.held.at[k, part], self.x_in.at[j - 1, k], self.x_sems.at[j - 1, k],
+                    me.at_x(j),
+                )
+
+    def run(self, between=None):
+        me = self.me
+        rows = self.total.shape[0]
+
+        def ready(k):
+            for j in range(1, me.inner):
+                arrived(self.x_in.at[j - 1, k], self.x_sems.at[j - 1, k], me.at_c)
+
+        def term(k, r):
+            mine = pl.ds(pl.multiple_of(me.x * rows + r.start, 16), r.size)
+            value = self.held[k, mine].astype(F32)
+            for j in range(1, me.inner):
+                value = value + self.x_in[j - 1, k, r].astype(F32)
+            return value
+
+        def store(r, value):
+            self.total[r] = value
+
+        line_sum(
+            me, self.sends, rows, term, ready, store, lambda r: self.total[r],
+            self.up, self.down, between,
+        )
+
+
 def sums_kernel(shape, *refs):
     inner, outer = shape
-    units, units_y, units_x = refs[:3]
-    refs = refs[3:]
-    (wide, narrow, sent, own, tokens, gain, d_middle, gain_two_grad, vectors, units_to) = refs[:10]
-    refs = refs[1:]
-    (wide_to, narrow_to, tokens_grad, gains, vectors_to) = refs[9:14]
-    wide_scratch, narrow_scratch = refs[14:20], refs[20:26]
-    (own_v, c_in, y_out, y_in, all_in, vec_in) = refs[26:32]
-    (send_sems, local_sems, c_sems, y_sems, all_sems, vec_sems) = refs[32:38]
-    wide_sems, narrow_sems = refs[38:42], refs[42:46]
-    units_v, units_y_in, units_x_in, unit_sems, units_y_sems, units_x_sems = refs[46:]
+    units, units_y, units_x, normed_rows_one, branch_rows, narrow, sent, own = refs[:8]
+    d_x, d_y, mixed, tokens, gain, d_middle, gain_two_grad, vectors = refs[8:16]
+    units_to, wide_to, narrow_to, tokens_grad, gains, vectors_to = refs[16:22]
+    refs = refs[22:]
+    wide_scratch, narrow_scratch = refs[:7], refs[7:13]
+    (own_v, c_in, y_out, y_in, all_in, vec_in) = refs[13:19]
+    (send_sems, local_sems, c_sems, y_sems, all_sems, vec_sems) = refs[19:25]
+    wide_sems, narrow_sems = refs[25:29], refs[29:33]
+    units_v, units_y_in, units_x_in, unit_sems, units_y_sems, units_x_sems = refs[33:]
     share = units.shape[3]
     me = Place(shape)
     rows = tokens.shape[0]
@@ -951,7 +1022,8 @@
     for at in order:
         sends.start(True, sent.at[at], c_in.at[at], c_sems.at[at], me.at_c)
     narrow_sum = RowsSum(me, sends, narrow, narrow_to, narrow_scratch, narrow_sems)
-    wide_sum = RowsSum(me, sends, wide, wide_to, wide_scratch, wide_sems)
+    factors = [(normed_rows_one, [d_x, d_y]), (branch_rows, [mixed])]
+    wide_sum = ProductsSum(me, sends, factors, wide_to, wide_scratch, wide_sems)
     narrow_sum.load()
     wide_sum.load()
     narrow_sum.begin(range(Z))
@@ -1049,7 +1121,6 @@
     z_stage, x_stage = stages[2], stages[3]
     exchange(vectors, vec_in, vec_sems, 0, x_stage)
     units_begin_x()
-    wide_sum.begin(range(Z))
 
     units_begin_y()
 
@@ -1058,19 +1129,22 @@
         arrived(c_in.at[at], c_sems.at[at], me.at_c)
         if i < outer - 1:
             each_rows(rows, 16, lambda r, i=i, at=at: y_out.__setitem__(
-                (i, r), (own_v[at, r] + c_in[at, r]).astype(BF16)))
+                (i, r), (own_v[at, r] + c_in[at, r].astype(F32)).astype(BF16)))
             sends.start(True, y_out.at[i], y_in.at[i], y_sems.at[i], me.at_y(i + 1))
     vectors_to[0] = gathered(vectors, vec_in, vec_sems, 0, x_stage)
     exchange(vectors_to.at[0], vec_in, vec_sems, len(x_stage), z_stage)
     narrow_sum.run()
     vectors_to[1] = gathered(vectors_to.at[0], vec_in, vec_sems, len(x_stage), z_stage)
     units_load.wait()
+    wide_sum.begin(range(1))
     unit_gate()
+    wide_sum.begin(range(1, 2))
     unit_up()
     unit_down()
+    wide_sum.begin(range(2, Z))
 
     def work(r):
-        d_normed = own_v[me.y, r] + c_in[me.y, r]
+        d_normed = own_v[me.y, r] + c_in[me.y, r].astype(F32)
         for i in range(outer - 1):
             d_normed = d_normed + y_in[i, r].astype(F32)
         stream = tokens[r].astype(F32)
@@ -1106,7 +1180,10 @@
     sends.finish()
 
 
-def last_sums(units, units_y, units_x, wide, narrow, sent, own, tokens, gain, d_middle, gain_two_grad, vectors):
+def last_sums(
+    units, units_y, units_x, normed_one, branch_rows, narrow, sent, own,
+    d_x, d_y, mixed, tokens, gain, d_middle, gain_two_grad, vectors,
+):
     inner, outer = sizes()
     rows, width = tokens.shape
     dma = pltpu.SemaphoreType.DMA
@@ -1122,24 +1199,30 @@
     copies = 2 * outer - 1 + 2 * (Z * (inner - 1) + 2 * (Z - 1))
     copies += peers + (inner - 1) + (Z - 1) + 2 * (outer - 1) + 2 * (inner - 1) + 3 * (Z - 1)
     _, _, unit_rows, share = units.shape
+    block = (unit_rows, d_x.shape[1] + d_y.shape[1] + mixed.shape[1])
     line_sems = [dma((Z,)), dma((inner - 1, Z)), dma((Z - 1,)), dma((Z - 1,))]
     return pl.pallas_call(
         functools.partial(sums_kernel, (inner, outer)),
         out_shape=(
             jax.ShapeDtypeStruct((3, unit_rows, Z * share), BF16),
-            jax.ShapeDtypeStruct(wide.shape[2:], F32),
+            jax.ShapeDtypeStruct(block, F32),
             jax.ShapeDtypeStruct(narrow.shape[2:], F32),
             jax.ShapeDtypeStruct((rows, width), BF16),
             jax.ShapeDtypeStruct((5, 16, width), F32),
             jax.ShapeDtypeStruct((2, *vectors.shape), F32),
         ),
-        in_specs=[anywhere] * 7 + [vmem] * 5,
+        in_specs=[anywhere] * 8 + [vmem] * 8,
         out_specs=(anywhere,) + (vmem,) * 5,
-        scratch_shapes=scratch(wide)
+        scratch_shapes=[
+            pltpu.VMEM((Z, inner * block[0], block[1]), BF16),
+            pltpu.VMEM((inner - 1, Z, *block), BF16),
+        ]
+        + [pltpu.VMEM((Z - 1, *block), BF16)] * 3
+        + [pltpu.VMEM(normed_one.shape, BF16), pltpu.VMEM(branch_rows.shape, BF16)]
         + scratch(narrow)
         + [
             pltpu.VMEM((outer, rows, width), F32),
-            pltpu.VMEM((outer, rows, width), F32),
+            pltpu.VMEM((outer, rows, width), BF16),
             pltpu.VMEM((outer - 1, rows, width), BF16),
             pltpu.VMEM((outer - 1, rows, width), BF16),
             pltpu.VMEM((peers, 16, width), F32),
@@ -1161,10 +1244,13 @@
             dma((inner - 1, 2)),
         ],
         compiler_params=pltpu.CompilerParams(
-            collective_id=5, has_side_effects=True, vmem_limit_bytes=58 * 1024 * 1024
+            collective_id=5, has_side_effects=True, vmem_limit_bytes=60 * 1024 * 1024
         ),
         name="last_sums",
-    )(units, units_y, units_x, wide, narrow, sent, own, tokens, gain, d_middle, gain_two_grad, vectors)
+    )(
+        units, units_y, units_x, normed_one, branch_rows, narrow, sent, own,
+        d_x, d_y, mixed, tokens, gain, d_middle, gain_two_grad, vectors,
+    )
 
 
 def scan_kernel(backward, factors, inflows, states, entered, products, ends, ends_in, carry, send_sems, arrivals):
@@ -1403,13 +1489,17 @@
     pre_parts = [
         multiply(of_head(conv_low, i), gate_all[i * block : (i + 1) * block]) for i in range(heads)
     ]
-    shared_pre = multiply(shared_conv, shared_rows).reshape(rows, 2, C, half)
-    shared_pre = pick(shared_pre, c, 2)
+    shared_columns = jnp.where(
+        c == 0,
+        jnp.concatenate([shared_rows[:, :half], shared_rows[:, block : block + half]], axis=1),
+        jnp.concatenate([shared_rows[:, half:block], shared_rows[:, block + half :]], axis=1),
+    )
+    shared_pre = multiply(shared_conv, shared_columns)
     decay_pre = decay_shift + jnp.concatenate(
-        [part[:, :block] for part in pre_parts] + [shared_pre[:, 0]], axis=1
+        [part[:, :block] for part in pre_parts] + [shared_pre[:, :half]], axis=1
     )
     input_pre = input_shift + jnp.concatenate(
-        [part[:, block:] for part in pre_parts] + [shared_pre[:, 1]], axis=1
+        [part[:, block:] for part in pre_parts] + [shared_pre[:, half:]], axis=1
     )
     (retain, inflow), terms_back = jax.vjp(
         recurrence_terms, decay_pre, input_pre, decay_log, conv_low.astype(F32)
@@ -1543,15 +1633,6 @@
         )
         return total.reshape(outer, rows_dev, width)
 
-    wide = jnp.concatenate(
-        [
-            contract_rows(group_one, d_x_branch),
-            contract_rows(group_one, d_y),
-            contract_rows(branch_rows, mixed_rows),
-        ],
-        axis=1,
-    )
-    wide = wide.astype(BF16).reshape(Z, inner, weight_rows, 3 * lru_cols)
     narrow = turned_back(gates_grad, 0).astype(BF16).reshape(Z, inner, chunk, 2 * block)
     narrow = jnp.pad(narrow, ((0, 0), (0, 0), (0, -chunk % 16), (0, 0)))
     own_sums = jnp.stack(
@@ -1561,12 +1642,12 @@
     )
     own_sums = turned_back(own_sums, 1)
     placed, wide, narrow, tokens_grad, gains, own_sums = last_sums(
-        units, units_y, units_x, wide, narrow, d_normed_one_of(1 - c), d_normed_one_of(c), tokens, gain_one[None],
-        d_middle, gain_two_grad, own_sums,
-    )
-    weight_grads = [
-        turned_back(wide[:, n * lru_cols : (n + 1) * lru_cols], 1) for n in range(3)
-    ]
+        units, units_y, units_x, group_one, branch_rows, narrow,
+        d_normed_one_of(1 - c).astype(BF16), d_normed_one_of(c),
+        turned_back(d_x_branch, 1), turned_back(d_y, 1), turned_back(mixed_rows, 1),
+        tokens, gain_one[None], d_middle, gain_two_grad, own_sums,
+    )
+    weight_grads = [wide[:, n * lru_cols : (n + 1) * lru_cols] for n in range(3)]
     gate_grad, up_grad, down_grad = (placed[n, :, :hidden_cols].astype(F32) for n in range(3))
     gains = gains[4].reshape(2, 8, width).sum(axis=1)
     gains = lax.dynamic_slice(gains, (0, (lax.axis_index("seq") * wt + w) * chunk), (2, chunk))

time: 905 us -> 858 us (0.948)
  matrix products: 139 us -> 118 us
  local copies, waits for them, and re-layouts: 54.4 us -> 34.6 us
    dot_general x12 -> x9, matrix products: 41.4 us -> 24.2 us  [contract_rows(): lax.dot_general(left_side, right_side, (((0,), (0,)), ((), ())), preferre...]
    dot_general x2 -> x0, local copies, waits for them, and re-layouts: 9.08 us -> none  [contract_rows(): lax.dot_general(left_side, right_side, (((0,), (0,)), ((), ())), preferre...]
  transfers between devices with their start and end apart: 6 -> 6, of which waited for: 3 -> 2; matrix products, arithmetic and copies ran while one was open for 4% -> 3% of each run, Pallas kernels for 0% -> 0%
where the time goes in v6:
time: 858 us; the launch traced here: 850 us
  Pallas kernels  617 us (72%)
  matrix products  118 us (14%)
  other arithmetic  48.9 us (6%)
  local copies, waits for them, and re-layouts  34.6 us (4%)
  starting transfers between devices  19.2 us (2%)
  waiting for transfers between devices  10.3 us (1%)
    pallas_call x1, Pallas kernels, gather_all(): pl.pallas_call(functools.partial(gather_kernel, (inner, outer)), out_shap...  214 us
    pallas_call x1, Pallas kernels, last_sums(): pl.pallas_call(functools.partial(sums_kernel, (inner, outer)), out_shape=...  192 us
    pallas_call x1, Pallas kernels, middle_and_rows(): pl.pallas_call(functools.partial(middle_kernel, (inner, outer)), out_shap...  112 us
    pallas_call x1, Pallas kernels, branch_and_group(): pl.pallas_call(functools.partial(branch_kernel, (inner, outer)), out_shap...  78.7 us
    dot_general x15, matrix products, contract_last(): lax.dot_general(left_side, right_side, (((1,), (1,)), ((), ())), preferre...  53.1 us
    dot_general x8, matrix products, multiply(): return jnp.dot(left_side, right_side, preferred_element_type=F32)  40.5 us
    dot_general x9, matrix products, contract_rows(): lax.dot_general(left_side, right_side, (((0,), (0,)), ((), ())), preferre...  24.2 us
    pallas_call x2, Pallas kernels, full_scan(): pl.pallas_call(functools.partial(scan_kernel, backward), out_shape=(jax.S...  19.8 us
  transfers between devices with their start and end apart: 6, of which 2 were waited for; matrix products, arithmetic and copies ran while one was open for 3% of the time, Pallas kernels for 0%

profile of v6, /device:TPU:2, one launch (start us, length us, event | category | flops | bytes accessed | tf_op | source)
XLA Modules:
  0.0 850.0 jit_solution(5840777076340782446)
XLA Ops:
  10.2 213.6 %gather_all.1 = (bf16[4,128,2560]{2,1,0:T(8,128)(2,1)}, bf16[2,4,128,2560]{3,2,1,0:T(8,128)(2,1)}, f32[32,16,128]{2,1,0:T(8,128)}, bf16[4,2,80,512]{3,2,1,0:T(8,...) custom-call(bf16[128,2560]{1,0:T(8,128)(2,1)} %refs_11_.1, ...), custom_call_target="tpu_custom_call" | custom-call | tf_op jit(solution)/shard_map/gather_all/pallas_call | solution.py:401
  231.2 5.1 fusion.137
  236.9 14.8 %collective-permute-start = (bf16[3,640]{1,0:T(4,128)(2,1)}, bf16[3,640]{1,0:T(4,128)(2,1)}, u32[]{:S(2)}, u32[]{:S(2)}) collective-permute-start(bf16[3,640]{1,0:T(4,128)(2,1)} %slice.527), channel_id=1, source_target_pairs={{0,4},{4,8},{8,12},{12,16},{16,20},{20,24},{24,28},{1,5},{5,9},{9,... | collective-permute-start | bytes 11528 | tf_op jit(solution)/shard_map/ppermute | solution.py:1477
  264.5 8.9 %scan_ahead.1 = (f32[512,640]{1,0:T(8,128)S(1)}, f32[1,640]{1,0:T(1,128)S(1)}) custom-call(f32[512,640]{1,0:T(8,128)S(1)} %get-tuple-element.161.factors, f32[512,640]{1,0:T(8,128)S(1)} %get-tuple-element.160.inflows), custom_call_target="tpu_custom_call" | custom-call | tf_op jit(solution)/shard_map/scan_ahead/pallas_call | solution.py:1348
  278.1 78.7 %branch_and_group.1 = (bf16[2,4,128,2560]{3,2,1,0:T(8,128)(2,1)S(1)}, f32[128,2560]{1,0:T(8,128)S(1)}, bf16[4,2,320,1024]{3,2,1,0:T(8,128)(2,1)}, bf16[4,2,320,1024]{3,2,1,0:T(8,128)(2,1)}) custom-call(f32[2,128,2560]{2,1,0:T(8,128)S(1)} %fusion.80.sent, f32[2,128,2560]{2,1,0:T(8,128)S(1)} %fusion.78.own, ...), custom_call_target="tpu_custom_call", output_to_operand_aliasing={{2}: (4, {}), {3}: (5, {})} | custom-call | tf_op jit(solution)/shard_map/branch_and_group/pallas_call | solution.py:602
  356.8 9.3 %fusion.139 = f32[1024,1024]{1,0:T(8,128)} fusion(bf16[1024,2560]{1,0:T(8,128)(2,1)S(1)} %bitcast.183, bf16[2560,1024]{1,0:T(8,128)(2,1)} %bitcast.248), kind=kOutput, calls=%fused_computation.266 | convolution fusion | flops 5368709120 | bytes 14680064 | tf_op jit(solution)/shard_map/dot_general | solution.py:73
  366.1 9.0 %fusion.138 = f32[1024,1024]{1,0:T(8,128)} fusion(bf16[1024,2560]{1,0:T(8,128)(2,1)} %bitcast.243, bf16[2560,1024]{1,0:T(8,128)(2,1)S(1)} %bitcast.220), kind=kOutput, calls=%fused_computation.265 | convolution fusion | flops 5368709120 | bytes 14680064 | tf_op jit(solution)/shard_map/dot_general | solution.py:73
  375.2 13.0 %multiply_convert_fusion.1 = (bf16[1024,1024]{1,0:T(8,128)(2,1)}, bf16[1024,1024]{1,0:T(8,128)(2,1)}, bf16[1024,1024]{1,0:T(8,128)(2,1)}) fusion(f32[1024,1024]{1,0:T(8,128)} %fusion.139, f32[1024,1024]{1,0:T(8,128)} %fusion.138, bf16[1024,2560]{1,0:T(8,128)(2,1)S(1)} %bitcast.184, bf16[2560,1024]{1,0:T(8,128)(2,1)S(1)} %bitcast.217), kind=kOutput, calls=%fused_computation.28 | convolution fusion | flops 5395972096 | bytes 25165824 | tf_op jit(solution)/shard_map/dot_general | solution.py:73
  388.1 8.2 fusion.67
  396.3 7.1 fusion.64
  403.4 4.2 convolution_convert_fusion.5
  407.7 4.2 convolution_convert_fusion.4
  411.9 4.2 convolution_convert_fusion.3
  416.2 4.2 convolution_convert_fusion.2
  421.5 3.2 convolution_convert_fusion.1
  424.7 3.2 convolution_convert_fusion
  427.9 7.2 add_convert_fusion
  435.1 6.8 convolution_add_fusion
  441.9 4.2 convolution_convert_fusion.6.refs_5_
  446.2 4.7 fusion.140.refs_6_
  453.6 112.4 %middle_and_rows.1 = (bf16[4,128,2560]{2,1,0:T(8,128)(2,1)}, f32[128,2560]{1,0:T(8,128)}, f32[16,2560]{1,0:T(8,128)}, bf16[128,2560]{1,0:T(8,128)(2,1)}, bf16[1,...) custom-call(bf16[4,128,2560]{2,1,0:T(8,128)(2,1)} %bitcast.227, ...), custom_call_target="tpu_custom_call" | custom-call | tf_op jit(solution)/shard_map/middle_and_rows/pallas_call | solution.py:846
  566.1 3.5 convert_add_fusion
  573.9 3.3 convert_multiply_fusion
  577.2 10.8 %scan_back.1 = (f32[512,640]{1,0:T(8,128)S(1)}, f32[1,640]{1,0:T(1,128)S(1)}) custom-call(f32[512,640]{1,0:T(8,128)S(1)} %get-tuple-element.161.factors, f32[512,640]{1,0:T(8,128)S(1)} %get-tuple-element.137.inflows), custom_call_target="tpu_custom_call" | custom-call | tf_op jit(solution)/shard_map/scan_back/pallas_call | solution.py:1348
  589.2 3.4 multiply_reduce_fusion.5
  592.7 2.9 fusion.123
  620.8 3.3 fusion.18
  624.1 3.1 fusion.16
  633.3 192.4 %last_sums.1 = (bf16[3,320,2048]{2,1,0:T(8,128)(2,1)}, f32[320,1920]{1,0:T(8,128)}, f32[80,512]{1,0:T(8,128)}, bf16[128,2560]{1,0:T(8,128)(2,1)}, f32[5,16,2560]{2,1,0:T(8,128)}, /*index=5*/f32[2,8,640]{2,1,0:T(8,128)}) custom-call(bf16[3,4,320,512]{3,2,1,0:T(8,128)(2,1)} %bitcast.196, bf16[1,6,320,512]{3,2,1,0:T(8,128)(2,1)} %pad_maximum_fusion.1.refs_1_, ...), custom_call_target="tpu_custom_call" | custom-call | tf_op jit(solution)/shard_map/last_sums/pallas_call | solution.py:1204
  826.7 3.2 fusion.127
  832.0 5.3 bitcast_convert_fusion
  837.9 7.9 collective-permute-done.5
  (288 shorter events, 82.1 us)
Async XLA Ops:
  226.1 5.1 copy-start.3
  231.2 20.5 %copy-start.30 = (bf16[4,2,80,512]{3,2,1,0:T(8,128)(2,1)S(1)}, bf16[4,2,80,512]{3,2,1,0:T(8,128)(2,1)}, u32[]{:S(2)}) copy-start(bf16[4,2,80,512]{3,2,1,0:T(8,128)(2,1)} %get-tuple-element.52) | copy-start | bytes 1966084
  236.3 15.7 %copy-start.47 = (bf16[512,1280]{1,0:T(8,128)(2,1)}, bf16[512,1280]{1,0:T(8,128)(2,1)S(1)}, u32[]{:S(2)}) copy-start(bf16[512,1280]{1,0:T(8,128)(2,1)S(1)} %get-tuple-element.197) | copy-start | bytes 3932164
  236.9 20.6 %collective-permute-start = (bf16[3,640]{1,0:T(4,128)(2,1)}, bf16[3,640]{1,0:T(4,128)(2,1)}, u32[]{:S(2)}, u32[]{:S(2)}) collective-permute-start(bf16[3,640]{1,0:T(4,128)(2,1)} %slice.527), channel_id=1, source_target_pairs={{0,4},{4,8},{8,12},{12,16},{16,20},{20,24},{24,28},{1,5},{5,9},{9,... | collective-permute-start | bytes 11528 | tf_op jit(solution)/shard_map/ppermute | solution.py:1477
  252.0 7.3 copy-start.31
  252.7 7.3 collective-permute-start.2
  256.8 21.3 %copy-start.2 = (f32[1,2560]{1,0:T(1,128)}, f32[1,2560]{1,0:T(1,128)S(1)}, u32[]{:S(2)}) copy-start(f32[1,2560]{1,0:T(1,128)S(1)} %slice.453.gain.refs_4_) | copy-start | bytes 30724
  259.8 2.1 collective-permute-start.1
  264.5 8.9 %copy-start.43 = (f32[512,1280]{1,0:T(8,128)S(1)}, f32[512,1280]{1,0:T(8,128)}, u32[]{:S(2)}) copy-start(f32[512,1280]{1,0:T(8,128)} %get-tuple-element.198) | copy-start | bytes 7864324
  356.8 9.4 %copy-start.1 = (f32[128,2560]{1,0:T(8,128)}, f32[128,2560]{1,0:T(8,128)S(1)}, u32[]{:S(2)}) copy-start(f32[128,2560]{1,0:T(8,128)S(1)} %get-tuple-element.61.refs_2_) | copy-start | bytes 3932164
  356.8 9.4 %copy-start.22 = (bf16[4,2,320,1024]{3,2,1,0:T(8,128)(2,1)S(1)}, bf16[4,2,320,1024]{3,2,1,0:T(8,128)(2,1)}, u32[]{:S(2)}) copy-start(bf16[4,2,320,1024]{3,2,1,0:T(8,128)(2,1)} %get-tuple-element.57) | copy-start | bytes 15728644
  356.8 18.4 %slice-start.2 = ((s8[5242880]{0:T(1024)(128)(4,1)}), s8[1048576]{0:T(1024)(128)(4,1)S(1)}, s32[]{:S(2)}) async-start(s8[5242880]{0:T(1024)(128)(4,1)} %bitcast.215), calls=%async_computation.2 | async-start | bytes 2097152
  366.1 9.0 %slice-start.3 = ((s8[5242880]{0:T(1024)(128)(4,1)}), s8[4194304]{0:T(1024)(128)(4,1)S(1)}, s32[]{:S(2)}) async-start(s8[5242880]{0:T(1024)(128)(4,1)} %bitcast.215), calls=%async_computation.3 | async-start | bytes 8388608
  388.1 8.2 copy-start.65
  407.7 4.2 copy-start.64
  411.9 9.6 %slice-start.10 = ((s8[5242880]{0:T(1024)(128)(4,1)}), s8[4194304]{0:T(1024)(128)(4,1)S(1)}, s32[]{:S(2)}) async-start(s8[5242880]{0:T(1024)(128)(4,1)} %bitcast.244), calls=%async_computation.10 | async-start | bytes 8388608
  416.1 4.2 copy-start.33
  416.1 5.4 slice-start.11
  424.7 26.1 %copy-start.14 = (bf16[2560,512]{1,0:T(8,128)(2,1)}, bf16[2560,512]{1,0:T(8,128)(2,1)S(1)}, u32[]{:S(2)}) copy-start(bf16[2560,512]{1,0:T(8,128)(2,1)S(1)} %convolution_convert_fusion.1) | copy-start | bytes 7864324
  427.9 24.6 %copy-start.19 = (bf16[2560,512]{1,0:T(8,128)(2,1)}, bf16[2560,512]{1,0:T(8,128)(2,1)S(1)}, u32[]{:S(2)}) copy-start(bf16[2560,512]{1,0:T(8,128)(2,1)S(1)} %convolution_convert_fusion) | copy-start | bytes 7864324
  435.1 6.8 copy-start.42
  566.1 3.5 copy-start.23
  566.1 3.5 copy-start.38
  600.6 9.2 %collective-permute-start.3 = (bf16[512,256]{1,0:T(8,128)(2,1)S(1)}, bf16[512,256]{1,0:T(8,128)(2,1)S(1)}, u32[]{:S(2)}, u32[]{:S(2)}) collective-permute-start(bf16[512,256]{1,0:T(8,128)(2,1)S(1)} %pad_maximum_fusion.14), channel_id=1, source_target_pairs={{0,1},{1,0},{2,3},{3,2},{4,5},{5,4},{6,7},{7,6},{8,9},{9,8},{10,11... | collective-permute-start | bytes 786440 | tf_op jit(solution)/shard_map/ppermute | solution.py:43
  613.6 6.5 collective-permute-start.4
  616.6 10.6 %slice-start = ((s8[6553600]{0:T(1024)(128)(4,1)}), s8[4194304]{0:T(1024)(128)(4,1)S(1)}, s32[]{:S(2)}) async-start(s8[6553600]{0:T(1024)(128)(4,1)} %bitcast.192), calls=%async_computation | async-start | bytes 8388608
  620.8 6.5 slice-start.1
  826.6 3.2 copy-start.56
  826.7 3.4 copy-start.49
  830.0 15.8 %collective-permute-start.5 = (f32[80,520]{1,0:T(8,128)S(1)}, f32[80,520]{1,0:T(8,128)S(1)}, u32[]{:S(2)}, u32[]{:S(2)}) collective-permute-start(f32[80,520]{1,0:T(8,128)S(1)} %pad_maximum_fusion.16), channel_id=1, source_target_pairs={{0,0},{4,1},{8,2},{12,3},{16,4},{20,5},{24,6},{28,7},{1,8},{5,9},{... | collective-permute-start | bytes 499208 | tf_op jit(solution)/shard_map/ppermute | solution.py:1656
  832.0 16.0 %copy-start.45 = (bf16[128,2560]{1,0:T(8,128)(2,1)S(1)}, bf16[128,2560]{1,0:T(8,128)(2,1)}, u32[]{:S(2)}) copy-start(bf16[128,2560]{1,0:T(8,128)(2,1)} %get-tuple-element.225) | copy-start | bytes 1966084
  837.3 11.5 %copy-start.46 = (bf16[128,2560]{1,0:T(8,128)(2,1)S(1)}, bf16[128,2560]{1,0:T(8,128)(2,1)}, u32[]{:S(2)}) copy-start(bf16[128,2560]{1,0:T(8,128)(2,1)} %get-tuple-element.226) | copy-start | bytes 1966084
  (52 other events, 92.7 us)

commit v7 on v6

--- a/solution.py
+++ b/solution.py
@@ -682,9 +682,9 @@
 
 
 class PlaneTerms:
-    def __init__(self, me, sends, parts, target, sems, over_x, blocks):
-        self.me, self.sends, self.parts, self.target, self.sems = me, sends, parts, target, sems
-        self.over_x, self.blocks = over_x, blocks
+    def __init__(self, me, sends, parts, over_x, blocks, scratch):
+        self.me, self.sends, self.parts, self.over_x, self.blocks = me, sends, parts, over_x, blocks
+        self.came, self.mine, self.sems, self.local_sems = scratch
 
     def begin(self):
         me = self.me
@@ -693,24 +693,65 @@
                 for i, part in enumerate(self.parts):
                     self.sends.start(
                         True, part.at[self.blocks, (me.x + j) % me.inner],
-                        self.target.at[j - 1, i], self.sems.at[j - 1, i], me.at_x(j),
+                        self.came.at[j - 1, i], self.sems.at[j - 1, i], me.at_x(j),
                     )
+            pairs = [(part.at[self.blocks, me.x], self.mine.at[i]) for i, part in enumerate(self.parts)]
         else:
             for i in range(1, me.outer):
                 self.sends.start(
-                    True, self.parts[i].at[self.blocks], self.target.at[i - 1],
+                    True, self.parts[i].at[self.blocks], self.came.at[i - 1],
                     self.sems.at[0, i - 1], me.at_y(-i),
                 )
-
-    def finish(self):
+            pairs = [(self.parts[0].at[self.blocks], self.mine)]
+        self.loads = self.moved(pairs)
+
+    def moved(self, pairs):
+        copies = [
+            pltpu.make_async_copy(source, target, self.local_sems.at[n])
+            for n, (source, target) in enumerate(pairs)
+        ]
+        for copy in copies:
+            copy.start()
+        return copies
+
+    def add(self):
         me = self.me
         if self.over_x:
-            for j in range(1, me.inner):
-                for i in range(me.outer):
-                    arrived(self.target.at[j - 1, i], self.sems.at[j - 1, i], me.at_c)
+            count, places = me.inner - 1, [(i,) for i in range(me.outer)]
         else:
-            for i in range(1, me.outer):
-                arrived(self.target.at[i - 1], self.sems.at[0, i - 1], me.at_c)
+            count, places = me.outer - 1, [()]
+        for n in range(count):
+            for place in places:
+                sems = self.sems.at[n, place[0]] if place else self.sems.at[0, n]
+                arrived(self.came.at[(n, *place)], sems, me.at_c)
+        for copy in self.loads:
+            copy.wait()
+        shape = self.mine.shape[:2]
+
+        def body(r):
+            for first in range(shape[0]):
+                for second in range(shape[1]):
+                    total = self.mine[first, second, r].astype(F32)
+                    for n in range(count):
+                        total = total + self.came[n, first, second, r].astype(F32)
+                    self.mine[first, second, r] = total.astype(BF16)
+
+        each_rows(self.mine.shape[2], 16, body)
+
+    def hand_on(self, kept, sent):
+        me = self.me
+        if self.over_x:
+            pairs = [(self.mine.at[i], kept if i == 0 else sent(i - 1)) for i in range(me.outer)]
+        else:
+            pairs = [
+                (self.mine.at[:, (me.x + j) % me.inner], kept if j == 0 else sent(j - 1))
+                for j in range(me.inner)
+            ]
+        self.loads = self.moved(pairs)
+
+    def finish(self):
+        for copy in self.loads:
+            copy.wait()
 
 
 def middle_kernel(shape, *refs):
@@ -718,11 +759,12 @@
     sent, own, middle, grads, gain, feed_sent, feed_own = refs[:7]
     parts = refs[7 : 7 + 3 * outer]
     rows_to, d_middle, gain_grad, block_out = refs[7 + 3 * outer : 11 + 3 * outer]
-    targets = refs[11 + 3 * outer : 15 + 3 * outer]
-    scratch = refs[15 + 3 * outer :]
+    targets = refs[11 + 3 * outer : 14 + 3 * outer]
+    scratch = refs[14 + 3 * outer :]
     middle_body(
         shape, sent, own, middle, grads, gain, feed_sent, feed_own, parts, targets,
-        rows_to, d_middle, gain_grad, block_out, scratch[:9], scratch[9:18], *scratch[18:],
+        rows_to, d_middle, gain_grad, block_out, scratch[:9], scratch[9:18],
+        [scratch[18 + 4 * n : 22 + 4 * n] for n in range(4)], *scratch[34:],
     )
 
 
@@ -741,7 +783,7 @@
                 True, self.sent.at[k], self.c_in.at[k], self.c_sems.at[k], self.me.at_c
             )
 
-    def run(self):
+    def run(self, between=None):
         def ready(k):
             arrived(self.c_in.at[k], self.c_sems.at[k], self.me.at_c)
 
@@ -753,26 +795,26 @@
 
         line_sum(
             self.me, self.sends, self.held.shape[1], term, ready, store,
-            lambda r: self.held[0, r], self.up, self.down,
+            lambda r: self.held[0, r], self.up, self.down, between,
         )
 
 
-def plane_units(me, sends, parts, targets, sems):
+def plane_units(me, sends, parts, scratch):
     outer = me.outer
     gate, up, down = (parts[n * outer : (n + 1) * outer] for n in range(3))
     every, low, high = slice(0, Z), slice(0, Z // 2), slice(Z // 2, Z)
     return [
-        PlaneTerms(me, sends, gate, targets[0], sems.at[0], True, every),
-        PlaneTerms(me, sends, up, targets[1], sems.at[1], False, every),
-        PlaneTerms(me, sends, down, targets[2], sems.at[2], True, low),
-        PlaneTerms(me, sends, down, targets[3], sems.at[3], False, high),
+        PlaneTerms(me, sends, gate, True, every, scratch[0]),
+        PlaneTerms(me, sends, up, False, every, scratch[1]),
+        PlaneTerms(me, sends, down, True, low, scratch[2]),
+        PlaneTerms(me, sends, down, False, high, scratch[3]),
     ]
 
 
 def middle_body(
     shape, sent, own, middle, grads, gain, feed_sent, feed_own, parts, targets,
-    rows_to, d_middle, gain_grad, block_out, sum_scratch, feed_scratch, low,
-    send_sems, local_sems, rows_sems, unit_sems,
+    rows_to, d_middle, gain_grad, block_out, sum_scratch, feed_scratch, unit_scratch, low,
+    send_sems, local_sems, rows_sems,
 ):
     me = Place(shape)
     rows = middle.shape[0]
@@ -784,7 +826,8 @@
     load.start()
     me.greet()
     total.begin()
-    units = plane_units(me, sends, parts, targets, unit_sems)
+    units = plane_units(me, sends, parts, unit_scratch)
+    units_to, units_y, units_x = targets
     for unit in units:
         unit.begin()
     feed_load.start()
@@ -812,7 +855,22 @@
     gather.begin()
     feed.begin()
     feed_load.wait()
-    feed.run()
+    half, extra = Z // 2, slice(Z, Z + Z // 2)
+
+    def between(t):
+        if t == 1:
+            units[0].add()
+            units[0].hand_on(units_to.at[0], lambda i: units_y.at[i, 0:Z])
+        if t == 2:
+            units[1].add()
+            units[1].hand_on(units_to.at[1], lambda j: units_x.at[j, 0:Z])
+        if t == 3:
+            units[2].add()
+            units[2].hand_on(units_to.at[2, 0:half], lambda i: units_y.at[i, extra])
+            units[3].add()
+            units[3].hand_on(units_to.at[2, half:Z], lambda j: units_x.at[j, extra])
+
+    feed.run(between)
     each_rows(rows, 16, lambda r: block_out.__setitem__(
         r, (middle[r] + feed.held[0, r]).astype(BF16)))
     gather.step()
@@ -827,21 +885,25 @@
     inner, outer = sizes()
     rows, width = middle.shape
     unit_rows, share = parts[0].shape[2:]
-    over_x, over_y = (inner - 1, outer), (outer - 1,)
+    block = (unit_rows, share)
     targets = [
-        jax.ShapeDtypeStruct(shape, BF16)
-        for shape in (
-            (*over_x, Z, unit_rows, share),
-            (*over_y, Z, inner, unit_rows, share),
-            (*over_x, Z // 2, unit_rows, share),
-            (*over_y, Z // 2, inner, unit_rows, share),
-        )
+        jax.ShapeDtypeStruct((*shape, *block), BF16)
+        for shape in ((3, Z), (outer - 1, Z + Z // 2), (inner - 1, Z + Z // 2))
     ]
     unit_copies = 2 * (inner - 1) * outer + 2 * (outer - 1)
     pair_scratch = [pltpu.VMEM((Z, rows, width), F32), pltpu.VMEM((Z, rows, width), BF16)]
     pair_scratch += [pltpu.VMEM((Z - 1, rows, width), BF16)] * 4
     dma = pltpu.SemaphoreType.DMA
     pair_scratch += [dma((Z,)), dma((Z - 1,)), dma((Z - 1,))]
+    unit_scratch = []
+    for came, mine in (
+        ((inner - 1, outer, Z), (outer, Z)),
+        ((outer - 1, Z, inner), (Z, inner)),
+        ((inner - 1, outer, Z // 2), (outer, Z // 2)),
+        ((outer - 1, Z // 2, inner), (Z // 2, inner)),
+    ):
+        unit_scratch += [pltpu.VMEM((*came, *block), BF16), pltpu.VMEM((*mine, *block), BF16)]
+        unit_scratch += [dma((inner - 1, outer)), dma((max(inner, outer),))]
     vmem, anywhere = pl.BlockSpec(memory_space=pltpu.VMEM), pl.BlockSpec(memory_space=pl.ANY)
     return pl.pallas_call(
         functools.partial(middle_kernel, (inner, outer)),
@@ -853,17 +915,17 @@
             *targets,
         ),
         in_specs=[anywhere, anywhere, vmem, vmem, vmem] + [anywhere] * (2 + 3 * outer),
-        out_specs=(anywhere, vmem, vmem, vmem) + (anywhere,) * 4,
+        out_specs=(anywhere, vmem, vmem, vmem) + (anywhere,) * 3,
         scratch_shapes=pair_scratch * 2
+        + unit_scratch
         + [
             pltpu.VMEM((rows, width), BF16),
             dma((2 * (Z + 2 * (Z - 1)) + 2 * outer + unit_copies,)),
             dma((3,)),
             dma((outer * C,)),
-            dma((4, inner - 1, outer)),
         ],
         compiler_params=pltpu.CompilerParams(
-            collective_id=2, has_side_effects=True, vmem_limit_bytes=56 * 1024 * 1024
+            collective_id=2, has_side_effects=True, vmem_limit_bytes=60 * 1024 * 1024
         ),
         name="middle_and_rows",
     )(sent, own, middle, grads, gain, feed_sent, feed_own, *parts)
@@ -1550,7 +1612,7 @@
     def feed_of(part):
         return contract_last(hidden[part], down_kernel).reshape(Z, rows_dev, width)
 
-    branch_rows, d_middle, gain_two_grad, block_out, *came = middle_and_rows(
+    branch_rows, d_middle, gain_two_grad, block_out, units, units_y, units_x = middle_and_rows(
         d_normed_of(slice(half_rows, None)).astype(BF16),
         d_normed_of(slice(0, half_rows)),
         middle,
@@ -1561,31 +1623,6 @@
         gate_terms + up_terms + down_terms,
     )
     branch_rows = branch_rows.reshape(-1, width)
-
-    def added_over_x(terms, moved):
-        return [
-            sum((moved[j - 1, i].astype(F32) for j in range(1, inner)), pick(term, x, 1).astype(F32))
-            for i, term in enumerate(terms)
-        ]
-
-    def added_over_y(term, moved):
-        return sum((moved[i - 1].astype(F32) for i in range(1, outer)), term.astype(F32))
-
-    half_z = Z // 2
-    gate_x = added_over_x(gate_terms, came[0])
-    up_y = added_over_y(up_terms[0], came[1])
-    down_x = added_over_x([term[:half_z] for term in down_terms], came[2])
-    down_y = added_over_y(down_terms[0][half_z:], came[3])
-    all_y = jnp.concatenate([up_y, down_y])
-    kept_x = pick(all_y, x, 1)
-    units = jnp.concatenate([gate_x[0], kept_x[:Z], down_x[0], kept_x[Z:]]).astype(BF16)
-    units = units.reshape(3, Z, weight_rows, -1)
-    units_y = jnp.stack(
-        [jnp.concatenate([gate_x[i], down_x[i]]).astype(BF16) for i in range(1, outer)]
-    )
-    units_x = jnp.stack(
-        [pick(all_y, (x + j) % inner, 1).astype(BF16) for j in range(1, inner)]
-    )
 
     d_mixed = multiply(branch_rows, out_kernel)
     d_lru = (d_mixed * y_gated).astype(BF16).astype(F32)

time: 858 us -> 839 us (0.978)
  other arithmetic: 48.9 us -> 36.6 us
  local copies, waits for them, and re-layouts: 34.6 us -> 25.7 us
  transfers between devices with their start and end apart: 6 -> 6, of which waited for: 2 -> 2; matrix products, arithmetic and copies ran while one was open for 3% -> 2% of each run, Pallas kernels for 0% -> 0%
where the time goes in v7:
time: 839 us; the launch traced here: 831 us
  Pallas kernels  621 us (74%)
  matrix products  116 us (14%)
  other arithmetic  36.6 us (4%)
  local copies, waits for them, and re-layouts  25.7 us (3%)
  starting transfers between devices  19.4 us (2%)
  waiting for transfers between devices  9.74 us (1%)
    pallas_call x1, Pallas kernels, gather_all(): pl.pallas_call(functools.partial(gather_kernel, (inner, outer)), out_shap...  214 us
    pallas_call x1, Pallas kernels, last_sums(): pl.pallas_call(functools.partial(sums_kernel, (inner, outer)), out_shape=...  197 us
    pallas_call x1, Pallas kernels, middle_and_rows(): pl.pallas_call(functools.partial(middle_kernel, (inner, outer)), out_shap...  114 us
    pallas_call x1, Pallas kernels, branch_and_group(): pl.pallas_call(functools.partial(branch_kernel, (inner, outer)), out_shap...  78.8 us
    dot_general x15, matrix products, contract_last(): lax.dot_general(left_side, right_side, (((1,), (1,)), ((), ())), preferre...  49.3 us
    dot_general x8, matrix products, multiply(): return jnp.dot(left_side, right_side, preferred_element_type=F32)  40.7 us
    dot_general x9, matrix products, contract_rows(): lax.dot_general(left_side, right_side, (((0,), (0,)), ((), ())), preferre...  26.3 us
    pallas_call x2, Pallas kernels, full_scan(): pl.pallas_call(functools.partial(scan_kernel, backward), out_shape=(jax.S...  17.8 us
  transfers between devices with their start and end apart: 6, of which 2 were waited for; matrix products, arithmetic and copies ran while one was open for 2% of the time, Pallas kernels for 0%

profile of v7, /device:TPU:2, one launch (start us, length us, event | category | flops | bytes accessed | tf_op | source)
XLA Modules:
  0.0 830.7 jit_solution(6916658883808621543)
XLA Ops:
  10.2 213.6 %gather_all.1 = (bf16[4,128,2560]{2,1,0:T(8,128)(2,1)}, bf16[2,4,128,2560]{3,2,1,0:T(8,128)(2,1)}, f32[32,16,128]{2,1,0:T(8,128)}, bf16[4,2,80,512]{3,2,1,0:T(8,...) custom-call(bf16[128,2560]{1,0:T(8,128)(2,1)} %refs_11_.1, ...), custom_call_target="tpu_custom_call" | custom-call | tf_op jit(solution)/shard_map/gather_all/pallas_call | solution.py:401
  231.2 5.0 fusion.124
  236.8 14.8 %collective-permute-start = (bf16[3,640]{1,0:T(4,128)(2,1)}, bf16[3,640]{1,0:T(4,128)(2,1)}, u32[]{:S(2)}, u32[]{:S(2)}) collective-permute-start(bf16[3,640]{1,0:T(4,128)(2,1)} %slice.472), channel_id=1, source_target_pairs={{0,4},{4,8},{8,12},{12,16},{16,20},{20,24},{24,28},{1,5},{5,9},{9,... | collective-permute-start | bytes 11528 | tf_op jit(solution)/shard_map/ppermute | solution.py:1539
  264.9 8.9 %scan_ahead.1 = (f32[512,640]{1,0:T(8,128)S(1)}, f32[1,640]{1,0:T(1,128)S(1)}) custom-call(f32[512,640]{1,0:T(8,128)S(1)} %get-tuple-element.153.factors, f32[512,640]{1,0:T(8,128)S(1)} %get-tuple-element.152.inflows), custom_call_target="tpu_custom_call" | custom-call | tf_op jit(solution)/shard_map/scan_ahead/pallas_call | solution.py:1410
  278.4 78.8 %branch_and_group.1 = (bf16[2,4,128,2560]{3,2,1,0:T(8,128)(2,1)S(1)}, f32[128,2560]{1,0:T(8,128)S(1)}, bf16[4,2,320,1024]{3,2,1,0:T(8,128)(2,1)}, bf16[4,2,320,1024]{3,2,1,0:T(8,128)(2,1)}) custom-call(f32[2,128,2560]{2,1,0:T(8,128)S(1)} %fusion.69.sent, f32[2,128,2560]{2,1,0:T(8,128)S(1)} %fusion.67.own, ...), custom_call_target="tpu_custom_call", output_to_operand_aliasing={{2}: (4, {}), {3}: (5, {})} | custom-call | tf_op jit(solution)/shard_map/branch_and_group/pallas_call | solution.py:602
  357.3 9.4 %fusion.126 = f32[1024,1024]{1,0:T(8,128)} fusion(bf16[1024,2560]{1,0:T(8,128)(2,1)S(1)} %bitcast.130, bf16[2560,1024]{1,0:T(8,128)(2,1)} %bitcast.190), kind=kOutput, calls=%fused_computation.239 | convolution fusion | flops 5368709120 | bytes 14680064 | tf_op jit(solution)/shard_map/dot_general | solution.py:73
  366.7 7.1 fusion.125
  373.9 10.9 %multiply_convert_fusion.1 = (bf16[1024,1024]{1,0:T(8,128)(2,1)S(1)}, bf16[1024,1024]{1,0:T(8,128)(2,1)S(1)}, bf16[1024,1024]{1,0:T(8,128)(2,1)S(1)}) fusion(f32[1024,1024]{1,0:T(8,128)} %fusion.126, f32[1024,1024]{1,0:T(8,128)} %fusion.125, bf16[1024,2560]{1,0:T(8,128)(2,1)S(1)} %bitcast.131, bf16[2560,1024]{1,0:T(8,128)(2,1)S(1)} %bitcast.155), kind=kOutput, calls=%fused_computation.23 | convolution fusion | flops 5395972096 | bytes 25165824 | tf_op jit(solution)/shard_map/dot_general | solution.py:73
  384.8 7.1 fusion.57
  391.8 7.5 fusion.54
  399.3 4.2 convolution_convert_fusion.5
  403.6 4.2 convolution_convert_fusion.4
  407.8 4.2 convolution_convert_fusion.3
  412.0 4.2 convolution_convert_fusion.2
  416.4 4.3 convolution_convert_fusion.1
  420.7 4.2 convolution_convert_fusion
  425.0 6.1 add_convert_fusion
  431.1 4.7 convolution_add_fusion
  435.8 4.5 convolution_convert_fusion.6.refs_5_
  440.3 4.6 fusion.127.refs_6_
  444.9 113.7 %middle_and_rows.1 = (bf16[4,128,2560]{2,1,0:T(8,128)(2,1)}, f32[128,2560]{1,0:T(8,128)}, f32[16,2560]{1,0:T(8,128)}, bf16[128,2560]{1,0:T(8,128)(2,1)}, bf16[3,...) custom-call(bf16[4,128,2560]{2,1,0:T(8,128)(2,1)} %bitcast.167, ...), custom_call_target="tpu_custom_call" | custom-call | tf_op jit(solution)/shard_map/middle_and_rows/pallas_call | solution.py:908
  558.6 6.5 convert_multiply_fusion
  565.1 8.9 %scan_back.1 = (f32[512,640]{1,0:T(8,128)S(1)}, f32[1,640]{1,0:T(1,128)S(1)}) custom-call(f32[512,640]{1,0:T(8,128)S(1)} %get-tuple-element.153.factors, f32[512,640]{1,0:T(8,128)S(1)} %get-tuple-element.135.inflows), custom_call_target="tpu_custom_call" | custom-call | tf_op jit(solution)/shard_map/scan_back/pallas_call | solution.py:1410
  575.6 3.5 multiply_reduce_fusion.5
  579.0 2.9 fusion.111
  597.6 3.3 fusion.14
  600.9 3.1 fusion.12
  606.4 2.8 convolution_add_fusion.1
  610.1 196.8 %last_sums.1 = (bf16[3,320,2048]{2,1,0:T(8,128)(2,1)}, f32[320,1920]{1,0:T(8,128)}, f32[80,512]{1,0:T(8,128)}, bf16[128,2560]{1,0:T(8,128)(2,1)}, f32[5,16,2560]{2,1,0:T(8,128)}, /*index=5*/f32[2,8,640]{2,1,0:T(8,128)}) custom-call(bf16[3,4,320,512]{3,2,1,0:T(8,128)(2,1)} %get-tuple-element.62.refs_0_, bf16[1,6,320,512]{3,2,1,0:T(8,128)(2,1)} %get-tuple-element.63.refs_1_, ...), custom_call_target="tpu_custom_call" | custom-call | tf_op jit(solution)/shard_map/last_sums/pallas_call | solution.py:1266
  807.9 3.2 fusion.114
  813.2 5.3 bitcast_convert_fusion
  819.1 7.5 collective-permute-done.5
  (247 shorter events, 62.7 us)
Async XLA Ops:
  5.0 2.7 copy-start.23
  226.1 5.1 copy-start.5
  231.2 20.4 %copy-start.19 = (bf16[4,2,80,512]{3,2,1,0:T(8,128)(2,1)S(1)}, bf16[4,2,80,512]{3,2,1,0:T(8,128)(2,1)}, u32[]{:S(2)}) copy-start(bf16[4,2,80,512]{3,2,1,0:T(8,128)(2,1)} %get-tuple-element.51) | copy-start | bytes 1966084
  236.2 15.7 %copy-start.31 = (bf16[512,1280]{1,0:T(8,128)(2,1)}, bf16[512,1280]{1,0:T(8,128)(2,1)S(1)}, u32[]{:S(2)}) copy-start(bf16[512,1280]{1,0:T(8,128)(2,1)S(1)} %get-tuple-element.187) | copy-start | bytes 3932164
  236.8 20.5 %collective-permute-start = (bf16[3,640]{1,0:T(4,128)(2,1)}, bf16[3,640]{1,0:T(4,128)(2,1)}, u32[]{:S(2)}, u32[]{:S(2)}) collective-permute-start(bf16[3,640]{1,0:T(4,128)(2,1)} %slice.472), channel_id=1, source_target_pairs={{0,4},{4,8},{8,12},{12,16},{16,20},{20,24},{24,28},{1,5},{5,9},{9,... | collective-permute-start | bytes 11528 | tf_op jit(solution)/shard_map/ppermute | solution.py:1539
  251.9 7.0 copy-start.20
  252.6 8.1 collective-permute-start.2
  256.7 21.7 %copy-start.2 = (f32[1,2560]{1,0:T(1,128)}, f32[1,2560]{1,0:T(1,128)S(1)}, u32[]{:S(2)}) copy-start(f32[1,2560]{1,0:T(1,128)S(1)} %slice.411.gain.refs_4_) | copy-start | bytes 30724
  258.2 4.4 copy-start.3
  260.4 1.9 collective-permute-start.1
  264.9 8.9 %copy-start.28 = (f32[512,1280]{1,0:T(8,128)S(1)}, f32[512,1280]{1,0:T(8,128)}, u32[]{:S(2)}) copy-start(f32[512,1280]{1,0:T(8,128)} %get-tuple-element.188) | copy-start | bytes 7864324
  274.3 2.9 copy-start.12
  278.4 88.3 %slice-start.10 = ((s8[5242880]{0:T(1024)(128)(4,1)}), s8[4194304]{0:T(1024)(128)(4,1)S(1)}, s32[]{:S(2)}) async-start(s8[5242880]{0:T(1024)(128)(4,1)} %bitcast.183), calls=%async_computation.10 | async-start | bytes 8388608
  357.3 9.5 %copy-start.1 = (f32[128,2560]{1,0:T(8,128)}, f32[128,2560]{1,0:T(8,128)S(1)}, u32[]{:S(2)}) copy-start(f32[128,2560]{1,0:T(8,128)S(1)} %get-tuple-element.60.refs_2_) | copy-start | bytes 3932164
  357.3 9.4 %copy-start.16 = (bf16[4,2,320,1024]{3,2,1,0:T(8,128)(2,1)S(1)}, bf16[4,2,320,1024]{3,2,1,0:T(8,128)(2,1)}, u32[]{:S(2)}) copy-start(bf16[4,2,320,1024]{3,2,1,0:T(8,128)(2,1)} %get-tuple-element.56) | copy-start | bytes 15728644
  357.3 9.4 %slice-start.11 = ((s8[5242880]{0:T(1024)(128)(4,1)}), s8[1048576]{0:T(1024)(128)(4,1)S(1)}, s32[]{:S(2)}) async-start(s8[5242880]{0:T(1024)(128)(4,1)} %bitcast.183), calls=%async_computation.11 | async-start | bytes 2097152
  357.3 16.6 %slice-start.2 = ((s8[5242880]{0:T(1024)(128)(4,1)}), s8[1048576]{0:T(1024)(128)(4,1)S(1)}, s32[]{:S(2)}) async-start(s8[5242880]{0:T(1024)(128)(4,1)} %bitcast.153), calls=%async_computation.2 | async-start | bytes 2097152
  366.7 7.2 slice-start.3
  407.8 8.6 %slice-start.12 = ((s8[5242880]{0:T(1024)(128)(4,1)}), s8[4194304]{0:T(1024)(128)(4,1)S(1)}, s32[]{:S(2)}) async-start(s8[5242880]{0:T(1024)(128)(4,1)} %bitcast.186), calls=%async_computation.12 | async-start | bytes 8388608
  412.0 4.4 slice-start.13
  420.7 10.4 %slice-start.14 = ((s8[5242880]{0:T(1024)(128)(4,1)}), s8[1048576]{0:T(1024)(128)(4,1)S(1)}, s32[]{:S(2)}) async-start(s8[5242880]{0:T(1024)(128)(4,1)} %bitcast.193), calls=%async_computation.14 | async-start | bytes 2097152
  424.9 6.1 slice-start.15
  565.1 9.0 %copy-start.15 = (f32[512,128]{1,0:T(8,128)S(1)}, f32[512,128]{1,0:T(8,128)}, u32[]{:S(2)}) copy-start(f32[512,128]{1,0:T(8,128)} %copy-done.14) | copy-start | bytes 786436
  584.5 2.3 collective-permute-start.3
  590.4 6.5 collective-permute-start.4
  593.6 10.4 %slice-start = ((s8[6553600]{0:T(1024)(128)(4,1)}), s8[4194304]{0:T(1024)(128)(4,1)S(1)}, s32[]{:S(2)}) async-start(s8[6553600]{0:T(1024)(128)(4,1)} %bitcast.139), calls=%async_computation | async-start | bytes 8388608
  597.6 6.5 slice-start.1
  807.9 3.2 copy-start.38
  807.9 3.4 copy-start.33
  811.3 15.4 %collective-permute-start.5 = (f32[80,520]{1,0:T(8,128)S(1)}, f32[80,520]{1,0:T(8,128)S(1)}, u32[]{:S(2)}, u32[]{:S(2)}) collective-permute-start(f32[80,520]{1,0:T(8,128)S(1)} %pad_maximum_fusion.14), channel_id=1, source_target_pairs={{0,0},{4,1},{8,2},{12,3},{16,4},{20,5},{24,6},{28,7},{1,8},{5,9},{... | collective-permute-start | bytes 499208 | tf_op jit(solution)/shard_map/ppermute | solution.py:1693
  813.2 15.6 %copy-start.29 = (bf16[128,2560]{1,0:T(8,128)(2,1)S(1)}, bf16[128,2560]{1,0:T(8,128)(2,1)}, u32[]{:S(2)}) copy-start(bf16[128,2560]{1,0:T(8,128)(2,1)} %get-tuple-element.215) | copy-start | bytes 1966084
  818.5 11.1 %copy-start.30 = (bf16[128,2560]{1,0:T(8,128)(2,1)S(1)}, bf16[128,2560]{1,0:T(8,128)(2,1)}, u32[]{:S(2)}) copy-start(bf16[128,2560]{1,0:T(8,128)(2,1)} %get-tuple-element.216) | copy-start | bytes 1966084
  (36 other events, 58.7 us)

commit v8 on v7

--- a/solution.py
+++ b/solution.py
@@ -436,6 +436,23 @@
 
     def at_y(self, by):
         return {"seq": self.s, "wt": (self.y + self.outer + by) % self.outer * C + self.c}
+
+    def greet_all(self):
+        barrier = pltpu.get_barrier_semaphore()
+        wt = self.outer * C
+        count = Z * self.inner * wt
+
+        def signal(i, carried):
+            @pl.when(i != self.s * wt + self.w)
+            def _():
+                pl.semaphore_signal(
+                    barrier, inc=1, device_id={"seq": i // wt, "wt": i % wt}, device_id_type=MESH
+                )
+
+            return carried
+
+        lax.fori_loop(0, count, signal, 0)
+        pl.semaphore_wait(barrier, count - 1)
 
     def greet(self):
         barrier = pltpu.get_barrier_semaphore()
@@ -749,6 +766,29 @@
             ]
         self.loads = self.moved(pairs)
 
+    def second(self, into, sems):
+        me = self.me
+        for j in range(1, me.inner):
+            self.sends.start(
+                True, self.mine.at[:, (me.x + j) % me.inner], into.at[j - 1], sems.at[j - 1],
+                me.at_x(j),
+            )
+
+    def add_second(self, into, sems, kept):
+        me = self.me
+        for j in range(1, me.inner):
+            arrived(into.at[j - 1], sems.at[j - 1], me.at_c)
+
+        def body(r):
+            for first in range(self.mine.shape[0]):
+                total = self.mine[first, me.x, r].astype(F32)
+                for j in range(1, me.inner):
+                    total = total + into[j - 1, first, r].astype(F32)
+                self.mine[first, me.x, r] = total.astype(BF16)
+
+        each_rows(self.mine.shape[2], 16, body)
+        self.loads = self.moved([(self.mine.at[:, me.x], kept)])
+
     def finish(self):
         for copy in self.loads:
             copy.wait()
@@ -814,7 +854,7 @@
 def middle_body(
     shape, sent, own, middle, grads, gain, feed_sent, feed_own, parts, targets,
     rows_to, d_middle, gain_grad, block_out, sum_scratch, feed_scratch, unit_scratch, low,
-    send_sems, local_sems, rows_sems,
+    up_in, send_sems, local_sems, rows_sems, up_sems,
 ):
     me = Place(shape)
     rows = middle.shape[0]
@@ -863,18 +903,19 @@
             units[0].hand_on(units_to.at[0], lambda i: units_y.at[i, 0:Z])
         if t == 2:
             units[1].add()
-            units[1].hand_on(units_to.at[1], lambda j: units_x.at[j, 0:Z])
+            units[1].second(up_in, up_sems)
         if t == 3:
             units[2].add()
             units[2].hand_on(units_to.at[2, 0:half], lambda i: units_y.at[i, extra])
             units[3].add()
-            units[3].hand_on(units_to.at[2, half:Z], lambda j: units_x.at[j, extra])
+            units[3].hand_on(units_to.at[2, half:Z], lambda j: units_x.at[j])
 
     feed.run(between)
     each_rows(rows, 16, lambda r: block_out.__setitem__(
         r, (middle[r] + feed.held[0, r]).astype(BF16)))
     gather.step()
     gather.finish()
+    units[1].add_second(up_in, up_sems, units_to.at[1])
     for unit in units:
         unit.finish()
     sends.finish()
@@ -888,9 +929,9 @@
     block = (unit_rows, share)
     targets = [
         jax.ShapeDtypeStruct((*shape, *block), BF16)
-        for shape in ((3, Z), (outer - 1, Z + Z // 2), (inner - 1, Z + Z // 2))
+        for shape in ((3, Z), (outer - 1, Z + Z // 2), (inner - 1, Z // 2))
     ]
-    unit_copies = 2 * (inner - 1) * outer + 2 * (outer - 1)
+    unit_copies = 2 * (inner - 1) * outer + 2 * (outer - 1) + (inner - 1)
     pair_scratch = [pltpu.VMEM((Z, rows, width), F32), pltpu.VMEM((Z, rows, width), BF16)]
     pair_scratch += [pltpu.VMEM((Z - 1, rows, width), BF16)] * 4
     dma = pltpu.SemaphoreType.DMA
@@ -920,9 +961,11 @@
         + unit_scratch
         + [
             pltpu.VMEM((rows, width), BF16),
+            pltpu.VMEM((inner - 1, Z, *block), BF16),
             dma((2 * (Z + 2 * (Z - 1)) + 2 * outer + unit_copies,)),
             dma((3,)),
             dma((outer * C,)),
+            dma((inner - 1,)),
         ],
         compiler_params=pltpu.CompilerParams(
             collective_id=2, has_side_effects=True, vmem_limit_bytes=60 * 1024 * 1024
@@ -1066,7 +1109,8 @@
     units_to, wide_to, narrow_to, tokens_grad, gains, vectors_to = refs[16:22]
     refs = refs[22:]
     wide_scratch, narrow_scratch = refs[:7], refs[7:13]
-    (own_v, c_in, y_out, y_in, all_in, vec_in) = refs[13:19]
+    (own_v, c_in, y_out, y_in, parts_out, parts_in, gains_v, vec_in) = refs[13:21]
+    refs = refs[2:]
     (send_sems, local_sems, c_sems, y_sems, all_sems, vec_sems) = refs[19:25]
     wide_sems, narrow_sems = refs[25:29], refs[29:33]
     units_v, units_y_in, units_x_in, unit_sems, units_y_sems, units_x_sems = refs[33:]
@@ -1078,7 +1122,7 @@
     load.start()
     units_load = pltpu.make_async_copy(units, units_v, local_sems.at[1])
     units_load.start()
-    me.greet()
+    me.greet_all()
 
     order = [(me.y + i) % outer for i in list(range(1, outer)) + [0]]
     for at in order:
@@ -1105,12 +1149,10 @@
                 )
 
     def units_begin_x():
-        for n, blocks in enumerate((every, extra)):
-            for j in range(1, inner):
-                sends.start(
-                    True, units_x.at[j - 1, blocks], units_x_in.at[j - 1, blocks],
-                    units_x_sems.at[j - 1, n], me.at_x(j),
-                )
+        for j in range(1, inner):
+            sends.start(
+                True, units_x.at[j - 1], units_x_in.at[j - 1], units_x_sems.at[j - 1], me.at_x(j)
+            )
 
     kept = []
 
@@ -1143,12 +1185,9 @@
 
     def unit_down():
         unit_add(2, low, units_y_in, extra, units_y_sems.at[:, 1], outer - 1)
-        unit_add(2, high, units_x_in, extra, units_x_sems.at[:, 1], inner - 1)
+        unit_add(2, high, units_x_in, low, units_x_sems, inner - 1)
         unit_pass_on(2)
 
-    def unit_up():
-        unit_add(1, every, units_x_in, every, units_x_sems.at[:, 0], inner - 1)
-        unit_pass_on(1)
 
     def units_finish():
         for n in range(3):
@@ -1170,21 +1209,51 @@
             total = total + into[first + n]
         return held[...] + total
 
-    stages = [
-        [me.at_c],
-        [me.at_y(i) for i in range(1, outer)],
-        [me.at_z((me.z + k) % Z) for k in range(1, Z)],
-        [me.at_x(j) for j in range(1, inner)],
-    ]
-    at_stage = [0]
-    for stage in stages:
-        at_stage.append(at_stage[-1] + len(stage))
-
-    z_stage, x_stage = stages[2], stages[3]
+    z_stage = [me.at_z((me.z + k) % Z) for k in range(1, Z)]
+    x_stage = [me.at_x(j) for j in range(1, inner)]
+
+    devices = Z * inner * outer * C
+    wt = outer * C
+    here = me.s * wt + me.w
+    width = tokens.shape[1]
+    channels = width // devices
+
+    def gains_cut():
+        for i in range(devices):
+            first = i * channels // LANES * LANES
+            first = min(first, width - 2 * LANES)
+            window = gains_v[:, first : first + 2 * LANES]
+            turn = i * channels - first
+            if turn:
+                window = pltpu.roll(window, 2 * LANES - turn, 1)
+            parts_out[i] = window[:, :LANES]
+
+    def gains_copy(i):
+        return pltpu.make_async_remote_copy(
+            src_ref=parts_out.at[i], dst_ref=parts_in.at[here],
+            send_sem=all_sems.at[0, i], recv_sem=all_sems.at[1, here],
+            device_id={"seq": i // wt, "wt": i % wt}, device_id_type=MESH,
+        )
+
+    def gains_send(i, carried):
+        pl.when(i != here)(lambda: gains_copy(i).start())
+        return carried
+
+    def gains_add(i, carried):
+        @pl.when(i != here)
+        def _():
+            gains_copy(i).wait_send()
+            arrived(parts_in.at[i], all_sems.at[1, i], me.at_c)
+            gains[...] += parts_in[i]
+
+        return carried
+
     exchange(vectors, vec_in, vec_sems, 0, x_stage)
     units_begin_x()
 
     units_begin_y()
+    units_load.wait()
+    unit_pass_on(1)
 
     load.wait()
     for i, at in enumerate(order):
@@ -1197,11 +1266,9 @@
     exchange(vectors_to.at[0], vec_in, vec_sems, len(x_stage), z_stage)
     narrow_sum.run()
     vectors_to[1] = gathered(vectors_to.at[0], vec_in, vec_sems, len(x_stage), z_stage)
-    units_load.wait()
     wide_sum.begin(range(1))
     unit_gate()
     wide_sum.begin(range(1, 2))
-    unit_up()
     unit_down()
     wide_sum.begin(range(2, Z))
 
@@ -1213,31 +1280,24 @@
         inverse = lax.rsqrt(jnp.mean(stream * stream, axis=1, keepdims=True) + EPSILON)
         normed = stream * inverse
         part = d_normed * normed
-        gains[0, 0:8] += part[0:8] + part[8:16]
+        gains_v[0:8] += part[0:8] + part[8:16]
         scaled = d_normed * gain[...]
         passed = inverse * (scaled - normed * jnp.mean(scaled * normed, axis=1, keepdims=True))
         tokens_grad[r] = (d_middle[r] + passed).astype(BF16)
-
-    def gains_step(n):
-        if n > 0:
-            gains[n] = gathered(
-                gains.at[n - 1], all_in, all_sems, at_stage[n - 1], stages[n - 1]
-            )
-        if n < len(stages):
-            exchange(gains.at[n], all_in, all_sems, at_stage[n], stages[n])
 
     def between(t):
         if t == 1:
             for i in range(outer - 1):
                 arrived(y_in.at[i], y_sems.at[i], me.at_c)
-            gains[0] = jnp.zeros_like(gains[0])
+            gains_v[...] = jnp.zeros_like(gains_v)
             each_rows(rows, 16, work)
-            gains[0, 8:16] = gain_two_grad[0:8] + gain_two_grad[8:16]
-        gains_step(t - 1)
+            gains_v[8:16] = gain_two_grad[0:8] + gain_two_grad[8:16]
+            gains_cut()
+            lax.fori_loop(0, devices, gains_send, 0)
 
     wide_sum.run(between)
-    for n in range(Z - 1, len(stages) + 1):
-        gains_step(n)
+    gains[...] = parts_out[here]
+    lax.fori_loop(0, devices, gains_add, 0)
     units_finish()
     sends.finish()
 
@@ -1257,9 +1317,9 @@
             pltpu.VMEM((Z - 1, *one), BF16)
         ] * 4
 
-    peers = 1 + (outer - 1) + (inner - 1) + (Z - 1)
+    devices = Z * inner * outer * C
     copies = 2 * outer - 1 + 2 * (Z * (inner - 1) + 2 * (Z - 1))
-    copies += peers + (inner - 1) + (Z - 1) + 2 * (outer - 1) + 2 * (inner - 1) + 3 * (Z - 1)
+    copies += (inner - 1) + (Z - 1) + 2 * (outer - 1) + 2 * (inner - 1) + 3 * (Z - 1)
     _, _, unit_rows, share = units.shape
     block = (unit_rows, d_x.shape[1] + d_y.shape[1] + mixed.shape[1])
     line_sems = [dma((Z,)), dma((inner - 1, Z)), dma((Z - 1,)), dma((Z - 1,))]
@@ -1270,7 +1330,7 @@
             jax.ShapeDtypeStruct(block, F32),
             jax.ShapeDtypeStruct(narrow.shape[2:], F32),
             jax.ShapeDtypeStruct((rows, width), BF16),
-            jax.ShapeDtypeStruct((5, 16, width), F32),
+            jax.ShapeDtypeStruct((16, LANES), F32),
             jax.ShapeDtypeStruct((2, *vectors.shape), F32),
         ),
         in_specs=[anywhere] * 8 + [vmem] * 8,
@@ -1287,13 +1347,15 @@
             pltpu.VMEM((outer, rows, width), BF16),
             pltpu.VMEM((outer - 1, rows, width), BF16),
             pltpu.VMEM((outer - 1, rows, width), BF16),
-            pltpu.VMEM((peers, 16, width), F32),
+            pltpu.VMEM((devices, 16, LANES), F32),
+            pltpu.VMEM((devices, 16, LANES), F32),
+            pltpu.VMEM((16, width), F32),
             pltpu.VMEM((inner - 1 + Z - 1, *vectors.shape), F32),
             dma((copies,)),
             dma((5,)),
             dma((outer,)),
             dma((outer - 1,)),
-            dma((peers,)),
+            dma((2, devices)),
             dma((inner - 1 + Z - 1,)),
         ]
         + line_sems * 2
@@ -1303,7 +1365,7 @@
             pltpu.VMEM(units_x.shape, BF16),
             dma((3, Z)),
             dma((outer - 1, 2)),
-            dma((inner - 1, 2)),
+            dma((inner - 1,)),
         ],
         compiler_params=pltpu.CompilerParams(
             collective_id=5, has_side_effects=True, vmem_limit_bytes=60 * 1024 * 1024
@@ -1686,8 +1748,7 @@
     )
     weight_grads = [wide[:, n * lru_cols : (n + 1) * lru_cols] for n in range(3)]
     gate_grad, up_grad, down_grad = (placed[n, :, :hidden_cols].astype(F32) for n in range(3))
-    gains = gains[4].reshape(2, 8, width).sum(axis=1)
-    gains = lax.dynamic_slice(gains, (0, (lax.axis_index("seq") * wt + w) * chunk), (2, chunk))
+    gains = gains.reshape(2, 8, LANES).sum(axis=1)[:, :chunk]
     sums = lax.dynamic_slice(own_sums[1], (0, lax.axis_index("seq") * chunk), (taps_count + 4, chunk))
     own_sums = jnp.concatenate([narrow[:chunk], sums.T], axis=1)
     own_sums = lax.ppermute(own_sums, ("seq", "wt"), [(to, at) for at, to in across])

time: 839 us -> 824 us (0.982)
  Pallas kernels: 621 us -> 607 us
    pallas_call x1, Pallas kernels: 197 us -> 175 us  [last_sums(): pl.pallas_call(functools.partial(sums_kernel, (inner, outer)), out_shape=...]
    pallas_call x1, Pallas kernels: 114 us -> 123 us  [middle_and_rows(): pl.pallas_call(functools.partial(middle_kernel, (inner, outer)), out_shap...]
where the time goes in v8:
time: 824 us; the launch traced here: 816 us
  Pallas kernels  607 us (74%)
  matrix products  116 us (14%)
  other arithmetic  36.4 us (4%)
  local copies, waits for them, and re-layouts  25.6 us (3%)
  starting transfers between devices  20 us (2%)
  waiting for transfers between devices  8.3 us (1%)
    pallas_call x1, Pallas kernels, gather_all(): pl.pallas_call(functools.partial(gather_kernel, (inner, outer)), out_shap...  214 us
    pallas_call x1, Pallas kernels, last_sums(): pl.pallas_call(functools.partial(sums_kernel, (inner, outer)), out_shape=...  175 us
    pallas_call x1, Pallas kernels, middle_and_rows(): pl.pallas_call(functools.partial(middle_kernel, (inner, outer)), out_shap...  123 us
    pallas_call x1, Pallas kernels, branch_and_group(): pl.pallas_call(functools.partial(branch_kernel, (inner, outer)), out_shap...  78.8 us
    dot_general x15, matrix products, contract_last(): lax.dot_general(left_side, right_side, (((1,), (1,)), ((), ())), preferre...  49.3 us
    dot_general x8, matrix products, multiply(): return jnp.dot(left_side, right_side, preferred_element_type=F32)  40.7 us
    dot_general x9, matrix products, contract_rows(): lax.dot_general(left_side, right_side, (((0,), (0,)), ((), ())), preferre...  26.3 us
    pallas_call x2, Pallas kernels, full_scan(): pl.pallas_call(functools.partial(scan_kernel, backward), out_shape=(jax.S...  16.6 us
  transfers between devices with their start and end apart: 6, of which 2 were waited for; matrix products, arithmetic and copies ran while one was open for 2% of the time, Pallas kernels for 0%

profile of v8, /device:TPU:2, one launch (start us, length us, event | category | flops | bytes accessed | tf_op | source)
XLA Modules:
  0.0 815.9 jit_solution(7872226154212396767)
XLA Ops:
  10.2 213.6 %gather_all.1 = (bf16[4,128,2560]{2,1,0:T(8,128)(2,1)}, bf16[2,4,128,2560]{3,2,1,0:T(8,128)(2,1)}, f32[32,16,128]{2,1,0:T(8,128)}, bf16[4,2,80,512]{3,2,1,0:T(8,...) custom-call(bf16[128,2560]{1,0:T(8,128)(2,1)} %refs_11_.1, ...), custom_call_target="tpu_custom_call" | custom-call | tf_op jit(solution)/shard_map/gather_all/pallas_call | solution.py:401
  231.2 5.0 fusion.124
  236.8 14.8 %collective-permute-start = (bf16[3,640]{1,0:T(4,128)(2,1)}, bf16[3,640]{1,0:T(4,128)(2,1)}, u32[]{:S(2)}, u32[]{:S(2)}) collective-permute-start(bf16[3,640]{1,0:T(4,128)(2,1)} %slice.471), channel_id=1, source_target_pairs={{0,4},{4,8},{8,12},{12,16},{16,20},{20,24},{24,28},{1,5},{5,9},{9,... | collective-permute-start | bytes 11528 | tf_op jit(solution)/shard_map/ppermute | solution.py:1601
  264.9 8.9 %scan_ahead.1 = (f32[512,640]{1,0:T(8,128)S(1)}, f32[1,640]{1,0:T(1,128)S(1)}) custom-call(f32[512,640]{1,0:T(8,128)S(1)} %get-tuple-element.153.factors, f32[512,640]{1,0:T(8,128)S(1)} %get-tuple-element.152.inflows), custom_call_target="tpu_custom_call" | custom-call | tf_op jit(solution)/shard_map/scan_ahead/pallas_call | solution.py:1472
  278.4 78.8 %branch_and_group.1 = (bf16[2,4,128,2560]{3,2,1,0:T(8,128)(2,1)S(1)}, f32[128,2560]{1,0:T(8,128)S(1)}, bf16[4,2,320,1024]{3,2,1,0:T(8,128)(2,1)}, bf16[4,2,320,1024]{3,2,1,0:T(8,128)(2,1)}) custom-call(f32[2,128,2560]{2,1,0:T(8,128)S(1)} %fusion.69.sent, f32[2,128,2560]{2,1,0:T(8,128)S(1)} %fusion.67.own, ...), custom_call_target="tpu_custom_call", output_to_operand_aliasing={{2}: (4, {}), {3}: (5, {})} | custom-call | tf_op jit(solution)/shard_map/branch_and_group/pallas_call | solution.py:619
  357.3 9.4 %fusion.126 = f32[1024,1024]{1,0:T(8,128)} fusion(bf16[1024,2560]{1,0:T(8,128)(2,1)S(1)} %bitcast.130, bf16[2560,1024]{1,0:T(8,128)(2,1)} %bitcast.190), kind=kOutput, calls=%fused_computation.238 | convolution fusion | flops 5368709120 | bytes 14680064 | tf_op jit(solution)/shard_map/dot_general | solution.py:73
  366.7 7.1 fusion.125
  373.9 10.9 %multiply_convert_fusion.1 = (bf16[1024,1024]{1,0:T(8,128)(2,1)S(1)}, bf16[1024,1024]{1,0:T(8,128)(2,1)S(1)}, bf16[1024,1024]{1,0:T(8,128)(2,1)S(1)}) fusion(f32[1024,1024]{1,0:T(8,128)} %fusion.126, f32[1024,1024]{1,0:T(8,128)} %fusion.125, bf16[1024,2560]{1,0:T(8,128)(2,1)S(1)} %bitcast.131, bf16[2560,1024]{1,0:T(8,128)(2,1)S(1)} %bitcast.155), kind=kOutput, calls=%fused_computation.23 | convolution fusion | flops 5395972096 | bytes 25165824 | tf_op jit(solution)/shard_map/dot_general | solution.py:73
  384.8 7.1 fusion.57
  391.9 7.5 fusion.54
  399.4 4.3 convolution_convert_fusion.5
  403.7 4.2 convolution_convert_fusion.4
  407.9 4.2 convolution_convert_fusion.3
  412.1 4.2 convolution_convert_fusion.2
  416.6 4.3 convolution_convert_fusion.1
  420.9 4.2 convolution_convert_fusion
  425.1 6.1 add_convert_fusion
  431.2 4.6 convolution_add_fusion
  435.9 4.4 convolution_convert_fusion.6.refs_5_
  440.3 4.7 fusion.127.refs_6_
  444.9 122.9 %middle_and_rows.1 = (bf16[4,128,2560]{2,1,0:T(8,128)(2,1)}, f32[128,2560]{1,0:T(8,128)}, f32[16,2560]{1,0:T(8,128)}, bf16[128,2560]{1,0:T(8,128)(2,1)}, bf16[3,...) custom-call(bf16[4,128,2560]{2,1,0:T(8,128)(2,1)} %bitcast.167, ...), custom_call_target="tpu_custom_call" | custom-call | tf_op jit(solution)/shard_map/middle_and_rows/pallas_call | solution.py:949
  567.8 6.5 convert_multiply_fusion
  574.4 7.7 scan_back.1
  583.7 3.5 multiply_reduce_fusion.5
  587.2 2.9 fusion.111
  598.5 3.2 collective-permute-start.4
  605.7 3.3 fusion.14
  609.0 3.1 fusion.12
  618.2 175.1 %last_sums.1 = (bf16[3,320,2048]{2,1,0:T(8,128)(2,1)}, f32[320,1920]{1,0:T(8,128)}, f32[80,512]{1,0:T(8,128)}, bf16[128,2560]{1,0:T(8,128)(2,1)}, f32[16,128]{1,0:T(8,128)}, /*index=5*/f32[2,8,640]{2,1,0:T(8,128)}) custom-call(bf16[3,4,320,512]{3,2,1,0:T(8,128)(2,1)} %get-tuple-element.62.refs_0_, bf16[1,6,320,512]{3,2,1,0:T(8,128)(2,1)} %get-tuple-element.63.refs_1_, ...), custom_call_target="tpu_custom_call" | custom-call | tf_op jit(solution)/shard_map/last_sums/pallas_call | solution.py:1326
  794.0 3.2 fusion.114
  799.3 5.3 bitcast_convert_fusion
  805.2 6.7 collective-permute-done.5
  (246 shorter events, 61.9 us)
Async XLA Ops:
  5.0 2.7 copy-start.23
  226.1 5.1 copy-start.5
  231.2 20.4 %copy-start.19 = (bf16[4,2,80,512]{3,2,1,0:T(8,128)(2,1)S(1)}, bf16[4,2,80,512]{3,2,1,0:T(8,128)(2,1)}, u32[]{:S(2)}) copy-start(bf16[4,2,80,512]{3,2,1,0:T(8,128)(2,1)} %get-tuple-element.51) | copy-start | bytes 1966084
  236.2 15.7 %copy-start.31 = (bf16[512,1280]{1,0:T(8,128)(2,1)}, bf16[512,1280]{1,0:T(8,128)(2,1)S(1)}, u32[]{:S(2)}) copy-start(bf16[512,1280]{1,0:T(8,128)(2,1)S(1)} %get-tuple-element.187) | copy-start | bytes 3932164
  236.8 20.5 %collective-permute-start = (bf16[3,640]{1,0:T(4,128)(2,1)}, bf16[3,640]{1,0:T(4,128)(2,1)}, u32[]{:S(2)}, u32[]{:S(2)}) collective-permute-start(bf16[3,640]{1,0:T(4,128)(2,1)} %slice.471), channel_id=1, source_target_pairs={{0,4},{4,8},{8,12},{12,16},{16,20},{20,24},{24,28},{1,5},{5,9},{9,... | collective-permute-start | bytes 11528 | tf_op jit(solution)/shard_map/ppermute | solution.py:1601
  251.9 7.0 copy-start.20
  252.6 8.1 collective-permute-start.2
  256.7 21.7 %copy-start.2 = (f32[1,2560]{1,0:T(1,128)}, f32[1,2560]{1,0:T(1,128)S(1)}, u32[]{:S(2)}) copy-start(f32[1,2560]{1,0:T(1,128)S(1)} %slice.411.gain.refs_4_) | copy-start | bytes 30724
  258.2 4.4 copy-start.3
  260.4 1.9 collective-permute-start.1
  264.9 8.9 %copy-start.28 = (f32[512,1280]{1,0:T(8,128)S(1)}, f32[512,1280]{1,0:T(8,128)}, u32[]{:S(2)}) copy-start(f32[512,1280]{1,0:T(8,128)} %get-tuple-element.188) | copy-start | bytes 7864324
  274.3 2.9 copy-start.12
  278.4 88.3 %slice-start.10 = ((s8[5242880]{0:T(1024)(128)(4,1)}), s8[4194304]{0:T(1024)(128)(4,1)S(1)}, s32[]{:S(2)}) async-start(s8[5242880]{0:T(1024)(128)(4,1)} %bitcast.183), calls=%async_computation.10 | async-start | bytes 8388608
  357.3 9.5 %copy-start.1 = (f32[128,2560]{1,0:T(8,128)}, f32[128,2560]{1,0:T(8,128)S(1)}, u32[]{:S(2)}) copy-start(f32[128,2560]{1,0:T(8,128)S(1)} %get-tuple-element.60.refs_2_) | copy-start | bytes 3932164
  357.3 9.4 %copy-start.16 = (bf16[4,2,320,1024]{3,2,1,0:T(8,128)(2,1)S(1)}, bf16[4,2,320,1024]{3,2,1,0:T(8,128)(2,1)}, u32[]{:S(2)}) copy-start(bf16[4,2,320,1024]{3,2,1,0:T(8,128)(2,1)} %get-tuple-element.56) | copy-start | bytes 15728644
  357.3 9.4 %slice-start.11 = ((s8[5242880]{0:T(1024)(128)(4,1)}), s8[1048576]{0:T(1024)(128)(4,1)S(1)}, s32[]{:S(2)}) async-start(s8[5242880]{0:T(1024)(128)(4,1)} %bitcast.183), calls=%async_computation.11 | async-start | bytes 2097152
  357.3 16.6 %slice-start.2 = ((s8[5242880]{0:T(1024)(128)(4,1)}), s8[1048576]{0:T(1024)(128)(4,1)S(1)}, s32[]{:S(2)}) async-start(s8[5242880]{0:T(1024)(128)(4,1)} %bitcast.153), calls=%async_computation.2 | async-start | bytes 2097152
  366.7 7.2 slice-start.3
  407.9 8.7 %slice-start.12 = ((s8[5242880]{0:T(1024)(128)(4,1)}), s8[4194304]{0:T(1024)(128)(4,1)S(1)}, s32[]{:S(2)}) async-start(s8[5242880]{0:T(1024)(128)(4,1)} %bitcast.186), calls=%async_computation.12 | async-start | bytes 8388608
  412.1 4.4 slice-start.13
  420.9 10.4 %slice-start.14 = ((s8[5242880]{0:T(1024)(128)(4,1)}), s8[1048576]{0:T(1024)(128)(4,1)S(1)}, s32[]{:S(2)}) async-start(s8[5242880]{0:T(1024)(128)(4,1)} %bitcast.193), calls=%async_computation.14 | async-start | bytes 2097152
  425.1 6.2 slice-start.15
  574.3 7.9 copy-start.15
  592.6 2.3 collective-permute-start.3
  598.5 6.5 collective-permute-start.4
  602.3 9.8 %slice-start = ((s8[6553600]{0:T(1024)(128)(4,1)}), s8[4194304]{0:T(1024)(128)(4,1)S(1)}, s32[]{:S(2)}) async-start(s8[6553600]{0:T(1024)(128)(4,1)} %bitcast.139), calls=%async_computation | async-start | bytes 8388608
  605.7 6.5 slice-start.1
  794.0 3.2 copy-start.38
  794.0 3.3 copy-start.33
  797.4 14.4 %collective-permute-start.5 = (f32[80,520]{1,0:T(8,128)S(1)}, f32[80,520]{1,0:T(8,128)S(1)}, u32[]{:S(2)}, u32[]{:S(2)}) collective-permute-start(f32[80,520]{1,0:T(8,128)S(1)} %pad_maximum_fusion.14), channel_id=1, source_target_pairs={{0,0},{4,1},{8,2},{12,3},{16,4},{20,5},{24,6},{28,7},{1,8},{5,9},{... | collective-permute-start | bytes 499208 | tf_op jit(solution)/shard_map/ppermute | solution.py:1754
  799.3 14.6 %copy-start.29 = (bf16[128,2560]{1,0:T(8,128)(2,1)S(1)}, bf16[128,2560]{1,0:T(8,128)(2,1)}, u32[]{:S(2)}) copy-start(bf16[128,2560]{1,0:T(8,128)(2,1)} %get-tuple-element.215) | copy-start | bytes 1966084
  804.6 10.2 %copy-start.30 = (bf16[128,2560]{1,0:T(8,128)(2,1)S(1)}, bf16[128,2560]{1,0:T(8,128)(2,1)}, u32[]{:S(2)}) copy-start(bf16[128,2560]{1,0:T(8,128)(2,1)} %get-tuple-element.216) | copy-start | bytes 1966084
  (36 other events, 58.7 us)

commit v9 on v8

--- a/solution.py
+++ b/solution.py
@@ -110,15 +110,16 @@
 def gather_kernel(shape, *refs):
     inner, outer = shape
     (tokens, grads, vectors, gates, xy, out, gate, up, down) = refs[:9]
-    (tokens_to, grads_to, vectors_to, gates_to, xy_to, out_to, gate_to, up_to, down_to) = refs[9:18]
-    gates_own, send_sems, local_sems, line_sems, plane_sems, rows_sems = refs[18:24]
-    vector_sems, turn_sems, group_sems = refs[24:]
+    (grads_to, vectors_to, gates_to, xy_to, out_to, gate_to, up_to, down_to) = refs[9:17]
+    rows_one, xy_one = refs[17:19]
+    gates_own, send_sems, local_sems, line_sems, plane_sems, rows_sems = refs[19:25]
+    vector_sems, turn_sems, group_sems, tokens_to, xy_v, vectors_v, spread, read_sems = refs[25:]
     seq, wt = Z * inner, outer * C
     s, w = lax.axis_index("seq"), lax.axis_index("wt")
     z, x, y, c = s // inner, s % inner, w // C, w % C
     sends = Sends(send_sems)
     group = GroupRows(Place(shape), sends, grads, grads_to, group_sems)
-    here = []
+    here, counter = [], iter(range(16))
 
     def at_z(to):
         return {"seq": to * inner + x, "wt": w}
@@ -132,7 +133,7 @@
     at_c = {"seq": s, "wt": y * C + 1 - c}
 
     def keep(source, target, waited=False):
-        copy = pltpu.make_async_copy(source, target, local_sems.at[len(here)])
+        copy = pltpu.make_async_copy(source, target, local_sems.at[next(counter)])
         copy.start()
         here.append((waited, copy))
         return copy
@@ -313,8 +314,74 @@
 
     pl.when(jnp.logical_not(here_too))(turn.start)
     pl.when(here_too)(stay.start)
+    def vector_wait(i, carried):
+        @pl.when(i != me)
+        def _():
+            vector_copy(i).wait_send()
+            arrived(vectors_to.at[i], vector_sems.at[1, i], at_c)
+
+        return carried
+
+    def first_projection():
+        lines[0].finish()
+        tokens_finish()
+        lax.fori_loop(0, seq * wt, vector_wait, 0)
+        for copy in here_first:
+            copy.wait()
+        rows_each = xy.shape[0]
+        copies = [pltpu.make_async_copy(vectors_to, vectors_v, read_sems.at[0])]
+        for z_at in range(Z):
+            for x_at in range(inner):
+                n = z_at * inner + x_at
+                copies.append(
+                    pltpu.make_async_copy(
+                        xy_to.at[z_at, x_at], xy_v.at[n * rows_each : (n + 1) * rows_each],
+                        read_sems.at[1 + n],
+                    )
+                )
+        for copy in copies:
+            copy.start()
+        copies[0].wait()
+        width = tokens.shape[1]
+        devices = seq * wt
+        channels = width // devices
+        spread[...] = jnp.zeros_like(spread)
+        for i in range(devices):
+            first = min(i * channels // LANES * LANES, width - 2 * LANES)
+            turn = i * channels - first
+            part = vectors_v[i, 0:8]
+            part = jnp.concatenate([part, jnp.zeros_like(part)], axis=1)
+            if turn:
+                part = pltpu.roll(part, turn, 1)
+            spread[:, first : first + 2 * LANES] += part
+        gain = spread[0:1]
+        count = tokens.shape[0]
+        for at in range(wt):
+
+            def norm(r, at=at):
+                stream = tokens_to[at, r].astype(F32)
+                inverse = lax.rsqrt(jnp.mean(stream * stream, axis=1, keepdims=True) + EPSILON)
+                rows_one[pl.ds(pl.multiple_of(at * count + r.start, 16), 16)] = (
+                    stream * inverse * gain
+                ).astype(BF16)
+
+            each_rows(count, 16, norm)
+        for copy in copies[1:]:
+            copy.wait()
+        tile = 2 * LANES
+
+        def project(n, carried):
+            down = pl.ds(pl.multiple_of(n % wt * count, LANES), count)
+            across = pl.ds(pl.multiple_of(n // wt * tile, tile), tile)
+            xy_one[down, across] = multiply(rows_one[down], xy_v[:, across])
+            return carried
+
+        lax.fori_loop(0, wt * (xy_v.shape[1] // tile), project, 0)
+
     lines[0].begin()
     tokens_begin()
+    here_first = [copy for _, copy in here]
+    here.clear()
 
     @pl.when(jnp.logical_not(here_too))
     def _():
@@ -344,29 +411,22 @@
     group.begin()
     for k in range(Z):
         planes[1].first(k)
+    for k in range(Z):
         planes[0].second(k)
-    for k in range(1, Z):
+    group.step(1)
+    first_projection()
+    for k in range(2, Z):
         group.step(k)
     group.finish()
 
-    for line in lines:
+    for line in lines[1:]:
         line.finish()
-    tokens_finish()
     for k in range(Z):
         planes[1].second(k)
         planes[2].second(k)
         planes[0].finish(k)
 
-    def vector_wait(i, carried):
-        @pl.when(i != me)
-        def _():
-            vector_copy(i).wait_send()
-            arrived(vectors_to.at[i], vector_sems.at[1, i], at_c)
-
-        return carried
-
     pl.when(jnp.logical_not(here_too))(turn.wait_send)
-    lax.fori_loop(0, seq * wt, vector_wait, 0)
     sends.finish()
     for waited, copy in here:
         if not waited:
@@ -385,7 +445,6 @@
         return buffer(Z, inner, rows, outer * columns // Z, like=weight)
 
     shapes = (
-        buffer(wt, *tokens.shape, like=tokens),
         buffer(C, Z, *grads.shape, like=grads),
         buffer(seq * wt, *vectors.shape, like=vectors),
         buffer(Z, inner, *gates.shape, like=gates),
@@ -394,6 +453,8 @@
         plane(gate),
         plane(up),
         plane(down),
+        buffer(wt * tokens.shape[0], tokens.shape[1], like=tokens),
+        jax.ShapeDtypeStruct((wt * tokens.shape[0], xy.shape[1]), F32),
     )
     copies = 3 * (2 + inner + (Z - 1) * 2 * inner) + 3 * (Z - 1 + Z * (inner + 2 * outer + inner * outer))
     copies += 2 * outer + 3 + 4 * Z
@@ -402,7 +463,7 @@
         functools.partial(gather_kernel, (inner, outer)),
         out_shape=shapes,
         in_specs=[pl.BlockSpec(memory_space=pl.ANY)] * 9,
-        out_specs=[pl.BlockSpec(memory_space=pl.ANY)] * 9,
+        out_specs=[pl.BlockSpec(memory_space=pl.ANY)] * 8 + [pl.BlockSpec(memory_space=pltpu.VMEM)] * 2,
         scratch_shapes=[
             pltpu.VMEM(gates.shape, gates.dtype),
             dma((copies,)),
@@ -413,8 +474,15 @@
             dma((2, seq * wt)),
             dma((3,)),
             dma((C, Z)),
+            pltpu.VMEM((wt, *tokens.shape), tokens.dtype),
+            pltpu.VMEM((Z * inner * xy.shape[0], xy.shape[1]), xy.dtype),
+            pltpu.VMEM((seq * wt, *vectors.shape), F32),
+            pltpu.VMEM((8, tokens.shape[1]), F32),
+            dma((1 + Z * inner,)),
         ],
-        compiler_params=pltpu.CompilerParams(collective_id=0, has_side_effects=True),
+        compiler_params=pltpu.CompilerParams(
+            collective_id=0, has_side_effects=True, vmem_limit_bytes=40 * 1024 * 1024
+        ),
         name="gather_all",
     )(tokens, grads, vectors, gates, xy, out, gate, up, down)
 
@@ -1502,11 +1570,6 @@
     )
 
 
-def normed_rows(stream):
-    inverse = lax.rsqrt(jnp.mean(stream * stream, axis=1, keepdims=True) + EPSILON)
-    return stream * inverse, inverse
-
-
 def per_device(
     tokens,
     norm1_gain,
@@ -1568,13 +1631,12 @@
 
     xy_unit = jnp.concatenate([turned(x_weight, 1), turned(y_weight, 1)], axis=1)
     (
-        group_tokens, grad_group, vectors, gate_all, xy_kernel, out_kernel,
-        gate_kernel, up_kernel, down_kernel,
+        grad_group, vectors, gate_all, xy_kernel, out_kernel, gate_kernel, up_kernel, down_kernel,
+        group_one, xy,
     ) = gather_all(
         tokens, out_grad, vectors, gates, xy_unit, turned(out_weight, 1),
         padded(gate_weight), padded(up_weight), padded(down_weight),
     )
-    group_tokens = group_tokens.reshape(-1, width)
     grad_group = grad_group.reshape(-1, width)
     vectors = jnp.moveaxis(vectors[:, : 6 + taps_count, :chunk], 0, 1).reshape(6 + taps_count, -1)
     gain_one, gain_two = vectors[0], vectors[1]
@@ -1591,10 +1653,7 @@
     shared_rows = in_order(gate_all[full:], partner_rows, 0)
 
     stream = tokens.astype(F32)
-    group_normed, _ = normed_rows(group_tokens.astype(F32))
-    group_one = (group_normed * gain_one).astype(BF16)
     rows = group_one.shape[0]
-    xy = multiply(group_one, xy_kernel)
     x_branch = xy[:, :lru_cols].astype(BF16)
     y_before = xy[:, lru_cols:]
     y_gated, gelu_y_back = jax.vjp(gelu_tanh, y_before)

time: 824 us -> 819 us (level)
    dot_general x8 -> x7, matrix products: 40.7 us -> 38.1 us  [multiply(): return jnp.dot(left_side, right_side, preferred_element_type=F32)]
  transfers between devices with their start and end apart: 6 -> 6, of which waited for: 2 -> 3; matrix products, arithmetic and copies ran while one was open for 2% -> 2% of each run, Pallas kernels for 0% -> 0%
where the time goes in v9:
time: 819 us; the launch traced here: 813 us
  Pallas kernels  608 us (74%)
  matrix products  117 us (14%)
  other arithmetic  28.9 us (4%)
  local copies, waits for them, and re-layouts  28.3 us (3%)
  starting transfers between devices  20.7 us (3%)
  waiting for transfers between devices  8.24 us (1%)
    pallas_call x1, Pallas kernels, gather_all(): pl.pallas_call(functools.partial(gather_kernel, (inner, outer)), out_shap...  213 us
    pallas_call x1, Pallas kernels, last_sums(): pl.pallas_call(functools.partial(sums_kernel, (inner, outer)), out_shape=...  175 us
    pallas_call x1, Pallas kernels, middle_and_rows(): pl.pallas_call(functools.partial(middle_kernel, (inner, outer)), out_shap...  120 us
    pallas_call x1, Pallas kernels, branch_and_group(): pl.pallas_call(functools.partial(branch_kernel, (inner, outer)), out_shap...  82.9 us
    dot_general x15, matrix products, contract_last(): lax.dot_general(left_side, right_side, (((1,), (1,)), ((), ())), preferre...  50.9 us
    dot_general x7, matrix products, multiply(): return jnp.dot(left_side, right_side, preferred_element_type=F32)  38.1 us
    dot_general x9, matrix products, contract_rows(): lax.dot_general(left_side, right_side, (((0,), (0,)), ((), ())), preferre...  28.3 us
  transfers between devices with their start and end apart: 6, of which 3 were waited for; matrix products, arithmetic and copies ran while one was open for 2% of the time, Pallas kernels for 0%

profile of v9, /device:TPU:2, one launch (start us, length us, event | category | flops | bytes accessed | tf_op | source)
XLA Modules:
  0.0 813.3 jit_solution(11291002393474141422)
XLA Ops:
  9.1 213.2 %gather_all.1 = (bf16[2,4,128,2560]{3,2,1,0:T(8,128)(2,1)}, f32[32,16,128]{2,1,0:T(8,128)S(1)}, bf16[4,2,80,512]{3,2,1,0:T(8,128)(2,1)S(1)}, bf16[4,2,320,1280]{...) custom-call(bf16[128,2560]{1,0:T(8,128)(2,1)S(1)} %copy-done, ...), custom_call_target="tpu_custom_call" | custom-call | tf_op jit(solution)/shard_map/gather_all/pallas_call | solution.py:462
  225.3 15.2 %collective-permute-start = (bf16[3,640]{1,0:T(4,128)(2,1)S(1)}, bf16[3,640]{1,0:T(4,128)(2,1)S(1)}, u32[]{:S(2)}, u32[]{:S(2)}) collective-permute-start(bf16[3,640]{1,0:T(4,128)(2,1)S(1)} %slice.470), channel_id=1, source_target_pairs={{0,4},{4,8},{8,12},{12,16},{16,20},{20,24},{24,28},{1,5},{5,9},{9,... | collective-permute-start | bytes 11528 | tf_op jit(solution)/shard_map/ppermute | solution.py:1660
  251.3 7.8 scan_ahead.1
  264.2 82.9 %branch_and_group.1 = (bf16[2,4,128,2560]{3,2,1,0:T(8,128)(2,1)S(1)}, f32[128,2560]{1,0:T(8,128)S(1)}, bf16[4,2,320,1024]{3,2,1,0:T(8,128)(2,1)}, bf16[4,2,320,1024]{3,2,1,0:T(8,128)(2,1)}) custom-call(f32[2,128,2560]{2,1,0:T(8,128)S(1)} %fusion.67.sent, f32[2,128,2560]{2,1,0:T(8,128)S(1)} %fusion.65.own, ...), custom_call_target="tpu_custom_call", output_to_operand_aliasing={{2}: (4, {}), {3}: (5, {})} | custom-call | tf_op jit(solution)/shard_map/branch_and_group/pallas_call | solution.py:687
  347.1 9.3 %fusion.122 = f32[1024,1024]{1,0:T(8,128)} fusion(bf16[1024,2560]{1,0:T(8,128)(2,1)S(1)} %bitcast.120, bf16[2560,1024]{1,0:T(8,128)(2,1)} %bitcast.173), kind=kOutput, calls=%fused_computation.230 | convolution fusion | flops 5368709120 | bytes 14680064 | tf_op jit(solution)/shard_map/dot_general | solution.py:73
  356.5 9.1 %fusion.121 = f32[1024,1024]{1,0:T(8,128)} fusion(bf16[1024,2560]{1,0:T(8,128)(2,1)} %bitcast.168, bf16[2560,1024]{1,0:T(8,128)(2,1)S(1)} %bitcast.147), kind=kOutput, calls=%fused_computation.229 | convolution fusion | flops 5368709120 | bytes 14680064 | tf_op jit(solution)/shard_map/dot_general | solution.py:73
  365.6 12.2 %multiply_convert_fusion = (bf16[1024,1024]{1,0:T(8,128)(2,1)S(1)}, bf16[1024,1024]{1,0:T(8,128)(2,1)}, bf16[1024,1024]{1,0:T(8,128)(2,1)S(1)}) fusion(f32[1024,1024]{1,0:T(8,128)} %fusion.122, f32[1024,1024]{1,0:T(8,128)} %fusion.121, bf16[1024,2560]{1,0:T(8,128)(2,1)S(1)} %bitcast.121, bf16[2560,1024]{1,0:T(8,128)(2,1)S(1)} %bitcast.144), kind=kOutput, calls=%fused_computation.18 | convolution fusion | flops 5395972096 | bytes 25165824 | tf_op jit(solution)/shard_map/dot_general | solution.py:73
  377.8 8.9 %fusion.55 = f32[512,2560]{1,0:T(8,128)} fusion(bf16[2560,1024]{1,0:T(8,128)(2,1)} %bitcast.174, bf16[1024,1024]{1,0:T(8,128)(2,1)} %get-tuple-element.142), kind=kOutput, calls=%fused_computation.103 | convolution fusion | flops 2684354560 | bytes 11534336 | tf_op jit(solution)/shard_map/dot_general | solution.py:61
  386.7 7.1 fusion.52
  393.8 4.3 convolution_convert_fusion.5
  398.1 4.2 convolution_convert_fusion.4
  402.3 4.2 convolution_convert_fusion.3
  406.5 4.2 convolution_convert_fusion.2
  410.9 4.2 convolution_convert_fusion.1
  415.2 4.2 convolution_convert_fusion
  419.4 6.3 add_convert_fusion
  425.7 4.7 convolution_add_fusion
  430.4 4.3 convolution_convert_fusion.6.refs_5_
  434.6 4.7 fusion.123.refs_6_
  439.3 120.5 %middle_and_rows.1 = (bf16[4,128,2560]{2,1,0:T(8,128)(2,1)}, f32[128,2560]{1,0:T(8,128)}, f32[16,2560]{1,0:T(8,128)}, bf16[128,2560]{1,0:T(8,128)(2,1)}, bf16[3,...) custom-call(bf16[4,128,2560]{2,1,0:T(8,128)(2,1)} %bitcast.156, ...), custom_call_target="tpu_custom_call" | custom-call | tf_op jit(solution)/shard_map/middle_and_rows/pallas_call | solution.py:1017
  559.8 6.7 convert_multiply_fusion
  566.6 8.0 scan_back.1
  576.2 3.5 multiply_reduce_fusion.4
  579.7 2.9 fusion.108
  591.0 3.5 multiply_reduce_fusion
  602.6 3.3 fusion.12
  605.9 3.2 fusion.10
  611.4 2.8 convolution_add_fusion.1
  615.2 175.2 %last_sums.1 = (bf16[3,320,2048]{2,1,0:T(8,128)(2,1)}, f32[320,1920]{1,0:T(8,128)}, f32[80,512]{1,0:T(8,128)}, bf16[128,2560]{1,0:T(8,128)(2,1)}, f32[16,128]{1,0:T(8,128)}, /*index=5*/f32[2,8,640]{2,1,0:T(8,128)}) custom-call(bf16[3,4,320,512]{3,2,1,0:T(8,128)(2,1)} %get-tuple-element.62.refs_0_, bf16[1,6,320,512]{3,2,1,0:T(8,128)(2,1)} %get-tuple-element.63.refs_1_, ...), custom_call_target="tpu_custom_call" | custom-call | tf_op jit(solution)/shard_map/last_sums/pallas_call | solution.py:1394
  791.1 3.2 fusion.111
  796.9 5.3 bitcast_convert_fusion
  802.7 6.5 collective-permute-done.5
  (262 shorter events, 55.6 us)
Async XLA Ops:
  225.3 19.3 %collective-permute-start = (bf16[3,640]{1,0:T(4,128)(2,1)S(1)}, bf16[3,640]{1,0:T(4,128)(2,1)S(1)}, u32[]{:S(2)}, u32[]{:S(2)}) collective-permute-start(bf16[3,640]{1,0:T(4,128)(2,1)S(1)} %slice.470), channel_id=1, source_target_pairs={{0,4},{4,8},{8,12},{12,16},{16,20},{20,24},{24,28},{1,5},{5,9},{9,... | collective-permute-start | bytes 11528 | tf_op jit(solution)/shard_map/ppermute | solution.py:1660
  240.9 6.4 collective-permute-start.2
  242.8 21.5 %copy-start.11 = (f32[1,2560]{1,0:T(1,128)}, f32[1,2560]{1,0:T(1,128)S(1)}, u32[]{:S(2)}) copy-start(f32[1,2560]{1,0:T(1,128)S(1)} %slice.410.gain.refs_4_) | copy-start | bytes 30724
  244.7 4.2 copy-start.12
  246.9 1.7 collective-permute-start.1
  247.1 4.1 copy-start.17
  251.3 7.8 copy-start.2
  259.1 3.9 copy-start.4
  347.1 9.4 %copy-start.10 = (f32[128,2560]{1,0:T(8,128)}, f32[128,2560]{1,0:T(8,128)S(1)}, u32[]{:S(2)}) copy-start(f32[128,2560]{1,0:T(8,128)S(1)} %get-tuple-element.60.refs_2_) | copy-start | bytes 3932164
  347.1 9.4 %copy-start.30 = (bf16[4,2,320,1024]{3,2,1,0:T(8,128)(2,1)S(1)}, bf16[4,2,320,1024]{3,2,1,0:T(8,128)(2,1)}, u32[]{:S(2)}) copy-start(bf16[4,2,320,1024]{3,2,1,0:T(8,128)(2,1)} %get-tuple-element.56) | copy-start | bytes 15728644
  347.1 18.4 %slice-start.2 = ((s8[5242880]{0:T(1024)(128)(4,1)}), s8[4194304]{0:T(1024)(128)(4,1)S(1)}, s32[]{:S(2)}) async-start(s8[5242880]{0:T(1024)(128)(4,1)} %bitcast.142), calls=%async_computation.2 | async-start | bytes 8388608
  356.5 9.1 %slice-start.3 = ((s8[5242880]{0:T(1024)(128)(4,1)}), s8[1048576]{0:T(1024)(128)(4,1)S(1)}, s32[]{:S(2)}) async-start(s8[5242880]{0:T(1024)(128)(4,1)} %bitcast.142), calls=%async_computation.3 | async-start | bytes 2097152
  377.8 28.7 %copy-start.56 = (bf16[1024,1024]{1,0:T(8,128)(2,1)}, bf16[1024,1024]{1,0:T(8,128)(2,1)S(1)}, u32[]{:S(2)}) copy-start(bf16[1024,1024]{1,0:T(8,128)(2,1)S(1)} %get-tuple-element.143) | copy-start | bytes 6291460
  377.8 8.9 %copy-start.58 = (bf16[1024,1024]{1,0:T(8,128)(2,1)S(1)}, bf16[1024,1024]{1,0:T(8,128)(2,1)}, u32[]{:S(2)}) copy-start(bf16[1024,1024]{1,0:T(8,128)(2,1)} %get-tuple-element.142) | copy-start | bytes 6291460
  402.3 8.6 %slice-start.10 = ((s8[5242880]{0:T(1024)(128)(4,1)}), s8[4194304]{0:T(1024)(128)(4,1)S(1)}, s32[]{:S(2)}) async-start(s8[5242880]{0:T(1024)(128)(4,1)} %bitcast.169), calls=%async_computation.10 | async-start | bytes 8388608
  406.5 4.4 slice-start.11
  415.2 4.2 copy-start.57
  415.2 10.5 %slice-start.12 = ((s8[5242880]{0:T(1024)(128)(4,1)}), s8[4194304]{0:T(1024)(128)(4,1)S(1)}, s32[]{:S(2)}) async-start(s8[5242880]{0:T(1024)(128)(4,1)} %bitcast.176), calls=%async_computation.12 | async-start | bytes 8388608
  419.4 6.3 slice-start.13
  439.3 120.5 %copy-start.3 = (f32[512,1280]{1,0:T(8,128)S(1)}, f32[512,1280]{1,0:T(8,128)}, u32[]{:S(2)}) copy-start(f32[512,1280]{1,0:T(8,128)} %copy-done.1) | copy-start | bytes 7864324
  559.8 14.9 %copy-start.28 = (f32[512,128]{1,0:T(8,128)S(1)}, f32[512,128]{1,0:T(8,128)}, u32[]{:S(2)}) copy-start(f32[512,128]{1,0:T(8,128)} %copy-done.27) | copy-start | bytes 786436
  566.5 8.2 %copy-start.13 = (f32[515,640]{1,0:T(8,128)S(1)}, f32[515,640]{1,0:T(8,128)}, u32[]{:S(2)}) copy-start(f32[515,640]{1,0:T(8,128)} %copy-done.12) | copy-start | bytes 3955204
  566.5 8.2 %copy-start.20 = (f32[512,256]{1,0:T(8,128)S(1)}, f32[512,256]{1,0:T(8,128)}, u32[]{:S(2)}) copy-start(f32[512,256]{1,0:T(8,128)} %copy-done.19) | copy-start | bytes 1572868
  566.5 8.2 %copy-start.22 = (f32[512,256]{1,0:T(8,128)S(1)}, f32[512,256]{1,0:T(8,128)}, u32[]{:S(2)}) copy-start(f32[512,256]{1,0:T(8,128)} %copy-done.21) | copy-start | bytes 1572868
  586.6 3.0 collective-permute-start.3
  594.4 7.4 copy-start.29
  595.4 6.5 collective-permute-start.4
  598.8 10.3 %slice-start = ((s8[6553600]{0:T(1024)(128)(4,1)}), s8[4194304]{0:T(1024)(128)(4,1)S(1)}, s32[]{:S(2)}) async-start(s8[6553600]{0:T(1024)(128)(4,1)} %bitcast.128), calls=%async_computation | async-start | bytes 8388608
  602.6 6.5 slice-start.1
  794.4 14.8 %collective-permute-start.5 = (f32[80,520]{1,0:T(8,128)S(1)}, f32[80,520]{1,0:T(8,128)S(1)}, u32[]{:S(2)}, u32[]{:S(2)}) collective-permute-start(f32[80,520]{1,0:T(8,128)S(1)} %pad_maximum_fusion.14), channel_id=1, source_target_pairs={{0,0},{4,1},{8,2},{12,3},{16,4},{20,5},{24,6},{28,7},{1,8},{5,9},{... | collective-permute-start | bytes 499208 | tf_op jit(solution)/shard_map/ppermute | solution.py:1813
  796.9 14.5 %copy-start.42 = (bf16[128,2560]{1,0:T(8,128)(2,1)S(1)}, bf16[128,2560]{1,0:T(8,128)(2,1)}, u32[]{:S(2)}) copy-start(bf16[128,2560]{1,0:T(8,128)(2,1)} %get-tuple-element.212) | copy-start | bytes 1966084
  802.2 10.0 %copy-start.43 = (bf16[128,2560]{1,0:T(8,128)(2,1)S(1)}, bf16[128,2560]{1,0:T(8,128)(2,1)}, u32[]{:S(2)}) copy-start(bf16[128,2560]{1,0:T(8,128)(2,1)} %get-tuple-element.213) | copy-start | bytes 1966084
  (47 other events, 80.2 us)

commit v10 on v9

--- a/solution.py
+++ b/solution.py
@@ -864,26 +864,23 @@
 
 def middle_kernel(shape, *refs):
     outer = shape[1]
-    sent, own, middle, grads, gain, feed_sent, feed_own = refs[:7]
+    sent, own, middle, grads, gain, hidden, down_kernel = refs[:7]
     parts = refs[7 : 7 + 3 * outer]
     rows_to, d_middle, gain_grad, block_out = refs[7 + 3 * outer : 11 + 3 * outer]
     targets = refs[11 + 3 * outer : 14 + 3 * outer]
     scratch = refs[14 + 3 * outer :]
     middle_body(
-        shape, sent, own, middle, grads, gain, feed_sent, feed_own, parts, targets,
-        rows_to, d_middle, gain_grad, block_out, scratch[:9], scratch[9:18],
-        [scratch[18 + 4 * n : 22 + 4 * n] for n in range(4)], *scratch[34:],
+        shape, sent, own, middle, grads, gain, hidden, down_kernel, parts, targets,
+        rows_to, d_middle, gain_grad, block_out, scratch[:8], scratch[8:16],
+        [scratch[16 + 4 * n : 20 + 4 * n] for n in range(4)], *scratch[32:],
     )
 
 
 class PairSum:
     def __init__(self, me, sends, sent, own, scratch):
         self.me, self.sends, self.sent = me, sends, sent
-        (
-            self.held, self.c_in, up_out, up_in, down_out, down_in,
-            self.c_sems, up_sems, down_sems,
-        ) = scratch
-        self.up, self.down = (up_out, up_in, up_sems), (down_out, down_in, down_sems)
+        self.held, self.c_in, out, up_in, down_in, self.c_sems, up_sems, down_sems = scratch
+        self.up, self.down = (out, up_in, up_sems), (out, down_in, down_sems)
 
     def begin(self):
         for k in line_order():
@@ -920,27 +917,52 @@
 
 
 def middle_body(
-    shape, sent, own, middle, grads, gain, feed_sent, feed_own, parts, targets,
+    shape, sent, own, middle, grads, gain, hidden, down_kernel, parts, targets,
     rows_to, d_middle, gain_grad, block_out, sum_scratch, feed_scratch, unit_scratch, low,
-    up_in, send_sems, local_sems, rows_sems, up_sems,
+    up_in, hidden_v, feed_sent, down_v, send_sems, local_sems, rows_sems, up_sems, down_sems,
 ):
     me = Place(shape)
     rows = middle.shape[0]
     sends = Sends(send_sems)
     total = PairSum(me, sends, sent, own, sum_scratch)
-    feed = PairSum(me, sends, feed_sent, feed_own, feed_scratch)
+    feed = PairSum(me, sends, feed_sent, None, feed_scratch)
     load = pltpu.make_async_copy(own, total.held, local_sems.at[0])
-    feed_load = pltpu.make_async_copy(feed_own, feed.held, local_sems.at[2])
+    hidden_load = pltpu.make_async_copy(hidden, hidden_v, local_sems.at[2])
     load.start()
+    hidden_load.start()
     me.greet()
     total.begin()
     units = plane_units(me, sends, parts, unit_scratch)
     units_to, units_y, units_x = targets
     for unit in units:
         unit.begin()
-    feed_load.start()
+
+    step = down_v.shape[1]
+    half_rows = Z * rows
+
+    def down_load(n, slot):
+        part = down_kernel.at[pl.ds(pl.multiple_of(n * step, LANES), step)]
+        return pltpu.make_async_copy(part, down_v.at[slot], down_sems.at[slot])
+
+    def feed_product(n, carried):
+        slot = n % 2
+        down_load(n, slot).wait()
+        pl.when(n + 1 < down_kernel.shape[0] // step)(lambda: down_load(n + 1, 1 - slot).start())
+        across = pl.ds(pl.multiple_of(n * step, LANES), step)
+        weight = down_v[slot]
+        for k in range(Z):
+            kept = hidden_v[k * rows : (k + 1) * rows]
+            other = hidden_v[half_rows + k * rows : half_rows + (k + 1) * rows]
+            feed.held[k, :, across] = contract_last(kept, weight)
+            feed_sent[k, :, across] = contract_last(other, weight).astype(BF16)
+        return carried
+
+    down_load(0, 0).start()
     load.wait()
-    total.run()
+    hidden_load.wait()
+    pieces = down_kernel.shape[0] // step
+    ends = [pieces * t // (Z - 1) for t in range(Z)]
+    total.run(lambda t: lax.fori_loop(ends[t - 1], ends[t], feed_product, 0))
     own_v = total.held
     gain_grad[...] = jnp.zeros_like(gain_grad)
 
@@ -962,7 +984,6 @@
     gather = WtRows(me, sends, low, rows_to, rows_sems)
     gather.begin()
     feed.begin()
-    feed_load.wait()
     half, extra = Z // 2, slice(Z, Z + Z // 2)
 
     def between(t):
@@ -990,7 +1011,7 @@
     keep.wait()
 
 
-def middle_and_rows(sent, own, middle, grads, gain, feed_sent, feed_own, parts):
+def middle_and_rows(sent, own, middle, grads, gain, hidden, down_kernel, parts):
     inner, outer = sizes()
     rows, width = middle.shape
     unit_rows, share = parts[0].shape[2:]
@@ -1001,7 +1022,7 @@
     ]
     unit_copies = 2 * (inner - 1) * outer + 2 * (outer - 1) + (inner - 1)
     pair_scratch = [pltpu.VMEM((Z, rows, width), F32), pltpu.VMEM((Z, rows, width), BF16)]
-    pair_scratch += [pltpu.VMEM((Z - 1, rows, width), BF16)] * 4
+    pair_scratch += [pltpu.VMEM((Z - 1, rows, width), BF16)] * 3
     dma = pltpu.SemaphoreType.DMA
     pair_scratch += [dma((Z,)), dma((Z - 1,)), dma((Z - 1,))]
     unit_scratch = []
@@ -1030,16 +1051,20 @@
         + [
             pltpu.VMEM((rows, width), BF16),
             pltpu.VMEM((inner - 1, Z, *block), BF16),
+            pltpu.VMEM(hidden.shape, BF16),
+            pltpu.VMEM((Z, rows, width), BF16),
+            pltpu.VMEM((2, 2 * LANES, hidden.shape[1]), BF16),
             dma((2 * (Z + 2 * (Z - 1)) + 2 * outer + unit_copies,)),
             dma((3,)),
             dma((outer * C,)),
             dma((inner - 1,)),
+            dma((2,)),
         ],
         compiler_params=pltpu.CompilerParams(
             collective_id=2, has_side_effects=True, vmem_limit_bytes=60 * 1024 * 1024
         ),
         name="middle_and_rows",
-    )(sent, own, middle, grads, gain, feed_sent, feed_own, *parts)
+    )(sent, own, middle, grads, gain, hidden, down_kernel, *parts)
 
 
 class RowsSum:
@@ -1730,17 +1755,14 @@
     gate_terms = terms_of(group_two, d_gate)
     up_terms = terms_of(group_two, d_up)
     down_terms = terms_of(grad_group, hidden)
-    def feed_of(part):
-        return contract_last(hidden[part], down_kernel).reshape(Z, rows_dev, width)
-
     branch_rows, d_middle, gain_two_grad, block_out, units, units_y, units_x = middle_and_rows(
         d_normed_of(slice(half_rows, None)).astype(BF16),
         d_normed_of(slice(0, half_rows)),
         middle,
         out_grad,
         gain_two[None],
-        feed_of(slice(half_rows, None)).astype(BF16),
-        feed_of(slice(0, half_rows)),
+        hidden,
+        down_kernel,
         gate_terms + up_terms + down_terms,
     )
     branch_rows = branch_rows.reshape(-1, width)

time: 819 us -> 803 us (0.980)
  matrix products: 117 us -> 101 us
    dot_general x15 -> x13, matrix products: 50.9 us -> 35.5 us  [contract_last(): lax.dot_general(left_side, right_side, (((1,), (1,)), ((), ())), preferre...]
where the time goes in v10:
time: 803 us; the launch traced here: 797 us
  Pallas kernels  608 us (76%)
  matrix products  101 us (13%)
  other arithmetic  29.3 us (4%)
  local copies, waits for them, and re-layouts  28.2 us (4%)
  starting transfers between devices  20.7 us (3%)
    pallas_call x1, Pallas kernels, gather_all(): pl.pallas_call(functools.partial(gather_kernel, (inner, outer)), out_shap...  213 us
    pallas_call x1, Pallas kernels, last_sums(): pl.pallas_call(functools.partial(sums_kernel, (inner, outer)), out_shape=...  175 us
    pallas_call x1, Pallas kernels, middle_and_rows(): pl.pallas_call(functools.partial(middle_kernel, (inner, outer)), out_shap...  120 us
    pallas_call x1, Pallas kernels, branch_and_group(): pl.pallas_call(functools.partial(branch_kernel, (inner, outer)), out_shap...  82.9 us
    dot_general x7, matrix products, multiply(): return jnp.dot(left_side, right_side, preferred_element_type=F32)  37.2 us
    dot_general x13, matrix products, contract_last(): lax.dot_general(left_side, right_side, (((1,), (1,)), ((), ())), preferre...  35.5 us
    dot_general x9, matrix products, contract_rows(): lax.dot_general(left_side, right_side, (((0,), (0,)), ((), ())), preferre...  28.4 us
  transfers between devices with their start and end apart: 6, of which 3 were waited for; matrix products, arithmetic and copies ran while one was open for 2% of the time, Pallas kernels for 0%

profile of v10, /device:TPU:2, one launch (start us, length us, event | category | flops | bytes accessed | tf_op | source)
XLA Modules:
  0.0 797.5 jit_solution(18391946114193396368)
XLA Ops:
  2.2 2.6 pad.16.refs_7_
  9.1 213.2 %gather_all.1 = (bf16[2,4,128,2560]{3,2,1,0:T(8,128)(2,1)}, f32[32,16,128]{2,1,0:T(8,128)S(1)}, bf16[4,2,80,512]{3,2,1,0:T(8,128)(2,1)S(1)}, bf16[4,2,320,1280]{...) custom-call(bf16[128,2560]{1,0:T(8,128)(2,1)S(1)} %copy-done, ...), custom_call_target="tpu_custom_call" | custom-call | tf_op jit(solution)/shard_map/gather_all/pallas_call | solution.py:462
  225.3 15.2 %collective-permute-start = (bf16[3,640]{1,0:T(4,128)(2,1)S(1)}, bf16[3,640]{1,0:T(4,128)(2,1)S(1)}, u32[]{:S(2)}, u32[]{:S(2)}) collective-permute-start(bf16[3,640]{1,0:T(4,128)(2,1)S(1)} %slice.462), channel_id=1, source_target_pairs={{0,4},{4,8},{8,12},{12,16},{16,20},{20,24},{24,28},{1,5},{5,9},{9,... | collective-permute-start | bytes 11528 | tf_op jit(solution)/shard_map/ppermute | solution.py:1685
  251.5 7.8 scan_ahead.1
  264.5 82.9 %branch_and_group.1 = (bf16[2,4,128,2560]{3,2,1,0:T(8,128)(2,1)S(1)}, f32[128,2560]{1,0:T(8,128)S(1)}, bf16[4,2,320,1024]{3,2,1,0:T(8,128)(2,1)}, bf16[4,2,320,1024]{3,2,1,0:T(8,128)(2,1)}) custom-call(f32[2,128,2560]{2,1,0:T(8,128)S(1)} %fusion.67.sent, f32[2,128,2560]{2,1,0:T(8,128)S(1)} %fusion.65.own, ...), custom_call_target="tpu_custom_call", output_to_operand_aliasing={{2}: (4, {}), {3}: (5, {})} | custom-call | tf_op jit(solution)/shard_map/branch_and_group/pallas_call | solution.py:687
  347.5 9.4 %fusion.121 = f32[1024,1024]{1,0:T(8,128)} fusion(bf16[1024,2560]{1,0:T(8,128)(2,1)S(1)} %bitcast.112, bf16[2560,1024]{1,0:T(8,128)(2,1)} %bitcast.162), kind=kOutput, calls=%fused_computation.228 | convolution fusion | flops 5368709120 | bytes 14680064 | tf_op jit(solution)/shard_map/dot_general | solution.py:73
  356.9 9.2 %fusion.120 = f32[1024,1024]{1,0:T(8,128)} fusion(bf16[1024,2560]{1,0:T(8,128)(2,1)} %bitcast.157, bf16[2560,1024]{1,0:T(8,128)(2,1)S(1)} %bitcast.125), kind=kOutput, calls=%fused_computation.227 | convolution fusion | flops 5368709120 | bytes 14680064 | tf_op jit(solution)/shard_map/dot_general | solution.py:73
  366.1 11.0 %multiply_convert_fusion = (bf16[1024,1024]{1,0:T(8,128)(2,1)S(1)}, bf16[1024,1024]{1,0:T(8,128)(2,1)S(1)}, bf16[1024,1024]{1,0:T(8,128)(2,1)S(1)}) fusion(f32[1024,1024]{1,0:T(8,128)} %fusion.121, f32[1024,1024]{1,0:T(8,128)} %fusion.120, bf16[1024,2560]{1,0:T(8,128)(2,1)S(1)} %bitcast.113, bf16[2560,1024]{1,0:T(8,128)(2,1)S(1)} %bitcast.138), kind=kOutput, calls=%fused_computation.17 | convolution fusion | flops 5395972096 | bytes 25165824 | tf_op jit(solution)/shard_map/dot_general | solution.py:73
  377.1 4.7 fusion.55
  381.9 4.9 fusion.52
  386.8 4.3 convolution_convert_fusion.5
  391.0 4.3 convolution_convert_fusion.4
  395.3 4.2 convolution_convert_fusion.3
  399.5 4.2 convolution_convert_fusion.2
  403.8 4.2 convolution_convert_fusion.1
  408.0 4.2 convolution_convert_fusion
  412.2 6.1 add_convert_fusion
  418.4 4.7 convolution_add_fusion
  423.1 120.5 %middle_and_rows.1 = (bf16[4,128,2560]{2,1,0:T(8,128)(2,1)}, f32[128,2560]{1,0:T(8,128)}, f32[16,2560]{1,0:T(8,128)}, bf16[128,2560]{1,0:T(8,128)(2,1)}, bf16[3,...) custom-call(bf16[4,128,2560]{2,1,0:T(8,128)(2,1)} %bitcast.147, ...), custom_call_target="tpu_custom_call" | custom-call | tf_op jit(solution)/shard_map/middle_and_rows/pallas_call | solution.py:1038
  543.6 6.8 convert_multiply_fusion
  550.4 8.0 %scan_back.1 = (f32[512,640]{1,0:T(8,128)S(1)}, f32[1,640]{1,0:T(1,128)S(1)}) custom-call(f32[512,640]{1,0:T(8,128)S(1)} %get-tuple-element.153.factors, f32[512,640]{1,0:T(8,128)S(1)} %get-tuple-element.137.inflows), custom_call_target="tpu_custom_call" | custom-call | tf_op jit(solution)/shard_map/scan_back/pallas_call | solution.py:1565
  560.1 3.5 multiply_reduce_fusion.4
  563.6 2.9 fusion.108
  574.9 3.5 multiply_reduce_fusion
  579.3 2.8 collective-permute-start.4
  586.5 3.3 fusion.12
  589.8 3.2 fusion.10
  595.3 2.8 convolution_add_fusion.1
  599.1 175.4 %last_sums.1 = (bf16[3,320,2048]{2,1,0:T(8,128)(2,1)}, f32[320,1920]{1,0:T(8,128)}, f32[80,512]{1,0:T(8,128)}, bf16[128,2560]{1,0:T(8,128)(2,1)}, f32[16,128]{1,0:T(8,128)}, /*index=5*/f32[2,8,640]{2,1,0:T(8,128)}) custom-call(bf16[3,4,320,512]{3,2,1,0:T(8,128)(2,1)} %get-tuple-element.62.refs_0_, bf16[1,6,320,512]{3,2,1,0:T(8,128)(2,1)} %get-tuple-element.63.refs_1_, ...), custom_call_target="tpu_custom_call" | custom-call | tf_op jit(solution)/shard_map/last_sums/pallas_call | solution.py:1419
  775.3 3.2 fusion.111
  781.1 5.3 bitcast_convert_fusion
  786.9 6.3 collective-permute-done.5
  (260 shorter events, 50.3 us)
Async XLA Ops:
  225.3 19.3 %collective-permute-start = (bf16[3,640]{1,0:T(4,128)(2,1)S(1)}, bf16[3,640]{1,0:T(4,128)(2,1)S(1)}, u32[]{:S(2)}, u32[]{:S(2)}) collective-permute-start(bf16[3,640]{1,0:T(4,128)(2,1)S(1)} %slice.462), channel_id=1, source_target_pairs={{0,4},{4,8},{8,12},{12,16},{16,20},{20,24},{24,28},{1,5},{5,9},{9,... | collective-permute-start | bytes 11528 | tf_op jit(solution)/shard_map/ppermute | solution.py:1685
  240.9 6.3 collective-permute-start.2
  242.8 21.7 %copy-start.11 = (f32[1,2560]{1,0:T(1,128)}, f32[1,2560]{1,0:T(1,128)S(1)}, u32[]{:S(2)}) copy-start(f32[1,2560]{1,0:T(1,128)S(1)} %slice.404.gain.refs_4_) | copy-start | bytes 30724
  244.7 4.2 copy-start.12
  246.9 1.7 collective-permute-start.1
  247.1 4.4 copy-start.18
  251.5 7.9 copy-start.2
  259.4 3.9 copy-start.4
  347.4 9.4 %copy-start.10 = (f32[128,2560]{1,0:T(8,128)}, f32[128,2560]{1,0:T(8,128)S(1)}, u32[]{:S(2)}) copy-start(f32[128,2560]{1,0:T(8,128)S(1)} %get-tuple-element.60.refs_2_) | copy-start | bytes 3932164
  347.4 9.4 %copy-start.14 = (bf16[4,2,320,1024]{3,2,1,0:T(8,128)(2,1)S(1)}, bf16[4,2,320,1024]{3,2,1,0:T(8,128)(2,1)}, u32[]{:S(2)}) copy-start(bf16[4,2,320,1024]{3,2,1,0:T(8,128)(2,1)} %get-tuple-element.56) | copy-start | bytes 15728644
  347.4 18.6 %slice-start.2 = ((s8[5242880]{0:T(1024)(128)(4,1)}), s8[4194304]{0:T(1024)(128)(4,1)S(1)}, s32[]{:S(2)}) async-start(s8[5242880]{0:T(1024)(128)(4,1)} %bitcast.136), calls=%async_computation.2 | async-start | bytes 8388608
  356.9 9.2 %slice-start.3 = ((s8[5242880]{0:T(1024)(128)(4,1)}), s8[1048576]{0:T(1024)(128)(4,1)S(1)}, s32[]{:S(2)}) async-start(s8[5242880]{0:T(1024)(128)(4,1)} %bitcast.136), calls=%async_computation.3 | async-start | bytes 2097152
  356.9 20.2 %slice-start.12 = ((s8[5242880]{0:T(1024)(128)(4,1)}), s8[1048576]{0:T(1024)(128)(4,1)S(1)}, s32[]{:S(2)}) async-start(s8[5242880]{0:T(1024)(128)(4,1)} %bitcast.163), calls=%async_computation.12 | async-start | bytes 2097152
  366.1 11.1 %slice-start.13 = ((s8[5242880]{0:T(1024)(128)(4,1)}), s8[4194304]{0:T(1024)(128)(4,1)S(1)}, s32[]{:S(2)}) async-start(s8[5242880]{0:T(1024)(128)(4,1)} %bitcast.163), calls=%async_computation.13 | async-start | bytes 8388608
  377.1 30.9 %copy-start.36 = (bf16[1024,1024]{1,0:T(8,128)(2,1)}, bf16[1024,1024]{1,0:T(8,128)(2,1)S(1)}, u32[]{:S(2)}) copy-start(bf16[1024,1024]{1,0:T(8,128)(2,1)S(1)} %get-tuple-element.141.refs_5_) | copy-start | bytes 6291460
  395.3 8.5 %slice-start.10 = ((s8[5242880]{0:T(1024)(128)(4,1)}), s8[4194304]{0:T(1024)(128)(4,1)S(1)}, s32[]{:S(2)}) async-start(s8[5242880]{0:T(1024)(128)(4,1)} %bitcast.158), calls=%async_computation.10 | async-start | bytes 8388608
  399.5 4.2 slice-start.11
  408.0 10.3 %slice-start.14 = ((s8[5242880]{0:T(1024)(128)(4,1)}), s8[4194304]{0:T(1024)(128)(4,1)S(1)}, s32[]{:S(2)}) async-start(s8[5242880]{0:T(1024)(128)(4,1)} %bitcast.167), calls=%async_computation.14 | async-start | bytes 8388608
  412.2 6.1 slice-start.15
  423.1 120.5 %copy-start.3 = (f32[512,1280]{1,0:T(8,128)S(1)}, f32[512,1280]{1,0:T(8,128)}, u32[]{:S(2)}) copy-start(f32[512,1280]{1,0:T(8,128)} %copy-done.1) | copy-start | bytes 7864324
  543.6 15.0 %copy-start.29 = (f32[512,128]{1,0:T(8,128)S(1)}, f32[512,128]{1,0:T(8,128)}, u32[]{:S(2)}) copy-start(f32[512,128]{1,0:T(8,128)} %copy-done.28) | copy-start | bytes 786436
  550.4 8.2 %copy-start.13 = (f32[515,640]{1,0:T(8,128)S(1)}, f32[515,640]{1,0:T(8,128)}, u32[]{:S(2)}) copy-start(f32[515,640]{1,0:T(8,128)} %copy-done.12) | copy-start | bytes 3955204
  550.4 8.2 %copy-start.21 = (f32[512,256]{1,0:T(8,128)S(1)}, f32[512,256]{1,0:T(8,128)}, u32[]{:S(2)}) copy-start(f32[512,256]{1,0:T(8,128)} %copy-done.20) | copy-start | bytes 1572868
  550.4 8.2 %copy-start.23 = (f32[512,256]{1,0:T(8,128)S(1)}, f32[512,256]{1,0:T(8,128)}, u32[]{:S(2)}) copy-start(f32[512,256]{1,0:T(8,128)} %copy-done.22) | copy-start | bytes 1572868
  570.5 3.0 collective-permute-start.3
  578.4 7.4 copy-start.30
  579.3 6.5 collective-permute-start.4
  582.7 10.3 %slice-start = ((s8[6553600]{0:T(1024)(128)(4,1)}), s8[4194304]{0:T(1024)(128)(4,1)S(1)}, s32[]{:S(2)}) async-start(s8[6553600]{0:T(1024)(128)(4,1)} %bitcast.120), calls=%async_computation | async-start | bytes 8388608
  586.5 6.5 slice-start.1
  778.6 14.5 %collective-permute-start.5 = (f32[80,520]{1,0:T(8,128)S(1)}, f32[80,520]{1,0:T(8,128)S(1)}, u32[]{:S(2)}, u32[]{:S(2)}) collective-permute-start(f32[80,520]{1,0:T(8,128)S(1)} %pad_maximum_fusion.14), channel_id=1, source_target_pairs={{0,0},{4,1},{8,2},{12,3},{16,4},{20,5},{24,6},{28,7},{1,8},{5,9},{... | collective-permute-start | bytes 499208 | tf_op jit(solution)/shard_map/ppermute | solution.py:1835
  781.1 14.3 %copy-start.43 = (bf16[128,2560]{1,0:T(8,128)(2,1)S(1)}, bf16[128,2560]{1,0:T(8,128)(2,1)}, u32[]{:S(2)}) copy-start(bf16[128,2560]{1,0:T(8,128)(2,1)} %get-tuple-element.210) | copy-start | bytes 1966084
  786.4 9.8 %copy-start.44 = (bf16[128,2560]{1,0:T(8,128)(2,1)S(1)}, bf16[128,2560]{1,0:T(8,128)(2,1)}, u32[]{:S(2)}) copy-start(bf16[128,2560]{1,0:T(8,128)(2,1)} %get-tuple-element.211) | copy-start | bytes 1966084
  (47 other events, 80.8 us)

commit v11 on v10

--- a/solution.py
+++ b/solution.py
@@ -639,7 +639,7 @@
         arrived(c_in.at[at], c_sems.at[at], me.at_c)
         if i < outer - 1:
             each_rows(rows, 16, lambda r, i=i, at=at: y_out.__setitem__(
-                (i, r), (own_v[at, r] + c_in[at, r]).astype(BF16)))
+                (i, r), (own_v[at, r] + c_in[at, r].astype(F32)).astype(BF16)))
             sends.start(True, y_out.at[i], y_in.at[i], y_sems.at[i], me.at_y(i + 1))
     for i in range(outer - 1):
         arrived(y_in.at[i], y_sems.at[i], me.at_c)
@@ -652,7 +652,7 @@
             )
 
     def work(r):
-        total = tokens[r].astype(F32) + own_v[me.y, r] + c_in[me.y, r]
+        total = tokens[r].astype(F32) + own_v[me.y, r] + c_in[me.y, r].astype(F32)
         for i in range(outer - 1):
             total = total + y_in[i, r].astype(F32)
         inverse = lax.rsqrt(jnp.mean(total * total, axis=1, keepdims=True) + EPSILON)
@@ -697,7 +697,7 @@
         input_output_aliases={4: 2, 5: 3},
         scratch_shapes=[
             pltpu.VMEM((outer, rows, width), F32),
-            pltpu.VMEM((outer, rows, width), F32),
+            pltpu.VMEM((outer, rows, width), BF16),
             pltpu.VMEM((outer - 1, rows, width), BF16),
             pltpu.VMEM((outer - 1, rows, width), BF16),
             pltpu.VMEM((rows, width), BF16),
@@ -1723,7 +1723,7 @@
         return contract_last(part, out_kernel).reshape(outer, rows_dev, width)
 
     group_two, middle, up_kernel, down_kernel = branch_and_group(
-        branch_of(1 - c), branch_of(c), tokens, gain_two[None], up_kernel, down_kernel
+        branch_of(1 - c).astype(BF16), branch_of(c), tokens, gain_two[None], up_kernel, down_kernel
     )
     up_kernel = up_kernel.reshape(width, -1)
     down_kernel = down_kernel.reshape(width, -1)

time: 803 us -> 802 us (level)
  no operation moved by 1% of the time
where the time goes in v11:
time: 802 us; the launch traced here: 797 us
  Pallas kernels  607 us (76%)
  matrix products  101 us (13%)
  other arithmetic  29.3 us (4%)
  local copies, waits for them, and re-layouts  28.2 us (4%)
  starting transfers between devices  20.7 us (3%)
    pallas_call x1, Pallas kernels, gather_all(): pl.pallas_call(functools.partial(gather_kernel, (inner, outer)), out_shap...  213 us
    pallas_call x1, Pallas kernels, last_sums(): pl.pallas_call(functools.partial(sums_kernel, (inner, outer)), out_shape=...  175 us
    pallas_call x1, Pallas kernels, middle_and_rows(): pl.pallas_call(functools.partial(middle_kernel, (inner, outer)), out_shap...  120 us
    pallas_call x1, Pallas kernels, branch_and_group(): pl.pallas_call(functools.partial(branch_kernel, (inner, outer)), out_shap...  82 us
    dot_general x7, matrix products, multiply(): return jnp.dot(left_side, right_side, preferred_element_type=F32)  37.2 us
    dot_general x13, matrix products, contract_last(): lax.dot_general(left_side, right_side, (((1,), (1,)), ((), ())), preferre...  35.5 us
    dot_general x9, matrix products, contract_rows(): lax.dot_general(left_side, right_side, (((0,), (0,)), ((), ())), preferre...  28.4 us
  transfers between devices with their start and end apart: 6, of which 3 were waited for; matrix products, arithmetic and copies ran while one was open for 2% of the time, Pallas kernels for 0%

profile of v11, /device:TPU:2, one launch (start us, length us, event | category | flops | bytes accessed | tf_op | source)
XLA Modules:
  0.0 796.5 jit_solution(12368008387817819842)
XLA Ops:
  2.2 2.6 pad.16.refs_7_
  9.1 213.2 %gather_all.1 = (bf16[2,4,128,2560]{3,2,1,0:T(8,128)(2,1)}, f32[32,16,128]{2,1,0:T(8,128)S(1)}, bf16[4,2,80,512]{3,2,1,0:T(8,128)(2,1)S(1)}, bf16[4,2,320,1280]{...) custom-call(bf16[128,2560]{1,0:T(8,128)(2,1)S(1)} %copy-done, ...), custom_call_target="tpu_custom_call" | custom-call | tf_op jit(solution)/shard_map/gather_all/pallas_call | solution.py:462
  225.3 15.2 %collective-permute-start = (bf16[3,640]{1,0:T(4,128)(2,1)S(1)}, bf16[3,640]{1,0:T(4,128)(2,1)S(1)}, u32[]{:S(2)}, u32[]{:S(2)}) collective-permute-start(bf16[3,640]{1,0:T(4,128)(2,1)S(1)} %slice.462), channel_id=1, source_target_pairs={{0,4},{4,8},{8,12},{12,16},{16,20},{20,24},{24,28},{1,5},{5,9},{9,... | collective-permute-start | bytes 11528 | tf_op jit(solution)/shard_map/ppermute | solution.py:1685
  251.5 7.8 scan_ahead.1
  264.5 82.0 %branch_and_group.1 = (bf16[2,4,128,2560]{3,2,1,0:T(8,128)(2,1)S(1)}, f32[128,2560]{1,0:T(8,128)S(1)}, bf16[4,2,320,1024]{3,2,1,0:T(8,128)(2,1)}, bf16[4,2,320,1024]{3,2,1,0:T(8,128)(2,1)}) custom-call(bf16[2,128,2560]{2,1,0:T(8,128)(2,1)S(1)} %convolution_convert_fusion.6.sent, ...), custom_call_target="tpu_custom_call", output_to_operand_aliasing={{2}: (4, {}), {3}: (5, {})} | custom-call | tf_op jit(solution)/shard_map/branch_and_group/pallas_call | solution.py:687
  346.5 9.4 %fusion.120 = f32[1024,1024]{1,0:T(8,128)} fusion(bf16[1024,2560]{1,0:T(8,128)(2,1)S(1)} %bitcast.112, bf16[2560,1024]{1,0:T(8,128)(2,1)} %bitcast.162), kind=kOutput, calls=%fused_computation.228 | convolution fusion | flops 5368709120 | bytes 14680064 | tf_op jit(solution)/shard_map/dot_general | solution.py:73
  355.9 9.2 %fusion.119 = f32[1024,1024]{1,0:T(8,128)} fusion(bf16[1024,2560]{1,0:T(8,128)(2,1)} %bitcast.157, bf16[2560,1024]{1,0:T(8,128)(2,1)S(1)} %bitcast.125), kind=kOutput, calls=%fused_computation.227 | convolution fusion | flops 5368709120 | bytes 14680064 | tf_op jit(solution)/shard_map/dot_general | solution.py:73
  365.1 11.0 %multiply_convert_fusion = (bf16[1024,1024]{1,0:T(8,128)(2,1)S(1)}, bf16[1024,1024]{1,0:T(8,128)(2,1)S(1)}, bf16[1024,1024]{1,0:T(8,128)(2,1)S(1)}) fusion(f32[1024,1024]{1,0:T(8,128)} %fusion.120, f32[1024,1024]{1,0:T(8,128)} %fusion.119, bf16[1024,2560]{1,0:T(8,128)(2,1)S(1)} %bitcast.113, bf16[2560,1024]{1,0:T(8,128)(2,1)S(1)} %bitcast.134), kind=kOutput, calls=%fused_computation.17 | convolution fusion | flops 5395972096 | bytes 25165824 | tf_op jit(solution)/shard_map/dot_general | solution.py:73
  376.2 4.7 fusion.55
  381.0 4.9 fusion.52
  385.8 4.3 convolution_convert_fusion.5
  390.1 4.3 convolution_convert_fusion.4
  394.4 4.2 convolution_convert_fusion.3
  398.6 4.2 convolution_convert_fusion.2
  402.8 4.2 convolution_convert_fusion.1
  407.1 4.2 convolution_convert_fusion
  411.3 6.1 add_convert_fusion
  417.4 4.7 convolution_add_fusion
  422.2 120.5 %middle_and_rows.1 = (bf16[4,128,2560]{2,1,0:T(8,128)(2,1)}, f32[128,2560]{1,0:T(8,128)}, f32[16,2560]{1,0:T(8,128)}, bf16[128,2560]{1,0:T(8,128)(2,1)}, bf16[3,...) custom-call(bf16[4,128,2560]{2,1,0:T(8,128)(2,1)} %bitcast.147, ...), custom_call_target="tpu_custom_call" | custom-call | tf_op jit(solution)/shard_map/middle_and_rows/pallas_call | solution.py:1038
  542.7 6.8 convert_multiply_fusion
  549.5 8.0 %scan_back.1 = (f32[512,640]{1,0:T(8,128)S(1)}, f32[1,640]{1,0:T(1,128)S(1)}) custom-call(f32[512,640]{1,0:T(8,128)S(1)} %get-tuple-element.153.factors, f32[512,640]{1,0:T(8,128)S(1)} %get-tuple-element.137.inflows), custom_call_target="tpu_custom_call" | custom-call | tf_op jit(solution)/shard_map/scan_back/pallas_call | solution.py:1565
  559.2 3.5 multiply_reduce_fusion.4
  562.7 2.9 fusion.107
  574.0 3.5 multiply_reduce_fusion
  578.4 2.8 collective-permute-start.4
  585.6 3.3 fusion.12
  588.9 3.2 fusion.10
  594.4 2.8 convolution_add_fusion.1
  598.2 175.4 %last_sums.1 = (bf16[3,320,2048]{2,1,0:T(8,128)(2,1)}, f32[320,1920]{1,0:T(8,128)}, f32[80,512]{1,0:T(8,128)}, bf16[128,2560]{1,0:T(8,128)(2,1)}, f32[16,128]{1,0:T(8,128)}, /*index=5*/f32[2,8,640]{2,1,0:T(8,128)}) custom-call(bf16[3,4,320,512]{3,2,1,0:T(8,128)(2,1)} %get-tuple-element.62.refs_0_, bf16[1,6,320,512]{3,2,1,0:T(8,128)(2,1)} %get-tuple-element.63.refs_1_, ...), custom_call_target="tpu_custom_call" | custom-call | tf_op jit(solution)/shard_map/last_sums/pallas_call | solution.py:1419
  774.4 3.2 fusion.110
  780.2 5.3 bitcast_convert_fusion
  786.0 6.2 collective-permute-done.5
  (260 shorter events, 50.2 us)
Async XLA Ops:
  225.3 19.3 %collective-permute-start = (bf16[3,640]{1,0:T(4,128)(2,1)S(1)}, bf16[3,640]{1,0:T(4,128)(2,1)S(1)}, u32[]{:S(2)}, u32[]{:S(2)}) collective-permute-start(bf16[3,640]{1,0:T(4,128)(2,1)S(1)} %slice.462), channel_id=1, source_target_pairs={{0,4},{4,8},{8,12},{12,16},{16,20},{20,24},{24,28},{1,5},{5,9},{9,... | collective-permute-start | bytes 11528 | tf_op jit(solution)/shard_map/ppermute | solution.py:1685
  240.9 6.3 collective-permute-start.2
  242.8 21.7 %copy-start.11 = (f32[1,2560]{1,0:T(1,128)}, f32[1,2560]{1,0:T(1,128)S(1)}, u32[]{:S(2)}) copy-start(f32[1,2560]{1,0:T(1,128)S(1)} %slice.404.gain.refs_4_) | copy-start | bytes 30724
  244.7 4.2 copy-start.12
  246.9 1.7 collective-permute-start.1
  247.1 4.4 copy-start.17
  247.2 4.3 copy-start.21
  251.5 7.9 copy-start.2
  346.5 9.4 %copy-start.10 = (f32[128,2560]{1,0:T(8,128)}, f32[128,2560]{1,0:T(8,128)S(1)}, u32[]{:S(2)}) copy-start(f32[128,2560]{1,0:T(8,128)S(1)} %get-tuple-element.60.refs_2_) | copy-start | bytes 3932164
  346.5 9.4 %copy-start.14 = (bf16[4,2,320,1024]{3,2,1,0:T(8,128)(2,1)S(1)}, bf16[4,2,320,1024]{3,2,1,0:T(8,128)(2,1)}, u32[]{:S(2)}) copy-start(bf16[4,2,320,1024]{3,2,1,0:T(8,128)(2,1)} %get-tuple-element.56) | copy-start | bytes 15728644
  346.5 18.6 %slice-start.2 = ((s8[5242880]{0:T(1024)(128)(4,1)}), s8[4194304]{0:T(1024)(128)(4,1)S(1)}, s32[]{:S(2)}) async-start(s8[5242880]{0:T(1024)(128)(4,1)} %bitcast.132), calls=%async_computation.2 | async-start | bytes 8388608
  355.9 9.2 %slice-start.3 = ((s8[5242880]{0:T(1024)(128)(4,1)}), s8[1048576]{0:T(1024)(128)(4,1)S(1)}, s32[]{:S(2)}) async-start(s8[5242880]{0:T(1024)(128)(4,1)} %bitcast.132), calls=%async_computation.3 | async-start | bytes 2097152
  355.9 20.2 %slice-start.12 = ((s8[5242880]{0:T(1024)(128)(4,1)}), s8[1048576]{0:T(1024)(128)(4,1)S(1)}, s32[]{:S(2)}) async-start(s8[5242880]{0:T(1024)(128)(4,1)} %bitcast.163), calls=%async_computation.12 | async-start | bytes 2097152
  365.1 11.1 %slice-start.13 = ((s8[5242880]{0:T(1024)(128)(4,1)}), s8[4194304]{0:T(1024)(128)(4,1)S(1)}, s32[]{:S(2)}) async-start(s8[5242880]{0:T(1024)(128)(4,1)} %bitcast.163), calls=%async_computation.13 | async-start | bytes 8388608
  376.2 30.9 %copy-start.36 = (bf16[1024,1024]{1,0:T(8,128)(2,1)}, bf16[1024,1024]{1,0:T(8,128)(2,1)S(1)}, u32[]{:S(2)}) copy-start(bf16[1024,1024]{1,0:T(8,128)(2,1)S(1)} %get-tuple-element.141.refs_5_) | copy-start | bytes 6291460
  394.4 8.5 %slice-start.10 = ((s8[5242880]{0:T(1024)(128)(4,1)}), s8[4194304]{0:T(1024)(128)(4,1)S(1)}, s32[]{:S(2)}) async-start(s8[5242880]{0:T(1024)(128)(4,1)} %bitcast.158), calls=%async_computation.10 | async-start | bytes 8388608
  398.6 4.2 slice-start.11
  407.1 10.3 %slice-start.14 = ((s8[5242880]{0:T(1024)(128)(4,1)}), s8[4194304]{0:T(1024)(128)(4,1)S(1)}, s32[]{:S(2)}) async-start(s8[5242880]{0:T(1024)(128)(4,1)} %bitcast.167), calls=%async_computation.14 | async-start | bytes 8388608
  411.3 6.1 slice-start.15
  422.2 120.5 %copy-start.3 = (f32[512,1280]{1,0:T(8,128)S(1)}, f32[512,1280]{1,0:T(8,128)}, u32[]{:S(2)}) copy-start(f32[512,1280]{1,0:T(8,128)} %copy-done.1) | copy-start | bytes 7864324
  542.7 15.0 %copy-start.28 = (f32[512,128]{1,0:T(8,128)S(1)}, f32[512,128]{1,0:T(8,128)}, u32[]{:S(2)}) copy-start(f32[512,128]{1,0:T(8,128)} %copy-done.27) | copy-start | bytes 786436
  549.5 8.2 %copy-start.13 = (f32[515,640]{1,0:T(8,128)S(1)}, f32[515,640]{1,0:T(8,128)}, u32[]{:S(2)}) copy-start(f32[515,640]{1,0:T(8,128)} %copy-done.12) | copy-start | bytes 3955204
  549.5 8.2 %copy-start.20 = (f32[512,256]{1,0:T(8,128)S(1)}, f32[512,256]{1,0:T(8,128)}, u32[]{:S(2)}) copy-start(f32[512,256]{1,0:T(8,128)} %copy-done.19) | copy-start | bytes 1572868
  549.5 8.2 %copy-start.22 = (f32[512,256]{1,0:T(8,128)S(1)}, f32[512,256]{1,0:T(8,128)}, u32[]{:S(2)}) copy-start(f32[512,256]{1,0:T(8,128)} %copy-done.21) | copy-start | bytes 1572868
  569.5 3.0 collective-permute-start.3
  577.4 7.4 copy-start.29
  578.4 6.5 collective-permute-start.4
  581.8 10.3 %slice-start = ((s8[6553600]{0:T(1024)(128)(4,1)}), s8[4194304]{0:T(1024)(128)(4,1)S(1)}, s32[]{:S(2)}) async-start(s8[6553600]{0:T(1024)(128)(4,1)} %bitcast.120), calls=%async_computation | async-start | bytes 8388608
  585.5 6.5 slice-start.1
  777.7 14.5 %collective-permute-start.5 = (f32[80,520]{1,0:T(8,128)S(1)}, f32[80,520]{1,0:T(8,128)S(1)}, u32[]{:S(2)}, u32[]{:S(2)}) collective-permute-start(f32[80,520]{1,0:T(8,128)S(1)} %pad_maximum_fusion.14), channel_id=1, source_target_pairs={{0,0},{4,1},{8,2},{12,3},{16,4},{20,5},{24,6},{28,7},{1,8},{5,9},{... | collective-permute-start | bytes 499208 | tf_op jit(solution)/shard_map/ppermute | solution.py:1835
  780.2 14.2 %copy-start.43 = (bf16[128,2560]{1,0:T(8,128)(2,1)S(1)}, bf16[128,2560]{1,0:T(8,128)(2,1)}, u32[]{:S(2)}) copy-start(bf16[128,2560]{1,0:T(8,128)(2,1)} %get-tuple-element.210) | copy-start | bytes 1966084
  785.5 9.8 %copy-start.44 = (bf16[128,2560]{1,0:T(8,128)(2,1)S(1)}, bf16[128,2560]{1,0:T(8,128)(2,1)}, u32[]{:S(2)}) copy-start(bf16[128,2560]{1,0:T(8,128)(2,1)} %get-tuple-element.211) | copy-start | bytes 1966084
  (47 other events, 82.9 us)

commit v12 on v10

--- a/solution.py
+++ b/solution.py
@@ -1508,7 +1508,7 @@
         return inflow[last], factor[last]
 
     held, product = lax.fori_loop(
-        0, rows // group, step, (jnp.zeros((1, width), F32), jnp.ones((1, width), F32))
+        0, rows // group, step, (jnp.zeros((1, width), F32), jnp.ones((1, width), F32)), unroll=4
     )
     ends[0:1] = product
     ends[1:2] = held
@@ -1549,7 +1549,7 @@
         states[where, :] += products[where, :] * entering
         return carried
 
-    lax.fori_loop(0, rows // group, spread, 0)
+    lax.fori_loop(0, rows // group, spread, 0, unroll=8)
 
     def sent(i, carried):
         pl.when(later(i))(lambda: copy_to(i).wait_send())

time: 803 us -> 803 us (level)
  no operation moved by 1% of the time
where the time goes in v12:
time: 803 us; the launch traced here: 798 us
  Pallas kernels  608 us (76%)
  matrix products  101 us (13%)
  other arithmetic  29.3 us (4%)
  local copies, waits for them, and re-layouts  28.2 us (4%)
  starting transfers between devices  20.5 us (3%)
  waiting for transfers between devices  8.27 us (1%)
    pallas_call x1, Pallas kernels, gather_all(): pl.pallas_call(functools.partial(gather_kernel, (inner, outer)), out_shap...  213 us
    pallas_call x1, Pallas kernels, last_sums(): pl.pallas_call(functools.partial(sums_kernel, (inner, outer)), out_shape=...  176 us
    pallas_call x1, Pallas kernels, middle_and_rows(): pl.pallas_call(functools.partial(middle_kernel, (inner, outer)), out_shap...  120 us
    pallas_call x1, Pallas kernels, branch_and_group(): pl.pallas_call(functools.partial(branch_kernel, (inner, outer)), out_shap...  82.6 us
    dot_general x7, matrix products, multiply(): return jnp.dot(left_side, right_side, preferred_element_type=F32)  37.2 us
    dot_general x13, matrix products, contract_last(): lax.dot_general(left_side, right_side, (((1,), (1,)), ((), ())), preferre...  35.5 us
    dot_general x9, matrix products, contract_rows(): lax.dot_general(left_side, right_side, (((0,), (0,)), ((), ())), preferre...  28.4 us
  transfers between devices with their start and end apart: 6, of which 3 were waited for; matrix products, arithmetic and copies ran while one was open for 2% of the time, Pallas kernels for 0%

profile of v12, /device:TPU:2, one launch (start us, length us, event | category | flops | bytes accessed | tf_op | source)
XLA Modules:
  0.0 797.6 jit_solution(15609700868147385284)
XLA Ops:
  2.2 2.6 pad.16.refs_7_
  9.1 213.2 %gather_all.1 = (bf16[2,4,128,2560]{3,2,1,0:T(8,128)(2,1)}, f32[32,16,128]{2,1,0:T(8,128)S(1)}, bf16[4,2,80,512]{3,2,1,0:T(8,128)(2,1)S(1)}, bf16[4,2,320,1280]{...) custom-call(bf16[128,2560]{1,0:T(8,128)(2,1)S(1)} %copy-done, ...), custom_call_target="tpu_custom_call" | custom-call | tf_op jit(solution)/shard_map/gather_all/pallas_call | solution.py:462
  225.3 15.2 %collective-permute-start = (bf16[3,640]{1,0:T(4,128)(2,1)S(1)}, bf16[3,640]{1,0:T(4,128)(2,1)S(1)}, u32[]{:S(2)}, u32[]{:S(2)}) collective-permute-start(bf16[3,640]{1,0:T(4,128)(2,1)S(1)} %slice.462), channel_id=1, source_target_pairs={{0,4},{4,8},{8,12},{12,16},{16,20},{20,24},{24,28},{1,5},{5,9},{9,... | collective-permute-start | bytes 11528 | tf_op jit(solution)/shard_map/ppermute | solution.py:1685
  251.5 7.8 scan_ahead.1
  264.5 82.6 %branch_and_group.1 = (bf16[2,4,128,2560]{3,2,1,0:T(8,128)(2,1)S(1)}, f32[128,2560]{1,0:T(8,128)S(1)}, bf16[4,2,320,1024]{3,2,1,0:T(8,128)(2,1)}, bf16[4,2,320,1024]{3,2,1,0:T(8,128)(2,1)}) custom-call(f32[2,128,2560]{2,1,0:T(8,128)S(1)} %fusion.67.sent, f32[2,128,2560]{2,1,0:T(8,128)S(1)} %fusion.65.own, ...), custom_call_target="tpu_custom_call", output_to_operand_aliasing={{2}: (4, {}), {3}: (5, {})} | custom-call | tf_op jit(solution)/shard_map/branch_and_group/pallas_call | solution.py:687
  347.2 9.4 %fusion.121 = f32[1024,1024]{1,0:T(8,128)} fusion(bf16[1024,2560]{1,0:T(8,128)(2,1)S(1)} %bitcast.112, bf16[2560,1024]{1,0:T(8,128)(2,1)} %bitcast.162), kind=kOutput, calls=%fused_computation.228 | convolution fusion | flops 5368709120 | bytes 14680064 | tf_op jit(solution)/shard_map/dot_general | solution.py:73
  356.6 9.2 %fusion.120 = f32[1024,1024]{1,0:T(8,128)} fusion(bf16[1024,2560]{1,0:T(8,128)(2,1)} %bitcast.157, bf16[2560,1024]{1,0:T(8,128)(2,1)S(1)} %bitcast.125), kind=kOutput, calls=%fused_computation.227 | convolution fusion | flops 5368709120 | bytes 14680064 | tf_op jit(solution)/shard_map/dot_general | solution.py:73
  365.8 11.0 %multiply_convert_fusion = (bf16[1024,1024]{1,0:T(8,128)(2,1)S(1)}, bf16[1024,1024]{1,0:T(8,128)(2,1)S(1)}, bf16[1024,1024]{1,0:T(8,128)(2,1)S(1)}) fusion(f32[1024,1024]{1,0:T(8,128)} %fusion.121, f32[1024,1024]{1,0:T(8,128)} %fusion.120, bf16[1024,2560]{1,0:T(8,128)(2,1)S(1)} %bitcast.113, bf16[2560,1024]{1,0:T(8,128)(2,1)S(1)} %bitcast.138), kind=kOutput, calls=%fused_computation.17 | convolution fusion | flops 5395972096 | bytes 25165824 | tf_op jit(solution)/shard_map/dot_general | solution.py:73
  376.9 4.7 fusion.55
  381.6 4.9 fusion.52
  386.5 4.3 convolution_convert_fusion.5
  390.8 4.3 convolution_convert_fusion.4
  395.0 4.2 convolution_convert_fusion.3
  399.2 4.2 convolution_convert_fusion.2
  403.5 4.2 convolution_convert_fusion.1
  407.7 4.2 convolution_convert_fusion
  412.0 6.1 add_convert_fusion
  418.1 4.7 convolution_add_fusion
  422.8 120.5 %middle_and_rows.1 = (bf16[4,128,2560]{2,1,0:T(8,128)(2,1)}, f32[128,2560]{1,0:T(8,128)}, f32[16,2560]{1,0:T(8,128)}, bf16[128,2560]{1,0:T(8,128)(2,1)}, bf16[3,...) custom-call(bf16[4,128,2560]{2,1,0:T(8,128)(2,1)} %bitcast.147, ...), custom_call_target="tpu_custom_call" | custom-call | tf_op jit(solution)/shard_map/middle_and_rows/pallas_call | solution.py:1038
  543.3 6.8 convert_multiply_fusion
  550.2 7.5 scan_back.1
  559.3 3.5 multiply_reduce_fusion.4
  562.8 2.9 fusion.108
  574.0 3.5 multiply_reduce_fusion
  578.4 3.2 collective-permute-start.4
  585.6 3.3 fusion.12
  588.9 3.2 fusion.10
  594.4 2.8 convolution_add_fusion.1
  598.3 176.3 %last_sums.1 = (bf16[3,320,2048]{2,1,0:T(8,128)(2,1)}, f32[320,1920]{1,0:T(8,128)}, f32[80,512]{1,0:T(8,128)}, bf16[128,2560]{1,0:T(8,128)(2,1)}, f32[16,128]{1,0:T(8,128)}, /*index=5*/f32[2,8,640]{2,1,0:T(8,128)}) custom-call(bf16[3,4,320,512]{3,2,1,0:T(8,128)(2,1)} %get-tuple-element.62.refs_0_, bf16[1,6,320,512]{3,2,1,0:T(8,128)(2,1)} %get-tuple-element.63.refs_1_, ...), custom_call_target="tpu_custom_call" | custom-call | tf_op jit(solution)/shard_map/last_sums/pallas_call | solution.py:1419
  775.3 3.2 fusion.111
  780.6 5.3 bitcast_convert_fusion
  786.4 7.0 collective-permute-done.5
  (260 shorter events, 49.4 us)
Async XLA Ops:
  225.3 19.3 %collective-permute-start = (bf16[3,640]{1,0:T(4,128)(2,1)S(1)}, bf16[3,640]{1,0:T(4,128)(2,1)S(1)}, u32[]{:S(2)}, u32[]{:S(2)}) collective-permute-start(bf16[3,640]{1,0:T(4,128)(2,1)S(1)} %slice.462), channel_id=1, source_target_pairs={{0,4},{4,8},{8,12},{12,16},{16,20},{20,24},{24,28},{1,5},{5,9},{9,... | collective-permute-start | bytes 11528 | tf_op jit(solution)/shard_map/ppermute | solution.py:1685
  240.9 6.3 collective-permute-start.2
  242.8 21.7 %copy-start.11 = (f32[1,2560]{1,0:T(1,128)}, f32[1,2560]{1,0:T(1,128)S(1)}, u32[]{:S(2)}) copy-start(f32[1,2560]{1,0:T(1,128)S(1)} %slice.404.gain.refs_4_) | copy-start | bytes 30724
  244.7 4.2 copy-start.12
  246.9 1.7 collective-permute-start.1
  247.1 4.4 copy-start.18
  251.5 7.9 copy-start.2
  259.4 3.9 copy-start.4
  347.2 9.4 %copy-start.10 = (f32[128,2560]{1,0:T(8,128)}, f32[128,2560]{1,0:T(8,128)S(1)}, u32[]{:S(2)}) copy-start(f32[128,2560]{1,0:T(8,128)S(1)} %get-tuple-element.60.refs_2_) | copy-start | bytes 3932164
  347.2 9.4 %copy-start.14 = (bf16[4,2,320,1024]{3,2,1,0:T(8,128)(2,1)S(1)}, bf16[4,2,320,1024]{3,2,1,0:T(8,128)(2,1)}, u32[]{:S(2)}) copy-start(bf16[4,2,320,1024]{3,2,1,0:T(8,128)(2,1)} %get-tuple-element.56) | copy-start | bytes 15728644
  347.2 18.6 %slice-start.2 = ((s8[5242880]{0:T(1024)(128)(4,1)}), s8[4194304]{0:T(1024)(128)(4,1)S(1)}, s32[]{:S(2)}) async-start(s8[5242880]{0:T(1024)(128)(4,1)} %bitcast.136), calls=%async_computation.2 | async-start | bytes 8388608
  356.6 9.2 %slice-start.3 = ((s8[5242880]{0:T(1024)(128)(4,1)}), s8[1048576]{0:T(1024)(128)(4,1)S(1)}, s32[]{:S(2)}) async-start(s8[5242880]{0:T(1024)(128)(4,1)} %bitcast.136), calls=%async_computation.3 | async-start | bytes 2097152
  356.6 20.2 %slice-start.12 = ((s8[5242880]{0:T(1024)(128)(4,1)}), s8[1048576]{0:T(1024)(128)(4,1)S(1)}, s32[]{:S(2)}) async-start(s8[5242880]{0:T(1024)(128)(4,1)} %bitcast.163), calls=%async_computation.12 | async-start | bytes 2097152
  365.8 11.1 %slice-start.13 = ((s8[5242880]{0:T(1024)(128)(4,1)}), s8[4194304]{0:T(1024)(128)(4,1)S(1)}, s32[]{:S(2)}) async-start(s8[5242880]{0:T(1024)(128)(4,1)} %bitcast.163), calls=%async_computation.13 | async-start | bytes 8388608
  376.8 30.9 %copy-start.36 = (bf16[1024,1024]{1,0:T(8,128)(2,1)}, bf16[1024,1024]{1,0:T(8,128)(2,1)S(1)}, u32[]{:S(2)}) copy-start(bf16[1024,1024]{1,0:T(8,128)(2,1)S(1)} %get-tuple-element.141.refs_5_) | copy-start | bytes 6291460
  395.0 8.5 %slice-start.10 = ((s8[5242880]{0:T(1024)(128)(4,1)}), s8[4194304]{0:T(1024)(128)(4,1)S(1)}, s32[]{:S(2)}) async-start(s8[5242880]{0:T(1024)(128)(4,1)} %bitcast.158), calls=%async_computation.10 | async-start | bytes 8388608
  399.2 4.2 slice-start.11
  407.7 10.3 %slice-start.14 = ((s8[5242880]{0:T(1024)(128)(4,1)}), s8[4194304]{0:T(1024)(128)(4,1)S(1)}, s32[]{:S(2)}) async-start(s8[5242880]{0:T(1024)(128)(4,1)} %bitcast.167), calls=%async_computation.14 | async-start | bytes 8388608
  412.0 6.1 slice-start.15
  422.8 120.5 %copy-start.3 = (f32[512,1280]{1,0:T(8,128)S(1)}, f32[512,1280]{1,0:T(8,128)}, u32[]{:S(2)}) copy-start(f32[512,1280]{1,0:T(8,128)} %copy-done.1) | copy-start | bytes 7864324
  543.3 14.5 %copy-start.29 = (f32[512,128]{1,0:T(8,128)S(1)}, f32[512,128]{1,0:T(8,128)}, u32[]{:S(2)}) copy-start(f32[512,128]{1,0:T(8,128)} %copy-done.28) | copy-start | bytes 786436
  550.1 7.7 copy-start.13
  550.2 7.6 copy-start.21
  550.2 7.6 copy-start.23
  569.6 3.0 collective-permute-start.3
  577.5 7.4 copy-start.30
  578.4 6.5 collective-permute-start.4
  582.2 9.9 %slice-start = ((s8[6553600]{0:T(1024)(128)(4,1)}), s8[4194304]{0:T(1024)(128)(4,1)S(1)}, s32[]{:S(2)}) async-start(s8[6553600]{0:T(1024)(128)(4,1)} %bitcast.120), calls=%async_computation | async-start | bytes 8388608
  585.6 6.5 slice-start.1
  778.6 14.7 %collective-permute-start.5 = (f32[80,520]{1,0:T(8,128)S(1)}, f32[80,520]{1,0:T(8,128)S(1)}, u32[]{:S(2)}, u32[]{:S(2)}) collective-permute-start(f32[80,520]{1,0:T(8,128)S(1)} %pad_maximum_fusion.14), channel_id=1, source_target_pairs={{0,0},{4,1},{8,2},{12,3},{16,4},{20,5},{24,6},{28,7},{1,8},{5,9},{... | collective-permute-start | bytes 499208 | tf_op jit(solution)/shard_map/ppermute | solution.py:1835
  780.6 15.0 %copy-start.43 = (bf16[128,2560]{1,0:T(8,128)(2,1)S(1)}, bf16[128,2560]{1,0:T(8,128)(2,1)}, u32[]{:S(2)}) copy-start(bf16[128,2560]{1,0:T(8,128)(2,1)} %get-tuple-element.210) | copy-start | bytes 1966084
  785.9 10.5 %copy-start.44 = (bf16[128,2560]{1,0:T(8,128)(2,1)S(1)}, bf16[128,2560]{1,0:T(8,128)(2,1)}, u32[]{:S(2)}) copy-start(bf16[128,2560]{1,0:T(8,128)(2,1)} %get-tuple-element.211) | copy-start | bytes 1966084
  (47 other events, 80.8 us)
